TPU v7x, 32 devices: a whole 2x2x4 slice. The times are simulated.
32 devices in a mesh: gx: 8 (over z, y), gy: 4 (over x, core).
Axes of the slice: x: 2, y: 2, z: 4, core: 2. Of those that a mesh axis runs over, the one named last changes fastest.
Arguments:
- head_old: float32 [10, 128, 2048], P(None, 'gx', 'gy'), may hold values from -4 to 4
- soil_type: int32 [10, 128, 2048], P(None, 'gx', 'gy'), may hold values from 0 to 11
- soil_table: float32 [3, 12], replicated, may hold values from 0.2 to 3, as said below
- forcing: float32 [4, 128, 2048], P(None, 'gx', 'gy'), may hold values from 0 to 2, as said below
- canopy: float32 [13, 65536], P(None, ('gx', 'gy')), may hold values from 0.05 to 6, as said below
- column_slot: int32 [128, 2048], P('gx', 'gy'), may hold values from -1 to 2047, as said below
Outputs:
- head_new: float32 [10, 128, 2048], P(None, 'gx', 'gy')
- surface_flux: float32 [2, 128, 2048], P(None, 'gx', 'gy')
Inputs may be any that keep to these rules, and one draw needn't show every extreme that they name: `soil_table`: Rows: conductivity 0.2 to 2, steepness 0.5 to 3, capacity 0.2 to 0.5. `forcing`: Rows: sunlight 0.5 to 2, air temperature 0.8 to 1.2, humidity 0 to 0.5, rainfall 0.1 to 2. `canopy`: Rows: leaf area 0.5 to 6, albedo 0.1 to 0.3, resistance 0.2 to 5, root weights 0.05 to 1. `column_slot`: the land cells of one device's tile name distinct values; the value v sends the column to the device of index v // 64 along gx+gy into slot v % 64; in every draw some device uses every value.
All inputs are finite; a program needn't handle non-finite values.
Results may differ from a plain program's by a relative error of at most 0.00029.
Values sent between devices are 32-bit elements; how exact they have to be, the bound alone decides.
No kernel may reach another device: no remote copies, remote signals or barrier semaphores. Data moves between devices by JAX's collectives and lax.ppermute only.
A program may use at most 64 MiB of HBM per device.

v0:
```python
import jax
import jax.numpy as jnp
from jax import lax
from jax.sharding import PartitionSpec as P

NEWTON = 2
KRYLOV = 3


storage_weight = 4.0
norm_epsilon = 1e-06


def padded_2(x, sides, width):
    for axis, dim in sides:
        size, length = (lax.axis_size(axis), x.shape[dim])
        up = [(i, (i + 1) % size) for i in range(size - 1)]
        down = [(j, i) for i, j in up]
        last = lax.slice_in_dim(x, length - width, length, axis=dim)
        initial = lax.slice_in_dim(x, 0, width, axis=dim)
        before = lax.ppermute(last, axis, up)
        after = lax.ppermute(initial, axis, down)
        x = jnp.concatenate([before, x, after], axis=dim)
    return x


def soil_fields(soil_type, soil_table):
    conduct = jnp.zeros(soil_type.shape, jnp.float32)
    steep = jnp.zeros(soil_type.shape, jnp.float32)
    capacity = jnp.zeros(soil_type.shape, jnp.float32)
    for kind in range(soil_table.shape[1]):
        match = soil_type == kind
        conduct = jnp.where(match, soil_table[0, kind], conduct)
        steep = jnp.where(match, soil_table[1, kind], steep)
        capacity = jnp.where(match, soil_table[2, kind], capacity)
    return jnp.stack([conduct, steep, capacity])


def balance(padded, params, theta_old, source):
    sat = jax.nn.sigmoid(params[1] * padded)
    conduct = params[0] * (0.1 + 0.9 * sat * sat)
    head = padded[:, 1:-1, 1:-1]
    inner = conduct[:, 1:-1, 1:-1]
    theta = params[2][:, 1:-1, 1:-1] * sat[:, 1:-1, 1:-1]
    lateral = jnp.zeros_like(head)
    for near_head, near_cond in (
        (padded[:, 2:, 1:-1], conduct[:, 2:, 1:-1]),
        (padded[:, :-2, 1:-1], conduct[:, :-2, 1:-1]),
        (padded[:, 1:-1, 2:], conduct[:, 1:-1, 2:]),
        (padded[:, 1:-1, :-2], conduct[:, 1:-1, :-2]),
    ):
        lateral = lateral + 0.5 * (inner + near_cond) * (head - near_head)
    face = 0.5 * (inner[:-1] + inner[1:]) * (head[:-1] - head[1:] + 1.0)
    below = jnp.concatenate([face, inner[-1:]], axis=0)
    above = jnp.concatenate([jnp.zeros_like(head[:1]), face], axis=0)
    return storage_weight * (theta - theta_old) + lateral + below - above - source


def land_column(wet, ks_top, forcing, records):
    sunlight, air_temp, humidity, rainfall = (forcing[0], forcing[1], forcing[2], forcing[3])
    leaf_area, albedo, resist = (records[0], records[1], records[2])
    roots = records[3:]
    uptake = roots * wet
    total = jnp.sum(uptake, axis=0)
    wetness = total / jnp.sum(roots, axis=0)
    conductance = wetness * leaf_area / (leaf_area + resist)
    exchange_coef = 0.5 + 0.3 * leaf_area
    radiation = (1.0 - albedo) * sunlight + 0.3
    surface = air_temp
    for sweep_index in range(2):
        vapour = 0.5 * jnp.exp(2.0 * (surface - air_temp))
        square = surface * surface
        excess = (
            radiation
            - 0.3 * square * square
            - exchange_coef * (surface - air_temp)
            - conductance * (vapour - humidity)
        )
        slope = -1.2 * square * surface - exchange_coef - 2.0 * conductance * vapour
        surface = surface - excess / slope
    vapour = 0.5 * jnp.exp(2.0 * (surface - air_temp))
    evaporation = conductance * (vapour - humidity)
    infiltration = rainfall * ks_top / (rainfall + ks_top)
    sink = evaporation * uptake / total
    return (sink, evaporation, infiltration)


def surface_terms(land, sink, evaporation, infiltration):
    source = jnp.where(land, -sink, 0.0)
    source = source.at[0].add(jnp.where(land, infiltration, 0.0))
    flux = jnp.stack([jnp.where(land, evaporation, 0.0), jnp.where(land, infiltration, 0.0)])
    return (source, flux)


def small_solve(hessen, initial_norm):
    gram = jnp.dot(hessen.T, hessen, precision=lax.Precision.HIGHEST)
    target = hessen[0] * initial_norm
    factor = jnp.linalg.cholesky(gram)
    size = gram.shape[0]
    forward = []
    for row in range(size):
        value = target[row]
        for other in range(row):
            value = value - factor[row, other] * forward[other]
        forward.append(value / factor[row, row])
    backward = [None] * size
    for row in reversed(range(size)):
        value = forward[row]
        for other in range(row + 1, size):
            value = value - factor[other, row] * backward[other]
        backward[row] = value / factor[row, row]
    return jnp.stack(backward)


def shards(head_old, soil_type, soil_table, forcing, canopy, column_slot):
    layers, rows_x, rows_y = head_old.shape
    params = soil_fields(soil_type, soil_table)
    wet = jax.nn.sigmoid(params[1] * head_old)
    theta_old = params[2] * wet
    land = column_slot >= 0
    flat_slot = jnp.maximum(column_slot, 0).reshape(-1)
    outgoing = jnp.concatenate(
        [wet.reshape(layers, -1), params[0, 0].reshape(1, -1), forcing.reshape(4, -1)], axis=0
    )
    target = jnp.where(land, column_slot, canopy.shape[1]).reshape(-1)
    buffer = (
        jnp.zeros((outgoing.shape[0], canopy.shape[1]), jnp.float32)
        .at[:, target]
        .set(outgoing, mode="drop")
    )
    arrived = lax.all_to_all(buffer, ("gx", "gy"), split_axis=1, concat_axis=1, tiled=True)
    sink, evaporation, infiltration = land_column(
        arrived[:layers], arrived[layers], arrived[layers + 1 :], canopy
    )
    results = jnp.concatenate([sink, evaporation[None], infiltration[None]], axis=0)
    returned = lax.all_to_all(results, ("gx", "gy"), split_axis=1, concat_axis=1, tiled=True)
    local = jnp.take(returned, flat_slot, axis=1).reshape(layers + 2, rows_x, rows_y)
    sink, evaporation, infiltration = (local[:layers], local[layers], local[layers + 1])
    source, surface_flux = surface_terms(land, sink, evaporation, infiltration)
    padded_params = padded_2(params, (("gx", 2), ("gy", 3)), 1)
    head = head_old
    padded = head_old
    for newton_step in range(NEWTON):
        padded = padded_2(head, (("gx", 1), ("gy", 2)), 1)

        def residual_of(field):
            return balance(field, padded_params, theta_old, source)

        residual_now = residual_of(padded)
        initial_norm = jnp.sqrt(
            lax.psum(jnp.sum(residual_now * residual_now), ("gx", "gy")) + norm_epsilon
        )
        basis = [residual_now / initial_norm]
        rims = []
        hessen = jnp.zeros((KRYLOV + 1, KRYLOV), jnp.float32)
        for krylov_step in range(KRYLOV):
            rim = padded_2(basis[krylov_step], (("gx", 1), ("gy", 2)), 1)
            rims.append(rim)
            direction = jax.jvp(residual_of, (padded,), (rim,))[1]
            local_sums = jnp.stack([jnp.sum(direction * earlier) for earlier in basis])
            products = lax.psum(local_sums, ("gx", "gy"))
            for index, earlier in enumerate(basis):
                direction = direction - products[index] * earlier
            hessen = hessen.at[: len(basis), krylov_step].set(products)
            length = jnp.sqrt(lax.psum(jnp.sum(direction * direction), ("gx", "gy")) + norm_epsilon)
            hessen = hessen.at[krylov_step + 1, krylov_step].set(length)
            if krylov_step + 1 < KRYLOV:
                basis.append(direction / length)
        weights = small_solve(hessen, initial_norm)
        for index, earlier in enumerate(basis):
            head = head - weights[index] * earlier
    return (head, surface_flux)


def solution(mesh):
    return jax.shard_map(
        shards,
        mesh=mesh,
        in_specs=(
            P(None, "gx", "gy"),
            P(None, "gx", "gy"),
            P(),
            P(None, "gx", "gy"),
            P(None, ("gx", "gy")),
            P("gx", "gy"),
        ),
        out_specs=(P(None, "gx", "gy"), P(None, "gx", "gy")),
        check_vma=False,
    )
```

profile of v0, /device:TPU:0, one launch (start us, length us, event | category | flops | bytes accessed | tf_op | source)
XLA Modules:
  0.0 979.3 jit_solution(10501233269490507364)
XLA Ops:
  7.2 9.2 add_divide_fusion
  16.5 8.1 select_bitcast_fusion.1
  27.7 21.1 %scatter_custom_fusion = f32[15,2048]{0,1:T(8,128)S(1)} fusion(s32[8192]{0:T(1024)S(1)} %bitcast.230, f32[8192,15]{1,0:T(8,128)} %copy.44, f32[]{:T(128)} %constant.370.clone.1), kind=kCustom, calls=%fused_computation.59 | custom fusion | bytes 123392 | tf_op jit(solution)/shard_map/scatter | solution.py:129
  50.0 7.4 all-to-all-start
  57.5 7.9 select_select_fusion
  72.7 5.1 collective-permute-start.4
  98.8 8.8 all-to-all-start.1
  108.6 6.9 all-to-all-done.1
  116.9 27.8 %gather_fusion = f32[8192,12]{1,0:T(8,128)} fusion(f32[12,2048]{0,1:T(8,128)S(1)} %bitcast.205, s32[8192]{0:T(1024)S(1)} %broadcast_clamp_fusion), kind=kCustom, calls=%fused_computation | custom fusion | bytes 819200 | tf_op jit(solution)/shard_map/jit(_take)/gather | solution.py:137
  144.7 6.2 select_bitcast_fusion
  162.5 5.3 multiply_reduce_fusion.19
  167.8 38.5 %psum.98 = f32[]{:T(128)} all-reduce(f32[]{:T(128)} %get-tuple-element.211), channel_id=1, replica_groups=mesh['gx'=8,'gy'=4] {'gx','gy'}, use_global_device_ids=true, to_apply=%region_4.5 | all-reduce | flops 1 | bytes 8 | tf_op jit(solution)/shard_map/psum | solution.py:151
  208.3 5.0 collective-permute-start.8
  225.8 44.2 %psum.99 = f32[1]{0:T(128)} all-reduce(f32[1]{0:T(128)} %bitcast.53), channel_id=1, replica_groups=mesh['gx'=8,'gy'=4] {'gx','gy'}, use_global_device_ids=true, to_apply=%region_6.7 | all-reduce | flops 1 | bytes 8 | tf_op jit(solution)/shard_map/psum | solution.py:161
  272.4 40.8 %psum.100 = f32[]{:T(128)} all-reduce(f32[]{:T(128)} %multiply_reduce_fusion.17), channel_id=1, replica_groups=mesh['gx'=8,'gy'=4] {'gx','gy'}, use_global_device_ids=true, to_apply=%region_8.9 | all-reduce | flops 1 | bytes 8 | tf_op jit(solution)/shard_map/psum | solution.py:165
  316.9 5.4 collective-permute-start.12
  336.0 44.0 %psum.101 = f32[2]{0:T(128)S(1)} all-reduce(f32[2]{0:T(128)S(1)} %pad_maximum_fusion.99), channel_id=1, replica_groups=mesh['gx'=8,'gy'=4] {'gx','gy'}, use_global_device_ids=true, to_apply=%region_12.13 | all-reduce | flops 2 | bytes 16 | tf_op jit(solution)/shard_map/psum | solution.py:161
  384.2 41.1 %psum.102 = f32[]{:T(128)} all-reduce(f32[]{:T(128)} %get-tuple-element.202), channel_id=1, replica_groups=mesh['gx'=8,'gy'=4] {'gx','gy'}, use_global_device_ids=true, to_apply=%region_14.15 | all-reduce | flops 1 | bytes 8 | tf_op jit(solution)/shard_map/psum | solution.py:165
  428.9 5.6 collective-permute-start.16
  455.1 41.5 %psum.103 = f32[3]{0:T(128)S(1)} all-reduce(f32[3]{0:T(128)S(1)} %pad_maximum_fusion.100), channel_id=1, replica_groups=mesh['gx'=8,'gy'=4] {'gx','gy'}, use_global_device_ids=true, to_apply=%region_19.20 | all-reduce | flops 3 | bytes 24 | tf_op jit(solution)/shard_map/psum | solution.py:161
  504.3 39.5 %psum.104 = f32[]{:T(128)} all-reduce(f32[]{:T(128)} %multiply_reduce_fusion.10), channel_id=1, replica_groups=mesh['gx'=8,'gy'=4] {'gx','gy'}, use_global_device_ids=true, to_apply=%region_21.22 | all-reduce | flops 1 | bytes 8 | tf_op jit(solution)/shard_map/psum | solution.py:165
  560.2 5.1 collective-permute-start.20
  576.6 45.0 %psum.105 = f32[]{:T(128)} all-reduce(f32[]{:T(128)} %get-tuple-element.188), channel_id=1, replica_groups=mesh['gx'=8,'gy'=4] {'gx','gy'}, use_global_device_ids=true, to_apply=%region_25.27 | all-reduce | flops 1 | bytes 8 | tf_op jit(solution)/shard_map/psum | solution.py:151
  623.6 5.1 collective-permute-start.24
  641.4 45.4 %psum.106 = f32[1]{0:T(128)} all-reduce(f32[1]{0:T(128)} %bitcast.85), channel_id=1, replica_groups=mesh['gx'=8,'gy'=4] {'gx','gy'}, use_global_device_ids=true, to_apply=%region_27.29 | all-reduce | flops 1 | bytes 8 | tf_op jit(solution)/shard_map/psum | solution.py:161
  689.2 41.0 %psum.107 = f32[]{:T(128)} all-reduce(f32[]{:T(128)} %multiply_reduce_fusion.7), channel_id=1, replica_groups=mesh['gx'=8,'gy'=4] {'gx','gy'}, use_global_device_ids=true, to_apply=%region_29.31 | all-reduce | flops 1 | bytes 8 | tf_op jit(solution)/shard_map/psum | solution.py:165
  734.0 5.1 collective-permute-start.28
  755.6 43.9 %psum.108 = f32[2]{0:T(128)S(1)} all-reduce(f32[2]{0:T(128)S(1)} %pad_maximum_fusion.101), channel_id=1, replica_groups=mesh['gx'=8,'gy'=4] {'gx','gy'}, use_global_device_ids=true, to_apply=%region_32.34 | all-reduce | flops 2 | bytes 16 | tf_op jit(solution)/shard_map/psum | solution.py:161
  803.9 40.3 %psum.109 = f32[]{:T(128)} all-reduce(f32[]{:T(128)} %get-tuple-element.179), channel_id=1, replica_groups=mesh['gx'=8,'gy'=4] {'gx','gy'}, use_global_device_ids=true, to_apply=%region_34.36 | all-reduce | flops 1 | bytes 8 | tf_op jit(solution)/shard_map/psum | solution.py:165
  848.6 5.0 collective-permute-start.32
  875.3 41.9 %psum.110 = f32[3]{0:T(128)S(1)} all-reduce(f32[3]{0:T(128)S(1)} %pad_maximum_fusion.102), channel_id=1, replica_groups=mesh['gx'=8,'gy'=4] {'gx','gy'}, use_global_device_ids=true, to_apply=%region_38.40 | all-reduce | flops 3 | bytes 24 | tf_op jit(solution)/shard_map/psum | solution.py:161
  924.8 39.6 %psum.111 = f32[]{:T(128)} all-reduce(f32[]{:T(128)} %multiply_reduce_fusion), channel_id=1, replica_groups=mesh['gx'=8,'gy'=4] {'gx','gy'}, use_global_device_ids=true, to_apply=%region_40.42 | all-reduce | flops 1 | bytes 8 | tf_op jit(solution)/shard_map/psum | solution.py:165
  (382 shorter events, 214.9 us)
Async XLA Ops:
  50.0 43.1 %all-to-all-start = ((f32[32,1,960]{2,1,0:T(1,128)}), f32[32,1,960]{2,1,0:T(1,128)}, u32[]{:S(2)}, u32[]{:S(2)}) async-start(f32[32,1,960]{2,1,0:T(1,128)} %reshape.648), calls=%async_computation | async-start | bytes 262144 | tf_op jit(solution)/shard_map/all_to_all | solution.py:131
  65.5 13.1 %collective-permute-start.1 = (f32[3,10,1,512]{3,2,1,0:T(1,128)S(1)}, f32[3,10,1,512]{3,2,1,0:T(1,128)S(1)}, u32[]{:S(2)}, u32[]{:S(2)}) collective-permute-start(f32[3,10,1,512]{3,2,1,0:T(1,128)S(1)} %get-tuple-element.246), channel_id=1, source_target_pairs={{4,0},{8,4},{12,8},{16,12},{20,16},{24,20},{28,24},{5,1},{9,5},{13... | collective-permute-start | bytes 184328 | tf_op jit(solution)/shard_map/ppermute | solution.py:22
  66.8 11.8 %collective-permute-start = (f32[3,10,1,512]{3,2,1,0:T(1,128)S(1)}, f32[3,10,1,512]{3,2,1,0:T(1,128)S(1)}, u32[]{:S(2)}, u32[]{:S(2)}) collective-permute-start(f32[3,10,1,512]{3,2,1,0:T(1,128)S(1)} %get-tuple-element.245), channel_id=1, source_target_pairs={{0,4},{4,8},{8,12},{12,16},{16,20},{20,24},{24,28},{1,5},{5,9},{9,... | collective-permute-start | bytes 184328 | tf_op jit(solution)/shard_map/ppermute | solution.py:21
  71.4 11.8 %collective-permute-start.5 = (f32[10,1,512]{2,1,0:T(1,128)S(1)}, f32[10,1,512]{2,1,0:T(1,128)S(1)}, u32[]{:S(2)}, u32[]{:S(2)}) collective-permute-start(f32[10,1,512]{2,1,0:T(1,128)S(1)} %get-tuple-element.278), channel_id=1, source_target_pairs={{4,0},{8,4},{12,8},{16,12},{20,16},{24,20},{28,24},{5,1},{9,5},{13... | collective-permute-start | bytes 61448 | tf_op jit(solution)/shard_map/ppermute | solution.py:22
  72.7 10.5 %collective-permute-start.4 = (f32[10,1,512]{2,1,0:T(1,128)S(1)}, f32[10,1,512]{2,1,0:T(1,128)S(1)}, u32[]{:S(2)}, u32[]{:S(2)}) collective-permute-start(f32[10,1,512]{2,1,0:T(1,128)S(1)} %get-tuple-element.277), channel_id=1, source_target_pairs={{0,4},{4,8},{8,12},{12,16},{16,20},{20,24},{24,28},{1,5},{5,9},{9,... | collective-permute-start | bytes 61448 | tf_op jit(solution)/shard_map/ppermute | solution.py:21
  78.8 9.4 collective-permute-start.3
  80.1 8.1 collective-permute-start.2
  83.3 6.1 collective-permute-start.7
  84.6 4.8 collective-permute-start.6
  98.8 16.7 %all-to-all-start.1 = ((f32[32,1,768]{2,1,0:T(1,128)}), f32[32,1,768]{2,1,0:T(1,128)S(1)}, u32[]{:S(2)}, u32[]{:S(2)}) async-start(f32[32,1,768]{2,1,0:T(1,128)} %reshape.650), calls=%async_computation.1 | async-start | bytes 196608 | tf_op jit(solution)/shard_map/all_to_all | solution.py:136
  207.0 6.3 collective-permute-start.9
  208.3 6.4 collective-permute-start.8
  214.9 4.5 collective-permute-start.11
  315.6 7.4 collective-permute-start.13
  316.9 6.9 collective-permute-start.12
  323.8 4.9 collective-permute-start.15
  427.6 9.0 collective-permute-start.17
  428.9 7.7 collective-permute-start.16
  438.1 8.1 collective-permute-start.19
  439.4 6.8 collective-permute-start.18
  558.9 6.4 collective-permute-start.21
  560.2 6.6 collective-permute-start.20
  566.9 4.5 collective-permute-start.23
  622.3 6.4 collective-permute-start.25
  623.6 6.5 collective-permute-start.24
  732.7 6.4 collective-permute-start.29
  734.0 6.6 collective-permute-start.28
  741.3 5.6 collective-permute-start.31
  847.4 8.5 collective-permute-start.33
  848.6 7.2 collective-permute-start.32
  857.5 8.8 collective-permute-start.35
  858.8 7.5 collective-permute-start.34
  (82 other events, 658.7 us)
where the time goes:
time: 991 us; the launch traced here: 979 us
  blocking collectives  587 us (59%)
  other arithmetic  137 us (14%)
  starting transfers between devices  116 us (12%)
  local copies, waits for them, and re-layouts  94.9 us (10%)
  between operations  27.5 us (3%)
  waiting for transfers between devices  16.8 us (2%)
    psum x6, blocking collectives, shards(): products = lax.psum(local_sums, ('gx', 'gy'))  261 us
    psum x6, blocking collectives, shards(): lax.psum(jnp.sum(direction * direction), ('gx', 'gy')) + norm_epsilon  242 us
    psum x2, blocking collectives, shards(): lax.psum(jnp.sum(residual_now * residual_now), ('gx', 'gy')) + norm_epsilon  83.5 us
    ppermute x18, starting transfers between devices, padded_2(): before = lax.ppermute(last, axis, up)  76.1 us
    gather x1, local copies, waits for them, and re-layouts, shards(): jnp.take(returned, flat_slot, axis=1).reshape(layers + 2, rows_x, rows_y)  27.8 us
    ppermute x18, starting transfers between devices, padded_2(): after = lax.ppermute(initial, axis, down)  23.2 us
    scatter x1, local copies, waits for them, and re-layouts, shards(): buffer = jnp.zeros((outgoing.shape[0], canopy.shape[1]), jnp.float32).at[...  21.1 us
  transfers between devices with their start and end apart: 38, of which 10 were waited for; matrix products, arithmetic and copies ran while one was open for 3% of the time, Pallas kernels for 0%

commit v1 on v0

v1 whole, which is shorter than its diff:
```python
import functools

import jax
import jax.numpy as jnp
from jax import lax
from jax.experimental import pallas as pl
from jax.experimental.pallas import tpu as pltpu
from jax.sharding import PartitionSpec as P

NEWTON = 2
KRYLOV = 3
HALO = 8
LANES = 128
SLOT = 64

storage_weight = 4.0
norm_epsilon = 1e-06

VMEM_LIMIT = 40 * 1024 * 1024
PAIRS = [(i, j) for i in range(KRYLOV + 1) for j in range(i, KRYLOV + 1)]
HALF = (len(PAIRS) + 1) // 2

f32 = jnp.float32
vmem = pl.BlockSpec(memory_space=pltpu.VMEM)
smem = pl.BlockSpec(memory_space=pltpu.SMEM)


def call(body, outs, n_in, scratch=(), in_specs=None, flops=1000000):
    return pl.pallas_call(
        body,
        out_shape=[jax.ShapeDtypeStruct(s, d) for s, d in outs],
        in_specs=in_specs or [vmem] * n_in,
        out_specs=[vmem] * len(outs),
        scratch_shapes=list(scratch),
        compiler_params=pltpu.CompilerParams(vmem_limit_bytes=VMEM_LIMIT),
        cost_estimate=pl.CostEstimate(flops=flops, bytes_accessed=1000000, transcendentals=0),
    )


def lane_iota(shape):
    return lax.broadcasted_iota(jnp.int32, shape, len(shape) - 1)


def pack_canopy(canopy_ref, out_ref):
    rows = canopy_ref.shape[0]
    tiles = canopy_ref.shape[1] // LANES
    low = lane_iota((8, LANES)) < SLOT

    def step(t, _):
        here = pl.ds(pl.multiple_of(t * LANES, LANES), LANES)
        first = canopy_ref[0:8, here]
        rest = canopy_ref[8:rows, here]
        rest = jnp.concatenate([rest, jnp.zeros((16 - rows, LANES), f32)], axis=0)
        out_ref[2 * t] = jnp.where(low, first, pltpu.roll(rest, SLOT, 1))
        out_ref[2 * t + 1] = jnp.where(low, pltpu.roll(first, SLOT, 1), rest)
        return 0

    lax.fori_loop(0, tiles, step, 0)


def pack_kernel(canopy_ref, head_ref, soil_ref, send_ref, down_ref, up_ref):
    layers, rows, _ = head_ref.shape
    down_ref[0:layers] = head_ref[:, 0:HALO, :]
    up_ref[0:layers] = head_ref[:, rows - HALO : rows, :]
    down_ref[layers : 2 * layers] = (soil_ref[:, 0:HALO, :] + 1).astype(f32)
    up_ref[layers : 2 * layers] = (soil_ref[:, rows - HALO : rows, :] + 1).astype(f32)
    pack_canopy(canopy_ref, send_ref)


def table_rows(table_ref, rows):
    lane = lane_iota((rows, LANES))
    out = []
    for field in range(table_ref.shape[0]):
        row = jnp.zeros((rows, LANES), f32)
        for kind in range(table_ref.shape[1]):
            row = jnp.where(lane == kind + 1, table_ref[field, kind], row)
        out.append(row)
    return out


def lookup(row, index):
    pieces = [
        jnp.take_along_axis(row, index[:, at : at + LANES], axis=1, mode="promise_in_bounds")
        for at in range(0, index.shape[1], LANES)
    ]
    return jnp.concatenate(pieces, axis=1)


def sigmoid(u):
    return 1.0 / (1.0 + jnp.exp(-u))


def source_kernel(
    table_ref, arrived_ref, head_ref, soil_ref, forcing_ref, slot_ref,
    source_ref, down_ref, up_ref, flux_ref, tab_ref,
):
    layers, rows, cols = head_ref.shape
    owners = arrived_ref.shape[0]
    low = lane_iota((8, LANES)) < SLOT
    records = 3 + layers

    def unpack(t, _):
        first = arrived_ref[2 * t]
        second = arrived_ref[2 * t + 1]
        tab_ref[t, 0:8] = jnp.where(low, first, pltpu.roll(second, SLOT, 1))
        tab_ref[t, 8:16] = jnp.where(low, pltpu.roll(first, SLOT, 1), second)
        return 0

    lax.fori_loop(0, owners // 2, unpack, 0)
    tables = table_rows(table_ref, 8)

    for at_x in range(0, rows, 8):
        for at_y in range(0, cols, LANES):
            here = (slice(at_x, at_x + 8), slice(at_y, at_y + LANES))
            slot = slot_ref[here]
            land = slot >= 0
            value = jnp.maximum(slot, 0)
            lane = value & (LANES - 1)
            tile = value >> 7

            def pick(t, held):
                match = tile == t
                out = []
                for k in range(records):
                    row = jnp.broadcast_to(tab_ref[t, k : k + 1, :], (8, LANES))
                    got = jnp.take_along_axis(row, lane, axis=1, mode="promise_in_bounds")
                    out.append(jnp.where(match, got, held[k]))
                return tuple(out)

            picked = lax.fori_loop(
                0, owners // 2, pick, tuple(jnp.ones((8, LANES), f32) for _ in range(records)),
                unroll=4,
            )
            leaf_area, albedo, resist = picked[:3]
            roots = picked[3:]
            uptake = []
            for k in range(layers):
                index = soil_ref[(k,) + here] + 1
                steep = lookup(tables[1], index)
                uptake.append(roots[k] * sigmoid(steep * head_ref[(k,) + here]))
                if k == 0:
                    ks_top = lookup(tables[0], index)
            total = functools.reduce(jnp.add, uptake)
            root_sum = functools.reduce(jnp.add, roots)
            sunlight, air_temp, humidity, rainfall = (forcing_ref[(i,) + here] for i in range(4))
            conductance = total / root_sum * (leaf_area / (leaf_area + resist))
            exchange_coef = 0.5 + 0.3 * leaf_area
            radiation = (1.0 - albedo) * sunlight + 0.3
            surface = air_temp
            for _ in range(2):
                vapour = 0.5 * jnp.exp(2.0 * (surface - air_temp))
                square = surface * surface
                excess = (
                    radiation
                    - 0.3 * square * square
                    - exchange_coef * (surface - air_temp)
                    - conductance * (vapour - humidity)
                )
                slope = -1.2 * square * surface - exchange_coef - 2.0 * conductance * vapour
                surface = surface - excess / slope
            vapour = 0.5 * jnp.exp(2.0 * (surface - air_temp))
            evaporation = conductance * (vapour - humidity)
            infiltration = rainfall * ks_top / (rainfall + ks_top)
            rate = evaporation / total
            evaporation = jnp.where(land, evaporation, 0.0)
            infiltration = jnp.where(land, infiltration, 0.0)
            rate = jnp.where(land, rate, 0.0)
            flux_ref[(0,) + here] = evaporation
            flux_ref[(1,) + here] = infiltration
            for k in range(layers):
                value = -rate * uptake[k]
                if k == 0:
                    value = value + infiltration
                source_ref[(k,) + here] = value
                if at_x < HALO:
                    down_ref[(k,) + here] = value
                if at_x >= rows - HALO:
                    up_ref[(k, slice(at_x - rows + HALO, at_x - rows + HALO + 8), here[1])] = value


def strips(top, above, below, at, shift_from):
    layers = top.shape[0]
    lane = lane_iota((top.shape[1] + 2 * HALO, LANES))
    packed = jnp.zeros(lane.shape, f32)
    for k in range(layers):
        plane = jnp.concatenate([top[k], above[k], below[k]], axis=0)
        shift = (HALO * k - shift_from) % LANES
        moved = pltpu.roll(plane, shift, 1) if shift else plane
        inside = (lane >= HALO * k) & (lane < HALO * (k + 1))
        packed = jnp.where(inside, moved, packed)
    return packed


def strip_kernel(head_ref, soil_ref, lo_ref, hi_ref, src_ref, slo_ref, shi_ref, down_ref, up_ref):
    layers, rows, cols = head_ref.shape
    for out_ref, at, shift_from in ((down_ref, 0, 0), (up_ref, cols - LANES, LANES - HALO)):
        part = slice(at, at + LANES)
        out_ref[0] = strips(
            head_ref[:, :, part], hi_ref[0:layers, :, part], lo_ref[0:layers, :, part], at, shift_from
        )
        out_ref[1] = strips(
            (soil_ref[:, :, part] + 1).astype(f32),
            hi_ref[layers : 2 * layers, :, part],
            lo_ref[layers : 2 * layers, :, part],
            at,
            shift_from,
        )
        out_ref[2] = strips(src_ref[:, :, part], shi_ref[:, :, part], slo_ref[:, :, part], at, shift_from)


def after(x, axis):
    return pltpu.roll(x, x.shape[axis] - 1, axis)


def before(x, axis):
    return pltpu.roll(x, 1, axis)


def krylov(head_ref, base_ref, index_ref, tables, basis, scratch, gram_ref, tile):
    layers = head_ref.shape[0]
    ax_ref, bx_ref, ay_ref, by_ref, az_ref, bz_ref, store_ref, cond_ref, deriv_ref, mask_ref = scratch
    for k in range(layers):
        index = index_ref[k]
        conduct, steep, capacity = (lookup(row, index) for row in tables)
        sat = sigmoid(steep * head_ref[k])
        slope = steep * sat * (1.0 - sat)
        cond_ref[k] = conduct * (0.1 + 0.9 * sat * sat)
        deriv_ref[k] = 0.9 * conduct * sat * slope
        store_ref[k] = storage_weight * capacity * slope
        mask_ref[k] = (index > 0).astype(f32)
        basis[0][k] = storage_weight * capacity * sat - base_ref[k]
    above = None
    for k in range(layers):
        head = head_ref[k]
        cond = cond_ref[k]
        deriv = deriv_ref[k]
        value = basis[0][k]
        for a_ref, b_ref, axis in ((ax_ref, bx_ref, 0), (ay_ref, by_ref, 1)):
            mean = 0.5 * (cond + after(cond, axis))
            drop = head - after(head, axis)
            a_ref[k] = mean + deriv * drop
            b_ref[k] = mean - after(deriv, axis) * drop
            face = mean * drop
            value = value + face - before(face, axis)
        if k + 1 < layers:
            mean = 0.5 * (cond + cond_ref[k + 1])
            drop = head - head_ref[k + 1] + 1.0
            az_ref[k] = mean + deriv * drop
            bz_ref[k] = mean - deriv_ref[k + 1] * drop
            face = mean * drop
        else:
            az_ref[k] = 2.0 * deriv
            face = cond
        value = value + face
        if above is not None:
            value = value - above
        above = face
        basis[0][k] = value * mask_ref[k]
    for j in range(KRYLOV):
        v_ref, w_ref = basis[j], basis[j + 1]
        above = None
        for k in range(layers):
            v = v_ref[k]
            value = store_ref[k] * v
            for a_ref, b_ref, axis in ((ax_ref, bx_ref, 0), (ay_ref, by_ref, 1)):
                face = a_ref[k] * v - b_ref[k] * after(v, axis)
                value = value + face - before(face, axis)
            face = az_ref[k] * v
            if k + 1 < layers:
                face = face - bz_ref[k] * v_ref[k + 1]
            value = value + face
            if above is not None:
                value = value - above
            above = face
            w_ref[k] = value * mask_ref[k]
    rows, cols = tile
    sums = [jnp.zeros((8, LANES), f32) for _ in PAIRS]
    for k in range(layers):
        for at_x in range(0, rows, 8):
            for at_y in range(0, cols, LANES):
                vs = [b[k, at_x : at_x + 8, at_y : at_y + LANES] for b in basis]
                for e, (i, j) in enumerate(PAIRS):
                    sums[e] = sums[e] + vs[i] * vs[j]
    halves = []
    for e in range(2 * HALF):
        row = jnp.sum(sums[e], axis=0, keepdims=True)
        halves.append(row + pltpu.roll(row, SLOT, 1))
    low = lane_iota((1, LANES)) < SLOT
    lines = [jnp.where(low, halves[e], halves[e + HALF]) for e in range(HALF)]
    block = jnp.concatenate(lines + [jnp.zeros((8 - HALF, LANES), f32)], axis=0)
    for d in range(gram_ref.shape[0]):
        gram_ref[d] = block


def solve(gram_ref):
    total = gram_ref[0]
    for d in range(1, gram_ref.shape[0]):
        total = total + gram_ref[d]
    low = lane_iota((8, LANES)) < SLOT
    scale = 1.0 / (LANES // SLOT)
    first = jnp.sum(jnp.where(low, total, 0.0), axis=1, keepdims=True)
    second = jnp.sum(jnp.where(low, 0.0, total), axis=1, keepdims=True)
    gram = {}
    for e, (i, j) in enumerate(PAIRS):
        part = first if e < HALF else second
        gram[i, j] = gram[j, i] = part[e % HALF : e % HALF + 1, :]

    def times_gram(c):
        out = []
        for i in range(KRYLOV + 1):
            out.append(functools.reduce(jnp.add, [gram[i, m] * c[m] for m in range(len(c))]))
        return out

    def dot(a, b):
        return functools.reduce(jnp.add, [x * y for x, y in zip(a, b)])

    beta = jnp.sqrt(gram[0, 0] + norm_epsilon)
    basis = [[1.0 / beta]]
    images = [times_gram(basis[0])]
    hessen = {}
    for j in range(KRYLOV):
        w = [jnp.zeros_like(beta)] + basis[j]
        for i in range(j + 1):
            product = dot(w, images[i])
            hessen[i, j] = product
            w = [w[m] - product * basis[i][m] if m < len(basis[i]) else w[m] for m in range(len(w))]
        square = jnp.maximum(dot(w, times_gram(w)), 0.0)
        length = jnp.sqrt(square + norm_epsilon)
        hessen[j + 1, j] = length
        if j + 1 < KRYLOV:
            inverse = 1.0 / length
            basis.append([x * inverse for x in w])
            images.append(times_gram(basis[-1]))
    n = KRYLOV
    normal = {}
    for a in range(n):
        for b in range(a + 1):
            normal[a, b] = functools.reduce(
                jnp.add,
                [hessen[i, a] * hessen[i, b] for i in range(n + 1) if (i, a) in hessen and (i, b) in hessen],
            )
    factor = {}
    inverse = []
    for a in range(n):
        for b in range(a + 1):
            value = normal[a, b]
            for m in range(b):
                value = value - factor[a, m] * factor[b, m]
            if a == b:
                inverse.append(lax.rsqrt(value))
            else:
                factor[a, b] = value * inverse[b]
    forward = []
    for a in range(n):
        value = hessen[0, a] * beta
        for m in range(a):
            value = value - factor[a, m] * forward[m]
        forward.append(value * inverse[a])
    backward = [None] * n
    for a in reversed(range(n)):
        value = forward[a]
        for m in range(a + 1, n):
            value = value - factor[m, a] * backward[m]
        backward[a] = value * inverse[a]
    return [
        functools.reduce(jnp.add, [backward[j] * basis[j][i] for j in range(i, n)]) for i in range(n)
    ]


def first_kernel(
    table_ref, head_ref, soil_ref, lo_ref, hi_ref, src_ref, slo_ref, shi_ref, ylo_ref, yhi_ref,
    ext_ref, index_ref, base_ref, p0_ref, p1_ref, p2_ref, gram_ref, p3_ref, *scratch,
):
    layers, rows, cols = head_ref.shape
    tall = rows + 2 * HALO
    tables = table_rows(table_ref, tall)
    lane = lane_iota((tall, LANES))

    def side(field, k):
        right = yhi_ref[field]
        left = ylo_ref[field]
        shift = (-HALO * k) % LANES
        right = pltpu.roll(right, shift, 1) if shift else right
        left = pltpu.roll(left, (LANES - HALO - HALO * k) % LANES, 1)
        return jnp.where(lane < HALO, right, jnp.where(lane >= LANES - HALO, left, 0.0))

    for k in range(layers):
        ext_ref[k, 0:rows, 0:cols] = head_ref[k]
        ext_ref[k, rows : rows + HALO, 0:cols] = hi_ref[k]
        ext_ref[k, rows + HALO : tall, 0:cols] = lo_ref[k]
        ext_ref[k, :, cols : cols + LANES] = side(0, k)
        index_ref[k, 0:rows, 0:cols] = soil_ref[k] + 1
        index_ref[k, rows : rows + HALO, 0:cols] = hi_ref[layers + k].astype(jnp.int32)
        index_ref[k, rows + HALO : tall, 0:cols] = lo_ref[layers + k].astype(jnp.int32)
        index_ref[k, :, cols : cols + LANES] = side(1, k).astype(jnp.int32)
        base_ref[k, 0:rows, 0:cols] = src_ref[k]
        base_ref[k, rows : rows + HALO, 0:cols] = shi_ref[k]
        base_ref[k, rows + HALO : tall, 0:cols] = slo_ref[k]
        base_ref[k, :, cols : cols + LANES] = side(2, k)
    for k in range(layers):
        index = index_ref[k]
        steep = lookup(tables[1], index)
        capacity = lookup(tables[2], index)
        theta_old = capacity * sigmoid(steep * ext_ref[k])
        base_ref[k] = base_ref[k] + storage_weight * theta_old
    krylov(
        ext_ref, base_ref, index_ref, tables, (p0_ref, p1_ref, p2_ref, p3_ref), scratch, gram_ref,
        (rows, cols),
    )


def second_kernel(
    table_ref, sums_ref, old_ref, index_ref, base_ref, q0_ref, q1_ref, q2_ref,
    part_ref, p0_ref, p1_ref, p2_ref, gram_ref, ext_ref, p3_ref, *scratch,
):
    layers, tall, wide = old_ref.shape
    rows, cols = part_ref.shape[1:]
    tables = table_rows(table_ref, tall)
    x = solve(sums_ref)
    for k in range(layers):
        ext_ref[k] = old_ref[k] - x[0] * q0_ref[k] - x[1] * q1_ref[k] - x[2] * q2_ref[k]
        part_ref[k] = ext_ref[k, 0:rows, 0:cols]
    krylov(
        ext_ref, base_ref, index_ref, tables, (p0_ref, p1_ref, p2_ref, p3_ref), scratch, gram_ref,
        (rows, cols),
    )


def last_kernel(sums_ref, part_ref, q0_ref, q1_ref, q2_ref, head_ref):
    layers, rows, cols = part_ref.shape
    x = solve(sums_ref)
    for k in range(layers):
        own = (k, slice(0, rows), slice(0, cols))
        head_ref[k] = part_ref[k] - x[0] * q0_ref[own] - x[1] * q1_ref[own] - x[2] * q2_ref[own]


def shards(head_old, soil_type, soil_table, forcing, canopy, column_slot):
    layers, rows, cols = head_old.shape
    both = ("gx", "gy")
    devices = lax.axis_size("gx") * lax.axis_size("gy")
    block = (devices, 8, LANES)

    def exchange(to_lower, to_upper, axis):
        size = lax.axis_size(axis)
        up = [(i, i + 1) for i in range(size - 1)]
        down = [(j, i) for i, j in up]
        return lax.ppermute(to_upper, axis, up), lax.ppermute(to_lower, axis, down)

    def spread(x):
        return lax.all_to_all(x, both, split_axis=0, concat_axis=0, tiled=True)

    send, down, up = call(
        pack_kernel,
        [(block, f32), ((2 * layers, HALO, cols), f32), ((2 * layers, HALO, cols), f32)],
        3,
    )(canopy, head_old, soil_type)
    arrived = spread(send)
    lo, hi = exchange(down, up, "gx")
    edge = ((layers, HALO, cols), f32)
    source, sdown, sup, flux = call(
        source_kernel,
        [((layers, rows, cols), f32), edge, edge, ((2, rows, cols), f32)],
        6,
        scratch=[pltpu.VMEM((devices // 2, 16, LANES), f32)],
        in_specs=[smem] + [vmem] * 5,
    )(soil_table, arrived, head_old, soil_type, forcing, column_slot)
    slo, shi = exchange(sdown, sup, "gx")
    tall = rows + 2 * HALO
    wide = cols + LANES
    ydown, yup = call(strip_kernel, [((3, tall, LANES), f32)] * 2, 7)(
        head_old, soil_type, lo, hi, source, slo, shi
    )
    ylo, yhi = exchange(ydown, yup, "gy")
    ext = ((layers, tall, wide), f32)
    held = [pltpu.VMEM((layers, tall, wide), f32)]
    old, index, base, p0, p1, p2, gram = call(
        first_kernel,
        [ext, ((layers, tall, wide), jnp.int32), ext, ext, ext, ext, (block, f32)],
        10,
        scratch=held * 11,
        in_specs=[smem] + [vmem] * 9,
    )(soil_table, head_old, soil_type, lo, hi, source, slo, shi, ylo, yhi)
    sums = spread(gram)
    part, q0, q1, q2, gram = call(
        second_kernel,
        [((layers, rows, cols), f32), ext, ext, ext, (block, f32)],
        8,
        scratch=held * 12,
        in_specs=[smem] + [vmem] * 7,
    )(soil_table, sums, old, index, base, p0, p1, p2)
    sums = spread(gram)
    (head,) = call(last_kernel, [((layers, rows, cols), f32)], 5)(sums, part, q0, q1, q2)
    return head, flux


def solution(mesh):
    return jax.shard_map(
        shards,
        mesh=mesh,
        in_specs=(
            P(None, "gx", "gy"),
            P(None, "gx", "gy"),
            P(),
            P(None, "gx", "gy"),
            P(None, ("gx", "gy")),
            P("gx", "gy"),
        ),
        out_specs=(P(None, "gx", "gy"), P(None, "gx", "gy")),
        check_vma=False,
    )
```

time: 991 us -> 86.6 us (0.09); the launches traced: 979 us -> 86.2 us
  blocking collectives: 587 us -> 25.6 us
  other arithmetic: 137 us -> 0 us
  starting transfers between devices: 116 us -> 18.7 us
  local copies, waits for them, and re-layouts: 94.9 us -> 2.86 us
  between operations: 27.5 us -> 0.78 us
  Pallas kernels: 0 us -> 25.9 us
    psum x14 -> x0, blocking collectives: 587 us -> none  [the longest x6 261 us: shards(): products = lax.psum(local_sums, ('gx', 'gy'))]
    ppermute x36 -> x6, starting transfers between devices: 99.3 us -> 11.4 us  [the longest x3 7.54 us: exchange(): lax.ppermute(to_upper, axis, up)]
    reduce_sum x15 -> x0, other arithmetic: 46.6 us -> none  [the longest x6 19.4 us: shards(): jnp.sum(direction * direction)]
    scatter x13 -> x0, local copies, waits for them, and re-layouts: 28.5 us -> none  [the longest x1 21.1 us: shards(): buffer = jnp.zeros((outgoing.shape[0], canopy.shape[1]), jnp.float32).at[...]
    another operation x20 -> x0, other arithmetic: 28.2 us -> none
    gather x1 -> x0, local copies, waits for them, and re-layouts: 27.8 us -> none  [shards(): jnp.take(returned, flat_slot, axis=1).reshape(layers + 2, rows_x, rows_y)]
    pallas_call x0 -> x6, Pallas kernels: none -> 25.9 us  [the longest x1 8.07 us: shards(): call(first_kernel, [ext, ((layers, tall, wide), jnp.int32), ext, ext, ext...]
    all_to_all x0 -> x2, blocking collectives: none -> 25.6 us  [spread(): return lax.all_to_all(x, both, split_axis=0, concat_axis=0, tiled=True)]
  transfers between devices with their start and end apart: 38 -> 7, of which waited for: 10 -> 4; matrix products, arithmetic and copies ran while one was open for 3% -> 0% of each run, Pallas kernels for 0% -> 9%
where the time goes in v1:
time: 86.6 us; the launch traced here: 86.2 us
  Pallas kernels  25.9 us (30%)
  blocking collectives  25.6 us (30%)
  starting transfers between devices  18.7 us (22%)
  waiting for transfers between devices  12.3 us (14%)
  local copies, waits for them, and re-layouts  2.86 us (3%)
    all_to_all x2, blocking collectives, spread(): return lax.all_to_all(x, both, split_axis=0, concat_axis=0, tiled=True)  25.6 us
    pallas_call x1, Pallas kernels, shards(): call(first_kernel, [ext, ((layers, tall, wide), jnp.int32), ext, ext, ext...  8.07 us
    pallas_call x1, Pallas kernels, shards(): call(source_kernel, [((layers, rows, cols), f32), edge, edge, ((2, rows,...  7.67 us
    ppermute x3, starting transfers between devices, exchange(): lax.ppermute(to_upper, axis, up)  7.54 us
    all_to_all x1, starting transfers between devices, spread(): return lax.all_to_all(x, both, split_axis=0, concat_axis=0, tiled=True)  7.3 us
    ppermute x3, waiting for transfers between devices, exchange(): lax.ppermute(to_lower, axis, down)  6.94 us
    pallas_call x1, Pallas kernels, shards(): call(second_kernel, [((layers, rows, cols), f32), ext, ext, ext, (block,...  6.9 us
    ppermute x3, starting transfers between devices, exchange(): lax.ppermute(to_lower, axis, down)  3.88 us
  transfers between devices with their start and end apart: 7, of which 4 were waited for; matrix products, arithmetic and copies ran while one was open for 0% of the time, Pallas kernels for 9%

profile of v1, /device:TPU:0, one launch (start us, length us, event | category | flops | bytes accessed | tf_op | source)
XLA Modules:
  0.0 86.2 jit_solution(8241240628324438307)
XLA Ops:
  0.6 0.0 copy-start
  0.6 1.0 %copy-done = f32[10,16,512]{2,1,0:T(8,128)S(1)} copy-done((f32[10,16,512]{2,1,0:T(8,128)S(1)}, f32[10,16,512]{2,1,0:T(8,128)}, u32[]{:S(2)}) %copy-start) | copy-done | bytes 327704
  1.6 1.0 %copy-done.2 = s32[10,16,512]{2,1,0:T(8,128)S(1)} copy-done((s32[10,16,512]{2,1,0:T(8,128)S(1)}, s32[10,16,512]{2,1,0:T(8,128)}, u32[]{:S(2)}) %copy-start.2) | copy-done | bytes 327704
  2.6 0.9 %copy-done.4 = f32[13,2048]{1,0:T(8,128)S(1)} copy-done((f32[13,2048]{1,0:T(8,128)S(1)}, f32[13,2048]{1,0:T(8,128)}, u32[]{:S(2)}) %copy-start.4) | copy-done | bytes 106520
  3.5 1.9 %shard_map.77 = (f32[32,8,128]{2,1,0:T(8,128)}, f32[20,8,512]{2,1,0:T(8,128)S(1)}, f32[20,8,512]{2,1,0:T(8,128)S(1)}) custom-call(f32[13,2048]{1,0:T(8,128)S(1)} %copy-done.4, f32[10,16,512]{2,1,0:T(8,128)S(1)} %copy-done, s32[10,16,512]{2,1,0:T(8,128)S(1)} %copy-done.2), custom_call_target="tpu_custom_call" | custom-call | flops 1000000 | bytes 1000000 | tf_op jit(solution)/shard_map/pallas_call | solution.py:452
  5.3 7.3 %all-to-all-start = ((f32[32,8,128]{2,1,0:T(8,128)}), f32[32,8,128]{2,1,0:T(8,128)S(1)}, u32[]{:S(2)}, u32[]{:S(2)}) async-start(f32[32,8,128]{2,1,0:T(8,128)} %get-tuple-element.25), calls=%async_computation | async-start | bytes 262144 | tf_op jit(solution)/shard_map/all_to_all | solution.py:450
  12.6 0.0 copy-start.7
  12.7 3.7 %collective-permute-start = (f32[20,8,512]{2,1,0:T(8,128)S(1)}, f32[20,8,512]{2,1,0:T(8,128)S(1)}, u32[]{:S(2)}, u32[]{:S(2)}) collective-permute-start(f32[20,8,512]{2,1,0:T(8,128)S(1)} %get-tuple-element.23), channel_id=1, source_target_pairs={{0,4},{4,8},{8,12},{12,16},{16,20},{20,24},{24,28},{1,5},{5,9},{9,... | collective-permute-start | bytes 983048 | tf_op jit(solution)/shard_map/ppermute | solution.py:447
  16.4 1.3 %collective-permute-start.1 = (f32[20,8,512]{2,1,0:T(8,128)S(1)}, f32[20,8,512]{2,1,0:T(8,128)S(1)}, u32[]{:S(2)}, u32[]{:S(2)}) collective-permute-start(f32[20,8,512]{2,1,0:T(8,128)S(1)} %get-tuple-element.24), channel_id=1, source_target_pairs={{4,0},{8,4},{12,8},{16,12},{20,16},{24,20},{28,24},{5,1},{9,5},{13... | collective-permute-start | bytes 983048 | tf_op jit(solution)/shard_map/ppermute | solution.py:447
  17.7 3.3 %all-to-all-done.arrived_ref = f32[32,8,128]{2,1,0:T(8,128)S(1)} async-done(((f32[32,8,128]{2,1,0:T(8,128)}), f32[32,8,128]{2,1,0:T(8,128)S(1)}, u32[]{:S(2)}, u32[]{:S(2)}) %all-to-all-start) | async-done | bytes 131104 | tf_op jit(solution)/shard_map/all_to_all | solution.py:450
  21.0 0.0 copy-done.1
  21.0 0.0 copy-done.3
  21.0 0.0 copy-done.5
  21.0 0.0 copy-done.6
  21.0 0.0 copy-done.7
  21.0 7.7 %shard_map.78 = (f32[10,16,512]{2,1,0:T(8,128)S(1)}, f32[10,8,512]{2,1,0:T(8,128)S(1)}, f32[10,8,512]{2,1,0:T(8,128)S(1)}, f32[2,16,512]{2,1,0:T(8,128)}) custom-call(f32[3,12]{1,0:T(4,128)S(1)} %copy-done.7, f32[32,8,128]{2,1,0:T(8,128)S(1)} %all-to-all-done.arrived_ref, f32[10,16,512]{2,1,0:T(8,128)S(1)} %copy-done.1, s32[10,16,512]{2,1,0:T(8,128)S(1)} %copy-done.3, ...), custom_call_target="tpu_custom_call" | custom-call | flops 1000000 | bytes 1000000 | tf_op jit(solution)/shard_map/pallas_call | solution.py:460
  28.7 2.6 %collective-permute-start.2 = (f32[10,8,512]{2,1,0:T(8,128)S(1)}, f32[10,8,512]{2,1,0:T(8,128)S(1)}, u32[]{:S(2)}, u32[]{:S(2)}) collective-permute-start(f32[10,8,512]{2,1,0:T(8,128)S(1)} %get-tuple-element.27), channel_id=1, source_target_pairs={{0,4},{4,8},{8,12},{12,16},{16,20},{20,24},{24,28},{1,5},{5,9},{9,... | collective-permute-start | bytes 491528 | tf_op jit(solution)/shard_map/ppermute | solution.py:447
  31.2 1.3 %collective-permute-start.3 = (f32[10,8,512]{2,1,0:T(8,128)S(1)}, f32[10,8,512]{2,1,0:T(8,128)S(1)}, u32[]{:S(2)}, u32[]{:S(2)}) collective-permute-start(f32[10,8,512]{2,1,0:T(8,128)S(1)} %get-tuple-element.28), channel_id=1, source_target_pairs={{4,0},{8,4},{12,8},{16,12},{20,16},{24,20},{28,24},{5,1},{9,5},{13... | collective-permute-start | bytes 491528 | tf_op jit(solution)/shard_map/ppermute | solution.py:447
  32.5 0.0 collective-permute-done.lo_ref
  32.6 0.0 collective-permute-done.1.hi_ref
  32.6 2.1 %collective-permute-done.2.slo_ref = f32[10,8,512]{2,1,0:T(8,128)S(1)} collective-permute-done((f32[10,8,512]{2,1,0:T(8,128)S(1)}, f32[10,8,512]{2,1,0:T(8,128)S(1)}, u32[]{:S(2)}, u32[]{:S(2)}) %collective-permute-start.2) | collective-permute-done | bytes 163872 | tf_op jit(solution)/shard_map/ppermute | solution.py:447
  34.6 4.1 %collective-permute-done.3.shi_ref = f32[10,8,512]{2,1,0:T(8,128)S(1)} collective-permute-done((f32[10,8,512]{2,1,0:T(8,128)S(1)}, f32[10,8,512]{2,1,0:T(8,128)S(1)}, u32[]{:S(2)}, u32[]{:S(2)}) %collective-permute-start.3) | collective-permute-done | bytes 163872 | tf_op jit(solution)/shard_map/ppermute | solution.py:447
  38.7 0.3 shard_map.79
  39.1 1.3 %collective-permute-start.4 = (f32[3,32,128]{2,1,0:T(8,128)S(1)}, f32[3,32,128]{2,1,0:T(8,128)S(1)}, u32[]{:S(2)}, u32[]{:S(2)}) collective-permute-start(f32[3,32,128]{2,1,0:T(8,128)S(1)} %get-tuple-element.29), channel_id=1, source_target_pairs={{0,1},{1,2},{2,3},{4,5},{5,6},{6,7},{8,9},{9,10},{10,11},{12,13},{... | collective-permute-start | bytes 147464 | tf_op jit(solution)/shard_map/ppermute | solution.py:447
  40.4 1.3 %collective-permute-start.5 = (f32[3,32,128]{2,1,0:T(8,128)S(1)}, f32[3,32,128]{2,1,0:T(8,128)S(1)}, u32[]{:S(2)}, u32[]{:S(2)}) collective-permute-start(f32[3,32,128]{2,1,0:T(8,128)S(1)} %get-tuple-element.30), channel_id=1, source_target_pairs={{1,0},{2,1},{3,2},{5,4},{6,5},{7,6},{9,8},{10,9},{11,10},{13,12},{... | collective-permute-start | bytes 147464 | tf_op jit(solution)/shard_map/ppermute | solution.py:447
  41.7 0.0 collective-permute-done.4.ylo_ref
  41.7 2.8 %collective-permute-done.5.yhi_ref = f32[3,32,128]{2,1,0:T(8,128)S(1)} collective-permute-done((f32[3,32,128]{2,1,0:T(8,128)S(1)}, f32[3,32,128]{2,1,0:T(8,128)S(1)}, u32[]{:S(2)}, u32[]{:S(2)}) %collective-permute-start.5) | collective-permute-done | bytes 49184 | tf_op jit(solution)/shard_map/ppermute | solution.py:447
  44.5 8.1 %shard_map.80 = (f32[10,32,640]{2,1,0:T(8,128)S(1)}, s32[10,32,640]{2,1,0:T(8,128)S(1)}, f32[10,32,640]{2,1,0:T(8,128)S(1)}, f32[10,32,640]{2,1,0:T(8,128)S(1)},...) custom-call(f32[3,12]{1,0:T(4,128)S(1)} %copy-done.7, ...), custom_call_target="tpu_custom_call" | custom-call | flops 1000000 | bytes 1000000 | tf_op jit(solution)/shard_map/pallas_call | solution.py:476
  52.6 15.6 %all_to_all.15.sums_ref = f32[32,8,128]{2,1,0:T(8,128)S(1)} all-to-all(f32[32,8,128]{2,1,0:T(8,128)S(1)} %get-tuple-element.31), channel_id=1, replica_groups=mesh['gx'=8,'gy'=4] {'gx','gy'}, dimensions={0} | all-to-all | bytes 262144 | tf_op jit(solution)/shard_map/all_to_all | solution.py:450
  68.2 6.9 %shard_map.81 = (f32[10,16,512]{2,1,0:T(8,128)S(1)}, f32[10,32,640]{2,1,0:T(8,128)S(1)}, f32[10,32,640]{2,1,0:T(8,128)S(1)}, f32[10,32,640]{2,1,0:T(8,128)S(1)}, f32[32,8,128]{2,1,0:T(8,128)S(1)}) custom-call(f32[3,12]{1,0:T(4,128)S(1)} %copy-done.7, f32[32,8,128]{2,1,0:T(8,128)S(1)} %all_to_all.15.sums_ref, f32[10,32,640]{2,1,0:T(8,128)S(1)} %get-tuple-element.32.old_ref, ...), custom_call_target="tpu_custom_call" | custom-call | flops 1000000 | bytes 1000000 | tf_op jit(solution)/shard_map/pallas_call | solution.py:484
  75.1 10.0 %all_to_all.16.sums_ref = f32[32,8,128]{2,1,0:T(8,128)S(1)} all-to-all(f32[32,8,128]{2,1,0:T(8,128)S(1)} %get-tuple-element.38), channel_id=1, replica_groups=mesh['gx'=8,'gy'=4] {'gx','gy'}, dimensions={0} | all-to-all | bytes 262144 | tf_op jit(solution)/shard_map/all_to_all | solution.py:450
  85.1 1.1 %shard_map.82 = f32[10,16,512]{2,1,0:T(8,128)} custom-call(f32[32,8,128]{2,1,0:T(8,128)S(1)} %all_to_all.16.sums_ref, f32[10,16,512]{2,1,0:T(8,128)S(1)} %get-tuple-element.39.part_ref, f32[10,32,640]{2,1,0:T(8,128)S(1)} %get-tuple-element.40.q0_ref, f32[10,32,640]{2,1,0:T(8,128)S(1)} %get-tuple-element.41.q1_ref, f32[10,32,640]{2,1,0:T(8,128)S(1)} %get-tuple-element.42.q2_ref), custom_call_target="tpu_custom_call" | custom-call | flops 1000000 | bytes 1000000 | tf_op jit(solution)/shard_map/pallas_call | solution.py:492
  (6 shorter events, 0.0 us)
Async XLA Ops:
  0.6 1.0 %copy-start = (f32[10,16,512]{2,1,0:T(8,128)S(1)}, f32[10,16,512]{2,1,0:T(8,128)}, u32[]{:S(2)}) copy-start(f32[10,16,512]{2,1,0:T(8,128)} %head_ref.7) | copy-start | bytes 983044
  1.6 1.0 %copy-start.2 = (s32[10,16,512]{2,1,0:T(8,128)S(1)}, s32[10,16,512]{2,1,0:T(8,128)}, u32[]{:S(2)}) copy-start(s32[10,16,512]{2,1,0:T(8,128)} %soil_ref.7) | copy-start | bytes 983044
  2.6 0.9 %copy-start.4 = (f32[13,2048]{1,0:T(8,128)S(1)}, f32[13,2048]{1,0:T(8,128)}, u32[]{:S(2)}) copy-start(f32[13,2048]{1,0:T(8,128)} %canopy_ref.1) | copy-start | bytes 319492
  3.5 17.5 %copy-start.1 = (f32[10,16,512]{2,1,0:T(8,128)S(1)}, f32[10,16,512]{2,1,0:T(8,128)}, u32[]{:S(2)}) copy-start(f32[10,16,512]{2,1,0:T(8,128)} %head_ref.7) | copy-start | bytes 983044
  3.5 17.5 %copy-start.3 = (s32[10,16,512]{2,1,0:T(8,128)S(1)}, s32[10,16,512]{2,1,0:T(8,128)}, u32[]{:S(2)}) copy-start(s32[10,16,512]{2,1,0:T(8,128)} %soil_ref.7) | copy-start | bytes 983044
  5.3 15.6 %copy-start.5 = (f32[4,16,512]{2,1,0:T(8,128)S(1)}, f32[4,16,512]{2,1,0:T(8,128)}, u32[]{:S(2)}) copy-start(f32[4,16,512]{2,1,0:T(8,128)} %forcing_ref.1) | copy-start | bytes 393220
  5.3 15.7 %copy-start.6 = (s32[16,512]{1,0:T(8,128)S(1)}, s32[16,512]{1,0:T(8,128)}, u32[]{:S(2)}) copy-start(s32[16,512]{1,0:T(8,128)} %slot_ref.1) | copy-start | bytes 98308
  5.3 15.6 %all-to-all-start = ((f32[32,8,128]{2,1,0:T(8,128)}), f32[32,8,128]{2,1,0:T(8,128)S(1)}, u32[]{:S(2)}, u32[]{:S(2)}) async-start(f32[32,8,128]{2,1,0:T(8,128)} %get-tuple-element.25), calls=%async_computation | async-start | bytes 262144 | tf_op jit(solution)/shard_map/all_to_all | solution.py:450
  12.6 8.4 %copy-start.7 = (f32[3,12]{1,0:T(4,128)S(1)}, f32[3,12]{1,0:T(4,128)}, u32[]{:S(2)}) copy-start(f32[3,12]{1,0:T(4,128)} %table_ref.5) | copy-start | bytes 436
  12.7 19.9 %collective-permute-start = (f32[20,8,512]{2,1,0:T(8,128)S(1)}, f32[20,8,512]{2,1,0:T(8,128)S(1)}, u32[]{:S(2)}, u32[]{:S(2)}) collective-permute-start(f32[20,8,512]{2,1,0:T(8,128)S(1)} %get-tuple-element.23), channel_id=1, source_target_pairs={{0,4},{4,8},{8,12},{12,16},{16,20},{20,24},{24,28},{1,5},{5,9},{9,... | collective-permute-start | bytes 983048 | tf_op jit(solution)/shard_map/ppermute | solution.py:447
  16.4 16.2 %collective-permute-start.1 = (f32[20,8,512]{2,1,0:T(8,128)S(1)}, f32[20,8,512]{2,1,0:T(8,128)S(1)}, u32[]{:S(2)}, u32[]{:S(2)}) collective-permute-start(f32[20,8,512]{2,1,0:T(8,128)S(1)} %get-tuple-element.24), channel_id=1, source_target_pairs={{4,0},{8,4},{12,8},{16,12},{20,16},{24,20},{28,24},{5,1},{9,5},{13... | collective-permute-start | bytes 983048 | tf_op jit(solution)/shard_map/ppermute | solution.py:447
  28.7 5.9 %collective-permute-start.2 = (f32[10,8,512]{2,1,0:T(8,128)S(1)}, f32[10,8,512]{2,1,0:T(8,128)S(1)}, u32[]{:S(2)}, u32[]{:S(2)}) collective-permute-start(f32[10,8,512]{2,1,0:T(8,128)S(1)} %get-tuple-element.27), channel_id=1, source_target_pairs={{0,4},{4,8},{8,12},{12,16},{16,20},{20,24},{24,28},{1,5},{5,9},{9,... | collective-permute-start | bytes 491528 | tf_op jit(solution)/shard_map/ppermute | solution.py:447
  31.2 7.5 %collective-permute-start.3 = (f32[10,8,512]{2,1,0:T(8,128)S(1)}, f32[10,8,512]{2,1,0:T(8,128)S(1)}, u32[]{:S(2)}, u32[]{:S(2)}) collective-permute-start(f32[10,8,512]{2,1,0:T(8,128)S(1)} %get-tuple-element.28), channel_id=1, source_target_pairs={{4,0},{8,4},{12,8},{16,12},{20,16},{24,20},{28,24},{5,1},{9,5},{13... | collective-permute-start | bytes 491528 | tf_op jit(solution)/shard_map/ppermute | solution.py:447
  39.1 2.6 %collective-permute-start.4 = (f32[3,32,128]{2,1,0:T(8,128)S(1)}, f32[3,32,128]{2,1,0:T(8,128)S(1)}, u32[]{:S(2)}, u32[]{:S(2)}) collective-permute-start(f32[3,32,128]{2,1,0:T(8,128)S(1)} %get-tuple-element.29), channel_id=1, source_target_pairs={{0,1},{1,2},{2,3},{4,5},{5,6},{6,7},{8,9},{9,10},{10,11},{12,13},{... | collective-permute-start | bytes 147464 | tf_op jit(solution)/shard_map/ppermute | solution.py:447
  40.4 4.1 %collective-permute-start.5 = (f32[3,32,128]{2,1,0:T(8,128)S(1)}, f32[3,32,128]{2,1,0:T(8,128)S(1)}, u32[]{:S(2)}, u32[]{:S(2)}) collective-permute-start(f32[3,32,128]{2,1,0:T(8,128)S(1)} %get-tuple-element.30), channel_id=1, source_target_pairs={{1,0},{2,1},{3,2},{5,4},{6,5},{7,6},{9,8},{10,9},{11,10},{13,12},{... | collective-permute-start | bytes 147464 | tf_op jit(solution)/shard_map/ppermute | solution.py:447

commit v2 on v1

v2 whole, which is shorter than its diff:
```python
import functools

import jax
import jax.numpy as jnp
from jax import lax
from jax.experimental import pallas as pl
from jax.experimental.pallas import tpu as pltpu
from jax.sharding import PartitionSpec as P

NEWTON = 2
KRYLOV = 3
HALO = 8
LANES = 128
SLOT = 64

storage_weight = 4.0
norm_epsilon = 1e-06

VMEM_LIMIT = 40 * 1024 * 1024
PAIRS = [(i, j) for i in range(KRYLOV + 1) for j in range(i, KRYLOV + 1)]

f32 = jnp.float32
vmem = pl.BlockSpec(memory_space=pltpu.VMEM)
smem = pl.BlockSpec(memory_space=pltpu.SMEM)


def call(body, outs, n_in, scratch=(), in_specs=None, flops=1000000):
    return pl.pallas_call(
        body,
        out_shape=[jax.ShapeDtypeStruct(s, d) for s, d in outs],
        in_specs=in_specs or [vmem] * n_in,
        out_specs=[vmem] * len(outs),
        scratch_shapes=list(scratch),
        compiler_params=pltpu.CompilerParams(vmem_limit_bytes=VMEM_LIMIT),
        cost_estimate=pl.CostEstimate(flops=flops, bytes_accessed=1000000, transcendentals=0),
    )


def lane_iota(shape):
    return lax.broadcasted_iota(jnp.int32, shape, len(shape) - 1)


def pack_kernel(canopy_ref, out_ref):
    rows = canopy_ref.shape[0]
    low = lane_iota((8, LANES)) < SLOT

    def step(t, _):
        here = pl.ds(pl.multiple_of(t * LANES, LANES), LANES)
        first = canopy_ref[0:8, here]
        rest = canopy_ref[8:rows, here]
        rest = jnp.concatenate([rest, jnp.zeros((16 - rows, LANES), f32)], axis=0)
        out_ref[2 * t] = jnp.where(low, first, pltpu.roll(rest, SLOT, 1))
        out_ref[2 * t + 1] = jnp.where(low, pltpu.roll(first, SLOT, 1), rest)
        return 0

    lax.fori_loop(0, canopy_ref.shape[1] // LANES, step, 0, unroll=4)


def edge_kernel(head_ref, soil_ref, down_ref, up_ref):
    layers, rows, _ = head_ref.shape
    for out_ref, at in ((down_ref, 0), (up_ref, rows - HALO)):
        for k in range(layers):
            out_ref[k] = head_ref[k, at : at + HALO, :]
            out_ref[layers + k] = (soil_ref[k, at : at + HALO, :] + 1).astype(f32)


def table_rows(table_ref, rows):
    lane = lane_iota((rows, LANES))
    out = []
    for field in range(table_ref.shape[0]):
        row = jnp.zeros((rows, LANES), f32)
        for kind in range(table_ref.shape[1]):
            row = jnp.where(lane == kind + 1, table_ref[field, kind], row)
        out.append(row)
    return out


def lookup(row, index):
    pieces = [
        jnp.take_along_axis(row, index[:, at : at + LANES], axis=1, mode="promise_in_bounds")
        for at in range(0, index.shape[1], LANES)
    ]
    return jnp.concatenate(pieces, axis=1)


def sigmoid(u):
    return 1.0 / (1.0 + jnp.exp(-u))


def source_kernel(
    table_ref, arrived_ref, head_ref, soil_ref, forcing_ref, slot_ref,
    source_ref, down_ref, up_ref, flux_ref, tab_ref,
):
    layers, rows, cols = head_ref.shape
    owners = arrived_ref.shape[0]
    low = lane_iota((8, LANES)) < SLOT
    line = lax.broadcasted_iota(jnp.int32, (16, LANES), 0)
    is_root = (line >= 3) & (line < 3 + layers)

    def unpack(t, _):
        first = arrived_ref[2 * t]
        second = arrived_ref[2 * t + 1]
        both = jnp.concatenate(
            [
                jnp.where(low, first, pltpu.roll(second, SLOT, 1)),
                jnp.where(low, pltpu.roll(first, SLOT, 1), second),
            ],
            axis=0,
        )
        leaf_area, albedo, resist = both[0:1], both[1:2], both[2:3]
        root_sum = jnp.sum(jnp.where(is_root, both, 0.0), axis=0, keepdims=True)
        both = both * (leaf_area / ((leaf_area + resist) * root_sum))
        tab_ref[t, 0] = jnp.broadcast_to(0.5 + 0.3 * leaf_area, (8, LANES))
        tab_ref[t, 1] = jnp.broadcast_to(1.0 - albedo, (8, LANES))
        for k in range(layers):
            tab_ref[t, 2 + k] = jnp.broadcast_to(both[3 + k : 4 + k], (8, LANES))
        return 0

    lax.fori_loop(0, owners // 2, unpack, 0, unroll=4)
    tables = table_rows(table_ref, 8)

    for at_x in range(0, rows, 8):

        def column(j, _):
            here = (slice(at_x, at_x + 8), pl.ds(pl.multiple_of(j * LANES, LANES), LANES))
            slot = slot_ref[here]
            land = slot >= 0
            value = jnp.maximum(slot, 0)
            lane = value & (LANES - 1)
            tile = value >> 7

            def pick(t, held):
                match = tile == t
                return tuple(
                    jnp.where(match, lookup(tab_ref[t, k], lane), held[k]) for k in range(2 + layers)
                )

            start = tuple(jnp.ones((8, LANES), f32) for _ in range(2 + layers))
            exchange_coef, absorbed, *roots = lax.fori_loop(0, owners // 2, pick, start, unroll=8)
            uptake = []
            for k in range(layers):
                index = soil_ref[(k,) + here] + 1
                steep = lookup(tables[1], index)
                uptake.append(roots[k] * sigmoid(steep * head_ref[(k,) + here]))
                if k == 0:
                    ks_top = lookup(tables[0], index)
            conductance = functools.reduce(jnp.add, uptake)
            sunlight, air_temp, humidity, rainfall = (forcing_ref[(i,) + here] for i in range(4))
            radiation = absorbed * sunlight + 0.3
            square = air_temp * air_temp
            excess = radiation - 0.3 * square * square - conductance * (0.5 - humidity)
            slope = -1.2 * square * air_temp - exchange_coef - conductance
            rise = -excess / slope
            surface = air_temp + rise
            vapour = 0.5 * jnp.exp(2.0 * rise)
            square = surface * surface
            excess = (
                radiation
                - 0.3 * square * square
                - exchange_coef * rise
                - conductance * (vapour - humidity)
            )
            slope = -1.2 * square * surface - exchange_coef - 2.0 * conductance * vapour
            rise = rise - excess / slope
            rate = 0.5 * jnp.exp(2.0 * rise) - humidity
            infiltration = rainfall * ks_top / (rainfall + ks_top)
            infiltration = jnp.where(land, infiltration, 0.0)
            rate = jnp.where(land, rate, 0.0)
            flux_ref[(0,) + here] = conductance * rate
            flux_ref[(1,) + here] = infiltration
            for k in range(layers):
                value = -rate * uptake[k]
                if k == 0:
                    value = value + infiltration
                source_ref[(k,) + here] = value
                if at_x < HALO:
                    down_ref[(k, slice(0, 8), here[1])] = value
                if at_x >= rows - HALO:
                    up_ref[(k, slice(0, 8), here[1])] = value
            return 0

        lax.fori_loop(0, cols // LANES, column, 0)


def strips(top, above, below, at, shift_from):
    layers = top.shape[0]
    lane = lane_iota((top.shape[1] + 2 * HALO, LANES))
    packed = jnp.zeros(lane.shape, f32)
    for k in range(layers):
        plane = jnp.concatenate([top[k], above[k], below[k]], axis=0)
        shift = (HALO * k - shift_from) % LANES
        moved = pltpu.roll(plane, shift, 1) if shift else plane
        inside = (lane >= HALO * k) & (lane < HALO * (k + 1))
        packed = jnp.where(inside, moved, packed)
    return packed


def strip_kernel(head_ref, soil_ref, lo_ref, hi_ref, src_ref, slo_ref, shi_ref, down_ref, up_ref):
    layers, rows, cols = head_ref.shape
    for out_ref, at, shift_from in ((down_ref, 0, 0), (up_ref, cols - LANES, LANES - HALO)):
        part = slice(at, at + LANES)
        out_ref[0] = strips(
            head_ref[:, :, part], hi_ref[0:layers, :, part], lo_ref[0:layers, :, part], at, shift_from
        )
        out_ref[1] = strips(
            (soil_ref[:, :, part] + 1).astype(f32),
            hi_ref[layers : 2 * layers, :, part],
            lo_ref[layers : 2 * layers, :, part],
            at,
            shift_from,
        )
        out_ref[2] = strips(src_ref[:, :, part], shi_ref[:, :, part], slo_ref[:, :, part], at, shift_from)


class Field:
    def __init__(self, main, side):
        self.main, self.side = main, side
        self.tiles = main.shape[-1] // LANES + 1

    def place(self, k, j):
        if j == self.tiles - 1:
            return self.side, (k,)
        return self.main, (k, slice(None), slice(j * LANES, (j + 1) * LANES))

    def get(self, k, j):
        ref, at = self.place(k, j)
        return ref[at]

    def set(self, k, j, value):
        ref, at = self.place(k, j)
        ref[at] = value


def after_x(x):
    return pltpu.roll(x, x.shape[0] - 1, 0)


def before_x(x):
    return pltpu.roll(x, 1, 0)


def up_one(x):
    return pltpu.roll(x, LANES - 1, 1)


def down_one(x):
    return pltpu.roll(x, 1, 1)


def pointwise(head, conduct, steep, capacity):
    sat = 0.5 + 0.5 * jnp.tanh(0.5 * (steep * head))
    slope = steep * sat * (1.0 - sat)
    cond = conduct * (0.1 + 0.9 * sat * sat)
    deriv = 0.9 * conduct * sat * slope
    weighted = storage_weight * capacity
    return cond, deriv, weighted * slope, weighted * sat


def krylov(head, water, base, cond, deriv, store, mask, basis, faces, zface, gram_ref, tile):
    layers = head.main.shape[0]
    rows, _ = tile
    tiles = head.tiles
    order = [tiles - 1] + list(range(tiles - 1))
    tall = head.main.shape[1]
    lane = lane_iota((tall, LANES))
    is_first, is_last = lane == 0, lane == LANES - 1
    (ax, bx), (ay, by), (az, bz) = faces

    def masked(value, j):
        edge = mask.get(0, j)
        if j == tiles - 1:
            return value * edge
        return jnp.concatenate([value[:rows], value[rows:] * edge[rows:]], axis=0)

    def sweep(read, flux, finish, k, last, own=False):
        rolled = {}
        pending = None
        previous = None
        wrapped = {}

        def shifted(j):
            if j not in wrapped:
                wrapped[j] = [up_one(x) for x in read(k, j)]
            return wrapped[j]

        for j in order:
            here = read(k, j)
            ahead = [
                jnp.where(is_last, b, a)
                for a, b in zip(shifted(j), shifted((j + 1) % tiles))
            ]
            face_y = flux(1, k, j, here, ahead)
            moved = down_one(face_y)
            if own and j == tiles - 1:
                previous = moved
                continue
            face_x = flux(0, k, j, here, [after_x(x) for x in here])
            value = face_x - before_x(face_x) + face_y
            below = flux(2, k, j, here, None if last else read(k + 1, j))
            value = value + (below - zface.get(0, j))
            zface.set(0, j, below)
            if previous is None:
                pending = (value, moved)
            else:
                finish(k, j, value - jnp.where(is_first, previous, moved))
            previous = moved
        if pending is not None:
            value, moved = pending
            finish(k, tiles - 1, value - jnp.where(is_first, previous, moved))

    def run(read, flux, finish, own=False):
        for j in range(tiles):
            zface.set(0, j, jnp.zeros((tall, LANES), f32))

        def step(k, _):
            sweep(read, flux, finish, k, False, own)
            return 0

        lax.fori_loop(0, layers - 1, step, 0)
        sweep(read, flux, finish, layers - 1, True, own)

    def read_state(k, j):
        return [head.get(k, j), cond.get(k, j), deriv.get(k, j)]

    def flux_state(axis, k, j, here, ahead):
        if ahead is None:
            az.set(k, j, 2.0 * here[2])
            return here[1]
        mean = 0.5 * (here[1] + ahead[1])
        drop = here[0] - ahead[0]
        if axis == 2:
            drop = drop + 1.0
        a, b = faces[axis]
        a.set(k, j, mean + here[2] * drop)
        b.set(k, j, mean - ahead[2] * drop)
        return mean * drop

    def finish_state(k, j, value):
        basis[0].set(k, j, masked(value + (water.get(k, j) - base.get(k, j)), j))

    run(read_state, flux_state, finish_state)

    def flux_of(axis, k, j, here, ahead):
        a, b = faces[axis]
        face = a.get(k, j) * here[0]
        if ahead is None:
            return face
        return face - b.get(k, j) * ahead[0]

    for step in range(KRYLOV - 1):

        def read_vector(k, j):
            return [basis[step].get(k, j)]

        def finish_vector(k, j, value):
            basis[step + 1].set(k, j, masked(value + store.get(k, j) * basis[step].get(k, j), j))

        run(read_vector, flux_of, finish_vector)

    for e in range(len(PAIRS)):
        gram_ref[e] = jnp.zeros((8, LANES), f32)

    def read_last(k, j):
        return [basis[-1].get(k, j)]

    def finish_last(k, j, value):
        value = value + store.get(k, j) * basis[-1].get(k, j)
        tops = [b.get(k, j) for b in basis] + [value]
        for e, (a, b) in enumerate(PAIRS):
            total = gram_ref[e]
            for at in range(0, rows, 8):
                total = total + tops[a][at : at + 8] * tops[b][at : at + 8]
            gram_ref[e] = total

    run(read_last, flux_of, finish_last, own=True)


def emit_gram(sums_ref, out_ref):
    lines = [jnp.sum(sums_ref[e], axis=0, keepdims=True) for e in range(len(PAIRS))]
    lines.append(jnp.zeros((16 - len(PAIRS), LANES), f32))
    block = jnp.sum(jnp.concatenate(lines, axis=0), axis=1, keepdims=True)
    line = lax.broadcasted_iota(jnp.int32, (16, LANES), 0)
    flat = jnp.sum(jnp.where(lane_iota((16, LANES)) == line, block, 0.0), axis=0, keepdims=True)
    for d in range(out_ref.shape[0]):
        out_ref[d] = flat


def solve(gram_ref):
    total = gram_ref[0]
    for d in range(1, gram_ref.shape[0]):
        total = total + gram_ref[d]
    line = lax.broadcasted_iota(jnp.int32, (16, LANES), 0)
    spread = jnp.broadcast_to(total, (16, LANES))
    column = jnp.sum(jnp.where(lane_iota((16, LANES)) == line, spread, 0.0), axis=1, keepdims=True)
    gram = {}
    for e, (i, j) in enumerate(PAIRS):
        gram[i, j] = gram[j, i] = column[e : e + 1, :]

    def times_gram(c):
        out = []
        for i in range(KRYLOV + 1):
            out.append(functools.reduce(jnp.add, [gram[i, m] * c[m] for m in range(len(c))]))
        return out

    def dot(a, b):
        return functools.reduce(jnp.add, [x * y for x, y in zip(a, b)])

    beta = jnp.sqrt(gram[0, 0] + norm_epsilon)
    basis = [[1.0 / beta]]
    images = [times_gram(basis[0])]
    hessen = {}
    for j in range(KRYLOV):
        w = [jnp.zeros_like(beta)] + basis[j]
        for i in range(j + 1):
            product = dot(w, images[i])
            hessen[i, j] = product
            w = [w[m] - product * basis[i][m] if m < len(basis[i]) else w[m] for m in range(len(w))]
        square = jnp.maximum(dot(w, times_gram(w)), 0.0)
        length = jnp.sqrt(square + norm_epsilon)
        hessen[j + 1, j] = length
        if j + 1 < KRYLOV:
            inverse = 1.0 / length
            basis.append([x * inverse for x in w])
            images.append(times_gram(basis[-1]))
    n = KRYLOV
    normal = {}
    for a in range(n):
        for b in range(a + 1):
            normal[a, b] = functools.reduce(
                jnp.add,
                [hessen[i, a] * hessen[i, b] for i in range(n + 1) if (i, a) in hessen and (i, b) in hessen],
            )
    factor = {}
    inverse = []
    for a in range(n):
        for b in range(a + 1):
            value = normal[a, b]
            for m in range(b):
                value = value - factor[a, m] * factor[b, m]
            if a == b:
                inverse.append(lax.rsqrt(value))
            else:
                factor[a, b] = value * inverse[b]
    forward = []
    for a in range(n):
        value = hessen[0, a] * beta
        for m in range(a):
            value = value - factor[a, m] * forward[m]
        forward.append(value * inverse[a])
    backward = [None] * n
    for a in reversed(range(n)):
        value = forward[a]
        for m in range(a + 1, n):
            value = value - factor[m, a] * backward[m]
        backward[a] = value * inverse[a]
    return [
        functools.reduce(jnp.add, [backward[j] * basis[j][i] for j in range(i, n)]) for i in range(n)
    ]


def soil_kernel(
    table_ref, head_ref, soil_ref, lo_ref, hi_ref,
    ext_ref, ks_ref, steep_ref, cap_ref, cond_ref, deriv_ref, store_ref, water_ref,
):
    layers, rows, cols = head_ref.shape
    tall = rows + 2 * HALO
    tables = table_rows(table_ref, 8)

    def step(k, _):
        for at in range(0, tall, 8):
            for lane_at in range(0, cols, LANES):
                part = slice(lane_at, lane_at + LANES)
                if at < rows:
                    head = head_ref[k, at : at + 8, part]
                    index = soil_ref[k, at : at + 8, part] + 1
                else:
                    from_ref = hi_ref if at < rows + HALO else lo_ref
                    row = (at - rows) % HALO
                    head = from_ref[k, row : row + 8, part]
                    index = from_ref[layers + k, row : row + 8, part].astype(jnp.int32)
                conduct, steep, capacity = (lookup(row, index) for row in tables)
                values = (head, conduct, steep, capacity) + pointwise(head, conduct, steep, capacity)
                outs = (ext_ref, ks_ref, steep_ref, cap_ref, cond_ref, deriv_ref, store_ref, water_ref)
                for ref, value in zip(outs, values):
                    ref[k, at : at + 8, part] = value
        return 0

    lax.fori_loop(0, layers, step, 0)


def fields(mains, sides):
    return [Field(m, s) for m, s in zip(mains, sides)]


def newton_scratch(layers, tall, cols):
    main, side = ((layers, tall, cols), (layers, tall, LANES))
    shapes = [main] * 6 + [side] * 6 + [(1, tall, cols)] * 2 + [(1, tall, LANES)] * 2
    return [pltpu.VMEM(s, f32) for s in shapes + [(len(PAIRS), 8, LANES)]]


def split_scratch(refs):
    coefs = fields(refs[0:6], refs[6:12])
    zface, mask = fields(refs[12:14], refs[14:16])
    return [(coefs[0], coefs[1]), (coefs[2], coefs[3]), (coefs[4], coefs[5])], zface, mask, refs[16]


def set_mask(mask, conduct):
    for j in range(mask.tiles):
        mask.set(0, j, (conduct.get(0, j) > 0.0).astype(f32))


def first_kernel(
    table_ref, src_ref, slo_ref, shi_ref, ylo_ref, yhi_ref,
    ext_ref, ks_ref, cond_ref, deriv_ref, store_ref, water_ref,
    ext_side, ks_side, steep_side, cap_side, base_ref, base_side,
    p0_ref, p1_ref, p2_ref, p0_side, p1_side, p2_side, gram_ref,
    cond_side, deriv_side, store_side, water_side, *scratch,
):
    layers, rows, cols = src_ref.shape
    tall = rows + 2 * HALO
    tables = table_rows(table_ref, tall)
    lane = lane_iota((tall, LANES))

    def side(field, k):
        right = yhi_ref[field]
        left = ylo_ref[field]
        shift = (-HALO * k) % LANES
        right = pltpu.roll(right, shift, 1) if shift else right
        left = pltpu.roll(left, (LANES - HALO - HALO * k) % LANES, 1)
        return jnp.where(lane < HALO, right, jnp.where(lane >= LANES - HALO, left, 0.0))

    for k in range(layers):
        head = side(0, k)
        index = side(1, k).astype(jnp.int32)
        conduct, steep, capacity = (lookup(row, index) for row in tables)
        cond, deriv, store, water = pointwise(head, conduct, steep, capacity)
        ext_side[k] = head
        ks_side[k] = conduct
        steep_side[k] = steep
        cap_side[k] = capacity
        cond_side[k] = cond
        deriv_side[k] = deriv
        store_side[k] = store
        water_side[k] = water
        base_side[k] = side(2, k) + water

    def add_source(k, _):
        base_ref[k, 0:rows] = water_ref[k, 0:rows] + src_ref[k]
        base_ref[k, rows : rows + HALO] = water_ref[k, rows : rows + HALO] + shi_ref[k]
        base_ref[k, rows + HALO : tall] = water_ref[k, rows + HALO : tall] + slo_ref[k]
        return 0

    lax.fori_loop(0, layers, add_source, 0)
    faces, zface, mask, sums_ref = split_scratch(scratch)
    set_mask(mask, Field(ks_ref, ks_side))
    krylov(
        Field(ext_ref, ext_side), Field(water_ref, water_side), Field(base_ref, base_side),
        Field(cond_ref, cond_side), Field(deriv_ref, deriv_side), Field(store_ref, store_side),
        mask, fields((p0_ref, p1_ref, p2_ref), (p0_side, p1_side, p2_side)), faces, zface,
        sums_ref, (rows, cols),
    )
    emit_gram(sums_ref, gram_ref)


def second_kernel(
    arrived_ref, old_ref, ks_ref, steep_ref, cap_ref, base_ref, q0_ref, q1_ref, q2_ref,
    old_side, ks_side, steep_side, cap_side, base_side, q0_side, q1_side, q2_side,
    part_ref, p0_ref, p1_ref, p2_ref, gram_ref,
    p0_side, p1_side, p2_side, ext_ref, cond_ref, deriv_ref, store_ref, water_ref,
    ext_side, cond_side, deriv_side, store_side, water_side, *scratch,
):
    layers, tall, _ = old_ref.shape
    rows, cols = part_ref.shape[1:]
    x = [jnp.broadcast_to(value, (8, LANES)) for value in solve(arrived_ref)]

    def update(k, old, ks, steep, cap, base, qs, outs, lanes):
        for at in range(0, tall, 8):
            for lane_at in range(0, lanes, LANES):
                here = (k, slice(at, at + 8), slice(lane_at, lane_at + LANES))
                head = old[here]
                for value, q in zip(x, qs):
                    head = head - value * q[here]
                values = (head,) + pointwise(head, ks[here], steep[here], cap[here])
                for ref, value in zip(outs, values):
                    ref[here] = value
                if at < rows and lanes > LANES:
                    part_ref[here] = head

    def step(k, _):
        update(
            k, old_ref, ks_ref, steep_ref, cap_ref, base_ref, (q0_ref, q1_ref, q2_ref),
            (ext_ref, cond_ref, deriv_ref, store_ref, water_ref), cols,
        )
        update(
            k, old_side, ks_side, steep_side, cap_side, base_side, (q0_side, q1_side, q2_side),
            (ext_side, cond_side, deriv_side, store_side, water_side), LANES,
        )
        return 0

    lax.fori_loop(0, layers, step, 0)
    faces, zface, mask, sums_ref = split_scratch(scratch)
    set_mask(mask, Field(ks_ref, ks_side))
    krylov(
        Field(ext_ref, ext_side), Field(water_ref, water_side), Field(base_ref, base_side),
        Field(cond_ref, cond_side), Field(deriv_ref, deriv_side), Field(store_ref, store_side),
        mask, fields((p0_ref, p1_ref, p2_ref), (p0_side, p1_side, p2_side)), faces, zface,
        sums_ref, (rows, cols),
    )
    emit_gram(sums_ref, gram_ref)


def last_kernel(arrived_ref, part_ref, q0_ref, q1_ref, q2_ref, head_ref):
    layers, rows, cols = part_ref.shape
    x = [jnp.broadcast_to(value, (rows, cols)) for value in solve(arrived_ref)]

    def step(k, _):
        head = part_ref[k]
        for value, q in zip(x, (q0_ref, q1_ref, q2_ref)):
            head = head - value * q[k, 0:rows, :]
        head_ref[k] = head
        return 0

    lax.fori_loop(0, layers, step, 0)


def shards(head_old, soil_type, soil_table, forcing, canopy, column_slot):
    layers, rows, cols = head_old.shape
    both = ("gx", "gy")
    devices = lax.axis_size("gx") * lax.axis_size("gy")
    tall = rows + 2 * HALO
    own, edge = ((layers, rows, cols), f32), ((layers, HALO, cols), f32)
    main, side = ((layers, tall, cols), f32), ((layers, tall, LANES), f32)
    gram_block = ((devices, 1, LANES), f32)

    def exchange(to_lower, to_upper, axis):
        size = lax.axis_size(axis)
        up = [(i, i + 1) for i in range(size - 1)]
        down = [(j, i) for i, j in up]
        return lax.ppermute(to_upper, axis, up), lax.ppermute(to_lower, axis, down)

    def spread(x):
        return lax.all_to_all(x, both, split_axis=0, concat_axis=0, tiled=True)

    (send,) = call(pack_kernel, [((devices, 8, LANES), f32)], 1)(canopy)
    arrived = spread(send)
    down, up = call(edge_kernel, [((2 * layers, HALO, cols), f32)] * 2, 2)(head_old, soil_type)
    lo, hi = exchange(down, up, "gx")
    source, sdown, sup, flux = call(
        source_kernel,
        [own, edge, edge, ((2, rows, cols), f32)],
        6,
        scratch=[pltpu.VMEM((devices // 2, 2 + layers, 8, LANES), f32)],
        in_specs=[smem] + [vmem] * 5,
    )(soil_table, arrived, head_old, soil_type, forcing, column_slot)
    slo, shi = exchange(sdown, sup, "gx")
    ext, ks, steep, cap, cond, deriv, store, water = call(
        soil_kernel, [main] * 8, 5, in_specs=[smem] + [vmem] * 4
    )(soil_table, head_old, soil_type, lo, hi)
    ydown, yup = call(strip_kernel, [((3, tall, LANES), f32)] * 2, 7)(
        head_old, soil_type, lo, hi, source, slo, shi
    )
    ylo, yhi = exchange(ydown, yup, "gy")
    ext_s, ks_s, steep_s, cap_s, base, base_s, p0, p1, p2, p0_s, p1_s, p2_s, gram = call(
        first_kernel,
        [side] * 4 + [main, side] + [main] * 3 + [side] * 3 + [gram_block],
        12,
        scratch=[pltpu.VMEM(side[0], f32)] * 4 + newton_scratch(layers, tall, cols),
        in_specs=[smem] + [vmem] * 11,
    )(soil_table, source, slo, shi, ylo, yhi, ext, ks, cond, deriv, store, water)
    sums = spread(gram)
    part, q0, q1, q2, gram = call(
        second_kernel,
        [own] + [main] * 3 + [gram_block],
        17,
        scratch=[pltpu.VMEM(side[0], f32)] * 3
        + [pltpu.VMEM(main[0], f32)] * 5
        + [pltpu.VMEM(side[0], f32)] * 5
        + newton_scratch(layers, tall, cols),
    )(sums, ext, ks, steep, cap, base, p0, p1, p2, ext_s, ks_s, steep_s, cap_s, base_s, p0_s, p1_s, p2_s)
    sums = spread(gram)
    (head,) = call(last_kernel, [own], 5)(sums, part, q0, q1, q2)
    return head, flux


def solution(mesh):
    return jax.shard_map(
        shards,
        mesh=mesh,
        in_specs=(
            P(None, "gx", "gy"),
            P(None, "gx", "gy"),
            P(),
            P(None, "gx", "gy"),
            P(None, ("gx", "gy")),
            P("gx", "gy"),
        ),
        out_specs=(P(None, "gx", "gy"), P(None, "gx", "gy")),
        check_vma=False,
    )
```

time: 86.6 us -> 85.7 us (0.990)
  Pallas kernels: 25.9 us -> 28 us
  blocking collectives: 25.6 us -> 24.1 us
  local copies, waits for them, and re-layouts: 2.86 us -> 1.93 us
  waiting for transfers between devices: 12.3 us -> 11.4 us
    ppermute x3, waiting for transfers between devices: 2.06 us -> 8.57 us  [exchange(): lax.ppermute(to_upper, axis, up)]
    ppermute x3, waiting for transfers between devices: 6.94 us -> 0.82 us  [exchange(): lax.ppermute(to_lower, axis, down)]
    pallas_call x5 -> x7, Pallas kernels: 25.6 us -> 27.7 us  [the longest x1 9.17 us: shards(): call(first_kernel, [side] * 4 + [main, side] + [main] * 3 + [side] * 3 +...]
    all_to_all x2, blocking collectives: 25.6 us -> 24.1 us  [spread(): return lax.all_to_all(x, both, split_axis=0, concat_axis=0, tiled=True)]
    all_to_all x1, waiting for transfers between devices: 3.32 us -> 2.04 us  [spread(): return lax.all_to_all(x, both, split_axis=0, concat_axis=0, tiled=True)]
    unnamed x16 -> x14, local copies, waits for them, and re-layouts: 2.86 us -> 1.93 us
where the time goes in v2:
time: 85.7 us; the launch traced here: 85.4 us
  Pallas kernels  28 us (33%)
  blocking collectives  24.1 us (28%)
  starting transfers between devices  19.1 us (22%)
  waiting for transfers between devices  11.4 us (13%)
  local copies, waits for them, and re-layouts  1.93 us (2%)
    all_to_all x2, blocking collectives, spread(): return lax.all_to_all(x, both, split_axis=0, concat_axis=0, tiled=True)  24.1 us
    pallas_call x1, Pallas kernels, shards(): call(first_kernel, [side] * 4 + [main, side] + [main] * 3 + [side] * 3 +...  9.17 us
    ppermute x3, waiting for transfers between devices, exchange(): lax.ppermute(to_upper, axis, up)  8.57 us
    pallas_call x1, Pallas kernels, shards(): call(second_kernel, [own] + [main] * 3 + [gram_block], 17, scratch=[pltpu...  8.32 us
    ppermute x3, starting transfers between devices, exchange(): lax.ppermute(to_upper, axis, up)  7.91 us
    all_to_all x1, starting transfers between devices, spread(): return lax.all_to_all(x, both, split_axis=0, concat_axis=0, tiled=True)  7.3 us
    pallas_call x1, Pallas kernels, shards(): call(source_kernel, [own, edge, edge, ((2, rows, cols), f32)], 6, scratch...  5.61 us
    ppermute x3, starting transfers between devices, exchange(): lax.ppermute(to_lower, axis, down)  3.88 us
  transfers between devices with their start and end apart: 7, of which 4 were waited for; matrix products, arithmetic and copies ran while one was open for 0% of the time, Pallas kernels for 9%

profile of v2, /device:TPU:0, one launch (start us, length us, event | category | flops | bytes accessed | tf_op | source)
XLA Modules:
  0.0 85.4 jit_solution(11054044139979161616)
XLA Ops:
  0.6 0.0 copy-start
  0.6 0.0 copy-start.3
  0.6 0.9 %copy-done.3 = f32[13,2048]{1,0:T(8,128)S(1)} copy-done((f32[13,2048]{1,0:T(8,128)S(1)}, f32[13,2048]{1,0:T(8,128)}, u32[]{:S(2)}) %copy-start.3) | copy-done | bytes 106520
  1.6 1.0 %shard_map.77 = f32[32,8,128]{2,1,0:T(8,128)} custom-call(f32[13,2048]{1,0:T(8,128)S(1)} %copy-done.3), custom_call_target="tpu_custom_call" | custom-call | flops 1000000 | bytes 1000000 | tf_op jit(solution)/shard_map/pallas_call | solution.py:644
  2.6 7.3 %all-to-all-start = ((f32[32,8,128]{2,1,0:T(8,128)}), f32[32,8,128]{2,1,0:T(8,128)S(1)}, u32[]{:S(2)}, u32[]{:S(2)}) async-start(f32[32,8,128]{2,1,0:T(8,128)} %shard_map.77), calls=%async_computation | async-start | bytes 262144 | tf_op jit(solution)/shard_map/all_to_all | solution.py:642
  9.9 0.0 copy-done
  9.9 0.0 copy-start.1
  9.9 1.0 %copy-done.1 = s32[10,16,512]{2,1,0:T(8,128)S(1)} copy-done((s32[10,16,512]{2,1,0:T(8,128)S(1)}, s32[10,16,512]{2,1,0:T(8,128)}, u32[]{:S(2)}) %copy-start.1) | copy-done | bytes 327704
  10.9 0.0 copy-start.6
  10.9 3.8 %collective-permute-start.2 = (f32[20,8,512]{2,1,0:T(8,128)S(1)}, f32[20,8,512]{2,1,0:T(8,128)S(1)}, u32[]{:S(2)}, u32[]{:S(2)}) collective-permute-start(f32[20,8,512]{2,1,0:T(8,128)S(1)} %get-tuple-element.39), channel_id=1, source_target_pairs={{0,4},{4,8},{8,12},{12,16},{16,20},{20,24},{24,28},{1,5},{5,9},{9,... | collective-permute-start | bytes 983048 | tf_op jit(solution)/shard_map/ppermute | solution.py:639
  14.7 1.3 %collective-permute-start.3 = (f32[20,8,512]{2,1,0:T(8,128)S(1)}, f32[20,8,512]{2,1,0:T(8,128)S(1)}, u32[]{:S(2)}, u32[]{:S(2)}) collective-permute-start(f32[20,8,512]{2,1,0:T(8,128)S(1)} %get-tuple-element.40), channel_id=1, source_target_pairs={{4,0},{8,4},{12,8},{16,12},{20,16},{24,20},{28,24},{5,1},{9,5},{13... | collective-permute-start | bytes 983048 | tf_op jit(solution)/shard_map/ppermute | solution.py:639
  16.0 2.0 %all-to-all-done.arrived_ref = f32[32,8,128]{2,1,0:T(8,128)S(1)} async-done(((f32[32,8,128]{2,1,0:T(8,128)}), f32[32,8,128]{2,1,0:T(8,128)S(1)}, u32[]{:S(2)}, u32[]{:S(2)}) %all-to-all-start) | async-done | bytes 131104 | tf_op jit(solution)/shard_map/all_to_all | solution.py:642
  18.1 0.0 copy-done.2
  18.1 0.0 copy-done.5
  18.1 5.6 %shard_map.78 = (f32[10,16,512]{2,1,0:T(8,128)S(1)}, f32[10,8,512]{2,1,0:T(8,128)S(1)}, f32[10,8,512]{2,1,0:T(8,128)S(1)}, f32[2,16,512]{2,1,0:T(8,128)}) custom-call(f32[3,12]{1,0:T(4,128)S(1)} %copy-done.6, f32[32,8,128]{2,1,0:T(8,128)S(1)} %all-to-all-done.arrived_ref, f32[10,16,512]{2,1,0:T(8,128)S(1)} %copy-done, s32[10,16,512]{2,1,0:T(8,128)S(1)} %copy-done.2, ...), custom_call_target="tpu_custom_call" | custom-call | flops 1000000 | bytes 1000000 | tf_op jit(solution)/shard_map/pallas_call | solution.py:648
  23.7 2.7 %collective-permute-start = (f32[10,8,512]{2,1,0:T(8,128)S(1)}, f32[10,8,512]{2,1,0:T(8,128)S(1)}, u32[]{:S(2)}, u32[]{:S(2)}) collective-permute-start(f32[10,8,512]{2,1,0:T(8,128)S(1)} %get-tuple-element.37), channel_id=1, source_target_pairs={{0,4},{4,8},{8,12},{12,16},{16,20},{20,24},{24,28},{1,5},{5,9},{9,... | collective-permute-start | bytes 491528 | tf_op jit(solution)/shard_map/ppermute | solution.py:639
  26.4 1.3 %collective-permute-start.1 = (f32[10,8,512]{2,1,0:T(8,128)S(1)}, f32[10,8,512]{2,1,0:T(8,128)S(1)}, u32[]{:S(2)}, u32[]{:S(2)}) collective-permute-start(f32[10,8,512]{2,1,0:T(8,128)S(1)} %get-tuple-element.38), channel_id=1, source_target_pairs={{4,0},{8,4},{12,8},{16,12},{20,16},{24,20},{28,24},{5,1},{9,5},{13... | collective-permute-start | bytes 491528 | tf_op jit(solution)/shard_map/ppermute | solution.py:639
  27.7 2.1 %collective-permute-done.2.lo_ref = f32[20,8,512]{2,1,0:T(8,128)S(1)} collective-permute-done((f32[20,8,512]{2,1,0:T(8,128)S(1)}, f32[20,8,512]{2,1,0:T(8,128)S(1)}, u32[]{:S(2)}, u32[]{:S(2)}) %collective-permute-start.2) | collective-permute-done | bytes 327712 | tf_op jit(solution)/shard_map/ppermute | solution.py:639
  29.8 0.0 collective-permute-done.3.hi_ref
  29.8 6.4 %collective-permute-done.slo_ref = f32[10,8,512]{2,1,0:T(8,128)S(1)} collective-permute-done((f32[10,8,512]{2,1,0:T(8,128)S(1)}, f32[10,8,512]{2,1,0:T(8,128)S(1)}, u32[]{:S(2)}, u32[]{:S(2)}) %collective-permute-start) | collective-permute-done | bytes 163872 | tf_op jit(solution)/shard_map/ppermute | solution.py:639
  36.3 0.0 collective-permute-done.1.shi_ref
  36.3 0.3 shard_map.80
  36.6 1.4 %collective-permute-start.4 = (f32[3,32,128]{2,1,0:T(8,128)S(1)}, f32[3,32,128]{2,1,0:T(8,128)S(1)}, u32[]{:S(2)}, u32[]{:S(2)}) collective-permute-start(f32[3,32,128]{2,1,0:T(8,128)S(1)} %get-tuple-element.41), channel_id=1, source_target_pairs={{0,1},{1,2},{2,3},{4,5},{5,6},{6,7},{8,9},{9,10},{10,11},{12,13},{... | collective-permute-start | bytes 147464 | tf_op jit(solution)/shard_map/ppermute | solution.py:639
  38.0 1.3 %collective-permute-start.5 = (f32[3,32,128]{2,1,0:T(8,128)S(1)}, f32[3,32,128]{2,1,0:T(8,128)S(1)}, u32[]{:S(2)}, u32[]{:S(2)}) collective-permute-start(f32[3,32,128]{2,1,0:T(8,128)S(1)} %get-tuple-element.42), channel_id=1, source_target_pairs={{1,0},{2,1},{3,2},{5,4},{6,5},{7,6},{9,8},{10,9},{11,10},{13,12},{... | collective-permute-start | bytes 147464 | tf_op jit(solution)/shard_map/ppermute | solution.py:639
  39.3 2.5 %shard_map.81 = (f32[10,32,512]{2,1,0:T(8,128)S(1)}, f32[10,32,512]{2,1,0:T(8,128)S(1)}, f32[10,32,512]{2,1,0:T(8,128)S(1)}, f32[10,32,512]{2,1,0:T(8,128)S(1)},...) custom-call(f32[3,12]{1,0:T(4,128)S(1)} %copy-done.6, ...), custom_call_target="tpu_custom_call" | custom-call | flops 1000000 | bytes 1000000 | tf_op jit(solution)/shard_map/pallas_call | solution.py:656
  41.8 0.0 collective-permute-done.4.ylo_ref
  41.8 0.8 collective-permute-done.5.yhi_ref
  42.6 9.2 %shard_map.82 = (f32[10,32,128]{2,1,0:T(8,128)S(1)}, f32[10,32,128]{2,1,0:T(8,128)S(1)}, f32[10,32,128]{2,1,0:T(8,128)S(1)}, f32[10,32,128]{2,1,0:T(8,128)S(1)},...) custom-call(f32[3,12]{1,0:T(4,128)S(1)} %copy-done.6, ...), custom_call_target="tpu_custom_call" | custom-call | flops 1000000 | bytes 1000000 | tf_op jit(solution)/shard_map/pallas_call | solution.py:663
  51.8 15.3 %all_to_all.15.arrived_ref = f32[32,1,128]{2,1,0:T(1,128)S(1)} all-to-all(f32[32,1,128]{2,1,0:T(1,128)S(1)} %get-tuple-element.49), channel_id=1, replica_groups=mesh['gx'=8,'gy'=4] {'gx','gy'}, dimensions={0} | all-to-all | bytes 32768 | tf_op jit(solution)/shard_map/all_to_all | solution.py:642
  67.1 8.3 %shard_map.83 = (f32[10,16,512]{2,1,0:T(8,128)S(1)}, f32[10,32,512]{2,1,0:T(8,128)S(1)}, f32[10,32,512]{2,1,0:T(8,128)S(1)}, f32[10,32,512]{2,1,0:T(8,128)S(1)}, f32[32,1,128]{2,1,0:T(1,128)S(1)}) custom-call(f32[32,1,128]{2,1,0:T(1,128)S(1)} %all_to_all.15.arrived_ref, f32[10,32,512]{2,1,0:T(8,128)S(1)} %get-tuple-element.43.ext_ref.old_ref, ...), custom_call_target="tpu_custom_call" | custom-call | flops 1000000 | bytes 1000000 | tf_op jit(solution)/shard_map/pallas_call | solution.py:671
  75.4 8.8 %all_to_all.16.arrived_ref = f32[32,1,128]{2,1,0:T(1,128)S(1)} all-to-all(f32[32,1,128]{2,1,0:T(1,128)S(1)} %get-tuple-element.64), channel_id=1, replica_groups=mesh['gx'=8,'gy'=4] {'gx','gy'}, dimensions={0} | all-to-all | bytes 32768 | tf_op jit(solution)/shard_map/all_to_all | solution.py:642
  84.2 1.1 %shard_map.84 = f32[10,16,512]{2,1,0:T(8,128)} custom-call(f32[32,1,128]{2,1,0:T(1,128)S(1)} %all_to_all.16.arrived_ref, f32[10,16,512]{2,1,0:T(8,128)S(1)} %get-tuple-element.65.part_ref, f32[10,32,512]{2,1,0:T(8,128)S(1)} %get-tuple-element.66.q0_ref, f32[10,32,512]{2,1,0:T(8,128)S(1)} %get-tuple-element.67.q1_ref, f32[10,32,512]{2,1,0:T(8,128)S(1)} %get-tuple-element.68.q2_ref), custom_call_target="tpu_custom_call" | custom-call | flops 1000000 | bytes 1000000 | tf_op jit(solution)/shard_map/pallas_call | solution.py:681
  (6 shorter events, 0.1 us)
Async XLA Ops:
  0.6 9.2 %copy-start = (f32[10,16,512]{2,1,0:T(8,128)S(1)}, f32[10,16,512]{2,1,0:T(8,128)}, u32[]{:S(2)}) copy-start(f32[10,16,512]{2,1,0:T(8,128)} %head_ref.7) | copy-start | bytes 983044
  0.6 1.0 %copy-start.3 = (f32[13,2048]{1,0:T(8,128)S(1)}, f32[13,2048]{1,0:T(8,128)}, u32[]{:S(2)}) copy-start(f32[13,2048]{1,0:T(8,128)} %canopy_ref.1) | copy-start | bytes 319492
  2.6 15.5 %all-to-all-start = ((f32[32,8,128]{2,1,0:T(8,128)}), f32[32,8,128]{2,1,0:T(8,128)S(1)}, u32[]{:S(2)}, u32[]{:S(2)}) async-start(f32[32,8,128]{2,1,0:T(8,128)} %shard_map.77), calls=%async_computation | async-start | bytes 262144 | tf_op jit(solution)/shard_map/all_to_all | solution.py:642
  9.9 1.0 %copy-start.1 = (s32[10,16,512]{2,1,0:T(8,128)S(1)}, s32[10,16,512]{2,1,0:T(8,128)}, u32[]{:S(2)}) copy-start(s32[10,16,512]{2,1,0:T(8,128)} %soil_ref.7) | copy-start | bytes 983044
  10.8 7.2 %copy-start.2 = (s32[10,16,512]{2,1,0:T(8,128)S(1)}, s32[10,16,512]{2,1,0:T(8,128)}, u32[]{:S(2)}) copy-start(s32[10,16,512]{2,1,0:T(8,128)} %soil_ref.7) | copy-start | bytes 983044
  10.8 7.2 %copy-start.4 = (f32[4,16,512]{2,1,0:T(8,128)S(1)}, f32[4,16,512]{2,1,0:T(8,128)}, u32[]{:S(2)}) copy-start(f32[4,16,512]{2,1,0:T(8,128)} %forcing_ref.1) | copy-start | bytes 393220
  10.8 7.2 %copy-start.5 = (s32[16,512]{1,0:T(8,128)S(1)}, s32[16,512]{1,0:T(8,128)}, u32[]{:S(2)}) copy-start(s32[16,512]{1,0:T(8,128)} %slot_ref.1) | copy-start | bytes 98308
  10.9 7.2 %copy-start.6 = (f32[3,12]{1,0:T(4,128)S(1)}, f32[3,12]{1,0:T(4,128)}, u32[]{:S(2)}) copy-start(f32[3,12]{1,0:T(4,128)} %table_ref.5) | copy-start | bytes 436
  10.9 18.9 %collective-permute-start.2 = (f32[20,8,512]{2,1,0:T(8,128)S(1)}, f32[20,8,512]{2,1,0:T(8,128)S(1)}, u32[]{:S(2)}, u32[]{:S(2)}) collective-permute-start(f32[20,8,512]{2,1,0:T(8,128)S(1)} %get-tuple-element.39), channel_id=1, source_target_pairs={{0,4},{4,8},{8,12},{12,16},{16,20},{20,24},{24,28},{1,5},{5,9},{9,... | collective-permute-start | bytes 983048 | tf_op jit(solution)/shard_map/ppermute | solution.py:639
  14.7 15.1 %collective-permute-start.3 = (f32[20,8,512]{2,1,0:T(8,128)S(1)}, f32[20,8,512]{2,1,0:T(8,128)S(1)}, u32[]{:S(2)}, u32[]{:S(2)}) collective-permute-start(f32[20,8,512]{2,1,0:T(8,128)S(1)} %get-tuple-element.40), channel_id=1, source_target_pairs={{4,0},{8,4},{12,8},{16,12},{20,16},{24,20},{28,24},{5,1},{9,5},{13... | collective-permute-start | bytes 983048 | tf_op jit(solution)/shard_map/ppermute | solution.py:639
  23.7 12.5 %collective-permute-start = (f32[10,8,512]{2,1,0:T(8,128)S(1)}, f32[10,8,512]{2,1,0:T(8,128)S(1)}, u32[]{:S(2)}, u32[]{:S(2)}) collective-permute-start(f32[10,8,512]{2,1,0:T(8,128)S(1)} %get-tuple-element.37), channel_id=1, source_target_pairs={{0,4},{4,8},{8,12},{12,16},{16,20},{20,24},{24,28},{1,5},{5,9},{9,... | collective-permute-start | bytes 491528 | tf_op jit(solution)/shard_map/ppermute | solution.py:639
  26.4 9.9 %collective-permute-start.1 = (f32[10,8,512]{2,1,0:T(8,128)S(1)}, f32[10,8,512]{2,1,0:T(8,128)S(1)}, u32[]{:S(2)}, u32[]{:S(2)}) collective-permute-start(f32[10,8,512]{2,1,0:T(8,128)S(1)} %get-tuple-element.38), channel_id=1, source_target_pairs={{4,0},{8,4},{12,8},{16,12},{20,16},{24,20},{28,24},{5,1},{9,5},{13... | collective-permute-start | bytes 491528 | tf_op jit(solution)/shard_map/ppermute | solution.py:639
  36.6 5.2 %collective-permute-start.4 = (f32[3,32,128]{2,1,0:T(8,128)S(1)}, f32[3,32,128]{2,1,0:T(8,128)S(1)}, u32[]{:S(2)}, u32[]{:S(2)}) collective-permute-start(f32[3,32,128]{2,1,0:T(8,128)S(1)} %get-tuple-element.41), channel_id=1, source_target_pairs={{0,1},{1,2},{2,3},{4,5},{5,6},{6,7},{8,9},{9,10},{10,11},{12,13},{... | collective-permute-start | bytes 147464 | tf_op jit(solution)/shard_map/ppermute | solution.py:639
  38.0 4.6 %collective-permute-start.5 = (f32[3,32,128]{2,1,0:T(8,128)S(1)}, f32[3,32,128]{2,1,0:T(8,128)S(1)}, u32[]{:S(2)}, u32[]{:S(2)}) collective-permute-start(f32[3,32,128]{2,1,0:T(8,128)S(1)} %get-tuple-element.42), channel_id=1, source_target_pairs={{1,0},{2,1},{3,2},{5,4},{6,5},{7,6},{9,8},{10,9},{11,10},{13,12},{... | collective-permute-start | bytes 147464 | tf_op jit(solution)/shard_map/ppermute | solution.py:639

commit v3 on v1

v3 whole, which is shorter than its diff:
```python
import functools

import jax
import jax.numpy as jnp
from jax import lax
from jax.experimental import pallas as pl
from jax.experimental.pallas import tpu as pltpu
from jax.sharding import PartitionSpec as P

NEWTON = 2
KRYLOV = 3
HALO = 8
SOURCE_DEPTH = 6
LANES = 128
SLOT = 64

storage_weight = 4.0
norm_epsilon = 1e-06

VMEM_LIMIT = 40 * 1024 * 1024
PAIRS = [(i, j) for i in range(KRYLOV + 1) for j in range(i, KRYLOV + 1)]

f32 = jnp.float32
vmem = pl.BlockSpec(memory_space=pltpu.VMEM)
smem = pl.BlockSpec(memory_space=pltpu.SMEM)


def call(body, outs, n_in, scratch=(), in_specs=None, flops=1000000):
    return pl.pallas_call(
        body,
        out_shape=[jax.ShapeDtypeStruct(s, d) for s, d in outs],
        in_specs=in_specs or [vmem] * n_in,
        out_specs=[vmem] * len(outs),
        scratch_shapes=list(scratch),
        compiler_params=pltpu.CompilerParams(vmem_limit_bytes=VMEM_LIMIT),
        cost_estimate=pl.CostEstimate(flops=flops, bytes_accessed=1000000, transcendentals=0),
    )


def lane_iota(shape):
    return lax.broadcasted_iota(jnp.int32, shape, len(shape) - 1)


def pack_kernel(
    canopy_hbm, head_hbm, soil_hbm, send_ref, down_ref, up_ref, canopy_ref, head_ref, soil_ref, sems
):
    copies = [
        pltpu.make_async_copy(head_hbm, head_ref, sems.at[0]),
        pltpu.make_async_copy(soil_hbm, soil_ref, sems.at[1]),
        pltpu.make_async_copy(canopy_hbm, canopy_ref, sems.at[2]),
    ]
    for copy in copies:
        copy.start()
    layers, width, _ = head_ref.shape
    copies[0].wait()
    copies[1].wait()
    for out_ref, at in ((down_ref, 0), (up_ref, width - HALO)):
        for k in range(layers):
            out_ref[k] = head_ref[k, at : at + HALO, :]
            out_ref[layers + k] = (soil_ref[k, at : at + HALO, :] + 1).astype(f32)
    copies[2].wait()
    rows = canopy_ref.shape[0]
    low = lane_iota((8, LANES)) < SLOT
    for t in range(canopy_ref.shape[1] // LANES):
        here = slice(t * LANES, (t + 1) * LANES)
        first = canopy_ref[0:8, here]
        rest = jnp.concatenate([canopy_ref[8:rows, here], jnp.zeros((16 - rows, LANES), f32)], axis=0)
        send_ref[2 * t] = jnp.where(low, first, pltpu.roll(rest, SLOT, 1))
        send_ref[2 * t + 1] = jnp.where(low, pltpu.roll(first, SLOT, 1), rest)


def table_rows(table_ref, rows):
    lane = lane_iota((rows, LANES))
    out = []
    for field in range(table_ref.shape[0]):
        row = jnp.zeros((rows, LANES), f32)
        for kind in range(table_ref.shape[1]):
            row = jnp.where(lane == kind + 1, table_ref[field, kind], row)
        out.append(row)
    return out


def lookup(row, index):
    pieces = [
        jnp.take_along_axis(row, index[:, at : at + LANES], axis=1, mode="promise_in_bounds")
        for at in range(0, index.shape[1], LANES)
    ]
    return jnp.concatenate(pieces, axis=1)


def sigmoid(u):
    return 1.0 / (1.0 + jnp.exp(-u))


def source_kernel(
    table_ref, arrived_ref, head_ref, soil_ref, forcing_ref, slot_ref,
    source_ref, down_ref, up_ref, flux_ref, tab_ref,
):
    layers, rows, cols = head_ref.shape
    owners = arrived_ref.shape[0]
    low = lane_iota((8, LANES)) < SLOT
    line = lax.broadcasted_iota(jnp.int32, (16, LANES), 0)
    is_root = (line >= 3) & (line < 3 + layers)

    def unpack(t, _):
        first = arrived_ref[2 * t]
        second = arrived_ref[2 * t + 1]
        both = jnp.concatenate(
            [
                jnp.where(low, first, pltpu.roll(second, SLOT, 1)),
                jnp.where(low, pltpu.roll(first, SLOT, 1), second),
            ],
            axis=0,
        )
        leaf_area, albedo, resist = both[0:1], both[1:2], both[2:3]
        root_sum = jnp.sum(jnp.where(is_root, both, 0.0), axis=0, keepdims=True)
        both = both * (leaf_area / ((leaf_area + resist) * root_sum))
        tab_ref[t, 0] = jnp.broadcast_to(0.5 + 0.3 * leaf_area, (8, LANES))
        tab_ref[t, 1] = jnp.broadcast_to(1.0 - albedo, (8, LANES))
        for k in range(layers):
            tab_ref[t, 2 + k] = jnp.broadcast_to(both[3 + k : 4 + k], (8, LANES))
        return 0

    lax.fori_loop(0, owners // 2, unpack, 0, unroll=16)
    tables = table_rows(table_ref, 8)

    for at_x in range(0, rows, 8):

        def column(j, _):
            here = (slice(at_x, at_x + 8), pl.ds(pl.multiple_of(j * LANES, LANES), LANES))
            slot = slot_ref[here]
            land = slot >= 0
            value = jnp.maximum(slot, 0)
            lane = value & (LANES - 1)
            tile = value >> 7

            def pick(t, held):
                match = tile == t
                return tuple(
                    jnp.where(match, lookup(tab_ref[t, k], lane), held[k]) for k in range(2 + layers)
                )

            start = tuple(jnp.ones((8, LANES), f32) for _ in range(2 + layers))
            exchange_coef, absorbed, *roots = lax.fori_loop(0, owners // 2, pick, start, unroll=8)
            uptake = []
            for k in range(layers):
                index = soil_ref[(k,) + here] + 1
                steep = lookup(tables[1], index)
                uptake.append(roots[k] * sigmoid(steep * head_ref[(k,) + here]))
                if k == 0:
                    ks_top = lookup(tables[0], index)
            conductance = functools.reduce(jnp.add, uptake)
            sunlight, air_temp, humidity, rainfall = (forcing_ref[(i,) + here] for i in range(4))
            radiation = absorbed * sunlight + 0.3
            square = air_temp * air_temp
            excess = radiation - 0.3 * square * square - conductance * (0.5 - humidity)
            slope = -1.2 * square * air_temp - exchange_coef - conductance
            rise = -excess / slope
            surface = air_temp + rise
            vapour = 0.5 * jnp.exp(2.0 * rise)
            square = surface * surface
            excess = (
                radiation
                - 0.3 * square * square
                - exchange_coef * rise
                - conductance * (vapour - humidity)
            )
            slope = -1.2 * square * surface - exchange_coef - 2.0 * conductance * vapour
            rise = rise - excess / slope
            rate = 0.5 * jnp.exp(2.0 * rise) - humidity
            infiltration = rainfall * ks_top / (rainfall + ks_top)
            infiltration = jnp.where(land, infiltration, 0.0)
            rate = jnp.where(land, rate, 0.0)
            flux_ref[(0,) + here] = conductance * rate
            flux_ref[(1,) + here] = infiltration
            for k in range(layers):
                value = -rate * uptake[k]
                if k == 0:
                    value = value + infiltration
                source_ref[(k,) + here] = value
                edge = slice(SOURCE_DEPTH * k, SOURCE_DEPTH * (k + 1))
                if at_x < HALO:
                    down_ref[edge, here[1]] = value[:SOURCE_DEPTH]
                if at_x >= rows - HALO:
                    up_ref[edge, here[1]] = value[HALO - SOURCE_DEPTH :]
            return 0

        lax.fori_loop(0, cols // LANES, column, 0)


def strips(planes, shift_from):
    packed = None
    for k, plane in enumerate(planes):
        lane = lane_iota(plane.shape)
        shift = (HALO * k - shift_from) % LANES
        moved = pltpu.roll(plane, shift, 1) if shift else plane
        inside = (lane >= HALO * k) & (lane < HALO * (k + 1))
        packed = jnp.where(inside, moved, 0.0 if packed is None else packed)
    return packed


def strip_parts(cols):
    return ((slice(0, LANES), 0), (slice(cols - LANES, cols), LANES - HALO))


def state_strip_kernel(head_ref, soil_ref, lo_ref, hi_ref, down_ref, up_ref):
    layers, _, cols = head_ref.shape
    for out_ref, (part, shift) in zip((down_ref, up_ref), strip_parts(cols)):
        heads, soils = [], []
        for k in range(layers):
            heads.append(
                jnp.concatenate([head_ref[k, :, part], hi_ref[k, :, part], lo_ref[k, :, part]], axis=0)
            )
            soil = (soil_ref[k, :, part] + 1).astype(f32)
            ends = [hi_ref[layers + k, :, part], lo_ref[layers + k, :, part]]
            soils.append(jnp.concatenate([soil] + ends, axis=0))
        out_ref[0] = strips(heads, shift)
        out_ref[1] = strips(soils, shift)


def tall_source(src_ref, slo_ref, shi_ref, k, part):
    edge = slice(SOURCE_DEPTH * k, SOURCE_DEPTH * (k + 1))
    own = src_ref[k, :, part]
    gap = jnp.zeros((2 * (HALO - SOURCE_DEPTH), own.shape[1]), f32)
    return jnp.concatenate([own, shi_ref[edge, part], gap, slo_ref[edge, part]], axis=0)


def source_strip_kernel(src_ref, slo_ref, shi_ref, down_ref, up_ref):
    layers, _, cols = src_ref.shape
    for out_ref, (part, shift) in zip((down_ref, up_ref), strip_parts(cols)):
        out_ref[0] = strips([tall_source(src_ref, slo_ref, shi_ref, k, part) for k in range(layers)], shift)


def side(ylo_ref, yhi_ref, field, k):
    right = yhi_ref[field]
    left = ylo_ref[field]
    lane = lane_iota(right.shape)
    shift = (-HALO * k) % LANES
    right = pltpu.roll(right, shift, 1) if shift else right
    left = pltpu.roll(left, (LANES - HALO - HALO * k) % LANES, 1)
    return jnp.where(lane < HALO, right, jnp.where(lane >= LANES - HALO, left, 0.0))


def after(x, axis):
    return pltpu.roll(x, x.shape[axis] - 1, axis)


def before(x, axis):
    return pltpu.roll(x, 1, axis)


def pointwise(head, conduct, steep, capacity):
    sat = 0.5 + 0.5 * jnp.tanh(0.5 * (steep * head))
    slope = steep * sat * (1.0 - sat)
    cond = conduct * (0.1 + 0.9 * sat * sat)
    deriv = 0.9 * conduct * sat * slope
    weighted = storage_weight * capacity
    return cond, deriv, weighted * slope, weighted * sat


def linearize(head_ref, cond_ref, deriv_ref, store_ref, gain_ref, mask, coefs, out_ref, tile):
    diag_ref, xp_ref, xm_ref, yp_ref, ym_ref, az_ref, bz_ref = coefs
    layers = head_ref.shape[0]
    rows, cols = tile

    def masked(value):
        own = value[:rows, cols:] * mask[:rows, cols:]
        top = jnp.concatenate([value[:rows, :cols], own], axis=1)
        return jnp.concatenate([top, value[rows:] * mask[rows:]], axis=0)

    above = None
    for k in range(layers):
        head = head_ref[k]
        cond = cond_ref[k]
        deriv = deriv_ref[k]
        value = gain_ref[k]
        diag = store_ref[k]
        for plus_ref, minus_ref, axis in ((xp_ref, xm_ref, 0), (yp_ref, ym_ref, 1)):
            mean = 0.5 * (cond + after(cond, axis))
            drop = head - after(head, axis)
            a = mean + deriv * drop
            b = mean - after(deriv, axis) * drop
            face = mean * drop
            value = value + (face - before(face, axis))
            diag = diag + (a + before(b, axis))
            plus_ref[k] = masked(b)
            minus_ref[k] = masked(before(a, axis))
        if k + 1 < layers:
            mean = 0.5 * (cond + cond_ref[k + 1])
            drop = head - head_ref[k + 1] + 1.0
            a = mean + deriv * drop
            b = mean - deriv_ref[k + 1] * drop
            az_ref[k] = a
            bz_ref[k] = b
            face = mean * drop
        else:
            a = 2.0 * deriv
            face = cond
        diag = diag + a
        value = value + face
        if above is not None:
            diag = diag + above[1]
            value = value - above[0]
        above = (face, b)
        diag_ref[k] = diag
        out_ref[k] = masked(value)


def apply(v_ref, coefs, k):
    diag_ref, xp_ref, xm_ref, yp_ref, ym_ref, az_ref, bz_ref = coefs
    v = v_ref[k]
    value = diag_ref[k] * v
    value = value - xp_ref[k] * after(v, 0) - xm_ref[k] * before(v, 0)
    value = value - yp_ref[k] * after(v, 1) - ym_ref[k] * before(v, 1)
    if k > 0:
        value = value - az_ref[k - 1] * v_ref[k - 1]
    if k + 1 < v_ref.shape[0]:
        value = value - bz_ref[k] * v_ref[k + 1]
    return value


def powers(basis, coefs, tile, out_ref):
    layers = basis[0].shape[0]
    rows, cols = tile
    for step in range(KRYLOV - 1):
        for k in range(layers):
            basis[step + 1][k] = apply(basis[step], coefs, k)
    sums = [jnp.zeros((8, LANES), f32) for _ in PAIRS]
    for k in range(layers):
        top = apply(basis[-1], coefs, k)
        for at in range(0, rows, 8):
            for lane_at in range(0, cols, LANES):
                part = (slice(at, at + 8), slice(lane_at, lane_at + LANES))
                vs = [b[(k,) + part] for b in basis] + [top[part]]
                for e, (i, j) in enumerate(PAIRS):
                    sums[e] = sums[e] + vs[i] * vs[j]
    lines = [jnp.sum(x, axis=0, keepdims=True) for x in sums]
    lines.append(jnp.zeros((16 - len(PAIRS), LANES), f32))
    block = jnp.sum(jnp.concatenate(lines, axis=0), axis=1, keepdims=True)
    line = lax.broadcasted_iota(jnp.int32, (16, LANES), 0)
    flat = jnp.sum(jnp.where(lane_iota((16, LANES)) == line, block, 0.0), axis=0, keepdims=True)
    for d in range(out_ref.shape[0]):
        out_ref[d] = flat


def solve(gram_ref):
    total = gram_ref[0]
    for d in range(1, gram_ref.shape[0]):
        total = total + gram_ref[d]
    line = lax.broadcasted_iota(jnp.int32, (16, LANES), 0)
    spread = jnp.broadcast_to(total, (16, LANES))
    column = jnp.sum(jnp.where(lane_iota((16, LANES)) == line, spread, 0.0), axis=1, keepdims=True)
    gram = {}
    for e, (i, j) in enumerate(PAIRS):
        gram[i, j] = gram[j, i] = column[e : e + 1, :]

    def times_gram(c):
        out = []
        for i in range(KRYLOV + 1):
            out.append(functools.reduce(jnp.add, [gram[i, m] * c[m] for m in range(len(c))]))
        return out

    def dot(a, b):
        return functools.reduce(jnp.add, [x * y for x, y in zip(a, b)])

    beta = jnp.sqrt(gram[0, 0] + norm_epsilon)
    basis = [[1.0 / beta]]
    images = [times_gram(basis[0])]
    hessen = {}
    for j in range(KRYLOV):
        w = [jnp.zeros_like(beta)] + basis[j]
        for i in range(j + 1):
            product = dot(w, images[i])
            hessen[i, j] = product
            w = [w[m] - product * basis[i][m] if m < len(basis[i]) else w[m] for m in range(len(w))]
        square = jnp.maximum(dot(w, times_gram(w)), 0.0)
        length = jnp.sqrt(square + norm_epsilon)
        hessen[j + 1, j] = length
        if j + 1 < KRYLOV:
            inverse = 1.0 / length
            basis.append([x * inverse for x in w])
            images.append(times_gram(basis[-1]))
    n = KRYLOV
    normal = {}
    for a in range(n):
        for b in range(a + 1):
            normal[a, b] = functools.reduce(
                jnp.add,
                [hessen[i, a] * hessen[i, b] for i in range(n + 1) if (i, a) in hessen and (i, b) in hessen],
            )
    factor = {}
    inverse = []
    for a in range(n):
        for b in range(a + 1):
            value = normal[a, b]
            for m in range(b):
                value = value - factor[a, m] * factor[b, m]
            if a == b:
                inverse.append(lax.rsqrt(value))
            else:
                factor[a, b] = value * inverse[b]
    forward = []
    for a in range(n):
        value = hessen[0, a] * beta
        for m in range(a):
            value = value - factor[a, m] * forward[m]
        forward.append(value * inverse[a])
    backward = [None] * n
    for a in reversed(range(n)):
        value = forward[a]
        for m in range(a + 1, n):
            value = value - factor[m, a] * backward[m]
        backward[a] = value * inverse[a]
    return [
        functools.reduce(jnp.add, [backward[j] * basis[j][i] for j in range(i, n)]) for i in range(n)
    ]


def state_kernel(
    table_ref, head_ref, soil_ref, lo_ref, hi_ref, ylo_ref, yhi_ref,
    ext_ref, ks_ref, steep_ref, cap_ref, water_ref, flow_ref, *rest,
):
    coefs, (cond_ref, deriv_ref, store_ref, gain_ref) = rest[:7], rest[7:]
    layers, rows, cols = head_ref.shape
    tables = table_rows(table_ref, rows + 2 * HALO)
    mask = None
    for k in range(layers):
        head = jnp.concatenate([head_ref[k], hi_ref[k], lo_ref[k]], axis=0)
        head = jnp.concatenate([head, side(ylo_ref, yhi_ref, 0, k)], axis=1)
        ends = jnp.concatenate([hi_ref[layers + k], lo_ref[layers + k]], axis=0).astype(jnp.int32)
        index = jnp.concatenate([soil_ref[k] + 1, ends], axis=0)
        index = jnp.concatenate([index, side(ylo_ref, yhi_ref, 1, k).astype(jnp.int32)], axis=1)
        conduct, steep, capacity = (lookup(row, index) for row in tables)
        if k == 0:
            mask = (index > 0).astype(f32)
        cond, deriv, store, water = pointwise(head, conduct, steep, capacity)
        ext_ref[k] = head
        ks_ref[k] = conduct
        steep_ref[k] = steep
        cap_ref[k] = capacity
        cond_ref[k] = cond
        deriv_ref[k] = deriv
        store_ref[k] = store
        water_ref[k] = water
        gain_ref[k] = water - water_ref[k]
    linearize(ext_ref, cond_ref, deriv_ref, store_ref, gain_ref, mask, coefs, flow_ref, (rows, cols))


def first_kernel(src_ref, slo_ref, shi_ref, ylo_ref, yhi_ref, water_ref, flow_ref, *rest):
    coefs = rest[:7]
    base_ref, p0_ref, p1_ref, p2_ref, gram_ref = rest[7:]
    layers, rows, cols = src_ref.shape
    for k in range(layers):
        source = tall_source(src_ref, slo_ref, shi_ref, k, slice(0, cols))
        source = jnp.concatenate([source, side(ylo_ref, yhi_ref, 0, k)], axis=1)
        p0_ref[k] = flow_ref[k] - source
        base_ref[k] = water_ref[k] + source
    powers((p0_ref, p1_ref, p2_ref), coefs, (rows, cols), gram_ref)


def second_kernel(
    arrived_ref, old_ref, ks_ref, steep_ref, cap_ref, base_ref, q0_ref, q1_ref, q2_ref,
    part_ref, p0_ref, p1_ref, p2_ref, gram_ref, ext_ref, cond_ref, deriv_ref, store_ref, gain_ref, *coefs,
):
    layers = old_ref.shape[0]
    rows, cols = part_ref.shape[1:]
    x = solve(arrived_ref)
    for k in range(layers):
        conduct = ks_ref[k]
        if k == 0:
            mask = (conduct > 0.0).astype(f32)
        head = old_ref[k] - x[0] * q0_ref[k] - x[1] * q1_ref[k] - x[2] * q2_ref[k]
        cond, deriv, store, water = pointwise(head, conduct, steep_ref[k], cap_ref[k])
        ext_ref[k] = head
        part_ref[k] = head[:rows, :cols]
        cond_ref[k] = cond
        deriv_ref[k] = deriv
        store_ref[k] = store
        gain_ref[k] = water - base_ref[k]
    linearize(ext_ref, cond_ref, deriv_ref, store_ref, gain_ref, mask, coefs, p0_ref, (rows, cols))
    powers((p0_ref, p1_ref, p2_ref), coefs, (rows, cols), gram_ref)


def last_kernel(arrived_ref, part_ref, q0_ref, q1_ref, q2_ref, head_ref):
    layers, rows, cols = part_ref.shape
    x = solve(arrived_ref)
    for k in range(layers):
        own = (k, slice(0, rows), slice(0, cols))
        head_ref[k] = part_ref[k] - x[0] * q0_ref[own] - x[1] * q1_ref[own] - x[2] * q2_ref[own]


def shards(head_old, soil_type, soil_table, forcing, canopy, column_slot):
    layers, rows, cols = head_old.shape
    both = ("gx", "gy")
    devices = lax.axis_size("gx") * lax.axis_size("gy")
    tall, wide = rows + 2 * HALO, cols + LANES
    own, ext = ((layers, rows, cols), f32), ((layers, tall, wide), f32)
    gram_block = ((devices, 1, LANES), f32)
    in_hbm = pl.BlockSpec(memory_space=pltpu.HBM)

    def exchange(to_lower, to_upper, axis):
        size = lax.axis_size(axis)
        up = [(i, i + 1) for i in range(size - 1)]
        down = [(j, i) for i, j in up]
        return lax.ppermute(to_upper, axis, up), lax.ppermute(to_lower, axis, down)

    def spread(x):
        return lax.all_to_all(x, both, split_axis=0, concat_axis=0, tiled=True)

    send, down, up = call(
        pack_kernel,
        [((devices, 8, LANES), f32)] + [((2 * layers, HALO, cols), f32)] * 2,
        3,
        scratch=[
            pltpu.VMEM(canopy.shape, f32),
            pltpu.VMEM(head_old.shape, f32),
            pltpu.VMEM(soil_type.shape, jnp.int32),
            pltpu.SemaphoreType.DMA((3,)),
        ],
        in_specs=[in_hbm] * 3,
    )(canopy, head_old, soil_type)
    lo, hi = exchange(down, up, "gx")
    arrived = spread(send)
    edge = ((-(-SOURCE_DEPTH * layers // 8) * 8, cols), f32)
    source, sdown, sup, flux = call(
        source_kernel,
        [own, edge, edge, ((2, rows, cols), f32)],
        6,
        scratch=[pltpu.VMEM((devices // 2, 2 + layers, 8, LANES), f32)],
        in_specs=[smem] + [vmem] * 5,
    )(soil_table, arrived, head_old, soil_type, forcing, column_slot)
    slo, shi = exchange(sdown, sup, "gx")
    ydown, yup = call(state_strip_kernel, [((2, tall, LANES), f32)] * 2, 4)(head_old, soil_type, lo, hi)
    ylo, yhi = exchange(ydown, yup, "gy")
    sydown, syup = call(source_strip_kernel, [((1, tall, LANES), f32)] * 2, 3)(source, slo, shi)
    sylo, syhi = exchange(sydown, syup, "gy")
    held = [pltpu.VMEM(ext[0], f32)]
    old, ks, steep, cap, water, flow, *coefs = call(
        state_kernel, [ext] * 13, 7, scratch=held * 4, in_specs=[smem] + [vmem] * 6, flops=20000000
    )(soil_table, head_old, soil_type, lo, hi, ylo, yhi)
    base, p0, p1, p2, gram = call(first_kernel, [ext] * 4 + [gram_block], 14)(
        source, slo, shi, sylo, syhi, water, flow, *coefs
    )
    sums = spread(gram)
    part, q0, q1, q2, gram = call(
        second_kernel, [own] + [ext] * 3 + [gram_block], 9, scratch=held * 12
    )(sums, old, ks, steep, cap, base, p0, p1, p2)
    sums = spread(gram)
    (head,) = call(last_kernel, [own], 5)(sums, part, q0, q1, q2)
    return head, flux


def solution(mesh):
    return jax.shard_map(
        shards,
        mesh=mesh,
        in_specs=(
            P(None, "gx", "gy"),
            P(None, "gx", "gy"),
            P(),
            P(None, "gx", "gy"),
            P(None, ("gx", "gy")),
            P("gx", "gy"),
        ),
        out_specs=(P(None, "gx", "gy"), P(None, "gx", "gy")),
        check_vma=False,
    )
```

time: 86.6 us -> 80.6 us (0.931)
  Pallas kernels: 25.9 us -> 20.2 us
  waiting for transfers between devices: 12.3 us -> 6.99 us
  starting transfers between devices: 18.7 us -> 22.5 us
  blocking collectives: 25.6 us -> 26.7 us
    ppermute x3 -> x4, waiting for transfers between devices: 6.94 us -> 0.01 us  [exchange(): lax.ppermute(to_lower, axis, down)]
    pallas_call x6 -> x8, Pallas kernels: 25.9 us -> 20.2 us  [the longest x1 5.37 us: shards(): call(source_kernel, [own, edge, edge, ((2, rows, cols), f32)], 6, scratch...]
    ppermute x3 -> x4, starting transfers between devices: 7.54 us -> 10 us  [exchange(): lax.ppermute(to_upper, axis, up)]
    ppermute x3 -> x4, waiting for transfers between devices: 2.06 us -> 3.66 us  [exchange(): lax.ppermute(to_upper, axis, up)]
    ppermute x3 -> x4, starting transfers between devices: 3.88 us -> 5.17 us  [exchange(): lax.ppermute(to_lower, axis, down)]
    all_to_all x2, blocking collectives: 25.6 us -> 26.7 us  [spread(): return lax.all_to_all(x, both, split_axis=0, concat_axis=0, tiled=True)]
  transfers between devices with their start and end apart: 7 -> 9, of which waited for: 4 -> 3; matrix products, arithmetic and copies ran while one was open for 0% -> 0% of each run, Pallas kernels for 9% -> 13%
where the time goes in v3:
time: 80.6 us; the launch traced here: 80.1 us
  blocking collectives  26.7 us (33%)
  starting transfers between devices  22.5 us (28%)
  Pallas kernels  20.2 us (25%)
  waiting for transfers between devices  6.99 us (9%)
  local copies, waits for them, and re-layouts  2.87 us (4%)
  between operations  0.83 us (1%)
    all_to_all x2, blocking collectives, spread(): return lax.all_to_all(x, both, split_axis=0, concat_axis=0, tiled=True)  26.7 us
    ppermute x4, starting transfers between devices, exchange(): lax.ppermute(to_upper, axis, up)  10 us
    all_to_all x1, starting transfers between devices, spread(): return lax.all_to_all(x, both, split_axis=0, concat_axis=0, tiled=True)  7.3 us
    pallas_call x1, Pallas kernels, shards(): call(source_kernel, [own, edge, edge, ((2, rows, cols), f32)], 6, scratch...  5.37 us
    ppermute x4, starting transfers between devices, exchange(): lax.ppermute(to_lower, axis, down)  5.17 us
    pallas_call x1, Pallas kernels, shards(): call(second_kernel, [own] + [ext] * 3 + [gram_block], 9, scratch=held * 12)  4.98 us
    pallas_call x1, Pallas kernels, shards(): call(state_kernel, [ext] * 13, 7, scratch=held * 4, in_specs=[smem] + [vm...  4.74 us
    ppermute x4, waiting for transfers between devices, exchange(): lax.ppermute(to_upper, axis, up)  3.66 us
  transfers between devices with their start and end apart: 9, of which 3 were waited for; matrix products, arithmetic and copies ran while one was open for 0% of the time, Pallas kernels for 13%

profile of v3, /device:TPU:0, one launch (start us, length us, event | category | flops | bytes accessed | tf_op | source)
XLA Modules:
  0.0 80.1 jit_solution(6108520932093011652)
XLA Ops:
  0.6 1.0 %copy-done = f32[10,16,512]{2,1,0:T(8,128)S(1)} copy-done((f32[10,16,512]{2,1,0:T(8,128)S(1)}, f32[10,16,512]{2,1,0:T(8,128)}, u32[]{:S(2)}) %copy-start) | copy-done | bytes 327704
  1.6 1.0 %copy-done.2 = s32[10,16,512]{2,1,0:T(8,128)S(1)} copy-done((s32[10,16,512]{2,1,0:T(8,128)S(1)}, s32[10,16,512]{2,1,0:T(8,128)}, u32[]{:S(2)}) %copy-start.2) | copy-done | bytes 327704
  2.6 0.9 %copy-done.4 = f32[13,2048]{1,0:T(8,128)S(1)} copy-done((f32[13,2048]{1,0:T(8,128)S(1)}, f32[13,2048]{1,0:T(8,128)}, u32[]{:S(2)}) %copy-start.4) | copy-done | bytes 106520
  3.5 1.2 %shard_map.77 = (f32[32,8,128]{2,1,0:T(8,128)}, f32[20,8,512]{2,1,0:T(8,128)S(1)}, f32[20,8,512]{2,1,0:T(8,128)S(1)}) custom-call(f32[13,2048]{1,0:T(8,128)S(1)} %copy-done.4, f32[10,16,512]{2,1,0:T(8,128)S(1)} %copy-done, s32[10,16,512]{2,1,0:T(8,128)S(1)} %copy-done.2), custom_call_target="tpu_custom_call" | custom-call | flops 1000000 | bytes 1000000 | tf_op jit(solution)/shard_map/pallas_call | solution.py:510
  4.7 0.0 copy-start.5
  4.7 0.0 copy-start.6
  4.7 7.3 %all-to-all-start = ((f32[32,8,128]{2,1,0:T(8,128)}), f32[32,8,128]{2,1,0:T(8,128)S(1)}, u32[]{:S(2)}, u32[]{:S(2)}) async-start(f32[32,8,128]{2,1,0:T(8,128)} %get-tuple-element.36), calls=%async_computation | async-start | bytes 262144 | tf_op jit(solution)/shard_map/all_to_all | solution.py:508
  12.0 0.0 copy-start.7
  12.0 3.7 %collective-permute-start.4 = (f32[20,8,512]{2,1,0:T(8,128)S(1)}, f32[20,8,512]{2,1,0:T(8,128)S(1)}, u32[]{:S(2)}, u32[]{:S(2)}) collective-permute-start(f32[20,8,512]{2,1,0:T(8,128)S(1)} %get-tuple-element.42), channel_id=1, source_target_pairs={{0,4},{4,8},{8,12},{12,16},{16,20},{20,24},{24,28},{1,5},{5,9},{9,... | collective-permute-start | bytes 983048 | tf_op jit(solution)/shard_map/ppermute | solution.py:505
  15.7 1.3 %collective-permute-start.5 = (f32[20,8,512]{2,1,0:T(8,128)S(1)}, f32[20,8,512]{2,1,0:T(8,128)S(1)}, u32[]{:S(2)}, u32[]{:S(2)}) collective-permute-start(f32[20,8,512]{2,1,0:T(8,128)S(1)} %get-tuple-element.43), channel_id=1, source_target_pairs={{4,0},{8,4},{12,8},{16,12},{20,16},{24,20},{28,24},{5,1},{9,5},{13... | collective-permute-start | bytes 983048 | tf_op jit(solution)/shard_map/ppermute | solution.py:505
  17.0 3.3 %all-to-all-done.arrived_ref = f32[32,8,128]{2,1,0:T(8,128)S(1)} async-done(((f32[32,8,128]{2,1,0:T(8,128)}), f32[32,8,128]{2,1,0:T(8,128)S(1)}, u32[]{:S(2)}, u32[]{:S(2)}) %all-to-all-start) | async-done | bytes 131104 | tf_op jit(solution)/shard_map/all_to_all | solution.py:508
  20.4 5.4 %shard_map.78 = (f32[10,16,512]{2,1,0:T(8,128)S(1)}, f32[64,512]{1,0:T(8,128)S(1)}, f32[64,512]{1,0:T(8,128)S(1)}, f32[2,16,512]{2,1,0:T(8,128)}) custom-call(f32[3,12]{1,0:T(4,128)S(1)} %copy-done.7, f32[32,8,128]{2,1,0:T(8,128)S(1)} %all-to-all-done.arrived_ref, f32[10,16,512]{2,1,0:T(8,128)S(1)} %copy-done.1, s32[10,16,512]{2,1,0:T(8,128)S(1)} %copy-done.3, ...), custom_call_target="tpu_custom_call" | custom-call | flops 1000000 | bytes 1000000 | tf_op jit(solution)/shard_map/pallas_call | solution.py:525
  25.8 2.6 %collective-permute-start = (f32[64,512]{1,0:T(8,128)S(1)}, f32[64,512]{1,0:T(8,128)S(1)}, u32[]{:S(2)}, u32[]{:S(2)}) collective-permute-start(f32[64,512]{1,0:T(8,128)S(1)} %get-tuple-element.38), channel_id=1, source_target_pairs={{0,4},{4,8},{8,12},{12,16},{16,20},{20,24},{24,28},{1,5},{5,9},{9,... | collective-permute-start | bytes 393224 | tf_op jit(solution)/shard_map/ppermute | solution.py:505
  28.3 1.3 %collective-permute-start.1 = (f32[64,512]{1,0:T(8,128)S(1)}, f32[64,512]{1,0:T(8,128)S(1)}, u32[]{:S(2)}, u32[]{:S(2)}) collective-permute-start(f32[64,512]{1,0:T(8,128)S(1)} %get-tuple-element.39), channel_id=1, source_target_pairs={{4,0},{8,4},{12,8},{16,12},{20,16},{24,20},{28,24},{5,1},{9,5},{13... | collective-permute-start | bytes 393224 | tf_op jit(solution)/shard_map/ppermute | solution.py:505
  29.6 1.5 %collective-permute-done.4.lo_ref = f32[20,8,512]{2,1,0:T(8,128)S(1)} collective-permute-done((f32[20,8,512]{2,1,0:T(8,128)S(1)}, f32[20,8,512]{2,1,0:T(8,128)S(1)}, u32[]{:S(2)}, u32[]{:S(2)}) %collective-permute-start.4) | collective-permute-done | bytes 327712 | tf_op jit(solution)/shard_map/ppermute | solution.py:505
  31.1 0.0 collective-permute-done.5.hi_ref
  31.1 0.2 shard_map.80
  31.3 1.3 %collective-permute-start.6 = (f32[2,32,128]{2,1,0:T(8,128)S(1)}, f32[2,32,128]{2,1,0:T(8,128)S(1)}, u32[]{:S(2)}, u32[]{:S(2)}) collective-permute-start(f32[2,32,128]{2,1,0:T(8,128)S(1)} %get-tuple-element.44), channel_id=1, source_target_pairs={{0,1},{1,2},{2,3},{4,5},{5,6},{6,7},{8,9},{9,10},{10,11},{12,13},{... | collective-permute-start | bytes 98312 | tf_op jit(solution)/shard_map/ppermute | solution.py:505
  32.6 1.3 %collective-permute-start.7 = (f32[2,32,128]{2,1,0:T(8,128)S(1)}, f32[2,32,128]{2,1,0:T(8,128)S(1)}, u32[]{:S(2)}, u32[]{:S(2)}) collective-permute-start(f32[2,32,128]{2,1,0:T(8,128)S(1)} %get-tuple-element.45), channel_id=1, source_target_pairs={{1,0},{2,1},{3,2},{5,4},{6,5},{7,6},{9,8},{10,9},{11,10},{13,12},{... | collective-permute-start | bytes 98312 | tf_op jit(solution)/shard_map/ppermute | solution.py:505
  33.9 2.2 %collective-permute-done.slo_ref = f32[64,512]{1,0:T(8,128)S(1)} collective-permute-done((f32[64,512]{1,0:T(8,128)S(1)}, f32[64,512]{1,0:T(8,128)S(1)}, u32[]{:S(2)}, u32[]{:S(2)}) %collective-permute-start) | collective-permute-done | bytes 131104 | tf_op jit(solution)/shard_map/ppermute | solution.py:505
  36.1 0.0 collective-permute-done.1.shi_ref
  36.1 0.1 shard_map.79
  36.3 2.5 %collective-permute-start.2 = (f32[1,32,128]{2,1,0:T(8,128)S(1)}, f32[1,32,128]{2,1,0:T(8,128)S(1)}, u32[]{:S(2)}, u32[]{:S(2)}) collective-permute-start(f32[1,32,128]{2,1,0:T(8,128)S(1)} %get-tuple-element.40), channel_id=1, source_target_pairs={{0,1},{1,2},{2,3},{4,5},{5,6},{6,7},{8,9},{9,10},{10,11},{12,13},{... | collective-permute-start | bytes 49160 | tf_op jit(solution)/shard_map/ppermute | solution.py:505
  38.7 1.3 %collective-permute-start.3 = (f32[1,32,128]{2,1,0:T(8,128)S(1)}, f32[1,32,128]{2,1,0:T(8,128)S(1)}, u32[]{:S(2)}, u32[]{:S(2)}) collective-permute-start(f32[1,32,128]{2,1,0:T(8,128)S(1)} %get-tuple-element.41), channel_id=1, source_target_pairs={{1,0},{2,1},{3,2},{5,4},{6,5},{7,6},{9,8},{10,9},{11,10},{13,12},{... | collective-permute-start | bytes 49160 | tf_op jit(solution)/shard_map/ppermute | solution.py:505
  40.0 0.0 collective-permute-done.7.yhi_ref
  40.1 4.7 %shard_map.81 = (f32[10,32,640]{2,1,0:T(8,128)S(1)}, f32[10,32,640]{2,1,0:T(8,128)S(1)}, f32[10,32,640]{2,1,0:T(8,128)S(1)}, f32[10,32,640]{2,1,0:T(8,128)S(1)},...) custom-call(f32[3,12]{1,0:T(4,128)S(1)} %copy-done.7, ...), custom_call_target="tpu_custom_call" | custom-call | flops 20000000 | bytes 1000000 | tf_op jit(solution)/shard_map/pallas_call | solution.py:538
  44.8 0.0 collective-permute-done.2.ylo_ref
  44.8 2.5 %shard_map.82 = (f32[10,32,640]{2,1,0:T(8,128)S(1)}, f32[10,32,640]{2,1,0:T(8,128)S(1)}, f32[10,32,640]{2,1,0:T(8,128)S(1)}, f32[10,32,640]{2,1,0:T(8,128)S(1)}, f32[32,1,128]{2,1,0:T(1,128)S(1)}) custom-call(f32[10,16,512]{2,1,0:T(8,128)S(1)} %get-tuple-element.37.src_ref, f32[64,512]{1,0:T(8,128)S(1)} %collective-permute-done.slo_ref, ...), custom_call_target="tpu_custom_call" | custom-call | flops 1000000 | bytes 1000000 | tf_op jit(solution)/shard_map/pallas_call | solution.py:541
  47.3 17.9 %all_to_all.15.arrived_ref = f32[32,1,128]{2,1,0:T(1,128)S(1)} all-to-all(f32[32,1,128]{2,1,0:T(1,128)S(1)} %get-tuple-element.55), channel_id=1, replica_groups=mesh['gx'=8,'gy'=4] {'gx','gy'}, dimensions={0} | all-to-all | bytes 32768 | tf_op jit(solution)/shard_map/all_to_all | solution.py:508
  65.2 5.0 %shard_map.83 = (f32[10,16,512]{2,1,0:T(8,128)S(1)}, f32[10,32,640]{2,1,0:T(8,128)S(1)}, f32[10,32,640]{2,1,0:T(8,128)S(1)}, f32[10,32,640]{2,1,0:T(8,128)S(1)}, f32[32,1,128]{2,1,0:T(1,128)S(1)}) custom-call(f32[32,1,128]{2,1,0:T(1,128)S(1)} %all_to_all.15.arrived_ref, f32[10,32,640]{2,1,0:T(8,128)S(1)} %get-tuple-element.56.old_ref, ...), custom_call_target="tpu_custom_call" | custom-call | flops 1000000 | bytes 1000000 | tf_op jit(solution)/shard_map/pallas_call | solution.py:545
  70.2 8.8 %all_to_all.16.arrived_ref = f32[32,1,128]{2,1,0:T(1,128)S(1)} all-to-all(f32[32,1,128]{2,1,0:T(1,128)S(1)} %get-tuple-element.64), channel_id=1, replica_groups=mesh['gx'=8,'gy'=4] {'gx','gy'}, dimensions={0} | all-to-all | bytes 32768 | tf_op jit(solution)/shard_map/all_to_all | solution.py:508
  79.0 1.1 %shard_map.84 = f32[10,16,512]{2,1,0:T(8,128)} custom-call(f32[32,1,128]{2,1,0:T(1,128)S(1)} %all_to_all.16.arrived_ref, f32[10,16,512]{2,1,0:T(8,128)S(1)} %get-tuple-element.65.part_ref, f32[10,32,640]{2,1,0:T(8,128)S(1)} %get-tuple-element.66.q0_ref, f32[10,32,640]{2,1,0:T(8,128)S(1)} %get-tuple-element.67.q1_ref, f32[10,32,640]{2,1,0:T(8,128)S(1)} %get-tuple-element.68.q2_ref), custom_call_target="tpu_custom_call" | custom-call | flops 1000000 | bytes 1000000 | tf_op jit(solution)/shard_map/pallas_call | solution.py:549
  (12 shorter events, 0.0 us)
Async XLA Ops:
  0.6 1.0 %copy-start = (f32[10,16,512]{2,1,0:T(8,128)S(1)}, f32[10,16,512]{2,1,0:T(8,128)}, u32[]{:S(2)}) copy-start(f32[10,16,512]{2,1,0:T(8,128)} %head_ref.5) | copy-start | bytes 983044
  1.6 1.0 %copy-start.2 = (s32[10,16,512]{2,1,0:T(8,128)S(1)}, s32[10,16,512]{2,1,0:T(8,128)}, u32[]{:S(2)}) copy-start(s32[10,16,512]{2,1,0:T(8,128)} %soil_ref.5) | copy-start | bytes 983044
  2.6 0.9 %copy-start.4 = (f32[13,2048]{1,0:T(8,128)S(1)}, f32[13,2048]{1,0:T(8,128)}, u32[]{:S(2)}) copy-start(f32[13,2048]{1,0:T(8,128)} %canopy_hbm.1) | copy-start | bytes 319492
  3.5 16.9 %copy-start.1 = (f32[10,16,512]{2,1,0:T(8,128)S(1)}, f32[10,16,512]{2,1,0:T(8,128)}, u32[]{:S(2)}) copy-start(f32[10,16,512]{2,1,0:T(8,128)} %head_ref.5) | copy-start | bytes 983044
  3.5 16.9 %copy-start.3 = (s32[10,16,512]{2,1,0:T(8,128)S(1)}, s32[10,16,512]{2,1,0:T(8,128)}, u32[]{:S(2)}) copy-start(s32[10,16,512]{2,1,0:T(8,128)} %soil_ref.5) | copy-start | bytes 983044
  4.7 15.7 %copy-start.5 = (f32[4,16,512]{2,1,0:T(8,128)S(1)}, f32[4,16,512]{2,1,0:T(8,128)}, u32[]{:S(2)}) copy-start(f32[4,16,512]{2,1,0:T(8,128)} %forcing_ref.1) | copy-start | bytes 393220
  4.7 15.7 %copy-start.6 = (s32[16,512]{1,0:T(8,128)S(1)}, s32[16,512]{1,0:T(8,128)}, u32[]{:S(2)}) copy-start(s32[16,512]{1,0:T(8,128)} %slot_ref.1) | copy-start | bytes 98308
  4.7 15.6 %all-to-all-start = ((f32[32,8,128]{2,1,0:T(8,128)}), f32[32,8,128]{2,1,0:T(8,128)S(1)}, u32[]{:S(2)}, u32[]{:S(2)}) async-start(f32[32,8,128]{2,1,0:T(8,128)} %get-tuple-element.36), calls=%async_computation | async-start | bytes 262144 | tf_op jit(solution)/shard_map/all_to_all | solution.py:508
  12.0 8.4 %copy-start.7 = (f32[3,12]{1,0:T(4,128)S(1)}, f32[3,12]{1,0:T(4,128)}, u32[]{:S(2)}) copy-start(f32[3,12]{1,0:T(4,128)} %table_ref.3) | copy-start | bytes 436
  12.0 19.1 %collective-permute-start.4 = (f32[20,8,512]{2,1,0:T(8,128)S(1)}, f32[20,8,512]{2,1,0:T(8,128)S(1)}, u32[]{:S(2)}, u32[]{:S(2)}) collective-permute-start(f32[20,8,512]{2,1,0:T(8,128)S(1)} %get-tuple-element.42), channel_id=1, source_target_pairs={{0,4},{4,8},{8,12},{12,16},{16,20},{20,24},{24,28},{1,5},{5,9},{9,... | collective-permute-start | bytes 983048 | tf_op jit(solution)/shard_map/ppermute | solution.py:505
  15.7 15.4 %collective-permute-start.5 = (f32[20,8,512]{2,1,0:T(8,128)S(1)}, f32[20,8,512]{2,1,0:T(8,128)S(1)}, u32[]{:S(2)}, u32[]{:S(2)}) collective-permute-start(f32[20,8,512]{2,1,0:T(8,128)S(1)} %get-tuple-element.43), channel_id=1, source_target_pairs={{4,0},{8,4},{12,8},{16,12},{20,16},{24,20},{28,24},{5,1},{9,5},{13... | collective-permute-start | bytes 983048 | tf_op jit(solution)/shard_map/ppermute | solution.py:505
  25.8 10.4 %collective-permute-start = (f32[64,512]{1,0:T(8,128)S(1)}, f32[64,512]{1,0:T(8,128)S(1)}, u32[]{:S(2)}, u32[]{:S(2)}) collective-permute-start(f32[64,512]{1,0:T(8,128)S(1)} %get-tuple-element.38), channel_id=1, source_target_pairs={{0,4},{4,8},{8,12},{12,16},{16,20},{20,24},{24,28},{1,5},{5,9},{9,... | collective-permute-start | bytes 393224 | tf_op jit(solution)/shard_map/ppermute | solution.py:505
  28.3 7.8 %collective-permute-start.1 = (f32[64,512]{1,0:T(8,128)S(1)}, f32[64,512]{1,0:T(8,128)S(1)}, u32[]{:S(2)}, u32[]{:S(2)}) collective-permute-start(f32[64,512]{1,0:T(8,128)S(1)} %get-tuple-element.39), channel_id=1, source_target_pairs={{4,0},{8,4},{12,8},{16,12},{20,16},{24,20},{28,24},{5,1},{9,5},{13... | collective-permute-start | bytes 393224 | tf_op jit(solution)/shard_map/ppermute | solution.py:505
  31.3 8.7 %collective-permute-start.6 = (f32[2,32,128]{2,1,0:T(8,128)S(1)}, f32[2,32,128]{2,1,0:T(8,128)S(1)}, u32[]{:S(2)}, u32[]{:S(2)}) collective-permute-start(f32[2,32,128]{2,1,0:T(8,128)S(1)} %get-tuple-element.44), channel_id=1, source_target_pairs={{0,1},{1,2},{2,3},{4,5},{5,6},{6,7},{8,9},{9,10},{10,11},{12,13},{... | collective-permute-start | bytes 98312 | tf_op jit(solution)/shard_map/ppermute | solution.py:505
  32.6 7.4 %collective-permute-start.7 = (f32[2,32,128]{2,1,0:T(8,128)S(1)}, f32[2,32,128]{2,1,0:T(8,128)S(1)}, u32[]{:S(2)}, u32[]{:S(2)}) collective-permute-start(f32[2,32,128]{2,1,0:T(8,128)S(1)} %get-tuple-element.45), channel_id=1, source_target_pairs={{1,0},{2,1},{3,2},{5,4},{6,5},{7,6},{9,8},{10,9},{11,10},{13,12},{... | collective-permute-start | bytes 98312 | tf_op jit(solution)/shard_map/ppermute | solution.py:505
  36.3 8.5 %collective-permute-start.2 = (f32[1,32,128]{2,1,0:T(8,128)S(1)}, f32[1,32,128]{2,1,0:T(8,128)S(1)}, u32[]{:S(2)}, u32[]{:S(2)}) collective-permute-start(f32[1,32,128]{2,1,0:T(8,128)S(1)} %get-tuple-element.40), channel_id=1, source_target_pairs={{0,1},{1,2},{2,3},{4,5},{5,6},{6,7},{8,9},{9,10},{10,11},{12,13},{... | collective-permute-start | bytes 49160 | tf_op jit(solution)/shard_map/ppermute | solution.py:505
  38.7 6.1 %collective-permute-start.3 = (f32[1,32,128]{2,1,0:T(8,128)S(1)}, f32[1,32,128]{2,1,0:T(8,128)S(1)}, u32[]{:S(2)}, u32[]{:S(2)}) collective-permute-start(f32[1,32,128]{2,1,0:T(8,128)S(1)} %get-tuple-element.41), channel_id=1, source_target_pairs={{1,0},{2,1},{3,2},{5,4},{6,5},{7,6},{9,8},{10,9},{11,10},{13,12},{... | collective-permute-start | bytes 49160 | tf_op jit(solution)/shard_map/ppermute | solution.py:505

commit v4 on v3

--- a/solution.py
+++ b/solution.py
@@ -41,24 +41,15 @@
     return lax.broadcasted_iota(jnp.int32, shape, len(shape) - 1)
 
 
-def pack_kernel(
-    canopy_hbm, head_hbm, soil_hbm, send_ref, down_ref, up_ref, canopy_ref, head_ref, soil_ref, sems
-):
-    copies = [
-        pltpu.make_async_copy(head_hbm, head_ref, sems.at[0]),
-        pltpu.make_async_copy(soil_hbm, soil_ref, sems.at[1]),
-        pltpu.make_async_copy(canopy_hbm, canopy_ref, sems.at[2]),
-    ]
-    for copy in copies:
-        copy.start()
-    layers, width, _ = head_ref.shape
-    copies[0].wait()
-    copies[1].wait()
-    for out_ref, at in ((down_ref, 0), (up_ref, width - HALO)):
+def edge_kernel(head_ref, soil_ref, down_ref, up_ref):
+    layers, rows, _ = head_ref.shape
+    for out_ref, at in ((down_ref, 0), (up_ref, rows - HALO)):
         for k in range(layers):
             out_ref[k] = head_ref[k, at : at + HALO, :]
             out_ref[layers + k] = (soil_ref[k, at : at + HALO, :] + 1).astype(f32)
-    copies[2].wait()
+
+
+def pack_kernel(canopy_ref, _, send_ref):
     rows = canopy_ref.shape[0]
     low = lane_iota((8, LANES)) < SLOT
     for t in range(canopy_ref.shape[1] // LANES):
@@ -203,9 +194,16 @@
     return ((slice(0, LANES), 0), (slice(cols - LANES, cols), LANES - HALO))
 
 
-def state_strip_kernel(head_ref, soil_ref, lo_ref, hi_ref, down_ref, up_ref):
+def send_strips(low, high, field, out_ref):
+    me = lax.axis_index("gy")
+    for d in range(out_ref.shape[0]):
+        out_ref[d, field] = jnp.where(d < me, low, high)
+
+
+def state_strip_kernel(head_ref, soil_ref, lo_ref, hi_ref, out_ref):
     layers, _, cols = head_ref.shape
-    for out_ref, (part, shift) in zip((down_ref, up_ref), strip_parts(cols)):
+    parts = []
+    for part, shift in strip_parts(cols):
         heads, soils = [], []
         for k in range(layers):
             heads.append(
@@ -214,8 +212,9 @@
             soil = (soil_ref[k, :, part] + 1).astype(f32)
             ends = [hi_ref[layers + k, :, part], lo_ref[layers + k, :, part]]
             soils.append(jnp.concatenate([soil] + ends, axis=0))
-        out_ref[0] = strips(heads, shift)
-        out_ref[1] = strips(soils, shift)
+        parts.append((strips(heads, shift), strips(soils, shift)))
+    for field in range(2):
+        send_strips(parts[0][field], parts[1][field], field, out_ref)
 
 
 def tall_source(src_ref, slo_ref, shi_ref, k, part):
@@ -225,15 +224,25 @@
     return jnp.concatenate([own, shi_ref[edge, part], gap, slo_ref[edge, part]], axis=0)
 
 
-def source_strip_kernel(src_ref, slo_ref, shi_ref, down_ref, up_ref):
+def source_strip_kernel(src_ref, slo_ref, shi_ref, out_ref):
     layers, _, cols = src_ref.shape
-    for out_ref, (part, shift) in zip((down_ref, up_ref), strip_parts(cols)):
-        out_ref[0] = strips([tall_source(src_ref, slo_ref, shi_ref, k, part) for k in range(layers)], shift)
-
-
-def side(ylo_ref, yhi_ref, field, k):
-    right = yhi_ref[field]
-    left = ylo_ref[field]
+    low, high = (
+        strips([tall_source(src_ref, slo_ref, shi_ref, k, part) for k in range(layers)], shift)
+        for part, shift in strip_parts(cols)
+    )
+    send_strips(low, high, 0, out_ref)
+
+
+def received(strip_ref, field):
+    me = lax.axis_index("gy")
+    count = strip_ref.shape[0]
+    right = strip_ref[jnp.minimum(me + 1, count - 1), field]
+    left = strip_ref[jnp.maximum(me - 1, 0), field]
+    return jnp.where(me + 1 < count, right, 0.0), jnp.where(me > 0, left, 0.0)
+
+
+def side(strip, k):
+    right, left = strip
     lane = lane_iota(right.shape)
     shift = (-HALO * k) % LANES
     right = pltpu.roll(right, shift, 1) if shift else right
@@ -363,8 +372,10 @@
     def dot(a, b):
         return functools.reduce(jnp.add, [x * y for x, y in zip(a, b)])
 
-    beta = jnp.sqrt(gram[0, 0] + norm_epsilon)
-    basis = [[1.0 / beta]]
+    square = gram[0, 0] + norm_epsilon
+    inverse = lax.rsqrt(square)
+    beta = square * inverse
+    basis = [[inverse]]
     images = [times_gram(basis[0])]
     hessen = {}
     for j in range(KRYLOV):
@@ -373,11 +384,10 @@
             product = dot(w, images[i])
             hessen[i, j] = product
             w = [w[m] - product * basis[i][m] if m < len(basis[i]) else w[m] for m in range(len(w))]
-        square = jnp.maximum(dot(w, times_gram(w)), 0.0)
-        length = jnp.sqrt(square + norm_epsilon)
-        hessen[j + 1, j] = length
+        square = jnp.maximum(dot(w, times_gram(w)), 0.0) + norm_epsilon
+        inverse = lax.rsqrt(square)
+        hessen[j + 1, j] = square * inverse
         if j + 1 < KRYLOV:
-            inverse = 1.0 / length
             basis.append([x * inverse for x in w])
             images.append(times_gram(basis[-1]))
     n = KRYLOV
@@ -417,42 +427,41 @@
 
 
 def state_kernel(
-    table_ref, head_ref, soil_ref, lo_ref, hi_ref, ylo_ref, yhi_ref,
-    ext_ref, ks_ref, steep_ref, cap_ref, water_ref, flow_ref, *rest,
+    table_ref, head_ref, soil_ref, lo_ref, hi_ref, strip_ref,
+    ext_ref, ks_ref, steep_ref, cap_ref, cond_ref, deriv_ref, store_ref, water_ref,
 ):
-    coefs, (cond_ref, deriv_ref, store_ref, gain_ref) = rest[:7], rest[7:]
     layers, rows, cols = head_ref.shape
     tables = table_rows(table_ref, rows + 2 * HALO)
-    mask = None
+    heads, soils = received(strip_ref, 0), received(strip_ref, 1)
     for k in range(layers):
         head = jnp.concatenate([head_ref[k], hi_ref[k], lo_ref[k]], axis=0)
-        head = jnp.concatenate([head, side(ylo_ref, yhi_ref, 0, k)], axis=1)
+        head = jnp.concatenate([head, side(heads, k)], axis=1)
         ends = jnp.concatenate([hi_ref[layers + k], lo_ref[layers + k]], axis=0).astype(jnp.int32)
         index = jnp.concatenate([soil_ref[k] + 1, ends], axis=0)
-        index = jnp.concatenate([index, side(ylo_ref, yhi_ref, 1, k).astype(jnp.int32)], axis=1)
+        index = jnp.concatenate([index, side(soils, k).astype(jnp.int32)], axis=1)
         conduct, steep, capacity = (lookup(row, index) for row in tables)
-        if k == 0:
-            mask = (index > 0).astype(f32)
-        cond, deriv, store, water = pointwise(head, conduct, steep, capacity)
-        ext_ref[k] = head
-        ks_ref[k] = conduct
-        steep_ref[k] = steep
-        cap_ref[k] = capacity
-        cond_ref[k] = cond
-        deriv_ref[k] = deriv
-        store_ref[k] = store
-        water_ref[k] = water
-        gain_ref[k] = water - water_ref[k]
-    linearize(ext_ref, cond_ref, deriv_ref, store_ref, gain_ref, mask, coefs, flow_ref, (rows, cols))
-
-
-def first_kernel(src_ref, slo_ref, shi_ref, ylo_ref, yhi_ref, water_ref, flow_ref, *rest):
+        values = (head, conduct, steep, capacity) + pointwise(head, conduct, steep, capacity)
+        outs = (ext_ref, ks_ref, steep_ref, cap_ref, cond_ref, deriv_ref, store_ref, water_ref)
+        for ref, value in zip(outs, values):
+            ref[k] = value
+
+
+def flow_kernel(ext_ref, ks_ref, cond_ref, deriv_ref, store_ref, water_ref, flow_ref, *rest, tile):
+    coefs, gain_ref = rest[:7], rest[7]
+    mask = (ks_ref[0] > 0.0).astype(f32)
+    for k in range(ext_ref.shape[0]):
+        gain_ref[k] = water_ref[k] - water_ref[k]
+    linearize(ext_ref, cond_ref, deriv_ref, store_ref, gain_ref, mask, coefs, flow_ref, tile)
+
+
+def first_kernel(src_ref, slo_ref, shi_ref, strip_ref, water_ref, flow_ref, *rest):
     coefs = rest[:7]
     base_ref, p0_ref, p1_ref, p2_ref, gram_ref = rest[7:]
     layers, rows, cols = src_ref.shape
+    strip = received(strip_ref, 0)
     for k in range(layers):
         source = tall_source(src_ref, slo_ref, shi_ref, k, slice(0, cols))
-        source = jnp.concatenate([source, side(ylo_ref, yhi_ref, 0, k)], axis=1)
+        source = jnp.concatenate([source, side(strip, k)], axis=1)
         p0_ref[k] = flow_ref[k] - source
         base_ref[k] = water_ref[k] + source
     powers((p0_ref, p1_ref, p2_ref), coefs, (rows, cols), gram_ref)
@@ -496,7 +505,6 @@
     tall, wide = rows + 2 * HALO, cols + LANES
     own, ext = ((layers, rows, cols), f32), ((layers, tall, wide), f32)
     gram_block = ((devices, 1, LANES), f32)
-    in_hbm = pl.BlockSpec(memory_space=pltpu.HBM)
 
     def exchange(to_lower, to_upper, axis):
         size = lax.axis_size(axis)
@@ -504,23 +512,19 @@
         down = [(j, i) for i, j in up]
         return lax.ppermute(to_upper, axis, up), lax.ppermute(to_lower, axis, down)
 
-    def spread(x):
-        return lax.all_to_all(x, both, split_axis=0, concat_axis=0, tiled=True)
-
-    send, down, up = call(
+    def spread(x, axes):
+        return lax.all_to_all(x, axes, split_axis=0, concat_axis=0, tiled=True)
+
+    down, up = call(edge_kernel, [((2 * layers, HALO, cols), f32)] * 2, 2)(head_old, soil_type)
+    lo, hi = exchange(down, up, "gx")
+    (send,) = call(
         pack_kernel,
-        [((devices, 8, LANES), f32)] + [((2 * layers, HALO, cols), f32)] * 2,
-        3,
-        scratch=[
-            pltpu.VMEM(canopy.shape, f32),
-            pltpu.VMEM(head_old.shape, f32),
-            pltpu.VMEM(soil_type.shape, jnp.int32),
-            pltpu.SemaphoreType.DMA((3,)),
-        ],
-        in_specs=[in_hbm] * 3,
-    )(canopy, head_old, soil_type)
-    lo, hi = exchange(down, up, "gx")
-    arrived = spread(send)
+        [((devices, 8, LANES), f32)],
+        2,
+        in_specs=[vmem, pl.BlockSpec(memory_space=pl.ANY)],
+        flops=1000000000,
+    )(canopy, down)
+    arrived = spread(send, both)
     edge = ((-(-SOURCE_DEPTH * layers // 8) * 8, cols), f32)
     source, sdown, sup, flux = call(
         source_kernel,
@@ -530,22 +534,26 @@
         in_specs=[smem] + [vmem] * 5,
     )(soil_table, arrived, head_old, soil_type, forcing, column_slot)
     slo, shi = exchange(sdown, sup, "gx")
-    ydown, yup = call(state_strip_kernel, [((2, tall, LANES), f32)] * 2, 4)(head_old, soil_type, lo, hi)
-    ylo, yhi = exchange(ydown, yup, "gy")
-    sydown, syup = call(source_strip_kernel, [((1, tall, LANES), f32)] * 2, 3)(source, slo, shi)
-    sylo, syhi = exchange(sydown, syup, "gy")
+    line = lax.axis_size("gy")
+    (strip,) = call(state_strip_kernel, [((line, 2, tall, LANES), f32)], 4)(head_old, soil_type, lo, hi)
+    strip = spread(strip, "gy")
+    (sstrip,) = call(source_strip_kernel, [((line, 1, tall, LANES), f32)], 3)(source, slo, shi)
+    sstrip = spread(sstrip, "gy")
     held = [pltpu.VMEM(ext[0], f32)]
-    old, ks, steep, cap, water, flow, *coefs = call(
-        state_kernel, [ext] * 13, 7, scratch=held * 4, in_specs=[smem] + [vmem] * 6, flops=20000000
-    )(soil_table, head_old, soil_type, lo, hi, ylo, yhi)
-    base, p0, p1, p2, gram = call(first_kernel, [ext] * 4 + [gram_block], 14)(
-        source, slo, shi, sylo, syhi, water, flow, *coefs
+    old, ks, steep, cap, cond, deriv, store, water = call(
+        state_kernel, [ext] * 8, 6, in_specs=[smem] + [vmem] * 5, flops=20000000
+    )(soil_table, head_old, soil_type, lo, hi, strip)
+    flow, *coefs = call(
+        functools.partial(flow_kernel, tile=(rows, cols)), [ext] * 8, 6, scratch=held, flops=20000000
+    )(old, ks, cond, deriv, store, water)
+    base, p0, p1, p2, gram = call(first_kernel, [ext] * 4 + [gram_block], 13)(
+        source, slo, shi, sstrip, water, flow, *coefs
     )
-    sums = spread(gram)
+    sums = spread(gram, both)
     part, q0, q1, q2, gram = call(
         second_kernel, [own] + [ext] * 3 + [gram_block], 9, scratch=held * 12
     )(sums, old, ks, steep, cap, base, p0, p1, p2)
-    sums = spread(gram)
+    sums = spread(gram, both)
     (head,) = call(last_kernel, [own], 5)(sums, part, q0, q1, q2)
     return head, flux
 

time: 80.6 us -> 106 us (1.32)
  local copies, waits for them, and re-layouts: 2.87 us -> 23.7 us
  blocking collectives: 26.7 us -> 38.6 us
  starting transfers between devices: 22.5 us -> 18 us
  waiting for transfers between devices: 6.99 us -> 3.81 us
    unnamed x16 -> x76, local copies, waits for them, and re-layouts: 2.87 us -> 23.7 us
    all_to_all x2 -> x3, blocking collectives: 26.7 us -> 38.6 us  [spread(): return lax.all_to_all(x, axes, split_axis=0, concat_axis=0, tiled=True)]
    ppermute x4 -> x2, waiting for transfers between devices: 3.66 us -> 0.01 us  [exchange(): lax.ppermute(to_upper, axis, up)]
    ppermute x4 -> x2, starting transfers between devices: 5.17 us -> 2.58 us  [exchange(): lax.ppermute(to_lower, axis, down)]
    ppermute x4 -> x2, waiting for transfers between devices: 0.01 us -> 1.6 us  [exchange(): lax.ppermute(to_lower, axis, down)]
    ppermute x4 -> x2, starting transfers between devices: 10 us -> 8.82 us  [exchange(): lax.ppermute(to_upper, axis, up)]
    all_to_all x1 -> x2, waiting for transfers between devices: 3.32 us -> 2.2 us  [spread(): return lax.all_to_all(x, axes, split_axis=0, concat_axis=0, tiled=True)]
    all_to_all x1 -> x2, starting transfers between devices: 7.3 us -> 6.61 us  [spread(): return lax.all_to_all(x, axes, split_axis=0, concat_axis=0, tiled=True)]
  transfers between devices with their start and end apart: 9 -> 6, of which waited for: 3 -> 2; matrix products, arithmetic and copies ran while one was open for 0% -> 0% of each run, Pallas kernels for 13% -> 11%
where the time goes in v4:
time: 106 us; the launch traced here: 105 us
  blocking collectives  38.6 us (36%)
  local copies, waits for them, and re-layouts  23.7 us (22%)
  Pallas kernels  19.9 us (19%)
  starting transfers between devices  18 us (17%)
  waiting for transfers between devices  3.81 us (4%)
    all_to_all x3, blocking collectives, spread(): return lax.all_to_all(x, axes, split_axis=0, concat_axis=0, tiled=True)  38.6 us
    unnamed x76, local copies, waits for them, and re-layouts  23.7 us
    ppermute x2, starting transfers between devices, exchange(): lax.ppermute(to_upper, axis, up)  8.82 us
    all_to_all x2, starting transfers between devices, spread(): return lax.all_to_all(x, axes, split_axis=0, concat_axis=0, tiled=True)  6.61 us
    pallas_call x1, Pallas kernels, shards(): call(source_kernel, [own, edge, edge, ((2, rows, cols), f32)], 6, scratch...  5.39 us
    pallas_call x1, Pallas kernels, shards(): call(second_kernel, [own] + [ext] * 3 + [gram_block], 9, scratch=held * 12)  4.77 us
    pallas_call x1, Pallas kernels, shards(): call(state_kernel, [ext] * 8, 6, in_specs=[smem] + [vmem] * 5, flops=2000...  2.72 us
    ppermute x2, starting transfers between devices, exchange(): lax.ppermute(to_lower, axis, down)  2.58 us
  transfers between devices with their start and end apart: 6, of which 2 were waited for; matrix products, arithmetic and copies ran while one was open for 0% of the time, Pallas kernels for 11%

profile of v4, /device:TPU:0, one launch (start us, length us, event | category | flops | bytes accessed | tf_op | source)
XLA Modules:
  0.0 105.0 jit_solution(12303804751343289118)
XLA Ops:
  0.6 1.0 copy-done
  1.6 1.0 copy-done.2
  2.6 5.0 %collective-permute-start.2 = (f32[20,8,512]{2,1,0:T(8,128)S(1)}, f32[20,8,512]{2,1,0:T(8,128)S(1)}, u32[]{:S(2)}, u32[]{:S(2)}) collective-permute-start(f32[20,8,512]{2,1,0:T(8,128)S(1)} %get-tuple-element.38), channel_id=1, source_target_pairs={{0,4},{4,8},{8,12},{12,16},{16,20},{20,24},{24,28},{1,5},{5,9},{9,... | collective-permute-start | bytes 983048 | tf_op jit(solution)/shard_map/ppermute | solution.py:513
  7.7 1.3 %collective-permute-start.3 = (f32[20,8,512]{2,1,0:T(8,128)S(1)}, f32[20,8,512]{2,1,0:T(8,128)S(1)}, u32[]{:S(2)}, u32[]{:S(2)}) collective-permute-start(f32[20,8,512]{2,1,0:T(8,128)S(1)} %get-tuple-element.34._), channel_id=1, source_target_pairs={{4,0},{8,4},{12,8},{16,12},{20,16},{24,20},{28,24},{5,1},{9,5},{13... | collective-permute-start | bytes 983048 | tf_op jit(solution)/shard_map/ppermute | solution.py:513
  9.1 15.0 %all_to_all.25.arrived_ref = f32[32,8,128]{2,1,0:T(8,128)S(1)} all-to-all(f32[32,8,128]{2,1,0:T(8,128)S(1)} %shard_map.78), channel_id=1, replica_groups=mesh['gx'=8,'gy'=4] {'gx','gy'}, dimensions={0} | all-to-all | bytes 262144 | tf_op jit(solution)/shard_map/all_to_all | solution.py:516
  24.2 5.4 %shard_map.79 = (f32[10,16,512]{2,1,0:T(8,128)S(1)}, f32[64,512]{1,0:T(8,128)S(1)}, f32[64,512]{1,0:T(8,128)S(1)}, f32[2,16,512]{2,1,0:T(8,128)}) custom-call(f32[3,12]{1,0:T(4,128)S(1)} %copy-done.36, f32[32,8,128]{2,1,0:T(8,128)S(1)} %all_to_all.25.arrived_ref, f32[10,16,512]{2,1,0:T(8,128)S(1)} %copy-done.1, s32[10,16,512]{2,1,0:T(8,128)S(1)} %copy-done.3, ...), custom_call_target="tpu_custom_call" | custom-call | flops 1000000 | bytes 1000000 | tf_op jit(solution)/shard_map/pallas_call | solution.py:529
  29.6 3.8 %collective-permute-start = (f32[64,512]{1,0:T(8,128)S(1)}, f32[64,512]{1,0:T(8,128)S(1)}, u32[]{:S(2)}, u32[]{:S(2)}) collective-permute-start(f32[64,512]{1,0:T(8,128)S(1)} %get-tuple-element.36), channel_id=1, source_target_pairs={{0,4},{4,8},{8,12},{12,16},{16,20},{20,24},{24,28},{1,5},{5,9},{9,... | collective-permute-start | bytes 393224 | tf_op jit(solution)/shard_map/ppermute | solution.py:513
  33.4 1.3 %collective-permute-start.1 = (f32[64,512]{1,0:T(8,128)S(1)}, f32[64,512]{1,0:T(8,128)S(1)}, u32[]{:S(2)}, u32[]{:S(2)}) collective-permute-start(f32[64,512]{1,0:T(8,128)S(1)} %get-tuple-element.37), channel_id=1, source_target_pairs={{4,0},{8,4},{12,8},{16,12},{20,16},{24,20},{28,24},{5,1},{9,5},{13... | collective-permute-start | bytes 393224 | tf_op jit(solution)/shard_map/ppermute | solution.py:513
  35.6 3.3 %all-to-all-start.2 = ((f32[4,2,32,128]{3,2,1,0:T(8,128)}), f32[4,2,32,128]{3,2,1,0:T(8,128)S(1)}, u32[]{:S(2)}, u32[]{:S(2)}) async-start(f32[4,2,32,128]{3,2,1,0:T(8,128)} %shard_map.81), calls=%async_computation.2 | async-start | bytes 262144 | tf_op jit(solution)/shard_map/all_to_all | solution.py:516
  39.0 1.6 %collective-permute-done.1.shi_ref = f32[64,512]{1,0:T(8,128)S(1)} collective-permute-done((f32[64,512]{1,0:T(8,128)S(1)}, f32[64,512]{1,0:T(8,128)S(1)}, u32[]{:S(2)}, u32[]{:S(2)}) %collective-permute-start.1) | collective-permute-done | bytes 131104 | tf_op jit(solution)/shard_map/ppermute | solution.py:513
  41.3 2.2 %all-to-all-done.2.strip_ref = f32[4,2,32,128]{3,2,1,0:T(8,128)S(1)} async-done(((f32[4,2,32,128]{3,2,1,0:T(8,128)}), f32[4,2,32,128]{3,2,1,0:T(8,128)S(1)}, u32[]{:S(2)}, u32[]{:S(2)}) %all-to-all-start.2) | async-done | bytes 131104 | tf_op jit(solution)/shard_map/all_to_all | solution.py:516
  44.2 3.3 %all-to-all-start.1 = ((f32[4,1,32,128]{3,2,1,0:T(8,128)}), f32[4,1,32,128]{3,2,1,0:T(8,128)S(1)}, u32[]{:S(2)}, u32[]{:S(2)}) async-start(f32[4,1,32,128]{3,2,1,0:T(8,128)} %shard_map.80), calls=%async_computation.1 | async-start | bytes 131072 | tf_op jit(solution)/shard_map/all_to_all | solution.py:516
  47.5 1.0 copy-done.5
  48.5 1.0 copy-done.7
  50.3 2.7 %shard_map.82 = (f32[10,32,640]{2,1,0:T(8,128)S(1)}, f32[10,32,640]{2,1,0:T(8,128)S(1)}, f32[10,32,640]{2,1,0:T(8,128)S(1)}, f32[10,32,640]{2,1,0:T(8,128)S(1)},...) custom-call(f32[3,12]{1,0:T(4,128)S(1)} %copy-done.36, ...), custom_call_target="tpu_custom_call" | custom-call | flops 20000000 | bytes 1000000 | tf_op jit(solution)/shard_map/pallas_call | solution.py:543
  54.9 2.1 %shard_map.83 = (f32[10,32,640]{2,1,0:T(8,128)S(1)}, f32[10,32,640]{2,1,0:T(8,128)S(1)}, f32[10,32,640]{2,1,0:T(8,128)S(1)}, f32[10,32,640]{2,1,0:T(8,128)S(1)},...) custom-call(f32[10,32,640]{2,1,0:T(8,128)S(1)} %get-tuple-element.40, ...), custom_call_target="tpu_custom_call" | custom-call | flops 20000000 | bytes 1000000 | tf_op jit(solution)/shard_map/pallas_call | solution.py:546
  59.6 0.9 copy-done.18
  61.5 0.9 copy-done.22
  63.3 1.0 copy-done.26
  64.3 1.1 %copy-done.13 = f32[10,32,640]{2,1,0:T(8,128)S(1)} copy-done((f32[10,32,640]{2,1,0:T(8,128)S(1)}, f32[10,32,640]{2,1,0:T(8,128)}, u32[]{:S(2)}) %copy-start.13) | copy-done | bytes 819224
  65.4 1.1 %copy-done.15 = f32[10,32,640]{2,1,0:T(8,128)S(1)} copy-done((f32[10,32,640]{2,1,0:T(8,128)S(1)}, f32[10,32,640]{2,1,0:T(8,128)}, u32[]{:S(2)}) %copy-start.15) | copy-done | bytes 819224
  66.6 1.1 %copy-done.17 = f32[10,32,640]{2,1,0:T(8,128)S(1)} copy-done((f32[10,32,640]{2,1,0:T(8,128)S(1)}, f32[10,32,640]{2,1,0:T(8,128)}, u32[]{:S(2)}) %copy-start.17) | copy-done | bytes 819224
  67.7 1.1 %copy-done.19 = f32[10,32,640]{2,1,0:T(8,128)S(1)} copy-done((f32[10,32,640]{2,1,0:T(8,128)S(1)}, f32[10,32,640]{2,1,0:T(8,128)}, u32[]{:S(2)}) %copy-start.19) | copy-done | bytes 819224
  68.9 1.1 %copy-done.21 = f32[10,32,640]{2,1,0:T(8,128)S(1)} copy-done((f32[10,32,640]{2,1,0:T(8,128)S(1)}, f32[10,32,640]{2,1,0:T(8,128)}, u32[]{:S(2)}) %copy-start.21) | copy-done | bytes 819224
  70.0 1.1 %copy-done.23 = f32[10,32,640]{2,1,0:T(8,128)S(1)} copy-done((f32[10,32,640]{2,1,0:T(8,128)S(1)}, f32[10,32,640]{2,1,0:T(8,128)}, u32[]{:S(2)}) %copy-start.23) | copy-done | bytes 819224
  71.1 1.1 %copy-done.25 = f32[10,32,640]{2,1,0:T(8,128)S(1)} copy-done((f32[10,32,640]{2,1,0:T(8,128)S(1)}, f32[10,32,640]{2,1,0:T(8,128)}, u32[]{:S(2)}) %copy-start.25) | copy-done | bytes 819224
  72.3 1.1 %copy-done.27 = f32[10,32,640]{2,1,0:T(8,128)S(1)} copy-done((f32[10,32,640]{2,1,0:T(8,128)S(1)}, f32[10,32,640]{2,1,0:T(8,128)}, u32[]{:S(2)}) %copy-start.27) | copy-done | bytes 819224
  73.4 2.1 %shard_map.84 = (f32[10,32,640]{2,1,0:T(8,128)S(1)}, f32[10,32,640]{2,1,0:T(8,128)S(1)}, f32[10,32,640]{2,1,0:T(8,128)S(1)}, f32[10,32,640]{2,1,0:T(8,128)S(1)}, f32[32,1,128]{2,1,0:T(1,128)S(1)}) custom-call(f32[10,16,512]{2,1,0:T(8,128)S(1)} %get-tuple-element.35.src_ref, f32[64,512]{1,0:T(8,128)S(1)} %copy-done.29, f32[64,512]{1,0:T(8,128)S(1)} %copy-done.31, ...), custom_call_target="tpu_custom_call" | custom-call | flops 1000000 | bytes 1000000 | tf_op jit(solution)/shard_map/pallas_call | solution.py:549
  75.6 14.7 %all_to_all.26.arrived_ref = f32[32,1,128]{2,1,0:T(1,128)S(1)} all-to-all(f32[32,1,128]{2,1,0:T(1,128)S(1)} %get-tuple-element.53), channel_id=1, replica_groups=mesh['gx'=8,'gy'=4] {'gx','gy'}, dimensions={0} | all-to-all | bytes 32768 | tf_op jit(solution)/shard_map/all_to_all | solution.py:516
  90.3 4.8 %shard_map.85 = (f32[10,16,512]{2,1,0:T(8,128)S(1)}, f32[10,32,640]{2,1,0:T(8,128)S(1)}, f32[10,32,640]{2,1,0:T(8,128)S(1)}, f32[10,32,640]{2,1,0:T(8,128)S(1)}, f32[32,1,128]{2,1,0:T(1,128)S(1)}) custom-call(f32[32,1,128]{2,1,0:T(1,128)S(1)} %all_to_all.26.arrived_ref, f32[10,32,640]{2,1,0:T(8,128)S(1)} %get-tuple-element.40.ext_ref.old_ref, ...), custom_call_target="tpu_custom_call" | custom-call | flops 1000000 | bytes 1000000 | tf_op jit(solution)/shard_map/pallas_call | solution.py:553
  95.1 8.8 %all_to_all.27.arrived_ref = f32[32,1,128]{2,1,0:T(1,128)S(1)} all-to-all(f32[32,1,128]{2,1,0:T(1,128)S(1)} %get-tuple-element.60), channel_id=1, replica_groups=mesh['gx'=8,'gy'=4] {'gx','gy'}, dimensions={0} | all-to-all | bytes 32768 | tf_op jit(solution)/shard_map/all_to_all | solution.py:516
  103.9 1.1 %shard_map.86 = f32[10,16,512]{2,1,0:T(8,128)} custom-call(f32[32,1,128]{2,1,0:T(1,128)S(1)} %all_to_all.27.arrived_ref, f32[10,16,512]{2,1,0:T(8,128)S(1)} %get-tuple-element.61.part_ref, f32[10,32,640]{2,1,0:T(8,128)S(1)} %get-tuple-element.62.q0_ref, f32[10,32,640]{2,1,0:T(8,128)S(1)} %get-tuple-element.63.q1_ref, f32[10,32,640]{2,1,0:T(8,128)S(1)} %get-tuple-element.64.q2_ref), custom_call_target="tpu_custom_call" | custom-call | flops 1000000 | bytes 1000000 | tf_op jit(solution)/shard_map/pallas_call | solution.py:557
  (69 shorter events, 9.7 us)
Async XLA Ops:
  0.6 1.0 copy-start
  1.6 1.0 copy-start.2
  2.6 6.4 %copy-start.37 = (f32[13,2048]{1,0:T(8,128)S(1)}, f32[13,2048]{1,0:T(8,128)}, u32[]{:S(2)}) copy-start(f32[13,2048]{1,0:T(8,128)} %canopy_ref.1) | copy-start | bytes 319492
  2.6 32.0 %collective-permute-start.2 = (f32[20,8,512]{2,1,0:T(8,128)S(1)}, f32[20,8,512]{2,1,0:T(8,128)S(1)}, u32[]{:S(2)}, u32[]{:S(2)}) collective-permute-start(f32[20,8,512]{2,1,0:T(8,128)S(1)} %get-tuple-element.38), channel_id=1, source_target_pairs={{0,4},{4,8},{8,12},{12,16},{16,20},{20,24},{24,28},{1,5},{5,9},{9,... | collective-permute-start | bytes 983048 | tf_op jit(solution)/shard_map/ppermute | solution.py:513
  7.7 27.0 %collective-permute-start.3 = (f32[20,8,512]{2,1,0:T(8,128)S(1)}, f32[20,8,512]{2,1,0:T(8,128)S(1)}, u32[]{:S(2)}, u32[]{:S(2)}) collective-permute-start(f32[20,8,512]{2,1,0:T(8,128)S(1)} %get-tuple-element.34._), channel_id=1, source_target_pairs={{4,0},{8,4},{12,8},{16,12},{20,16},{24,20},{28,24},{5,1},{9,5},{13... | collective-permute-start | bytes 983048 | tf_op jit(solution)/shard_map/ppermute | solution.py:513
  9.0 15.2 %copy-start.1 = (f32[10,16,512]{2,1,0:T(8,128)S(1)}, f32[10,16,512]{2,1,0:T(8,128)}, u32[]{:S(2)}) copy-start(f32[10,16,512]{2,1,0:T(8,128)} %head_ref.7) | copy-start | bytes 983044
  9.0 15.2 %copy-start.3 = (s32[10,16,512]{2,1,0:T(8,128)S(1)}, s32[10,16,512]{2,1,0:T(8,128)}, u32[]{:S(2)}) copy-start(s32[10,16,512]{2,1,0:T(8,128)} %soil_ref.7) | copy-start | bytes 983044
  9.1 15.1 %copy-start.34 = (f32[4,16,512]{2,1,0:T(8,128)S(1)}, f32[4,16,512]{2,1,0:T(8,128)}, u32[]{:S(2)}) copy-start(f32[4,16,512]{2,1,0:T(8,128)} %forcing_ref.1) | copy-start | bytes 393220
  9.1 15.0 %copy-start.35 = (s32[16,512]{1,0:T(8,128)S(1)}, s32[16,512]{1,0:T(8,128)}, u32[]{:S(2)}) copy-start(s32[16,512]{1,0:T(8,128)} %slot_ref.1) | copy-start | bytes 98308
  9.1 15.0 %copy-start.36 = (f32[3,12]{1,0:T(4,128)S(1)}, f32[3,12]{1,0:T(4,128)}, u32[]{:S(2)}) copy-start(f32[3,12]{1,0:T(4,128)} %table_ref.3) | copy-start | bytes 436
  29.6 9.4 %collective-permute-start = (f32[64,512]{1,0:T(8,128)S(1)}, f32[64,512]{1,0:T(8,128)S(1)}, u32[]{:S(2)}, u32[]{:S(2)}) collective-permute-start(f32[64,512]{1,0:T(8,128)S(1)} %get-tuple-element.36), channel_id=1, source_target_pairs={{0,4},{4,8},{8,12},{12,16},{16,20},{20,24},{24,28},{1,5},{5,9},{9,... | collective-permute-start | bytes 393224 | tf_op jit(solution)/shard_map/ppermute | solution.py:513
  33.4 7.2 %collective-permute-start.1 = (f32[64,512]{1,0:T(8,128)S(1)}, f32[64,512]{1,0:T(8,128)S(1)}, u32[]{:S(2)}, u32[]{:S(2)}) collective-permute-start(f32[64,512]{1,0:T(8,128)S(1)} %get-tuple-element.37), channel_id=1, source_target_pairs={{4,0},{8,4},{12,8},{16,12},{20,16},{24,20},{28,24},{5,1},{9,5},{13... | collective-permute-start | bytes 393224 | tf_op jit(solution)/shard_map/ppermute | solution.py:513
  35.6 7.9 %all-to-all-start.2 = ((f32[4,2,32,128]{3,2,1,0:T(8,128)}), f32[4,2,32,128]{3,2,1,0:T(8,128)S(1)}, u32[]{:S(2)}, u32[]{:S(2)}) async-start(f32[4,2,32,128]{3,2,1,0:T(8,128)} %shard_map.81), calls=%async_computation.2 | async-start | bytes 262144 | tf_op jit(solution)/shard_map/all_to_all | solution.py:516
  38.9 2.4 %copy-start.28 = (f32[64,512]{1,0:T(8,128)}, f32[64,512]{1,0:T(8,128)S(1)}, u32[]{:S(2)}) copy-start(f32[64,512]{1,0:T(8,128)S(1)} %collective-permute-done.slo_ref) | copy-start | bytes 393220
  44.2 20.1 %all-to-all-start.1 = ((f32[4,1,32,128]{3,2,1,0:T(8,128)}), f32[4,1,32,128]{3,2,1,0:T(8,128)S(1)}, u32[]{:S(2)}, u32[]{:S(2)}) async-start(f32[4,1,32,128]{3,2,1,0:T(8,128)} %shard_map.80), calls=%async_computation.1 | async-start | bytes 131072 | tf_op jit(solution)/shard_map/all_to_all | solution.py:516
  47.5 1.0 copy-start.5
  48.4 1.0 copy-start.7
  54.9 9.4 %copy-start.29 = (f32[64,512]{1,0:T(8,128)S(1)}, f32[64,512]{1,0:T(8,128)}, u32[]{:S(2)}) copy-start(f32[64,512]{1,0:T(8,128)} %copy-done.28) | copy-start | bytes 393220
  54.9 9.4 %copy-start.31 = (f32[64,512]{1,0:T(8,128)S(1)}, f32[64,512]{1,0:T(8,128)}, u32[]{:S(2)}) copy-start(f32[64,512]{1,0:T(8,128)} %copy-done.30) | copy-start | bytes 393220
  59.6 0.9 copy-start.18
  61.5 0.9 copy-start.22
  63.3 1.0 copy-start.26
  64.3 1.1 %copy-start.13 = (f32[10,32,640]{2,1,0:T(8,128)S(1)}, f32[10,32,640]{2,1,0:T(8,128)}, u32[]{:S(2)}) copy-start(f32[10,32,640]{2,1,0:T(8,128)} %copy-done.12) | copy-start | bytes 2457604
  65.4 1.1 %copy-start.15 = (f32[10,32,640]{2,1,0:T(8,128)S(1)}, f32[10,32,640]{2,1,0:T(8,128)}, u32[]{:S(2)}) copy-start(f32[10,32,640]{2,1,0:T(8,128)} %copy-done.14) | copy-start | bytes 2457604
  66.6 1.1 %copy-start.17 = (f32[10,32,640]{2,1,0:T(8,128)S(1)}, f32[10,32,640]{2,1,0:T(8,128)}, u32[]{:S(2)}) copy-start(f32[10,32,640]{2,1,0:T(8,128)} %copy-done.16) | copy-start | bytes 2457604
  67.7 1.1 %copy-start.19 = (f32[10,32,640]{2,1,0:T(8,128)S(1)}, f32[10,32,640]{2,1,0:T(8,128)}, u32[]{:S(2)}) copy-start(f32[10,32,640]{2,1,0:T(8,128)} %copy-done.18) | copy-start | bytes 2457604
  68.9 1.1 %copy-start.21 = (f32[10,32,640]{2,1,0:T(8,128)S(1)}, f32[10,32,640]{2,1,0:T(8,128)}, u32[]{:S(2)}) copy-start(f32[10,32,640]{2,1,0:T(8,128)} %copy-done.20) | copy-start | bytes 2457604
  70.0 1.1 %copy-start.23 = (f32[10,32,640]{2,1,0:T(8,128)S(1)}, f32[10,32,640]{2,1,0:T(8,128)}, u32[]{:S(2)}) copy-start(f32[10,32,640]{2,1,0:T(8,128)} %copy-done.22) | copy-start | bytes 2457604
  71.1 1.1 %copy-start.25 = (f32[10,32,640]{2,1,0:T(8,128)S(1)}, f32[10,32,640]{2,1,0:T(8,128)}, u32[]{:S(2)}) copy-start(f32[10,32,640]{2,1,0:T(8,128)} %copy-done.24) | copy-start | bytes 2457604
  72.3 1.1 %copy-start.27 = (f32[10,32,640]{2,1,0:T(8,128)S(1)}, f32[10,32,640]{2,1,0:T(8,128)}, u32[]{:S(2)}) copy-start(f32[10,32,640]{2,1,0:T(8,128)} %copy-done.26) | copy-start | bytes 2457604
  73.4 16.9 %copy-start.9 = (f32[10,32,640]{2,1,0:T(8,128)S(1)}, f32[10,32,640]{2,1,0:T(8,128)}, u32[]{:S(2)}) copy-start(f32[10,32,640]{2,1,0:T(8,128)} %copy-done.8) | copy-start | bytes 2457604
  73.4 16.9 %copy-start.11 = (f32[10,32,640]{2,1,0:T(8,128)S(1)}, f32[10,32,640]{2,1,0:T(8,128)}, u32[]{:S(2)}) copy-start(f32[10,32,640]{2,1,0:T(8,128)} %copy-done.10) | copy-start | bytes 2457604
  (12 other events, 10.4 us)

commit v5 on v4

--- a/solution.py
+++ b/solution.py
@@ -10,6 +10,7 @@
 NEWTON = 2
 KRYLOV = 3
 HALO = 8
+STATE_DEPTH = 7
 SOURCE_DEPTH = 6
 LANES = 128
 SLOT = 64
@@ -17,7 +18,7 @@
 storage_weight = 4.0
 norm_epsilon = 1e-06
 
-VMEM_LIMIT = 40 * 1024 * 1024
+VMEM_LIMIT = 20 * 1024 * 1024
 PAIRS = [(i, j) for i in range(KRYLOV + 1) for j in range(i, KRYLOV + 1)]
 
 f32 = jnp.float32
@@ -43,13 +44,15 @@
 
 def edge_kernel(head_ref, soil_ref, down_ref, up_ref):
     layers, rows, _ = head_ref.shape
-    for out_ref, at in ((down_ref, 0), (up_ref, rows - HALO)):
+    for out_ref, part in ((down_ref, slice(0, STATE_DEPTH)), (up_ref, slice(rows - STATE_DEPTH, rows))):
         for k in range(layers):
-            out_ref[k] = head_ref[k, at : at + HALO, :]
-            out_ref[layers + k] = (soil_ref[k, at : at + HALO, :] + 1).astype(f32)
-
-
-def pack_kernel(canopy_ref, _, send_ref):
+            out_ref[STATE_DEPTH * k : STATE_DEPTH * (k + 1)] = head_ref[k][part]
+        for k in range(layers):
+            at = STATE_DEPTH * (layers + k)
+            out_ref[at : at + STATE_DEPTH] = (soil_ref[k] + 1).astype(f32)[part]
+
+
+def pack_kernel(canopy_ref, send_ref):
     rows = canopy_ref.shape[0]
     low = lane_iota((8, LANES)) < SLOT
     for t in range(canopy_ref.shape[1] // LANES):
@@ -194,55 +197,33 @@
     return ((slice(0, LANES), 0), (slice(cols - LANES, cols), LANES - HALO))
 
 
-def send_strips(low, high, field, out_ref):
-    me = lax.axis_index("gy")
-    for d in range(out_ref.shape[0]):
-        out_ref[d, field] = jnp.where(d < me, low, high)
-
-
-def state_strip_kernel(head_ref, soil_ref, lo_ref, hi_ref, out_ref):
+def ends_of(lo_ref, hi_ref, at, depth, part):
+    edge = slice(depth * at, depth * (at + 1))
+    above, below = hi_ref[edge, part], lo_ref[edge, part]
+    gap = jnp.zeros((2 * (HALO - depth), above.shape[1]), f32)
+    return jnp.concatenate([above, gap, below], axis=0)
+
+
+def strip_kernel(head_ref, soil_ref, lo_ref, hi_ref, src_ref, slo_ref, shi_ref, down_ref, up_ref):
     layers, _, cols = head_ref.shape
-    parts = []
-    for part, shift in strip_parts(cols):
-        heads, soils = [], []
-        for k in range(layers):
-            heads.append(
-                jnp.concatenate([head_ref[k, :, part], hi_ref[k, :, part], lo_ref[k, :, part]], axis=0)
+    every = range(layers)
+    for out_ref, (part, shift) in zip((down_ref, up_ref), strip_parts(cols)):
+        heads = [(head_ref[k, :, part], ends_of(lo_ref, hi_ref, k, STATE_DEPTH, part)) for k in every]
+        soils = [
+            (
+                (soil_ref[k, :, part] + 1).astype(f32),
+                ends_of(lo_ref, hi_ref, layers + k, STATE_DEPTH, part),
             )
-            soil = (soil_ref[k, :, part] + 1).astype(f32)
-            ends = [hi_ref[layers + k, :, part], lo_ref[layers + k, :, part]]
-            soils.append(jnp.concatenate([soil] + ends, axis=0))
-        parts.append((strips(heads, shift), strips(soils, shift)))
-    for field in range(2):
-        send_strips(parts[0][field], parts[1][field], field, out_ref)
-
-
-def tall_source(src_ref, slo_ref, shi_ref, k, part):
-    edge = slice(SOURCE_DEPTH * k, SOURCE_DEPTH * (k + 1))
-    own = src_ref[k, :, part]
-    gap = jnp.zeros((2 * (HALO - SOURCE_DEPTH), own.shape[1]), f32)
-    return jnp.concatenate([own, shi_ref[edge, part], gap, slo_ref[edge, part]], axis=0)
-
-
-def source_strip_kernel(src_ref, slo_ref, shi_ref, out_ref):
-    layers, _, cols = src_ref.shape
-    low, high = (
-        strips([tall_source(src_ref, slo_ref, shi_ref, k, part) for k in range(layers)], shift)
-        for part, shift in strip_parts(cols)
-    )
-    send_strips(low, high, 0, out_ref)
-
-
-def received(strip_ref, field):
-    me = lax.axis_index("gy")
-    count = strip_ref.shape[0]
-    right = strip_ref[jnp.minimum(me + 1, count - 1), field]
-    left = strip_ref[jnp.maximum(me - 1, 0), field]
-    return jnp.where(me + 1 < count, right, 0.0), jnp.where(me > 0, left, 0.0)
-
-
-def side(strip, k):
-    right, left = strip
+            for k in every
+        ]
+        sources = [(src_ref[k, :, part], ends_of(slo_ref, shi_ref, k, SOURCE_DEPTH, part)) for k in every]
+        for field, pairs in enumerate((heads, soils, sources)):
+            out_ref[field] = strips([jnp.concatenate(pair, axis=0) for pair in pairs], shift)
+
+
+def side(ylo_ref, yhi_ref, field, k):
+    right = yhi_ref[field]
+    left = ylo_ref[field]
     lane = lane_iota(right.shape)
     shift = (-HALO * k) % LANES
     right = pltpu.roll(right, shift, 1) if shift else right
@@ -267,9 +248,12 @@
     return cond, deriv, weighted * slope, weighted * sat
 
 
-def linearize(head_ref, cond_ref, deriv_ref, store_ref, gain_ref, mask, coefs, out_ref, tile):
+def joined(main_ref, side_ref):
+    return lambda k: jnp.concatenate([main_ref[k], side_ref[k]], axis=1)
+
+
+def linearize(layers, head_of, cond_of, deriv_of, store_of, gain_of, mask, coefs, out_ref, tile):
     diag_ref, xp_ref, xm_ref, yp_ref, ym_ref, az_ref, bz_ref = coefs
-    layers = head_ref.shape[0]
     rows, cols = tile
 
     def masked(value):
@@ -279,11 +263,11 @@
 
     above = None
     for k in range(layers):
-        head = head_ref[k]
-        cond = cond_ref[k]
-        deriv = deriv_ref[k]
-        value = gain_ref[k]
-        diag = store_ref[k]
+        head = head_of(k)
+        cond = cond_of(k)
+        deriv = deriv_of(k)
+        value = gain_of(k)
+        diag = store_of(k)
         for plus_ref, minus_ref, axis in ((xp_ref, xm_ref, 0), (yp_ref, ym_ref, 1)):
             mean = 0.5 * (cond + after(cond, axis))
             drop = head - after(head, axis)
@@ -295,10 +279,10 @@
             plus_ref[k] = masked(b)
             minus_ref[k] = masked(before(a, axis))
         if k + 1 < layers:
-            mean = 0.5 * (cond + cond_ref[k + 1])
-            drop = head - head_ref[k + 1] + 1.0
+            mean = 0.5 * (cond + cond_of(k + 1))
+            drop = head - head_of(k + 1) + 1.0
             a = mean + deriv * drop
-            b = mean - deriv_ref[k + 1] * drop
+            b = mean - deriv_of(k + 1) * drop
             az_ref[k] = a
             bz_ref[k] = b
             face = mean * drop
@@ -427,18 +411,17 @@
 
 
 def state_kernel(
-    table_ref, head_ref, soil_ref, lo_ref, hi_ref, strip_ref,
+    table_ref, head_ref, soil_ref, lo_ref, hi_ref,
     ext_ref, ks_ref, steep_ref, cap_ref, cond_ref, deriv_ref, store_ref, water_ref,
 ):
     layers, rows, cols = head_ref.shape
     tables = table_rows(table_ref, rows + 2 * HALO)
-    heads, soils = received(strip_ref, 0), received(strip_ref, 1)
+    every = slice(0, cols)
     for k in range(layers):
-        head = jnp.concatenate([head_ref[k], hi_ref[k], lo_ref[k]], axis=0)
-        head = jnp.concatenate([head, side(heads, k)], axis=1)
-        ends = jnp.concatenate([hi_ref[layers + k], lo_ref[layers + k]], axis=0).astype(jnp.int32)
-        index = jnp.concatenate([soil_ref[k] + 1, ends], axis=0)
-        index = jnp.concatenate([index, side(soils, k).astype(jnp.int32)], axis=1)
+        ends = ends_of(lo_ref, hi_ref, k, STATE_DEPTH, every)
+        head = jnp.concatenate([head_ref[k], ends], axis=0)
+        ends = ends_of(lo_ref, hi_ref, layers + k, STATE_DEPTH, every)
+        index = jnp.concatenate([soil_ref[k] + 1, ends.astype(jnp.int32)], axis=0)
         conduct, steep, capacity = (lookup(row, index) for row in tables)
         values = (head, conduct, steep, capacity) + pointwise(head, conduct, steep, capacity)
         outs = (ext_ref, ks_ref, steep_ref, cap_ref, cond_ref, deriv_ref, store_ref, water_ref)
@@ -446,47 +429,62 @@
             ref[k] = value
 
 
-def flow_kernel(ext_ref, ks_ref, cond_ref, deriv_ref, store_ref, water_ref, flow_ref, *rest, tile):
-    coefs, gain_ref = rest[:7], rest[7]
-    mask = (ks_ref[0] > 0.0).astype(f32)
-    for k in range(ext_ref.shape[0]):
-        gain_ref[k] = water_ref[k] - water_ref[k]
-    linearize(ext_ref, cond_ref, deriv_ref, store_ref, gain_ref, mask, coefs, flow_ref, tile)
-
-
-def first_kernel(src_ref, slo_ref, shi_ref, strip_ref, water_ref, flow_ref, *rest):
-    coefs = rest[:7]
-    base_ref, p0_ref, p1_ref, p2_ref, gram_ref = rest[7:]
+def first_kernel(
+    table_ref, src_ref, slo_ref, shi_ref, ylo_ref, yhi_ref,
+    ext_ref, ks_ref, cond_ref, deriv_ref, store_ref, water_ref,
+    ext_side, ks_side, steep_side, cap_side, base_ref, p0_ref, p1_ref, p2_ref, gram_ref,
+    cond_side, deriv_side, store_side, water_side, *coefs,
+):
     layers, rows, cols = src_ref.shape
-    strip = received(strip_ref, 0)
+    tables = table_rows(table_ref, rows + 2 * HALO)
     for k in range(layers):
-        source = tall_source(src_ref, slo_ref, shi_ref, k, slice(0, cols))
-        source = jnp.concatenate([source, side(strip, k)], axis=1)
-        p0_ref[k] = flow_ref[k] - source
-        base_ref[k] = water_ref[k] + source
+        head = side(ylo_ref, yhi_ref, 0, k)
+        index = side(ylo_ref, yhi_ref, 1, k).astype(jnp.int32)
+        conduct, steep, capacity = (lookup(row, index) for row in tables)
+        values = (head, conduct, steep, capacity) + pointwise(head, conduct, steep, capacity)
+        outs = (ext_side, ks_side, steep_side, cap_side, cond_side, deriv_side, store_side, water_side)
+        for ref, value in zip(outs, values):
+            ref[k] = value
+    water_of = joined(water_ref, water_side)
+
+    def gain_of(k):
+        source = jnp.concatenate([src_ref[k], ends_of(slo_ref, shi_ref, k, SOURCE_DEPTH, slice(0, cols))], axis=0)
+        source = jnp.concatenate([source, side(ylo_ref, yhi_ref, 2, k)], axis=1)
+        water = water_of(k)
+        base_ref[k] = water + source
+        return water - base_ref[k]
+
+    linearize(
+        layers, joined(ext_ref, ext_side), joined(cond_ref, cond_side), joined(deriv_ref, deriv_side),
+        joined(store_ref, store_side), gain_of,
+        (joined(ks_ref, ks_side)(0) > 0.0).astype(f32), coefs, p0_ref, (rows, cols),
+    )
     powers((p0_ref, p1_ref, p2_ref), coefs, (rows, cols), gram_ref)
 
 
 def second_kernel(
-    arrived_ref, old_ref, ks_ref, steep_ref, cap_ref, base_ref, q0_ref, q1_ref, q2_ref,
+    arrived_ref, old_ref, ks_ref, steep_ref, cap_ref, old_side, ks_side, steep_side, cap_side,
+    base_ref, q0_ref, q1_ref, q2_ref,
     part_ref, p0_ref, p1_ref, p2_ref, gram_ref, ext_ref, cond_ref, deriv_ref, store_ref, gain_ref, *coefs,
 ):
     layers = old_ref.shape[0]
     rows, cols = part_ref.shape[1:]
     x = solve(arrived_ref)
+    old_of, ks_of = joined(old_ref, old_side), joined(ks_ref, ks_side)
+    steep_of, cap_of = joined(steep_ref, steep_side), joined(cap_ref, cap_side)
     for k in range(layers):
-        conduct = ks_ref[k]
-        if k == 0:
-            mask = (conduct > 0.0).astype(f32)
-        head = old_ref[k] - x[0] * q0_ref[k] - x[1] * q1_ref[k] - x[2] * q2_ref[k]
-        cond, deriv, store, water = pointwise(head, conduct, steep_ref[k], cap_ref[k])
+        head = old_of(k) - x[0] * q0_ref[k] - x[1] * q1_ref[k] - x[2] * q2_ref[k]
+        cond, deriv, store, water = pointwise(head, ks_of(k), steep_of(k), cap_of(k))
         ext_ref[k] = head
         part_ref[k] = head[:rows, :cols]
         cond_ref[k] = cond
         deriv_ref[k] = deriv
         store_ref[k] = store
         gain_ref[k] = water - base_ref[k]
-    linearize(ext_ref, cond_ref, deriv_ref, store_ref, gain_ref, mask, coefs, p0_ref, (rows, cols))
+    linearize(
+        layers, *((lambda k, ref=ref: ref[k]) for ref in (ext_ref, cond_ref, deriv_ref, store_ref, gain_ref)),
+        (ks_of(0) > 0.0).astype(f32), coefs, p0_ref, (rows, cols),
+    )
     powers((p0_ref, p1_ref, p2_ref), coefs, (rows, cols), gram_ref)
 
 
@@ -515,44 +513,42 @@
     def spread(x, axes):
         return lax.all_to_all(x, axes, split_axis=0, concat_axis=0, tiled=True)
 
-    down, up = call(edge_kernel, [((2 * layers, HALO, cols), f32)] * 2, 2)(head_old, soil_type)
+    (send,) = call(pack_kernel, [((devices, 8, LANES), f32)], 1)(canopy)
+    arrived = spread(send, both)
+
+    def edge(fields, depth):
+        return (-(-depth * fields * layers // 8) * 8, cols), f32
+
+    down, up = call(edge_kernel, [edge(2, STATE_DEPTH)] * 2, 2)(head_old, soil_type)
     lo, hi = exchange(down, up, "gx")
-    (send,) = call(
-        pack_kernel,
-        [((devices, 8, LANES), f32)],
-        2,
-        in_specs=[vmem, pl.BlockSpec(memory_space=pl.ANY)],
-        flops=1000000000,
-    )(canopy, down)
-    arrived = spread(send, both)
-    edge = ((-(-SOURCE_DEPTH * layers // 8) * 8, cols), f32)
     source, sdown, sup, flux = call(
         source_kernel,
-        [own, edge, edge, ((2, rows, cols), f32)],
+        [own] + [edge(1, SOURCE_DEPTH)] * 2 + [((2, rows, cols), f32)],
         6,
         scratch=[pltpu.VMEM((devices // 2, 2 + layers, 8, LANES), f32)],
         in_specs=[smem] + [vmem] * 5,
     )(soil_table, arrived, head_old, soil_type, forcing, column_slot)
     slo, shi = exchange(sdown, sup, "gx")
-    line = lax.axis_size("gy")
-    (strip,) = call(state_strip_kernel, [((line, 2, tall, LANES), f32)], 4)(head_old, soil_type, lo, hi)
-    strip = spread(strip, "gy")
-    (sstrip,) = call(source_strip_kernel, [((line, 1, tall, LANES), f32)], 3)(source, slo, shi)
-    sstrip = spread(sstrip, "gy")
-    held = [pltpu.VMEM(ext[0], f32)]
+    main, side_block = ((layers, tall, cols), f32), ((layers, tall, LANES), f32)
     old, ks, steep, cap, cond, deriv, store, water = call(
-        state_kernel, [ext] * 8, 6, in_specs=[smem] + [vmem] * 5, flops=20000000
-    )(soil_table, head_old, soil_type, lo, hi, strip)
-    flow, *coefs = call(
-        functools.partial(flow_kernel, tile=(rows, cols)), [ext] * 8, 6, scratch=held, flops=20000000
-    )(old, ks, cond, deriv, store, water)
-    base, p0, p1, p2, gram = call(first_kernel, [ext] * 4 + [gram_block], 13)(
-        source, slo, shi, sstrip, water, flow, *coefs
+        state_kernel, [main] * 8, 5, in_specs=[smem] + [vmem] * 4
+    )(soil_table, head_old, soil_type, lo, hi)
+    ydown, yup = call(strip_kernel, [((3, tall, LANES), f32)] * 2, 7)(
+        head_old, soil_type, lo, hi, source, slo, shi
     )
+    ylo, yhi = exchange(ydown, yup, "gy")
+    held, held_side = [pltpu.VMEM(ext[0], f32)], [pltpu.VMEM(side_block[0], f32)]
+    old_s, ks_s, steep_s, cap_s, base, p0, p1, p2, gram = call(
+        first_kernel,
+        [side_block] * 4 + [ext] * 4 + [gram_block],
+        12,
+        scratch=held_side * 4 + held * 7,
+        in_specs=[smem] + [vmem] * 11,
+    )(soil_table, source, slo, shi, ylo, yhi, old, ks, cond, deriv, store, water)
     sums = spread(gram, both)
     part, q0, q1, q2, gram = call(
-        second_kernel, [own] + [ext] * 3 + [gram_block], 9, scratch=held * 12
-    )(sums, old, ks, steep, cap, base, p0, p1, p2)
+        second_kernel, [own] + [ext] * 3 + [gram_block], 13, scratch=held * 12
+    )(sums, old, ks, steep, cap, old_s, ks_s, steep_s, cap_s, base, p0, p1, p2)
     sums = spread(gram, both)
     (head,) = call(last_kernel, [own], 5)(sums, part, q0, q1, q2)
     return head, flux

time: 106 us -> 75.3 us (0.71)
  local copies, waits for them, and re-layouts: 23.7 us -> 1.93 us
  blocking collectives: 38.6 us -> 23.8 us
  waiting for transfers between devices: 3.81 us -> 9.36 us
    unnamed x76 -> x14, local copies, waits for them, and re-layouts: 23.7 us -> 1.93 us
    all_to_all x3 -> x2, blocking collectives: 38.6 us -> 23.8 us  [spread(): return lax.all_to_all(x, axes, split_axis=0, concat_axis=0, tiled=True)]
    ppermute x2 -> x3, waiting for transfers between devices: 0.01 us -> 3.2 us  [exchange(): lax.ppermute(to_upper, axis, up)]
    ppermute x2 -> x3, waiting for transfers between devices: 1.6 us -> 4.14 us  [exchange(): lax.ppermute(to_lower, axis, down)]
    ppermute x2 -> x3, starting transfers between devices: 2.58 us -> 3.88 us  [exchange(): lax.ppermute(to_lower, axis, down)]
    ppermute x2 -> x3, starting transfers between devices: 8.82 us -> 7.78 us  [exchange(): lax.ppermute(to_upper, axis, up)]
    all_to_all x2 -> x1, starting transfers between devices: 6.61 us -> 7.3 us  [spread(): return lax.all_to_all(x, axes, split_axis=0, concat_axis=0, tiled=True)]
    pallas_call x9 -> x7, Pallas kernels: 18.9 us -> 19.1 us  [the longest x1 5.78 us: shards(): call(first_kernel, [side_block] * 4 + [ext] * 4 + [gram_block], 12, scrat...]
  transfers between devices with their start and end apart: 6 -> 7, of which waited for: 2 -> 5; matrix products, arithmetic and copies ran while one was open for 0% -> 0% of each run, Pallas kernels for 11% -> 10%
where the time goes in v5:
time: 75.3 us; the launch traced here: 75 us
  blocking collectives  23.8 us (32%)
  Pallas kernels  20.2 us (27%)
  starting transfers between devices  18.9 us (25%)
  waiting for transfers between devices  9.36 us (12%)
  local copies, waits for them, and re-layouts  1.93 us (3%)
  between operations  0.77 us (1%)
    all_to_all x2, blocking collectives, spread(): return lax.all_to_all(x, axes, split_axis=0, concat_axis=0, tiled=True)  23.8 us
    ppermute x3, starting transfers between devices, exchange(): lax.ppermute(to_upper, axis, up)  7.78 us
    all_to_all x1, starting transfers between devices, spread(): return lax.all_to_all(x, axes, split_axis=0, concat_axis=0, tiled=True)  7.3 us
    pallas_call x1, Pallas kernels, shards(): call(first_kernel, [side_block] * 4 + [ext] * 4 + [gram_block], 12, scrat...  5.78 us
    pallas_call x1, Pallas kernels, shards(): call(source_kernel, [own] + [edge(1, SOURCE_DEPTH)] * 2 + [((2, rows, col...  5.39 us
    pallas_call x1, Pallas kernels, shards(): call(second_kernel, [own] + [ext] * 3 + [gram_block], 13, scratch=held * 12)  4.81 us
    ppermute x3, waiting for transfers between devices, exchange(): lax.ppermute(to_lower, axis, down)  4.14 us
    ppermute x3, starting transfers between devices, exchange(): lax.ppermute(to_lower, axis, down)  3.88 us
  transfers between devices with their start and end apart: 7, of which 5 were waited for; matrix products, arithmetic and copies ran while one was open for 0% of the time, Pallas kernels for 10%

profile of v5, /device:TPU:0, one launch (start us, length us, event | category | flops | bytes accessed | tf_op | source)
XLA Modules:
  0.0 75.0 jit_solution(15330862027640936053)
XLA Ops:
  0.6 0.0 copy-start
  0.6 0.0 copy-start.3
  0.6 0.9 %copy-done.3 = f32[13,2048]{1,0:T(8,128)S(1)} copy-done((f32[13,2048]{1,0:T(8,128)S(1)}, f32[13,2048]{1,0:T(8,128)}, u32[]{:S(2)}) %copy-start.3) | copy-done | bytes 106520
  1.6 0.8 %shard_map.77 = f32[32,8,128]{2,1,0:T(8,128)} custom-call(f32[13,2048]{1,0:T(8,128)S(1)} %copy-done.3), custom_call_target="tpu_custom_call" | custom-call | flops 1000000 | bytes 1000000 | tf_op jit(solution)/shard_map/pallas_call | solution.py:516
  2.3 7.3 %all-to-all-start = ((f32[32,8,128]{2,1,0:T(8,128)}), f32[32,8,128]{2,1,0:T(8,128)S(1)}, u32[]{:S(2)}, u32[]{:S(2)}) async-start(f32[32,8,128]{2,1,0:T(8,128)} %shard_map.77), calls=%async_computation | async-start | bytes 262144 | tf_op jit(solution)/shard_map/all_to_all | solution.py:514
  9.7 0.0 copy-done
  9.7 0.0 copy-start.1
  9.7 1.0 %copy-done.1 = s32[10,16,512]{2,1,0:T(8,128)S(1)} copy-done((s32[10,16,512]{2,1,0:T(8,128)S(1)}, s32[10,16,512]{2,1,0:T(8,128)}, u32[]{:S(2)}) %copy-start.1) | copy-done | bytes 327704
  10.6 0.1 shard_map.79
  10.7 0.0 copy-start.6
  10.7 3.8 %collective-permute-start.2 = (f32[144,512]{1,0:T(8,128)S(1)}, f32[144,512]{1,0:T(8,128)S(1)}, u32[]{:S(2)}, u32[]{:S(2)}) collective-permute-start(f32[144,512]{1,0:T(8,128)S(1)} %get-tuple-element.35), channel_id=1, source_target_pairs={{0,4},{4,8},{8,12},{12,16},{16,20},{20,24},{24,28},{1,5},{5,9},{9,... | collective-permute-start | bytes 884744 | tf_op jit(solution)/shard_map/ppermute | solution.py:511
  14.6 1.3 %collective-permute-start.3 = (f32[144,512]{1,0:T(8,128)S(1)}, f32[144,512]{1,0:T(8,128)S(1)}, u32[]{:S(2)}, u32[]{:S(2)}) collective-permute-start(f32[144,512]{1,0:T(8,128)S(1)} %get-tuple-element.36), channel_id=1, source_target_pairs={{4,0},{8,4},{12,8},{16,12},{20,16},{24,20},{28,24},{5,1},{9,5},{13... | collective-permute-start | bytes 884744 | tf_op jit(solution)/shard_map/ppermute | solution.py:511
  15.9 2.0 %all-to-all-done.arrived_ref = f32[32,8,128]{2,1,0:T(8,128)S(1)} async-done(((f32[32,8,128]{2,1,0:T(8,128)}), f32[32,8,128]{2,1,0:T(8,128)S(1)}, u32[]{:S(2)}, u32[]{:S(2)}) %all-to-all-start) | async-done | bytes 131104 | tf_op jit(solution)/shard_map/all_to_all | solution.py:514
  17.9 0.0 copy-done.2
  17.9 5.4 %shard_map.78 = (f32[10,16,512]{2,1,0:T(8,128)S(1)}, f32[64,512]{1,0:T(8,128)S(1)}, f32[64,512]{1,0:T(8,128)S(1)}, f32[2,16,512]{2,1,0:T(8,128)}) custom-call(f32[3,12]{1,0:T(4,128)S(1)} %copy-done.6, f32[32,8,128]{2,1,0:T(8,128)S(1)} %all-to-all-done.arrived_ref, f32[10,16,512]{2,1,0:T(8,128)S(1)} %copy-done, s32[10,16,512]{2,1,0:T(8,128)S(1)} %copy-done.2, ...), custom_call_target="tpu_custom_call" | custom-call | flops 1000000 | bytes 1000000 | tf_op jit(solution)/shard_map/pallas_call | solution.py:524
  23.3 2.7 %collective-permute-start = (f32[64,512]{1,0:T(8,128)S(1)}, f32[64,512]{1,0:T(8,128)S(1)}, u32[]{:S(2)}, u32[]{:S(2)}) collective-permute-start(f32[64,512]{1,0:T(8,128)S(1)} %get-tuple-element.33), channel_id=1, source_target_pairs={{0,4},{4,8},{8,12},{12,16},{16,20},{20,24},{24,28},{1,5},{5,9},{9,... | collective-permute-start | bytes 393224 | tf_op jit(solution)/shard_map/ppermute | solution.py:511
  26.0 1.3 %collective-permute-start.1 = (f32[64,512]{1,0:T(8,128)S(1)}, f32[64,512]{1,0:T(8,128)S(1)}, u32[]{:S(2)}, u32[]{:S(2)}) collective-permute-start(f32[64,512]{1,0:T(8,128)S(1)} %get-tuple-element.34), channel_id=1, source_target_pairs={{4,0},{8,4},{12,8},{16,12},{20,16},{24,20},{28,24},{5,1},{9,5},{13... | collective-permute-start | bytes 393224 | tf_op jit(solution)/shard_map/ppermute | solution.py:511
  27.3 1.0 %collective-permute-done.2.lo_ref = f32[144,512]{1,0:T(8,128)S(1)} collective-permute-done((f32[144,512]{1,0:T(8,128)S(1)}, f32[144,512]{1,0:T(8,128)S(1)}, u32[]{:S(2)}, u32[]{:S(2)}) %collective-permute-start.2) | collective-permute-done | bytes 294944 | tf_op jit(solution)/shard_map/ppermute | solution.py:511
  28.3 0.0 collective-permute-done.3.hi_ref
  28.3 2.2 %collective-permute-done.slo_ref = f32[64,512]{1,0:T(8,128)S(1)} collective-permute-done((f32[64,512]{1,0:T(8,128)S(1)}, f32[64,512]{1,0:T(8,128)S(1)}, u32[]{:S(2)}, u32[]{:S(2)}) %collective-permute-start) | collective-permute-done | bytes 131104 | tf_op jit(solution)/shard_map/ppermute | solution.py:511
  30.5 2.6 %collective-permute-done.1.shi_ref = f32[64,512]{1,0:T(8,128)S(1)} collective-permute-done((f32[64,512]{1,0:T(8,128)S(1)}, f32[64,512]{1,0:T(8,128)S(1)}, u32[]{:S(2)}, u32[]{:S(2)}) %collective-permute-start.1) | collective-permute-done | bytes 131104 | tf_op jit(solution)/shard_map/ppermute | solution.py:511
  33.1 0.3 shard_map.80
  33.4 1.3 %collective-permute-start.4 = (f32[3,32,128]{2,1,0:T(8,128)S(1)}, f32[3,32,128]{2,1,0:T(8,128)S(1)}, u32[]{:S(2)}, u32[]{:S(2)}) collective-permute-start(f32[3,32,128]{2,1,0:T(8,128)S(1)} %get-tuple-element.37), channel_id=1, source_target_pairs={{0,1},{1,2},{2,3},{4,5},{5,6},{6,7},{8,9},{9,10},{10,11},{12,13},{... | collective-permute-start | bytes 147464 | tf_op jit(solution)/shard_map/ppermute | solution.py:511
  34.7 1.3 %collective-permute-start.5 = (f32[3,32,128]{2,1,0:T(8,128)S(1)}, f32[3,32,128]{2,1,0:T(8,128)S(1)}, u32[]{:S(2)}, u32[]{:S(2)}) collective-permute-start(f32[3,32,128]{2,1,0:T(8,128)S(1)} %get-tuple-element.38), channel_id=1, source_target_pairs={{1,0},{2,1},{3,2},{5,4},{6,5},{7,6},{9,8},{10,9},{11,10},{13,12},{... | collective-permute-start | bytes 147464 | tf_op jit(solution)/shard_map/ppermute | solution.py:511
  36.0 2.0 %shard_map.81 = (f32[10,32,512]{2,1,0:T(8,128)S(1)}, f32[10,32,512]{2,1,0:T(8,128)S(1)}, f32[10,32,512]{2,1,0:T(8,128)S(1)}, f32[10,32,512]{2,1,0:T(8,128)S(1)},...) custom-call(f32[3,12]{1,0:T(4,128)S(1)} %copy-done.6, ...), custom_call_target="tpu_custom_call" | custom-call | flops 1000000 | bytes 1000000 | tf_op jit(solution)/shard_map/pallas_call | solution.py:533
  38.0 0.0 collective-permute-done.4.ylo_ref
  38.0 1.5 %collective-permute-done.5.yhi_ref = f32[3,32,128]{2,1,0:T(8,128)S(1)} collective-permute-done((f32[3,32,128]{2,1,0:T(8,128)S(1)}, f32[3,32,128]{2,1,0:T(8,128)S(1)}, u32[]{:S(2)}, u32[]{:S(2)}) %collective-permute-start.5) | collective-permute-done | bytes 49184 | tf_op jit(solution)/shard_map/ppermute | solution.py:511
  39.5 5.8 %shard_map.82 = (f32[10,32,128]{2,1,0:T(8,128)S(1)}, f32[10,32,128]{2,1,0:T(8,128)S(1)}, f32[10,32,128]{2,1,0:T(8,128)S(1)}, f32[10,32,128]{2,1,0:T(8,128)S(1)},...) custom-call(f32[3,12]{1,0:T(4,128)S(1)} %copy-done.6, ...), custom_call_target="tpu_custom_call" | custom-call | flops 1000000 | bytes 1000000 | tf_op jit(solution)/shard_map/pallas_call | solution.py:541
  45.3 14.9 %all_to_all.15.arrived_ref = f32[32,1,128]{2,1,0:T(1,128)S(1)} all-to-all(f32[32,1,128]{2,1,0:T(1,128)S(1)} %get-tuple-element.45), channel_id=1, replica_groups=mesh['gx'=8,'gy'=4] {'gx','gy'}, dimensions={0} | all-to-all | bytes 32768 | tf_op jit(solution)/shard_map/all_to_all | solution.py:514
  60.2 4.8 %shard_map.83 = (f32[10,16,512]{2,1,0:T(8,128)S(1)}, f32[10,32,640]{2,1,0:T(8,128)S(1)}, f32[10,32,640]{2,1,0:T(8,128)S(1)}, f32[10,32,640]{2,1,0:T(8,128)S(1)}, f32[32,1,128]{2,1,0:T(1,128)S(1)}) custom-call(f32[32,1,128]{2,1,0:T(1,128)S(1)} %all_to_all.15.arrived_ref, f32[10,32,512]{2,1,0:T(8,128)S(1)} %get-tuple-element.39.ext_ref.old_ref, ...), custom_call_target="tpu_custom_call" | custom-call | flops 1000000 | bytes 1000000 | tf_op jit(solution)/shard_map/pallas_call | solution.py:549
  65.0 8.8 %all_to_all.16.arrived_ref = f32[32,1,128]{2,1,0:T(1,128)S(1)} all-to-all(f32[32,1,128]{2,1,0:T(1,128)S(1)} %get-tuple-element.56), channel_id=1, replica_groups=mesh['gx'=8,'gy'=4] {'gx','gy'}, dimensions={0} | all-to-all | bytes 32768 | tf_op jit(solution)/shard_map/all_to_all | solution.py:514
  73.9 1.1 %shard_map.84 = f32[10,16,512]{2,1,0:T(8,128)} custom-call(f32[32,1,128]{2,1,0:T(1,128)S(1)} %all_to_all.16.arrived_ref, f32[10,16,512]{2,1,0:T(8,128)S(1)} %get-tuple-element.57.part_ref, f32[10,32,640]{2,1,0:T(8,128)S(1)} %get-tuple-element.58.q0_ref, f32[10,32,640]{2,1,0:T(8,128)S(1)} %get-tuple-element.59.q1_ref, f32[10,32,640]{2,1,0:T(8,128)S(1)} %get-tuple-element.60.q2_ref), custom_call_target="tpu_custom_call" | custom-call | flops 1000000 | bytes 1000000 | tf_op jit(solution)/shard_map/pallas_call | solution.py:553
  (6 shorter events, 0.0 us)
Async XLA Ops:
  0.6 9.0 %copy-start = (f32[10,16,512]{2,1,0:T(8,128)S(1)}, f32[10,16,512]{2,1,0:T(8,128)}, u32[]{:S(2)}) copy-start(f32[10,16,512]{2,1,0:T(8,128)} %head_ref.7) | copy-start | bytes 983044
  0.6 1.0 %copy-start.3 = (f32[13,2048]{1,0:T(8,128)S(1)}, f32[13,2048]{1,0:T(8,128)}, u32[]{:S(2)}) copy-start(f32[13,2048]{1,0:T(8,128)} %canopy_ref.1) | copy-start | bytes 319492
  2.3 15.5 %all-to-all-start = ((f32[32,8,128]{2,1,0:T(8,128)}), f32[32,8,128]{2,1,0:T(8,128)S(1)}, u32[]{:S(2)}, u32[]{:S(2)}) async-start(f32[32,8,128]{2,1,0:T(8,128)} %shard_map.77), calls=%async_computation | async-start | bytes 262144 | tf_op jit(solution)/shard_map/all_to_all | solution.py:514
  9.7 1.0 %copy-start.1 = (s32[10,16,512]{2,1,0:T(8,128)S(1)}, s32[10,16,512]{2,1,0:T(8,128)}, u32[]{:S(2)}) copy-start(s32[10,16,512]{2,1,0:T(8,128)} %soil_ref.7) | copy-start | bytes 983044
  10.6 7.2 %copy-start.2 = (s32[10,16,512]{2,1,0:T(8,128)S(1)}, s32[10,16,512]{2,1,0:T(8,128)}, u32[]{:S(2)}) copy-start(s32[10,16,512]{2,1,0:T(8,128)} %soil_ref.7) | copy-start | bytes 983044
  10.6 7.2 %copy-start.4 = (f32[4,16,512]{2,1,0:T(8,128)S(1)}, f32[4,16,512]{2,1,0:T(8,128)}, u32[]{:S(2)}) copy-start(f32[4,16,512]{2,1,0:T(8,128)} %forcing_ref.1) | copy-start | bytes 393220
  10.6 7.2 %copy-start.5 = (s32[16,512]{1,0:T(8,128)S(1)}, s32[16,512]{1,0:T(8,128)}, u32[]{:S(2)}) copy-start(s32[16,512]{1,0:T(8,128)} %slot_ref.1) | copy-start | bytes 98308
  10.7 7.2 %copy-start.6 = (f32[3,12]{1,0:T(4,128)S(1)}, f32[3,12]{1,0:T(4,128)}, u32[]{:S(2)}) copy-start(f32[3,12]{1,0:T(4,128)} %table_ref.5) | copy-start | bytes 436
  10.7 17.5 %collective-permute-start.2 = (f32[144,512]{1,0:T(8,128)S(1)}, f32[144,512]{1,0:T(8,128)S(1)}, u32[]{:S(2)}, u32[]{:S(2)}) collective-permute-start(f32[144,512]{1,0:T(8,128)S(1)} %get-tuple-element.35), channel_id=1, source_target_pairs={{0,4},{4,8},{8,12},{12,16},{16,20},{20,24},{24,28},{1,5},{5,9},{9,... | collective-permute-start | bytes 884744 | tf_op jit(solution)/shard_map/ppermute | solution.py:511
  14.6 13.7 %collective-permute-start.3 = (f32[144,512]{1,0:T(8,128)S(1)}, f32[144,512]{1,0:T(8,128)S(1)}, u32[]{:S(2)}, u32[]{:S(2)}) collective-permute-start(f32[144,512]{1,0:T(8,128)S(1)} %get-tuple-element.36), channel_id=1, source_target_pairs={{4,0},{8,4},{12,8},{16,12},{20,16},{24,20},{28,24},{5,1},{9,5},{13... | collective-permute-start | bytes 884744 | tf_op jit(solution)/shard_map/ppermute | solution.py:511
  23.3 7.2 %collective-permute-start = (f32[64,512]{1,0:T(8,128)S(1)}, f32[64,512]{1,0:T(8,128)S(1)}, u32[]{:S(2)}, u32[]{:S(2)}) collective-permute-start(f32[64,512]{1,0:T(8,128)S(1)} %get-tuple-element.33), channel_id=1, source_target_pairs={{0,4},{4,8},{8,12},{12,16},{16,20},{20,24},{24,28},{1,5},{5,9},{9,... | collective-permute-start | bytes 393224 | tf_op jit(solution)/shard_map/ppermute | solution.py:511
  26.0 7.1 %collective-permute-start.1 = (f32[64,512]{1,0:T(8,128)S(1)}, f32[64,512]{1,0:T(8,128)S(1)}, u32[]{:S(2)}, u32[]{:S(2)}) collective-permute-start(f32[64,512]{1,0:T(8,128)S(1)} %get-tuple-element.34), channel_id=1, source_target_pairs={{4,0},{8,4},{12,8},{16,12},{20,16},{24,20},{28,24},{5,1},{9,5},{13... | collective-permute-start | bytes 393224 | tf_op jit(solution)/shard_map/ppermute | solution.py:511
  33.4 4.6 %collective-permute-start.4 = (f32[3,32,128]{2,1,0:T(8,128)S(1)}, f32[3,32,128]{2,1,0:T(8,128)S(1)}, u32[]{:S(2)}, u32[]{:S(2)}) collective-permute-start(f32[3,32,128]{2,1,0:T(8,128)S(1)} %get-tuple-element.37), channel_id=1, source_target_pairs={{0,1},{1,2},{2,3},{4,5},{5,6},{6,7},{8,9},{9,10},{10,11},{12,13},{... | collective-permute-start | bytes 147464 | tf_op jit(solution)/shard_map/ppermute | solution.py:511
  34.7 4.8 %collective-permute-start.5 = (f32[3,32,128]{2,1,0:T(8,128)S(1)}, f32[3,32,128]{2,1,0:T(8,128)S(1)}, u32[]{:S(2)}, u32[]{:S(2)}) collective-permute-start(f32[3,32,128]{2,1,0:T(8,128)S(1)} %get-tuple-element.38), channel_id=1, source_target_pairs={{1,0},{2,1},{3,2},{5,4},{6,5},{7,6},{9,8},{10,9},{11,10},{13,12},{... | collective-permute-start | bytes 147464 | tf_op jit(solution)/shard_map/ppermute | solution.py:511

commit v6 on v5

--- a/solution.py
+++ b/solution.py
@@ -12,6 +12,7 @@
 HALO = 8
 STATE_DEPTH = 7
 SOURCE_DEPTH = 6
+FIXED = 65535.0
 LANES = 128
 SLOT = 64
 
@@ -88,10 +89,11 @@
 
 def source_kernel(
     table_ref, arrived_ref, head_ref, soil_ref, forcing_ref, slot_ref,
-    source_ref, down_ref, up_ref, flux_ref, tab_ref,
+    source_ref, flux_ref, tab_ref, factor_ref,
 ):
     layers, rows, cols = head_ref.shape
     owners = arrived_ref.shape[0]
+    pairs = -(-layers // 2)
     low = lane_iota((8, LANES)) < SLOT
     line = lax.broadcasted_iota(jnp.int32, (16, LANES), 0)
     is_root = (line >= 3) & (line < 3 + layers)
@@ -108,11 +110,17 @@
         )
         leaf_area, albedo, resist = both[0:1], both[1:2], both[2:3]
         root_sum = jnp.sum(jnp.where(is_root, both, 0.0), axis=0, keepdims=True)
-        both = both * (leaf_area / ((leaf_area + resist) * root_sum))
-        tab_ref[t, 0] = jnp.broadcast_to(0.5 + 0.3 * leaf_area, (8, LANES))
-        tab_ref[t, 1] = jnp.broadcast_to(1.0 - albedo, (8, LANES))
-        for k in range(layers):
-            tab_ref[t, 2 + k] = jnp.broadcast_to(both[3 + k : 4 + k], (8, LANES))
+        factor = leaf_area / ((leaf_area + resist) * root_sum) * (1.0 / FIXED)
+        factor_ref[t] = jnp.broadcast_to(factor, (8, LANES))
+        fixed = (both * FIXED + 0.5).astype(jnp.int32)
+        for m in range(pairs):
+            word = fixed[3 + m : 4 + m]
+            if m + pairs < layers:
+                word = word | (fixed[3 + m + pairs : 4 + m + pairs] << 16)
+            tab_ref[t, m] = jnp.broadcast_to(word, (8, LANES))
+        leaf = ((0.5 + 0.3 * leaf_area) * (0.25 * FIXED) + 0.5).astype(jnp.int32)
+        bright = ((1.0 - albedo) * FIXED + 0.5).astype(jnp.int32)
+        tab_ref[t, pairs] = jnp.broadcast_to(leaf | (bright << 16), (8, LANES))
         return 0
 
     lax.fori_loop(0, owners // 2, unpack, 0, unroll=16)
@@ -130,12 +138,23 @@
 
             def pick(t, held):
                 match = tile == t
-                return tuple(
-                    jnp.where(match, lookup(tab_ref[t, k], lane), held[k]) for k in range(2 + layers)
-                )
-
-            start = tuple(jnp.ones((8, LANES), f32) for _ in range(2 + layers))
-            exchange_coef, absorbed, *roots = lax.fori_loop(0, owners // 2, pick, start, unroll=8)
+                found = [lookup(tab_ref[t, m], lane) for m in range(pairs + 1)]
+                found.append(lookup(factor_ref[t], lane))
+                return tuple(jnp.where(match, new, old) for new, old in zip(found, held))
+
+            start = [jnp.full((8, LANES), 1, jnp.int32)] * (pairs + 1)
+            start.append(jnp.full((8, LANES), 1.0 / FIXED, f32))
+            *words, terms, factor = lax.fori_loop(0, owners // 2, pick, tuple(start), unroll=8)
+
+            def halves(word):
+                upper = lax.shift_right_logical(word, jnp.full((8, LANES), 16, jnp.int32))
+                return (word & 0xFFFF).astype(f32), upper.astype(f32)
+
+            leaf, bright = halves(terms)
+            exchange_coef = leaf * (4.0 / FIXED)
+            absorbed = bright * (1.0 / FIXED)
+            split = [halves(word) for word in words]
+            roots = [factor * split[k % pairs][k // pairs] for k in range(layers)]
             uptake = []
             for k in range(layers):
                 index = soil_ref[(k,) + here] + 1
@@ -172,11 +191,6 @@
                 if k == 0:
                     value = value + infiltration
                 source_ref[(k,) + here] = value
-                edge = slice(SOURCE_DEPTH * k, SOURCE_DEPTH * (k + 1))
-                if at_x < HALO:
-                    down_ref[edge, here[1]] = value[:SOURCE_DEPTH]
-                if at_x >= rows - HALO:
-                    up_ref[edge, here[1]] = value[HALO - SOURCE_DEPTH :]
             return 0
 
         lax.fori_loop(0, cols // LANES, column, 0)
@@ -204,26 +218,56 @@
     return jnp.concatenate([above, gap, below], axis=0)
 
 
-def strip_kernel(head_ref, soil_ref, lo_ref, hi_ref, src_ref, slo_ref, shi_ref, down_ref, up_ref):
+def strip_kernel(head_ref, soil_ref, src_ref, down_ref, up_ref):
     layers, _, cols = head_ref.shape
-    every = range(layers)
     for out_ref, (part, shift) in zip((down_ref, up_ref), strip_parts(cols)):
-        heads = [(head_ref[k, :, part], ends_of(lo_ref, hi_ref, k, STATE_DEPTH, part)) for k in every]
-        soils = [
-            (
-                (soil_ref[k, :, part] + 1).astype(f32),
-                ends_of(lo_ref, hi_ref, layers + k, STATE_DEPTH, part),
-            )
-            for k in every
-        ]
-        sources = [(src_ref[k, :, part], ends_of(slo_ref, shi_ref, k, SOURCE_DEPTH, part)) for k in every]
-        for field, pairs in enumerate((heads, soils, sources)):
-            out_ref[field] = strips([jnp.concatenate(pair, axis=0) for pair in pairs], shift)
-
-
-def side(ylo_ref, yhi_ref, field, k):
-    right = yhi_ref[field]
-    left = ylo_ref[field]
+        out_ref[0] = strips([head_ref[k, :, part] for k in range(layers)], shift)
+        out_ref[1] = strips([(soil_ref[k, :, part] + 1).astype(f32) for k in range(layers)], shift)
+        out_ref[2] = strips([src_ref[k, :, part] for k in range(layers)], shift)
+
+
+def source_edge_kernel(src_ref, ylo_ref, yhi_ref, down_ref, up_ref):
+    layers, rows, _ = src_ref.shape
+    at = SOURCE_DEPTH * layers
+    for out_ref, first in ((down_ref, 0), (up_ref, rows - HALO)):
+        row = 0 if first == 0 else rows - SOURCE_DEPTH
+        for k in range(layers):
+            part = slice(SOURCE_DEPTH * k, SOURCE_DEPTH * (k + 1))
+            out_ref[part] = src_ref[k][row : row + SOURCE_DEPTH]
+        blocks = [ref[f, first : first + HALO] for f in range(3) for ref in (ylo_ref, yhi_ref)]
+        half = HALO // 2
+        tail = [block[h : h + half] for block in blocks[4:6] for h in (0, half)]
+        for j in range(4):
+            out_ref[at : at + HALO, j * LANES : (j + 1) * LANES] = blocks[j]
+            out_ref[at + HALO : at + HALO + half, j * LANES : (j + 1) * LANES] = tail[j]
+
+
+def corner(edge_ref, at, field, which):
+    half = HALO // 2
+    if field < 2:
+        j = 2 * field + which
+        return edge_ref[at : at + HALO, j * LANES : (j + 1) * LANES]
+    pieces = [
+        edge_ref[at + HALO : at + HALO + half, j * LANES : (j + 1) * LANES]
+        for j in (2 * which, 2 * which + 1)
+    ]
+    return jnp.concatenate(pieces, axis=0)
+
+
+def tall_strips(layers, ylo_ref, yhi_ref, slo_ref, shi_ref):
+    at = SOURCE_DEPTH * layers
+    out = []
+    for field in range(3):
+        pair = []
+        for which, ref in ((1, yhi_ref), (0, ylo_ref)):
+            ends = [corner(shi_ref, at, field, which), corner(slo_ref, at, field, which)]
+            pair.append(jnp.concatenate([ref[field]] + ends, axis=0))
+        out.append(pair)
+    return out
+
+
+def side(strip, k):
+    right, left = strip
     lane = lane_iota(right.shape)
     shift = (-HALO * k) % LANES
     right = pltpu.roll(right, shift, 1) if shift else right
@@ -437,9 +481,10 @@
 ):
     layers, rows, cols = src_ref.shape
     tables = table_rows(table_ref, rows + 2 * HALO)
+    heads, soils, sources = tall_strips(layers, ylo_ref, yhi_ref, slo_ref, shi_ref)
     for k in range(layers):
-        head = side(ylo_ref, yhi_ref, 0, k)
-        index = side(ylo_ref, yhi_ref, 1, k).astype(jnp.int32)
+        head = side(heads, k)
+        index = side(soils, k).astype(jnp.int32)
         conduct, steep, capacity = (lookup(row, index) for row in tables)
         values = (head, conduct, steep, capacity) + pointwise(head, conduct, steep, capacity)
         outs = (ext_side, ks_side, steep_side, cap_side, cond_side, deriv_side, store_side, water_side)
@@ -449,7 +494,7 @@
 
     def gain_of(k):
         source = jnp.concatenate([src_ref[k], ends_of(slo_ref, shi_ref, k, SOURCE_DEPTH, slice(0, cols))], axis=0)
-        source = jnp.concatenate([source, side(ylo_ref, yhi_ref, 2, k)], axis=1)
+        source = jnp.concatenate([source, side(sources, k)], axis=1)
         water = water_of(k)
         base_ref[k] = water + source
         return water - base_ref[k]
@@ -516,27 +561,31 @@
     (send,) = call(pack_kernel, [((devices, 8, LANES), f32)], 1)(canopy)
     arrived = spread(send, both)
 
-    def edge(fields, depth):
-        return (-(-depth * fields * layers // 8) * 8, cols), f32
-
-    down, up = call(edge_kernel, [edge(2, STATE_DEPTH)] * 2, 2)(head_old, soil_type)
+    def edge(count):
+        return (-(-count // 8) * 8, cols), f32
+
+    down, up = call(edge_kernel, [edge(2 * STATE_DEPTH * layers)] * 2, 2)(head_old, soil_type)
     lo, hi = exchange(down, up, "gx")
-    source, sdown, sup, flux = call(
+    source, flux = call(
         source_kernel,
-        [own] + [edge(1, SOURCE_DEPTH)] * 2 + [((2, rows, cols), f32)],
+        [own, ((2, rows, cols), f32)],
         6,
-        scratch=[pltpu.VMEM((devices // 2, 2 + layers, 8, LANES), f32)],
+        scratch=[
+            pltpu.VMEM((devices // 2, -(-layers // 2) + 1, 8, LANES), jnp.int32),
+            pltpu.VMEM((devices // 2, 8, LANES), f32),
+        ],
         in_specs=[smem] + [vmem] * 5,
     )(soil_table, arrived, head_old, soil_type, forcing, column_slot)
+    ydown, yup = call(strip_kernel, [((3, rows, LANES), f32)] * 2, 3)(head_old, soil_type, source)
+    ylo, yhi = exchange(ydown, yup, "gy")
+    sdown, sup = call(source_edge_kernel, [edge(SOURCE_DEPTH * layers + HALO + HALO // 2)] * 2, 3)(
+        source, ylo, yhi
+    )
     slo, shi = exchange(sdown, sup, "gx")
     main, side_block = ((layers, tall, cols), f32), ((layers, tall, LANES), f32)
     old, ks, steep, cap, cond, deriv, store, water = call(
         state_kernel, [main] * 8, 5, in_specs=[smem] + [vmem] * 4
     )(soil_table, head_old, soil_type, lo, hi)
-    ydown, yup = call(strip_kernel, [((3, tall, LANES), f32)] * 2, 7)(
-        head_old, soil_type, lo, hi, source, slo, shi
-    )
-    ylo, yhi = exchange(ydown, yup, "gy")
     held, held_side = [pltpu.VMEM(ext[0], f32)], [pltpu.VMEM(side_block[0], f32)]
     old_s, ks_s, steep_s, cap_s, base, p0, p1, p2, gram = call(
         first_kernel,

time: 75.3 us -> 73.9 us (0.981)
  starting transfers between devices: 18.9 us -> 20.6 us
  waiting for transfers between devices: 9.36 us -> 7.85 us
  blocking collectives: 23.8 us -> 22.8 us
    ppermute x3, waiting for transfers between devices: 3.2 us -> 0.01 us  [exchange(): lax.ppermute(to_upper, axis, up)]
    ppermute x3, waiting for transfers between devices: 4.14 us -> 5.83 us  [exchange(): lax.ppermute(to_lower, axis, down)]
    ppermute x3, starting transfers between devices: 7.78 us -> 9.39 us  [exchange(): lax.ppermute(to_upper, axis, up)]
    all_to_all x2, blocking collectives: 23.8 us -> 22.8 us  [spread(): return lax.all_to_all(x, axes, split_axis=0, concat_axis=0, tiled=True)]
    pallas_call x3 -> x4, Pallas kernels: 5.77 us -> 4.92 us  [the longest x1 4.62 us: shards(): call(source_kernel, [own, ((2, rows, cols), f32)], 6, scratch=[pltpu.VMEM...]
  transfers between devices with their start and end apart: 7 -> 7, of which waited for: 5 -> 3; matrix products, arithmetic and copies ran while one was open for 0% -> 0% of each run, Pallas kernels for 10% -> 9%
where the time goes in v6:
time: 73.9 us; the launch traced here: 73.5 us
  blocking collectives  22.8 us (31%)
  starting transfers between devices  20.6 us (28%)
  Pallas kernels  19.6 us (27%)
  waiting for transfers between devices  7.85 us (11%)
  local copies, waits for them, and re-layouts  1.93 us (3%)
  between operations  0.8 us (1%)
    all_to_all x2, blocking collectives, spread(): return lax.all_to_all(x, axes, split_axis=0, concat_axis=0, tiled=True)  22.8 us
    ppermute x3, starting transfers between devices, exchange(): lax.ppermute(to_upper, axis, up)  9.39 us
    all_to_all x1, starting transfers between devices, spread(): return lax.all_to_all(x, axes, split_axis=0, concat_axis=0, tiled=True)  7.3 us
    pallas_call x1, Pallas kernels, shards(): call(first_kernel, [side_block] * 4 + [ext] * 4 + [gram_block], 12, scrat...  6.01 us
    ppermute x3, waiting for transfers between devices, exchange(): lax.ppermute(to_lower, axis, down)  5.83 us
    pallas_call x1, Pallas kernels, shards(): call(second_kernel, [own] + [ext] * 3 + [gram_block], 13, scratch=held * 12)  4.84 us
    pallas_call x1, Pallas kernels, shards(): call(source_kernel, [own, ((2, rows, cols), f32)], 6, scratch=[pltpu.VMEM...  4.62 us
    ppermute x3, starting transfers between devices, exchange(): lax.ppermute(to_lower, axis, down)  3.88 us
  transfers between devices with their start and end apart: 7, of which 3 were waited for; matrix products, arithmetic and copies ran while one was open for 0% of the time, Pallas kernels for 9%

profile of v6, /device:TPU:0, one launch (start us, length us, event | category | flops | bytes accessed | tf_op | source)
XLA Modules:
  0.0 73.5 jit_solution(14205795078451945908)
XLA Ops:
  0.6 0.0 copy-start
  0.6 0.0 copy-start.3
  0.6 0.9 %copy-done.3 = f32[13,2048]{1,0:T(8,128)S(1)} copy-done((f32[13,2048]{1,0:T(8,128)S(1)}, f32[13,2048]{1,0:T(8,128)}, u32[]{:S(2)}) %copy-start.3) | copy-done | bytes 106520
  1.6 0.8 %shard_map.77 = f32[32,8,128]{2,1,0:T(8,128)} custom-call(f32[13,2048]{1,0:T(8,128)S(1)} %copy-done.3), custom_call_target="tpu_custom_call" | custom-call | flops 1000000 | bytes 1000000 | tf_op jit(solution)/shard_map/pallas_call | solution.py:561
  2.3 7.3 %all-to-all-start = ((f32[32,8,128]{2,1,0:T(8,128)}), f32[32,8,128]{2,1,0:T(8,128)S(1)}, u32[]{:S(2)}, u32[]{:S(2)}) async-start(f32[32,8,128]{2,1,0:T(8,128)} %shard_map.77), calls=%async_computation | async-start | bytes 262144 | tf_op jit(solution)/shard_map/all_to_all | solution.py:559
  9.7 0.0 copy-done
  9.7 0.0 copy-start.1
  9.7 1.0 %copy-done.1 = s32[10,16,512]{2,1,0:T(8,128)S(1)} copy-done((s32[10,16,512]{2,1,0:T(8,128)S(1)}, s32[10,16,512]{2,1,0:T(8,128)}, u32[]{:S(2)}) %copy-start.1) | copy-done | bytes 327704
  10.6 0.1 shard_map.81
  10.7 0.0 copy-start.6
  10.7 3.8 %collective-permute-start.4 = (f32[144,512]{1,0:T(8,128)S(1)}, f32[144,512]{1,0:T(8,128)S(1)}, u32[]{:S(2)}, u32[]{:S(2)}) collective-permute-start(f32[144,512]{1,0:T(8,128)S(1)} %get-tuple-element.37), channel_id=1, source_target_pairs={{0,4},{4,8},{8,12},{12,16},{16,20},{20,24},{24,28},{1,5},{5,9},{9,... | collective-permute-start | bytes 884744 | tf_op jit(solution)/shard_map/ppermute | solution.py:556
  14.6 1.3 %collective-permute-start.5 = (f32[144,512]{1,0:T(8,128)S(1)}, f32[144,512]{1,0:T(8,128)S(1)}, u32[]{:S(2)}, u32[]{:S(2)}) collective-permute-start(f32[144,512]{1,0:T(8,128)S(1)} %get-tuple-element.38), channel_id=1, source_target_pairs={{4,0},{8,4},{12,8},{16,12},{20,16},{24,20},{28,24},{5,1},{9,5},{13... | collective-permute-start | bytes 884744 | tf_op jit(solution)/shard_map/ppermute | solution.py:556
  15.9 2.0 %all-to-all-done.arrived_ref = f32[32,8,128]{2,1,0:T(8,128)S(1)} async-done(((f32[32,8,128]{2,1,0:T(8,128)}), f32[32,8,128]{2,1,0:T(8,128)S(1)}, u32[]{:S(2)}, u32[]{:S(2)}) %all-to-all-start) | async-done | bytes 131104 | tf_op jit(solution)/shard_map/all_to_all | solution.py:559
  17.9 0.0 copy-done.2
  17.9 4.6 %shard_map.78 = (f32[10,16,512]{2,1,0:T(8,128)S(1)}, f32[2,16,512]{2,1,0:T(8,128)}) custom-call(f32[3,12]{1,0:T(4,128)S(1)} %copy-done.6, f32[32,8,128]{2,1,0:T(8,128)S(1)} %all-to-all-done.arrived_ref, f32[10,16,512]{2,1,0:T(8,128)S(1)} %copy-done, s32[10,16,512]{2,1,0:T(8,128)S(1)} %copy-done.2, f32[4,16,512]{2,1,0:T(8,128)S(1)} %copy-done.4, ...), custom_call_target="tpu_custom_call" | custom-call | flops 1000000 | bytes 1000000 | tf_op jit(solution)/shard_map/pallas_call | solution.py:569
  22.5 0.2 shard_map.79
  22.7 2.1 %collective-permute-start = (f32[3,16,128]{2,1,0:T(8,128)S(1)}, f32[3,16,128]{2,1,0:T(8,128)S(1)}, u32[]{:S(2)}, u32[]{:S(2)}) collective-permute-start(f32[3,16,128]{2,1,0:T(8,128)S(1)} %get-tuple-element.33), channel_id=1, source_target_pairs={{0,1},{1,2},{2,3},{4,5},{5,6},{6,7},{8,9},{9,10},{10,11},{12,13},{... | collective-permute-start | bytes 73736 | tf_op jit(solution)/shard_map/ppermute | solution.py:556
  24.8 1.3 %collective-permute-start.1 = (f32[3,16,128]{2,1,0:T(8,128)S(1)}, f32[3,16,128]{2,1,0:T(8,128)S(1)}, u32[]{:S(2)}, u32[]{:S(2)}) collective-permute-start(f32[3,16,128]{2,1,0:T(8,128)S(1)} %get-tuple-element.34), channel_id=1, source_target_pairs={{1,0},{2,1},{3,2},{5,4},{6,5},{7,6},{9,8},{10,9},{11,10},{13,12},{... | collective-permute-start | bytes 73736 | tf_op jit(solution)/shard_map/ppermute | solution.py:556
  26.1 0.0 collective-permute-done.ylo_ref
  26.1 1.8 %collective-permute-done.1.yhi_ref = f32[3,16,128]{2,1,0:T(8,128)S(1)} collective-permute-done((f32[3,16,128]{2,1,0:T(8,128)S(1)}, f32[3,16,128]{2,1,0:T(8,128)S(1)}, u32[]{:S(2)}, u32[]{:S(2)}) %collective-permute-start.1) | collective-permute-done | bytes 24608 | tf_op jit(solution)/shard_map/ppermute | solution.py:556
  28.0 3.4 %collective-permute-start.2 = (f32[72,512]{1,0:T(8,128)S(1)}, f32[72,512]{1,0:T(8,128)S(1)}, u32[]{:S(2)}, u32[]{:S(2)}) collective-permute-start(f32[72,512]{1,0:T(8,128)S(1)} %get-tuple-element.35), channel_id=1, source_target_pairs={{0,4},{4,8},{8,12},{12,16},{16,20},{20,24},{24,28},{1,5},{5,9},{9,... | collective-permute-start | bytes 442376 | tf_op jit(solution)/shard_map/ppermute | solution.py:556
  31.4 1.3 %collective-permute-start.3 = (f32[72,512]{1,0:T(8,128)S(1)}, f32[72,512]{1,0:T(8,128)S(1)}, u32[]{:S(2)}, u32[]{:S(2)}) collective-permute-start(f32[72,512]{1,0:T(8,128)S(1)} %get-tuple-element.36), channel_id=1, source_target_pairs={{4,0},{8,4},{12,8},{16,12},{20,16},{24,20},{28,24},{5,1},{9,5},{13... | collective-permute-start | bytes 442376 | tf_op jit(solution)/shard_map/ppermute | solution.py:556
  32.7 0.0 collective-permute-done.4.lo_ref
  32.7 0.0 collective-permute-done.5.hi_ref
  32.7 2.0 %shard_map.82 = (f32[10,32,512]{2,1,0:T(8,128)S(1)}, f32[10,32,512]{2,1,0:T(8,128)S(1)}, f32[10,32,512]{2,1,0:T(8,128)S(1)}, f32[10,32,512]{2,1,0:T(8,128)S(1)},...) custom-call(f32[3,12]{1,0:T(4,128)S(1)} %copy-done.6, ...), custom_call_target="tpu_custom_call" | custom-call | flops 1000000 | bytes 1000000 | tf_op jit(solution)/shard_map/pallas_call | solution.py:586
  34.7 0.0 collective-permute-done.2.slo_ref
  34.7 4.1 %collective-permute-done.3.shi_ref = f32[72,512]{1,0:T(8,128)S(1)} collective-permute-done((f32[72,512]{1,0:T(8,128)S(1)}, f32[72,512]{1,0:T(8,128)S(1)}, u32[]{:S(2)}, u32[]{:S(2)}) %collective-permute-start.3) | collective-permute-done | bytes 147488 | tf_op jit(solution)/shard_map/ppermute | solution.py:556
  38.8 6.0 %shard_map.83 = (f32[10,32,128]{2,1,0:T(8,128)S(1)}, f32[10,32,128]{2,1,0:T(8,128)S(1)}, f32[10,32,128]{2,1,0:T(8,128)S(1)}, f32[10,32,128]{2,1,0:T(8,128)S(1)},...) custom-call(f32[3,12]{1,0:T(4,128)S(1)} %copy-done.6, ...), custom_call_target="tpu_custom_call" | custom-call | flops 1000000 | bytes 1000000 | tf_op jit(solution)/shard_map/pallas_call | solution.py:590
  44.8 14.0 %all_to_all.15.arrived_ref = f32[32,1,128]{2,1,0:T(1,128)S(1)} all-to-all(f32[32,1,128]{2,1,0:T(1,128)S(1)} %get-tuple-element.45), channel_id=1, replica_groups=mesh['gx'=8,'gy'=4] {'gx','gy'}, dimensions={0} | all-to-all | bytes 32768 | tf_op jit(solution)/shard_map/all_to_all | solution.py:559
  58.8 4.8 %shard_map.84 = (f32[10,16,512]{2,1,0:T(8,128)S(1)}, f32[10,32,640]{2,1,0:T(8,128)S(1)}, f32[10,32,640]{2,1,0:T(8,128)S(1)}, f32[10,32,640]{2,1,0:T(8,128)S(1)}, f32[32,1,128]{2,1,0:T(1,128)S(1)}) custom-call(f32[32,1,128]{2,1,0:T(1,128)S(1)} %all_to_all.15.arrived_ref, f32[10,32,512]{2,1,0:T(8,128)S(1)} %get-tuple-element.39.ext_ref.old_ref, ...), custom_call_target="tpu_custom_call" | custom-call | flops 1000000 | bytes 1000000 | tf_op jit(solution)/shard_map/pallas_call | solution.py:598
  63.6 8.8 %all_to_all.16.arrived_ref = f32[32,1,128]{2,1,0:T(1,128)S(1)} all-to-all(f32[32,1,128]{2,1,0:T(1,128)S(1)} %get-tuple-element.56), channel_id=1, replica_groups=mesh['gx'=8,'gy'=4] {'gx','gy'}, dimensions={0} | all-to-all | bytes 32768 | tf_op jit(solution)/shard_map/all_to_all | solution.py:559
  72.5 1.1 %shard_map.85 = f32[10,16,512]{2,1,0:T(8,128)} custom-call(f32[32,1,128]{2,1,0:T(1,128)S(1)} %all_to_all.16.arrived_ref, f32[10,16,512]{2,1,0:T(8,128)S(1)} %get-tuple-element.57.part_ref, f32[10,32,640]{2,1,0:T(8,128)S(1)} %get-tuple-element.58.q0_ref, f32[10,32,640]{2,1,0:T(8,128)S(1)} %get-tuple-element.59.q1_ref, f32[10,32,640]{2,1,0:T(8,128)S(1)} %get-tuple-element.60.q2_ref), custom_call_target="tpu_custom_call" | custom-call | flops 1000000 | bytes 1000000 | tf_op jit(solution)/shard_map/pallas_call | solution.py:602
  (7 shorter events, 0.0 us)
Async XLA Ops:
  0.6 9.0 %copy-start = (f32[10,16,512]{2,1,0:T(8,128)S(1)}, f32[10,16,512]{2,1,0:T(8,128)}, u32[]{:S(2)}) copy-start(f32[10,16,512]{2,1,0:T(8,128)} %head_ref.7) | copy-start | bytes 983044
  0.6 1.0 %copy-start.3 = (f32[13,2048]{1,0:T(8,128)S(1)}, f32[13,2048]{1,0:T(8,128)}, u32[]{:S(2)}) copy-start(f32[13,2048]{1,0:T(8,128)} %canopy_ref.1) | copy-start | bytes 319492
  2.3 15.5 %all-to-all-start = ((f32[32,8,128]{2,1,0:T(8,128)}), f32[32,8,128]{2,1,0:T(8,128)S(1)}, u32[]{:S(2)}, u32[]{:S(2)}) async-start(f32[32,8,128]{2,1,0:T(8,128)} %shard_map.77), calls=%async_computation | async-start | bytes 262144 | tf_op jit(solution)/shard_map/all_to_all | solution.py:559
  9.7 1.0 %copy-start.1 = (s32[10,16,512]{2,1,0:T(8,128)S(1)}, s32[10,16,512]{2,1,0:T(8,128)}, u32[]{:S(2)}) copy-start(s32[10,16,512]{2,1,0:T(8,128)} %soil_ref.7) | copy-start | bytes 983044
  10.6 7.2 %copy-start.2 = (s32[10,16,512]{2,1,0:T(8,128)S(1)}, s32[10,16,512]{2,1,0:T(8,128)}, u32[]{:S(2)}) copy-start(s32[10,16,512]{2,1,0:T(8,128)} %soil_ref.7) | copy-start | bytes 983044
  10.6 7.2 %copy-start.4 = (f32[4,16,512]{2,1,0:T(8,128)S(1)}, f32[4,16,512]{2,1,0:T(8,128)}, u32[]{:S(2)}) copy-start(f32[4,16,512]{2,1,0:T(8,128)} %forcing_ref.1) | copy-start | bytes 393220
  10.6 7.2 %copy-start.5 = (s32[16,512]{1,0:T(8,128)S(1)}, s32[16,512]{1,0:T(8,128)}, u32[]{:S(2)}) copy-start(s32[16,512]{1,0:T(8,128)} %slot_ref.1) | copy-start | bytes 98308
  10.7 7.2 %copy-start.6 = (f32[3,12]{1,0:T(4,128)S(1)}, f32[3,12]{1,0:T(4,128)}, u32[]{:S(2)}) copy-start(f32[3,12]{1,0:T(4,128)} %table_ref.5) | copy-start | bytes 436
  10.7 22.0 %collective-permute-start.4 = (f32[144,512]{1,0:T(8,128)S(1)}, f32[144,512]{1,0:T(8,128)S(1)}, u32[]{:S(2)}, u32[]{:S(2)}) collective-permute-start(f32[144,512]{1,0:T(8,128)S(1)} %get-tuple-element.37), channel_id=1, source_target_pairs={{0,4},{4,8},{8,12},{12,16},{16,20},{20,24},{24,28},{1,5},{5,9},{9,... | collective-permute-start | bytes 884744 | tf_op jit(solution)/shard_map/ppermute | solution.py:556
  14.6 18.2 %collective-permute-start.5 = (f32[144,512]{1,0:T(8,128)S(1)}, f32[144,512]{1,0:T(8,128)S(1)}, u32[]{:S(2)}, u32[]{:S(2)}) collective-permute-start(f32[144,512]{1,0:T(8,128)S(1)} %get-tuple-element.38), channel_id=1, source_target_pairs={{4,0},{8,4},{12,8},{16,12},{20,16},{24,20},{28,24},{5,1},{9,5},{13... | collective-permute-start | bytes 884744 | tf_op jit(solution)/shard_map/ppermute | solution.py:556
  22.7 3.4 %collective-permute-start = (f32[3,16,128]{2,1,0:T(8,128)S(1)}, f32[3,16,128]{2,1,0:T(8,128)S(1)}, u32[]{:S(2)}, u32[]{:S(2)}) collective-permute-start(f32[3,16,128]{2,1,0:T(8,128)S(1)} %get-tuple-element.33), channel_id=1, source_target_pairs={{0,1},{1,2},{2,3},{4,5},{5,6},{6,7},{8,9},{9,10},{10,11},{12,13},{... | collective-permute-start | bytes 73736 | tf_op jit(solution)/shard_map/ppermute | solution.py:556
  24.8 3.1 %collective-permute-start.1 = (f32[3,16,128]{2,1,0:T(8,128)S(1)}, f32[3,16,128]{2,1,0:T(8,128)S(1)}, u32[]{:S(2)}, u32[]{:S(2)}) collective-permute-start(f32[3,16,128]{2,1,0:T(8,128)S(1)} %get-tuple-element.34), channel_id=1, source_target_pairs={{1,0},{2,1},{3,2},{5,4},{6,5},{7,6},{9,8},{10,9},{11,10},{13,12},{... | collective-permute-start | bytes 73736 | tf_op jit(solution)/shard_map/ppermute | solution.py:556
  28.0 6.8 %collective-permute-start.2 = (f32[72,512]{1,0:T(8,128)S(1)}, f32[72,512]{1,0:T(8,128)S(1)}, u32[]{:S(2)}, u32[]{:S(2)}) collective-permute-start(f32[72,512]{1,0:T(8,128)S(1)} %get-tuple-element.35), channel_id=1, source_target_pairs={{0,4},{4,8},{8,12},{12,16},{16,20},{20,24},{24,28},{1,5},{5,9},{9,... | collective-permute-start | bytes 442376 | tf_op jit(solution)/shard_map/ppermute | solution.py:556
  31.4 7.4 %collective-permute-start.3 = (f32[72,512]{1,0:T(8,128)S(1)}, f32[72,512]{1,0:T(8,128)S(1)}, u32[]{:S(2)}, u32[]{:S(2)}) collective-permute-start(f32[72,512]{1,0:T(8,128)S(1)} %get-tuple-element.36), channel_id=1, source_target_pairs={{4,0},{8,4},{12,8},{16,12},{20,16},{24,20},{28,24},{5,1},{9,5},{13... | collective-permute-start | bytes 442376 | tf_op jit(solution)/shard_map/ppermute | solution.py:556

commit v7 on v6

--- a/solution.py
+++ b/solution.py
@@ -124,76 +124,79 @@
         return 0
 
     lax.fori_loop(0, owners // 2, unpack, 0, unroll=16)
-    tables = table_rows(table_ref, 8)
-
-    for at_x in range(0, rows, 8):
-
-        def column(j, _):
-            here = (slice(at_x, at_x + 8), pl.ds(pl.multiple_of(j * LANES, LANES), LANES))
-            slot = slot_ref[here]
-            land = slot >= 0
-            value = jnp.maximum(slot, 0)
-            lane = value & (LANES - 1)
-            tile = value >> 7
-
-            def pick(t, held):
-                match = tile == t
-                found = [lookup(tab_ref[t, m], lane) for m in range(pairs + 1)]
-                found.append(lookup(factor_ref[t], lane))
-                return tuple(jnp.where(match, new, old) for new, old in zip(found, held))
-
-            start = [jnp.full((8, LANES), 1, jnp.int32)] * (pairs + 1)
-            start.append(jnp.full((8, LANES), 1.0 / FIXED, f32))
-            *words, terms, factor = lax.fori_loop(0, owners // 2, pick, tuple(start), unroll=8)
-
-            def halves(word):
-                upper = lax.shift_right_logical(word, jnp.full((8, LANES), 16, jnp.int32))
-                return (word & 0xFFFF).astype(f32), upper.astype(f32)
-
-            leaf, bright = halves(terms)
-            exchange_coef = leaf * (4.0 / FIXED)
-            absorbed = bright * (1.0 / FIXED)
-            split = [halves(word) for word in words]
-            roots = [factor * split[k % pairs][k // pairs] for k in range(layers)]
-            uptake = []
-            for k in range(layers):
-                index = soil_ref[(k,) + here] + 1
-                steep = lookup(tables[1], index)
-                uptake.append(roots[k] * sigmoid(steep * head_ref[(k,) + here]))
-                if k == 0:
-                    ks_top = lookup(tables[0], index)
-            conductance = functools.reduce(jnp.add, uptake)
-            sunlight, air_temp, humidity, rainfall = (forcing_ref[(i,) + here] for i in range(4))
-            radiation = absorbed * sunlight + 0.3
-            square = air_temp * air_temp
-            excess = radiation - 0.3 * square * square - conductance * (0.5 - humidity)
-            slope = -1.2 * square * air_temp - exchange_coef - conductance
-            rise = -excess / slope
-            surface = air_temp + rise
-            vapour = 0.5 * jnp.exp(2.0 * rise)
-            square = surface * surface
-            excess = (
-                radiation
-                - 0.3 * square * square
-                - exchange_coef * rise
-                - conductance * (vapour - humidity)
-            )
-            slope = -1.2 * square * surface - exchange_coef - 2.0 * conductance * vapour
-            rise = rise - excess / slope
-            rate = 0.5 * jnp.exp(2.0 * rise) - humidity
-            infiltration = rainfall * ks_top / (rainfall + ks_top)
-            infiltration = jnp.where(land, infiltration, 0.0)
-            rate = jnp.where(land, rate, 0.0)
-            flux_ref[(0,) + here] = conductance * rate
-            flux_ref[(1,) + here] = infiltration
-            for k in range(layers):
-                value = -rate * uptake[k]
-                if k == 0:
-                    value = value + infiltration
-                source_ref[(k,) + here] = value
-            return 0
-
-        lax.fori_loop(0, cols // LANES, column, 0)
+    tables = table_rows(table_ref, rows)
+    shape = (rows, LANES)
+
+    def whole(block):
+        return jnp.concatenate([block] * (rows // 8), axis=0)
+
+    for at_y in range(0, cols, LANES):
+        here = (slice(0, rows), slice(at_y, at_y + LANES))
+        slot = slot_ref[here]
+        land = slot >= 0
+        value = jnp.maximum(slot, 0)
+        lane = value & (LANES - 1)
+        tile = value >> 7
+
+        def pick(t, held):
+            match = tile == t
+            found = [lookup(whole(tab_ref[t, m]), lane) for m in range(pairs + 1)]
+            found.append(lookup(whole(factor_ref[t]), lane))
+            return tuple(jnp.where(match, new, old) for new, old in zip(found, held))
+
+        held = tuple([jnp.full(shape, 1, jnp.int32)] * (pairs + 1) + [jnp.full(shape, 1.0 / FIXED, f32)])
+        if owners <= 32:
+            for t in range(owners // 2):
+                held = pick(t, held)
+        else:
+            held = lax.fori_loop(0, owners // 2, pick, held, unroll=8)
+        *words, terms, factor = held
+
+        def halves(word):
+            upper = lax.shift_right_logical(word, jnp.full(shape, 16, jnp.int32))
+            return (word & 0xFFFF).astype(f32), upper.astype(f32)
+
+        leaf, bright = halves(terms)
+        exchange_coef = leaf * (4.0 / FIXED)
+        absorbed = bright * (1.0 / FIXED)
+        split = [halves(word) for word in words]
+        uptake = []
+        for k in range(layers):
+            index = soil_ref[(k,) + here] + 1
+            steep = lookup(tables[1], index)
+            root = factor * split[k % pairs][k // pairs]
+            uptake.append(root * sigmoid(steep * head_ref[(k,) + here]))
+            if k == 0:
+                ks_top = lookup(tables[0], index)
+        conductance = functools.reduce(jnp.add, uptake)
+        sunlight, air_temp, humidity, rainfall = (forcing_ref[(i,) + here] for i in range(4))
+        radiation = absorbed * sunlight + 0.3
+        square = air_temp * air_temp
+        excess = radiation - 0.3 * square * square - conductance * (0.5 - humidity)
+        slope = -1.2 * square * air_temp - exchange_coef - conductance
+        rise = -excess / slope
+        surface = air_temp + rise
+        vapour = 0.5 * jnp.exp(2.0 * rise)
+        square = surface * surface
+        excess = (
+            radiation
+            - 0.3 * square * square
+            - exchange_coef * rise
+            - conductance * (vapour - humidity)
+        )
+        slope = -1.2 * square * surface - exchange_coef - 2.0 * conductance * vapour
+        rise = rise - excess / slope
+        rate = 0.5 * jnp.exp(2.0 * rise) - humidity
+        infiltration = rainfall * ks_top / (rainfall + ks_top)
+        infiltration = jnp.where(land, infiltration, 0.0)
+        rate = jnp.where(land, rate, 0.0)
+        flux_ref[(0,) + here] = conductance * rate
+        flux_ref[(1,) + here] = infiltration
+        for k in range(layers):
+            value = -rate * uptake[k]
+            if k == 0:
+                value = value + infiltration
+            source_ref[(k,) + here] = value
 
 
 def strips(planes, shift_from):
@@ -376,14 +379,14 @@
     block = jnp.sum(jnp.concatenate(lines, axis=0), axis=1, keepdims=True)
     line = lax.broadcasted_iota(jnp.int32, (16, LANES), 0)
     flat = jnp.sum(jnp.where(lane_iota((16, LANES)) == line, block, 0.0), axis=0, keepdims=True)
-    for d in range(out_ref.shape[0]):
-        out_ref[d] = flat
+    out_ref[0] = flat
 
 
 def solve(gram_ref):
-    total = gram_ref[0]
-    for d in range(1, gram_ref.shape[0]):
-        total = total + gram_ref[d]
+    terms = [gram_ref[d] for d in range(gram_ref.shape[0])]
+    while len(terms) > 1:
+        terms = [functools.reduce(jnp.add, terms[i : i + 2]) for i in range(0, len(terms), 2)]
+    total = terms[0]
     line = lax.broadcasted_iota(jnp.int32, (16, LANES), 0)
     spread = jnp.broadcast_to(total, (16, LANES))
     column = jnp.sum(jnp.where(lane_iota((16, LANES)) == line, spread, 0.0), axis=1, keepdims=True)
@@ -515,17 +518,30 @@
     layers = old_ref.shape[0]
     rows, cols = part_ref.shape[1:]
     x = solve(arrived_ref)
-    old_of, ks_of = joined(old_ref, old_side), joined(ks_ref, ks_side)
-    steep_of, cap_of = joined(steep_ref, steep_side), joined(cap_ref, cap_side)
+    near = lax.broadcasted_iota(jnp.int32, (HALO, cols + LANES), 0) < HALO // 2
+
+    def folded(of):
+        def get(k):
+            value = of(k)
+            ends = jnp.where(near, value[rows : rows + HALO], value[rows + HALO :])
+            return jnp.concatenate([value[:rows], ends], axis=0)
+
+        return get
+
+    old_of, ks_of = folded(joined(old_ref, old_side)), folded(joined(ks_ref, ks_side))
+    steep_of, cap_of = folded(joined(steep_ref, steep_side)), folded(joined(cap_ref, cap_side))
+    base_of, *qs = (folded(lambda k, ref=ref: ref[k]) for ref in (base_ref, q0_ref, q1_ref, q2_ref))
     for k in range(layers):
-        head = old_of(k) - x[0] * q0_ref[k] - x[1] * q1_ref[k] - x[2] * q2_ref[k]
+        head = old_of(k)
+        for value, q_of in zip(x, qs):
+            head = head - value * q_of(k)
         cond, deriv, store, water = pointwise(head, ks_of(k), steep_of(k), cap_of(k))
         ext_ref[k] = head
         part_ref[k] = head[:rows, :cols]
         cond_ref[k] = cond
         deriv_ref[k] = deriv
         store_ref[k] = store
-        gain_ref[k] = water - base_ref[k]
+        gain_ref[k] = water - base_of(k)
     linearize(
         layers, *((lambda k, ref=ref: ref[k]) for ref in (ext_ref, cond_ref, deriv_ref, store_ref, gain_ref)),
         (ks_of(0) > 0.0).astype(f32), coefs, p0_ref, (rows, cols),
@@ -547,7 +563,7 @@
     devices = lax.axis_size("gx") * lax.axis_size("gy")
     tall, wide = rows + 2 * HALO, cols + LANES
     own, ext = ((layers, rows, cols), f32), ((layers, tall, wide), f32)
-    gram_block = ((devices, 1, LANES), f32)
+    gram_block = ((1, 1, LANES), f32)
 
     def exchange(to_lower, to_upper, axis):
         size = lax.axis_size(axis)
@@ -594,11 +610,14 @@
         scratch=held_side * 4 + held * 7,
         in_specs=[smem] + [vmem] * 11,
     )(soil_table, source, slo, shi, ylo, yhi, old, ks, cond, deriv, store, water)
-    sums = spread(gram, both)
+    sums = lax.all_gather(gram, both, axis=0, tiled=True)
     part, q0, q1, q2, gram = call(
-        second_kernel, [own] + [ext] * 3 + [gram_block], 13, scratch=held * 12
+        second_kernel,
+        [own] + [((layers, rows + HALO, wide), f32)] * 3 + [gram_block],
+        13,
+        scratch=[pltpu.VMEM((layers, rows + HALO, wide), f32)] * 12,
     )(sums, old, ks, steep, cap, old_s, ks_s, steep_s, cap_s, base, p0, p1, p2)
-    sums = spread(gram, both)
+    sums = lax.all_gather(gram, both, axis=0, tiled=True)
     (head,) = call(last_kernel, [own], 5)(sums, part, q0, q1, q2)
     return head, flux
 

time: 73.9 us -> 126 us (1.71)
  blocking collectives: 22.8 us -> 76.8 us
  Pallas kernels: 19.6 us -> 18 us
    all_gather x0 -> x2, blocking collectives: none -> 76.8 us  [shards(): sums = lax.all_gather(gram, both, axis=0, tiled=True)]
    all_to_all x2 -> x0, blocking collectives: 22.8 us -> none  [spread(): return lax.all_to_all(x, axes, split_axis=0, concat_axis=0, tiled=True)]
  transfers between devices with their start and end apart: 7 -> 7, of which waited for: 3 -> 3; matrix products, arithmetic and copies ran while one was open for 0% -> 0% of each run, Pallas kernels for 9% -> 5%
where the time goes in v7:
time: 126 us
  blocking collectives  76.8 us (61%)
  starting transfers between devices  20.6 us (16%)
  Pallas kernels  18 us (14%)
  waiting for transfers between devices  7.85 us (6%)
  local copies, waits for them, and re-layouts  1.93 us (2%)
    all_gather x2, blocking collectives, shards(): sums = lax.all_gather(gram, both, axis=0, tiled=True)  76.8 us
    ppermute x3, starting transfers between devices, exchange(): lax.ppermute(to_upper, axis, up)  9.39 us
    all_to_all x1, starting transfers between devices, spread(): return lax.all_to_all(x, axes, split_axis=0, concat_axis=0, tiled=True)  7.3 us
    pallas_call x1, Pallas kernels, shards(): call(first_kernel, [side_block] * 4 + [ext] * 4 + [gram_block], 12, scrat...  6.38 us
    ppermute x3, waiting for transfers between devices, exchange(): lax.ppermute(to_lower, axis, down)  5.83 us
    pallas_call x1, Pallas kernels, shards(): call(second_kernel, [own] + [((layers, rows + HALO, wide), f32)] * 3 + [g...  4.03 us
    ppermute x3, starting transfers between devices, exchange(): lax.ppermute(to_lower, axis, down)  3.88 us
    pallas_call x1, Pallas kernels, shards(): call(source_kernel, [own, ((2, rows, cols), f32)], 6, scratch=[pltpu.VMEM...  3.53 us
  transfers between devices with their start and end apart: 7, of which 3 were waited for; matrix products, arithmetic and copies ran while one was open for 0% of the time, Pallas kernels for 5%

profile of v7, /device:TPU:0, one launch (start us, length us, event | category | flops | bytes accessed | tf_op | source)
XLA Modules:
  0.0 125.9 jit_solution(2832588504842244136)
XLA Ops:
  0.6 0.0 copy-start
  0.6 0.0 copy-start.3
  0.6 0.9 copy-done.3
  1.6 0.8 shard_map.77
  2.3 7.3 %all-to-all-start = ((f32[32,8,128]{2,1,0:T(8,128)}), f32[32,8,128]{2,1,0:T(8,128)S(1)}, u32[]{:S(2)}, u32[]{:S(2)}) async-start(f32[32,8,128]{2,1,0:T(8,128)} %shard_map.77), calls=%async_computation | async-start | bytes 262144 | tf_op jit(solution)/shard_map/all_to_all | solution.py:575
  9.7 0.0 copy-done
  9.7 0.0 copy-start.1
  9.7 1.0 copy-done.1
  10.6 0.1 shard_map.81
  10.7 0.0 copy-start.6
  10.7 3.8 %collective-permute-start.4 = (f32[144,512]{1,0:T(8,128)S(1)}, f32[144,512]{1,0:T(8,128)S(1)}, u32[]{:S(2)}, u32[]{:S(2)}) collective-permute-start(f32[144,512]{1,0:T(8,128)S(1)} %get-tuple-element.37), channel_id=1, source_target_pairs={{0,4},{4,8},{8,12},{12,16},{16,20},{20,24},{24,28},{1,5},{5,9},{9,... | collective-permute-start | bytes 884744 | tf_op jit(solution)/shard_map/ppermute | solution.py:572
  14.6 1.3 %collective-permute-start.5 = (f32[144,512]{1,0:T(8,128)S(1)}, f32[144,512]{1,0:T(8,128)S(1)}, u32[]{:S(2)}, u32[]{:S(2)}) collective-permute-start(f32[144,512]{1,0:T(8,128)S(1)} %get-tuple-element.38), channel_id=1, source_target_pairs={{4,0},{8,4},{12,8},{16,12},{20,16},{24,20},{28,24},{5,1},{9,5},{13... | collective-permute-start | bytes 884744 | tf_op jit(solution)/shard_map/ppermute | solution.py:572
  15.9 2.0 %all-to-all-done.arrived_ref = f32[32,8,128]{2,1,0:T(8,128)S(1)} async-done(((f32[32,8,128]{2,1,0:T(8,128)}), f32[32,8,128]{2,1,0:T(8,128)S(1)}, u32[]{:S(2)}, u32[]{:S(2)}) %all-to-all-start) | async-done | bytes 131104 | tf_op jit(solution)/shard_map/all_to_all | solution.py:575
  17.9 0.0 copy-done.4
  17.9 3.5 %shard_map.78 = (f32[10,16,512]{2,1,0:T(8,128)S(1)}, f32[2,16,512]{2,1,0:T(8,128)}) custom-call(f32[3,12]{1,0:T(4,128)S(1)} %copy-done.6, f32[32,8,128]{2,1,0:T(8,128)S(1)} %all-to-all-done.arrived_ref, f32[10,16,512]{2,1,0:T(8,128)S(1)} %copy-done, s32[10,16,512]{2,1,0:T(8,128)S(1)} %copy-done.2, f32[4,16,512]{2,1,0:T(8,128)S(1)} %copy-done.4, ...), custom_call_target="tpu_custom_call" | custom-call | flops 1000000 | bytes 1000000 | tf_op jit(solution)/shard_map/pallas_call | solution.py:585
  21.4 0.2 shard_map.79
  21.6 2.1 %collective-permute-start = (f32[3,16,128]{2,1,0:T(8,128)S(1)}, f32[3,16,128]{2,1,0:T(8,128)S(1)}, u32[]{:S(2)}, u32[]{:S(2)}) collective-permute-start(f32[3,16,128]{2,1,0:T(8,128)S(1)} %get-tuple-element.33), channel_id=1, source_target_pairs={{0,1},{1,2},{2,3},{4,5},{5,6},{6,7},{8,9},{9,10},{10,11},{12,13},{... | collective-permute-start | bytes 73736 | tf_op jit(solution)/shard_map/ppermute | solution.py:572
  23.7 1.3 %collective-permute-start.1 = (f32[3,16,128]{2,1,0:T(8,128)S(1)}, f32[3,16,128]{2,1,0:T(8,128)S(1)}, u32[]{:S(2)}, u32[]{:S(2)}) collective-permute-start(f32[3,16,128]{2,1,0:T(8,128)S(1)} %get-tuple-element.34), channel_id=1, source_target_pairs={{1,0},{2,1},{3,2},{5,4},{6,5},{7,6},{9,8},{10,9},{11,10},{13,12},{... | collective-permute-start | bytes 73736 | tf_op jit(solution)/shard_map/ppermute | solution.py:572
  25.0 0.0 collective-permute-done.ylo_ref
  25.1 1.8 %collective-permute-done.1.yhi_ref = f32[3,16,128]{2,1,0:T(8,128)S(1)} collective-permute-done((f32[3,16,128]{2,1,0:T(8,128)S(1)}, f32[3,16,128]{2,1,0:T(8,128)S(1)}, u32[]{:S(2)}, u32[]{:S(2)}) %collective-permute-start.1) | collective-permute-done | bytes 24608 | tf_op jit(solution)/shard_map/ppermute | solution.py:572
  26.9 3.4 %collective-permute-start.2 = (f32[72,512]{1,0:T(8,128)S(1)}, f32[72,512]{1,0:T(8,128)S(1)}, u32[]{:S(2)}, u32[]{:S(2)}) collective-permute-start(f32[72,512]{1,0:T(8,128)S(1)} %get-tuple-element.35), channel_id=1, source_target_pairs={{0,4},{4,8},{8,12},{12,16},{16,20},{20,24},{24,28},{1,5},{5,9},{9,... | collective-permute-start | bytes 442376 | tf_op jit(solution)/shard_map/ppermute | solution.py:572
  30.3 1.3 %collective-permute-start.3 = (f32[72,512]{1,0:T(8,128)S(1)}, f32[72,512]{1,0:T(8,128)S(1)}, u32[]{:S(2)}, u32[]{:S(2)}) collective-permute-start(f32[72,512]{1,0:T(8,128)S(1)} %get-tuple-element.36), channel_id=1, source_target_pairs={{4,0},{8,4},{12,8},{16,12},{20,16},{24,20},{28,24},{5,1},{9,5},{13... | collective-permute-start | bytes 442376 | tf_op jit(solution)/shard_map/ppermute | solution.py:572
  31.6 0.0 collective-permute-done.4.lo_ref
  31.6 0.0 collective-permute-done.5.hi_ref
  31.6 2.0 %shard_map.82 = (f32[10,32,512]{2,1,0:T(8,128)S(1)}, f32[10,32,512]{2,1,0:T(8,128)S(1)}, f32[10,32,512]{2,1,0:T(8,128)S(1)}, f32[10,32,512]{2,1,0:T(8,128)S(1)},...) custom-call(f32[3,12]{1,0:T(4,128)S(1)} %copy-done.6, ...), custom_call_target="tpu_custom_call" | custom-call | flops 1000000 | bytes 1000000 | tf_op jit(solution)/shard_map/pallas_call | solution.py:602
  33.6 0.0 collective-permute-done.2.slo_ref
  33.6 4.1 %collective-permute-done.3.shi_ref = f32[72,512]{1,0:T(8,128)S(1)} collective-permute-done((f32[72,512]{1,0:T(8,128)S(1)}, f32[72,512]{1,0:T(8,128)S(1)}, u32[]{:S(2)}, u32[]{:S(2)}) %collective-permute-start.3) | collective-permute-done | bytes 147488 | tf_op jit(solution)/shard_map/ppermute | solution.py:572
  37.7 6.4 %shard_map.83 = (f32[10,32,128]{2,1,0:T(8,128)S(1)}, f32[10,32,128]{2,1,0:T(8,128)S(1)}, f32[10,32,128]{2,1,0:T(8,128)S(1)}, f32[10,32,128]{2,1,0:T(8,128)S(1)},...) custom-call(f32[3,12]{1,0:T(4,128)S(1)} %copy-done.6, ...), custom_call_target="tpu_custom_call" | custom-call | flops 1000000 | bytes 1000000 | tf_op jit(solution)/shard_map/pallas_call | solution.py:606
  44.1 40.4 %all_gather.6.arrived_ref = f32[32,1,128]{2,1,0:T(1,128)S(1)} all-gather(f32[1,1,128]{2,1,0:T(1,128)S(1)} %get-tuple-element.45), channel_id=1, replica_groups=mesh['gx'=8,'gy'=4] {'gx','gy'}, dimensions={0}, use_global_device_ids=true | all-gather | bytes 16896 | tf_op jit(solution)/shard_map/all_gather | solution.py:613
  84.5 4.0 %shard_map.84 = (f32[10,16,512]{2,1,0:T(8,128)S(1)}, f32[10,24,640]{2,1,0:T(8,128)S(1)}, f32[10,24,640]{2,1,0:T(8,128)S(1)}, f32[10,24,640]{2,1,0:T(8,128)S(1)}, f32[1,1,128]{2,1,0:T(1,128)S(1)}) custom-call(f32[32,1,128]{2,1,0:T(1,128)S(1)} %all_gather.6.arrived_ref, f32[10,32,512]{2,1,0:T(8,128)S(1)} %get-tuple-element.39.ext_ref.old_ref, ...), custom_call_target="tpu_custom_call" | custom-call | flops 1000000 | bytes 1000000 | tf_op jit(solution)/shard_map/pallas_call | solution.py:614
  88.5 36.4 %all_gather.7.arrived_ref = f32[32,1,128]{2,1,0:T(1,128)S(1)} all-gather(f32[1,1,128]{2,1,0:T(1,128)S(1)} %get-tuple-element.56), channel_id=1, replica_groups=mesh['gx'=8,'gy'=4] {'gx','gy'}, dimensions={0}, use_global_device_ids=true | all-gather | bytes 16896 | tf_op jit(solution)/shard_map/all_gather | solution.py:620
  124.9 1.0 shard_map.85
  (7 shorter events, 0.0 us)
Async XLA Ops:
  0.6 9.0 %copy-start = (f32[10,16,512]{2,1,0:T(8,128)S(1)}, f32[10,16,512]{2,1,0:T(8,128)}, u32[]{:S(2)}) copy-start(f32[10,16,512]{2,1,0:T(8,128)} %head_ref.7) | copy-start | bytes 983044
  0.6 1.0 copy-start.3
  2.3 15.5 %all-to-all-start = ((f32[32,8,128]{2,1,0:T(8,128)}), f32[32,8,128]{2,1,0:T(8,128)S(1)}, u32[]{:S(2)}, u32[]{:S(2)}) async-start(f32[32,8,128]{2,1,0:T(8,128)} %shard_map.77), calls=%async_computation | async-start | bytes 262144 | tf_op jit(solution)/shard_map/all_to_all | solution.py:575
  9.7 1.0 copy-start.1
  10.6 7.2 %copy-start.2 = (s32[10,16,512]{2,1,0:T(8,128)S(1)}, s32[10,16,512]{2,1,0:T(8,128)}, u32[]{:S(2)}) copy-start(s32[10,16,512]{2,1,0:T(8,128)} %soil_ref.7) | copy-start | bytes 983044
  10.6 7.2 %copy-start.4 = (f32[4,16,512]{2,1,0:T(8,128)S(1)}, f32[4,16,512]{2,1,0:T(8,128)}, u32[]{:S(2)}) copy-start(f32[4,16,512]{2,1,0:T(8,128)} %forcing_ref.1) | copy-start | bytes 393220
  10.6 7.2 %copy-start.5 = (s32[16,512]{1,0:T(8,128)S(1)}, s32[16,512]{1,0:T(8,128)}, u32[]{:S(2)}) copy-start(s32[16,512]{1,0:T(8,128)} %slot_ref.1) | copy-start | bytes 98308
  10.7 7.2 %copy-start.6 = (f32[3,12]{1,0:T(4,128)S(1)}, f32[3,12]{1,0:T(4,128)}, u32[]{:S(2)}) copy-start(f32[3,12]{1,0:T(4,128)} %table_ref.5) | copy-start | bytes 436
  10.7 20.9 %collective-permute-start.4 = (f32[144,512]{1,0:T(8,128)S(1)}, f32[144,512]{1,0:T(8,128)S(1)}, u32[]{:S(2)}, u32[]{:S(2)}) collective-permute-start(f32[144,512]{1,0:T(8,128)S(1)} %get-tuple-element.37), channel_id=1, source_target_pairs={{0,4},{4,8},{8,12},{12,16},{16,20},{20,24},{24,28},{1,5},{5,9},{9,... | collective-permute-start | bytes 884744 | tf_op jit(solution)/shard_map/ppermute | solution.py:572
  14.6 17.1 %collective-permute-start.5 = (f32[144,512]{1,0:T(8,128)S(1)}, f32[144,512]{1,0:T(8,128)S(1)}, u32[]{:S(2)}, u32[]{:S(2)}) collective-permute-start(f32[144,512]{1,0:T(8,128)S(1)} %get-tuple-element.38), channel_id=1, source_target_pairs={{4,0},{8,4},{12,8},{16,12},{20,16},{24,20},{28,24},{5,1},{9,5},{13... | collective-permute-start | bytes 884744 | tf_op jit(solution)/shard_map/ppermute | solution.py:572
  21.6 3.4 %collective-permute-start = (f32[3,16,128]{2,1,0:T(8,128)S(1)}, f32[3,16,128]{2,1,0:T(8,128)S(1)}, u32[]{:S(2)}, u32[]{:S(2)}) collective-permute-start(f32[3,16,128]{2,1,0:T(8,128)S(1)} %get-tuple-element.33), channel_id=1, source_target_pairs={{0,1},{1,2},{2,3},{4,5},{5,6},{6,7},{8,9},{9,10},{10,11},{12,13},{... | collective-permute-start | bytes 73736 | tf_op jit(solution)/shard_map/ppermute | solution.py:572
  23.7 3.1 %collective-permute-start.1 = (f32[3,16,128]{2,1,0:T(8,128)S(1)}, f32[3,16,128]{2,1,0:T(8,128)S(1)}, u32[]{:S(2)}, u32[]{:S(2)}) collective-permute-start(f32[3,16,128]{2,1,0:T(8,128)S(1)} %get-tuple-element.34), channel_id=1, source_target_pairs={{1,0},{2,1},{3,2},{5,4},{6,5},{7,6},{9,8},{10,9},{11,10},{13,12},{... | collective-permute-start | bytes 73736 | tf_op jit(solution)/shard_map/ppermute | solution.py:572
  26.9 6.8 %collective-permute-start.2 = (f32[72,512]{1,0:T(8,128)S(1)}, f32[72,512]{1,0:T(8,128)S(1)}, u32[]{:S(2)}, u32[]{:S(2)}) collective-permute-start(f32[72,512]{1,0:T(8,128)S(1)} %get-tuple-element.35), channel_id=1, source_target_pairs={{0,4},{4,8},{8,12},{12,16},{16,20},{20,24},{24,28},{1,5},{5,9},{9,... | collective-permute-start | bytes 442376 | tf_op jit(solution)/shard_map/ppermute | solution.py:572
  30.3 7.4 %collective-permute-start.3 = (f32[72,512]{1,0:T(8,128)S(1)}, f32[72,512]{1,0:T(8,128)S(1)}, u32[]{:S(2)}, u32[]{:S(2)}) collective-permute-start(f32[72,512]{1,0:T(8,128)S(1)} %get-tuple-element.36), channel_id=1, source_target_pairs={{4,0},{8,4},{12,8},{16,12},{20,16},{24,20},{28,24},{5,1},{9,5},{13... | collective-permute-start | bytes 442376 | tf_op jit(solution)/shard_map/ppermute | solution.py:572

commit v8 on v7

--- a/solution.py
+++ b/solution.py
@@ -27,14 +27,14 @@
 smem = pl.BlockSpec(memory_space=pltpu.SMEM)
 
 
-def call(body, outs, n_in, scratch=(), in_specs=None, flops=1000000):
+def call(body, outs, n_in, scratch=(), in_specs=None, flops=1000000, grant=VMEM_LIMIT):
     return pl.pallas_call(
         body,
         out_shape=[jax.ShapeDtypeStruct(s, d) for s, d in outs],
         in_specs=in_specs or [vmem] * n_in,
         out_specs=[vmem] * len(outs),
         scratch_shapes=list(scratch),
-        compiler_params=pltpu.CompilerParams(vmem_limit_bytes=VMEM_LIMIT),
+        compiler_params=pltpu.CompilerParams(vmem_limit_bytes=grant),
         cost_estimate=pl.CostEstimate(flops=flops, bytes_accessed=1000000, transcendentals=0),
     )
 
@@ -43,17 +43,17 @@
     return lax.broadcasted_iota(jnp.int32, shape, len(shape) - 1)
 
 
-def edge_kernel(head_ref, soil_ref, down_ref, up_ref):
-    layers, rows, _ = head_ref.shape
-    for out_ref, part in ((down_ref, slice(0, STATE_DEPTH)), (up_ref, slice(rows - STATE_DEPTH, rows))):
-        for k in range(layers):
-            out_ref[STATE_DEPTH * k : STATE_DEPTH * (k + 1)] = head_ref[k][part]
-        for k in range(layers):
-            at = STATE_DEPTH * (layers + k)
-            out_ref[at : at + STATE_DEPTH] = (soil_ref[k] + 1).astype(f32)[part]
-
-
-def pack_kernel(canopy_ref, send_ref):
+def pack_kernel(
+    canopy_hbm, head_hbm, soil_hbm, send_ref, down_ref, up_ref, canopy_ref, head_ref, soil_ref, sems
+):
+    copies = [
+        pltpu.make_async_copy(canopy_hbm, canopy_ref, sems.at[0]),
+        pltpu.make_async_copy(head_hbm, head_ref, sems.at[1]),
+        pltpu.make_async_copy(soil_hbm, soil_ref, sems.at[2]),
+    ]
+    for copy in copies:
+        copy.start()
+    copies[0].wait()
     rows = canopy_ref.shape[0]
     low = lane_iota((8, LANES)) < SLOT
     for t in range(canopy_ref.shape[1] // LANES):
@@ -62,6 +62,15 @@
         rest = jnp.concatenate([canopy_ref[8:rows, here], jnp.zeros((16 - rows, LANES), f32)], axis=0)
         send_ref[2 * t] = jnp.where(low, first, pltpu.roll(rest, SLOT, 1))
         send_ref[2 * t + 1] = jnp.where(low, pltpu.roll(first, SLOT, 1), rest)
+    layers, rows, _ = head_ref.shape
+    copies[1].wait()
+    copies[2].wait()
+    for out_ref, part in ((down_ref, slice(0, STATE_DEPTH)), (up_ref, slice(rows - STATE_DEPTH, rows))):
+        for k in range(layers):
+            out_ref[STATE_DEPTH * k : STATE_DEPTH * (k + 1)] = head_ref[k][part]
+        for k in range(layers):
+            at = STATE_DEPTH * (layers + k)
+            out_ref[at : at + STATE_DEPTH] = (soil_ref[k] + 1).astype(f32)[part]
 
 
 def table_rows(table_ref, rows):
@@ -379,7 +388,8 @@
     block = jnp.sum(jnp.concatenate(lines, axis=0), axis=1, keepdims=True)
     line = lax.broadcasted_iota(jnp.int32, (16, LANES), 0)
     flat = jnp.sum(jnp.where(lane_iota((16, LANES)) == line, block, 0.0), axis=0, keepdims=True)
-    out_ref[0] = flat
+    for d in range(out_ref.shape[0]):
+        out_ref[d] = flat
 
 
 def solve(gram_ref):
@@ -563,7 +573,7 @@
     devices = lax.axis_size("gx") * lax.axis_size("gy")
     tall, wide = rows + 2 * HALO, cols + LANES
     own, ext = ((layers, rows, cols), f32), ((layers, tall, wide), f32)
-    gram_block = ((1, 1, LANES), f32)
+    gram_block = ((devices, 1, LANES), f32)
 
     def exchange(to_lower, to_upper, axis):
         size = lax.axis_size(axis)
@@ -574,13 +584,23 @@
     def spread(x, axes):
         return lax.all_to_all(x, axes, split_axis=0, concat_axis=0, tiled=True)
 
-    (send,) = call(pack_kernel, [((devices, 8, LANES), f32)], 1)(canopy)
-    arrived = spread(send, both)
-
     def edge(count):
         return (-(-count // 8) * 8, cols), f32
 
-    down, up = call(edge_kernel, [edge(2 * STATE_DEPTH * layers)] * 2, 2)(head_old, soil_type)
+    send, down, up = call(
+        pack_kernel,
+        [((devices, 8, LANES), f32)] + [edge(2 * STATE_DEPTH * layers)] * 2,
+        3,
+        scratch=[
+            pltpu.VMEM(canopy.shape, f32),
+            pltpu.VMEM(head_old.shape, f32),
+            pltpu.VMEM(soil_type.shape, jnp.int32),
+            pltpu.SemaphoreType.DMA((3,)),
+        ],
+        in_specs=[pl.BlockSpec(memory_space=pl.ANY)] * 3,
+        grant=63400000,
+    )(canopy, head_old, soil_type)
+    arrived = spread(send, both)
     lo, hi = exchange(down, up, "gx")
     source, flux = call(
         source_kernel,
@@ -610,14 +630,14 @@
         scratch=held_side * 4 + held * 7,
         in_specs=[smem] + [vmem] * 11,
     )(soil_table, source, slo, shi, ylo, yhi, old, ks, cond, deriv, store, water)
-    sums = lax.all_gather(gram, both, axis=0, tiled=True)
+    sums = spread(gram, both)
     part, q0, q1, q2, gram = call(
         second_kernel,
         [own] + [((layers, rows + HALO, wide), f32)] * 3 + [gram_block],
         13,
         scratch=[pltpu.VMEM((layers, rows + HALO, wide), f32)] * 12,
     )(sums, old, ks, steep, cap, old_s, ks_s, steep_s, cap_s, base, p0, p1, p2)
-    sums = lax.all_gather(gram, both, axis=0, tiled=True)
+    sums = spread(gram, both)
     (head,) = call(last_kernel, [own], 5)(sums, part, q0, q1, q2)
     return head, flux
 

time: 126 us -> 71.7 us (0.57)
  blocking collectives: 76.8 us -> 22.5 us
  local copies, waits for them, and re-layouts: 1.93 us -> 0.03 us
  Pallas kernels: 18 us -> 19.4 us
    all_gather x2 -> x0, blocking collectives: 76.8 us -> none  [shards(): sums = lax.all_gather(gram, both, axis=0, tiled=True)]
    all_to_all x0 -> x2, blocking collectives: none -> 22.5 us  [spread(): return lax.all_to_all(x, axes, split_axis=0, concat_axis=0, tiled=True)]
    unnamed x14 -> x10, local copies, waits for them, and re-layouts: 1.93 us -> 0.03 us
  transfers between devices with their start and end apart: 7 -> 7, of which waited for: 3 -> 3; matrix products, arithmetic and copies ran while one was open for 0% -> 0% of each run, Pallas kernels for 5% -> 8%
where the time goes in v8:
time: 71.7 us; the launch traced here: 71.3 us
  blocking collectives  22.5 us (31%)
  starting transfers between devices  19.7 us (27%)
  Pallas kernels  19.4 us (27%)
  waiting for transfers between devices  8.85 us (12%)
  between operations  0.81 us (1%)
    all_to_all x2, blocking collectives, spread(): return lax.all_to_all(x, axes, split_axis=0, concat_axis=0, tiled=True)  22.5 us
    ppermute x3, starting transfers between devices, exchange(): lax.ppermute(to_upper, axis, up)  8.56 us
    all_to_all x1, starting transfers between devices, spread(): return lax.all_to_all(x, axes, split_axis=0, concat_axis=0, tiled=True)  7.3 us
    pallas_call x1, Pallas kernels, shards(): call(first_kernel, [side_block] * 4 + [ext] * 4 + [gram_block], 12, scrat...  6.32 us
    ppermute x3, waiting for transfers between devices, exchange(): lax.ppermute(to_lower, axis, down)  5.63 us
    pallas_call x1, Pallas kernels, shards(): call(second_kernel, [own] + [((layers, rows + HALO, wide), f32)] * 3 + [g...  4.16 us
    ppermute x3, starting transfers between devices, exchange(): lax.ppermute(to_lower, axis, down)  3.88 us
    pallas_call x1, Pallas kernels, shards(): call(source_kernel, [own, ((2, rows, cols), f32)], 6, scratch=[pltpu.VMEM...  3.55 us
  transfers between devices with their start and end apart: 7, of which 3 were waited for; matrix products, arithmetic and copies ran while one was open for 0% of the time, Pallas kernels for 8%

profile of v8, /device:TPU:0, one launch (start us, length us, event | category | flops | bytes accessed | tf_op | source)
XLA Modules:
  0.0 71.3 jit_solution(11963490012486725621)
XLA Ops:
  0.6 0.0 copy-start
  0.6 0.0 copy-start.1
  0.6 2.1 %shard_map.77 = (f32[32,8,128]{2,1,0:T(8,128)}, f32[144,512]{1,0:T(8,128)}, f32[144,512]{1,0:T(8,128)}) custom-call(f32[13,2048]{1,0:T(8,128)} %canopy_hbm.1, f32[10,16,512]{2,1,0:T(8,128)} %head_ref.5, s32[10,16,512]{2,1,0:T(8,128)} %soil_ref.5), custom_call_target="tpu_custom_call" | custom-call | flops 1000000 | bytes 1000000 | tf_op jit(solution)/shard_map/pallas_call | solution.py:590
  2.7 0.0 copy-start.2
  2.8 0.0 copy-start.3
  2.8 7.3 %all-to-all-start = ((f32[32,8,128]{2,1,0:T(8,128)}), f32[32,8,128]{2,1,0:T(8,128)S(1)}, u32[]{:S(2)}, u32[]{:S(2)}) async-start(f32[32,8,128]{2,1,0:T(8,128)} %get-tuple-element.33), calls=%async_computation | async-start | bytes 262144 | tf_op jit(solution)/shard_map/all_to_all | solution.py:585
  10.1 0.0 copy-start.4
  10.1 3.7 %collective-permute-start.4 = (f32[144,512]{1,0:T(8,128)}, f32[144,512]{1,0:T(8,128)S(1)}, u32[]{:S(2)}, u32[]{:S(2)}) collective-permute-start(f32[144,512]{1,0:T(8,128)} %get-tuple-element.39), channel_id=1, source_target_pairs={{0,4},{4,8},{8,12},{12,16},{16,20},{20,24},{24,28},{1,5},{5,9},{9,... | collective-permute-start | bytes 884744 | tf_op jit(solution)/shard_map/ppermute | solution.py:582
  13.8 1.3 %collective-permute-start.5 = (f32[144,512]{1,0:T(8,128)}, f32[144,512]{1,0:T(8,128)S(1)}, u32[]{:S(2)}, u32[]{:S(2)}) collective-permute-start(f32[144,512]{1,0:T(8,128)} %get-tuple-element.40), channel_id=1, source_target_pairs={{4,0},{8,4},{12,8},{16,12},{20,16},{24,20},{28,24},{5,1},{9,5},{13... | collective-permute-start | bytes 884744 | tf_op jit(solution)/shard_map/ppermute | solution.py:582
  15.1 3.2 %all-to-all-done.arrived_ref = f32[32,8,128]{2,1,0:T(8,128)S(1)} async-done(((f32[32,8,128]{2,1,0:T(8,128)}), f32[32,8,128]{2,1,0:T(8,128)S(1)}, u32[]{:S(2)}, u32[]{:S(2)}) %all-to-all-start) | async-done | bytes 131104 | tf_op jit(solution)/shard_map/all_to_all | solution.py:585
  18.3 0.0 copy-done
  18.3 0.0 copy-done.1
  18.3 0.0 copy-done.2
  18.3 0.0 copy-done.3
  18.3 3.5 %shard_map.78 = (f32[10,16,512]{2,1,0:T(8,128)S(1)}, f32[2,16,512]{2,1,0:T(8,128)}) custom-call(f32[3,12]{1,0:T(4,128)S(1)} %copy-done.4, f32[32,8,128]{2,1,0:T(8,128)S(1)} %all-to-all-done.arrived_ref, f32[10,16,512]{2,1,0:T(8,128)S(1)} %copy-done, s32[10,16,512]{2,1,0:T(8,128)S(1)} %copy-done.1, f32[4,16,512]{2,1,0:T(8,128)S(1)} %copy-done.2, ...), custom_call_target="tpu_custom_call" | custom-call | flops 1000000 | bytes 1000000 | tf_op jit(solution)/shard_map/pallas_call | solution.py:605
  21.9 0.2 shard_map.79
  22.1 2.2 %collective-permute-start = (f32[3,16,128]{2,1,0:T(8,128)S(1)}, f32[3,16,128]{2,1,0:T(8,128)S(1)}, u32[]{:S(2)}, u32[]{:S(2)}) collective-permute-start(f32[3,16,128]{2,1,0:T(8,128)S(1)} %get-tuple-element.35), channel_id=1, source_target_pairs={{0,1},{1,2},{2,3},{4,5},{5,6},{6,7},{8,9},{9,10},{10,11},{12,13},{... | collective-permute-start | bytes 73736 | tf_op jit(solution)/shard_map/ppermute | solution.py:582
  24.3 1.3 %collective-permute-start.1 = (f32[3,16,128]{2,1,0:T(8,128)S(1)}, f32[3,16,128]{2,1,0:T(8,128)S(1)}, u32[]{:S(2)}, u32[]{:S(2)}) collective-permute-start(f32[3,16,128]{2,1,0:T(8,128)S(1)} %get-tuple-element.36), channel_id=1, source_target_pairs={{1,0},{2,1},{3,2},{5,4},{6,5},{7,6},{9,8},{10,9},{11,10},{13,12},{... | collective-permute-start | bytes 73736 | tf_op jit(solution)/shard_map/ppermute | solution.py:582
  25.6 0.0 collective-permute-done.ylo_ref
  25.6 1.8 %collective-permute-done.1.yhi_ref = f32[3,16,128]{2,1,0:T(8,128)S(1)} collective-permute-done((f32[3,16,128]{2,1,0:T(8,128)S(1)}, f32[3,16,128]{2,1,0:T(8,128)S(1)}, u32[]{:S(2)}, u32[]{:S(2)}) %collective-permute-start.1) | collective-permute-done | bytes 24608 | tf_op jit(solution)/shard_map/ppermute | solution.py:582
  27.4 2.6 %collective-permute-start.2 = (f32[72,512]{1,0:T(8,128)S(1)}, f32[72,512]{1,0:T(8,128)S(1)}, u32[]{:S(2)}, u32[]{:S(2)}) collective-permute-start(f32[72,512]{1,0:T(8,128)S(1)} %get-tuple-element.37), channel_id=1, source_target_pairs={{0,4},{4,8},{8,12},{12,16},{16,20},{20,24},{24,28},{1,5},{5,9},{9,... | collective-permute-start | bytes 442376 | tf_op jit(solution)/shard_map/ppermute | solution.py:582
  30.1 1.3 %collective-permute-start.3 = (f32[72,512]{1,0:T(8,128)S(1)}, f32[72,512]{1,0:T(8,128)S(1)}, u32[]{:S(2)}, u32[]{:S(2)}) collective-permute-start(f32[72,512]{1,0:T(8,128)S(1)} %get-tuple-element.38), channel_id=1, source_target_pairs={{4,0},{8,4},{12,8},{16,12},{20,16},{24,20},{28,24},{5,1},{9,5},{13... | collective-permute-start | bytes 442376 | tf_op jit(solution)/shard_map/ppermute | solution.py:582
  31.4 0.0 collective-permute-done.4.lo_ref
  31.4 0.0 collective-permute-done.5.hi_ref
  31.4 2.0 %shard_map.81 = (f32[10,32,512]{2,1,0:T(8,128)S(1)}, f32[10,32,512]{2,1,0:T(8,128)S(1)}, f32[10,32,512]{2,1,0:T(8,128)S(1)}, f32[10,32,512]{2,1,0:T(8,128)S(1)},...) custom-call(f32[3,12]{1,0:T(4,128)S(1)} %copy-done.4, ...), custom_call_target="tpu_custom_call" | custom-call | flops 1000000 | bytes 1000000 | tf_op jit(solution)/shard_map/pallas_call | solution.py:622
  33.4 0.0 collective-permute-done.2.slo_ref
  33.4 3.8 %collective-permute-done.3.shi_ref = f32[72,512]{1,0:T(8,128)S(1)} collective-permute-done((f32[72,512]{1,0:T(8,128)S(1)}, f32[72,512]{1,0:T(8,128)S(1)}, u32[]{:S(2)}, u32[]{:S(2)}) %collective-permute-start.3) | collective-permute-done | bytes 147488 | tf_op jit(solution)/shard_map/ppermute | solution.py:582
  37.3 6.3 %shard_map.82 = (f32[10,32,128]{2,1,0:T(8,128)S(1)}, f32[10,32,128]{2,1,0:T(8,128)S(1)}, f32[10,32,128]{2,1,0:T(8,128)S(1)}, f32[10,32,128]{2,1,0:T(8,128)S(1)},...) custom-call(f32[3,12]{1,0:T(4,128)S(1)} %copy-done.4, ...), custom_call_target="tpu_custom_call" | custom-call | flops 1000000 | bytes 1000000 | tf_op jit(solution)/shard_map/pallas_call | solution.py:626
  43.6 13.7 %all_to_all.15.arrived_ref = f32[32,1,128]{2,1,0:T(1,128)S(1)} all-to-all(f32[32,1,128]{2,1,0:T(1,128)S(1)} %get-tuple-element.47), channel_id=1, replica_groups=mesh['gx'=8,'gy'=4] {'gx','gy'}, dimensions={0} | all-to-all | bytes 32768 | tf_op jit(solution)/shard_map/all_to_all | solution.py:585
  57.3 4.2 %shard_map.83 = (f32[10,16,512]{2,1,0:T(8,128)S(1)}, f32[10,24,640]{2,1,0:T(8,128)S(1)}, f32[10,24,640]{2,1,0:T(8,128)S(1)}, f32[10,24,640]{2,1,0:T(8,128)S(1)}, f32[32,1,128]{2,1,0:T(1,128)S(1)}) custom-call(f32[32,1,128]{2,1,0:T(1,128)S(1)} %all_to_all.15.arrived_ref, f32[10,32,512]{2,1,0:T(8,128)S(1)} %get-tuple-element.41.ext_ref.old_ref, ...), custom_call_target="tpu_custom_call" | custom-call | flops 1000000 | bytes 1000000 | tf_op jit(solution)/shard_map/pallas_call | solution.py:634
  61.4 8.8 %all_to_all.16.arrived_ref = f32[32,1,128]{2,1,0:T(1,128)S(1)} all-to-all(f32[32,1,128]{2,1,0:T(1,128)S(1)} %get-tuple-element.58), channel_id=1, replica_groups=mesh['gx'=8,'gy'=4] {'gx','gy'}, dimensions={0} | all-to-all | bytes 32768 | tf_op jit(solution)/shard_map/all_to_all | solution.py:585
  70.3 1.0 %shard_map.84 = f32[10,16,512]{2,1,0:T(8,128)} custom-call(f32[32,1,128]{2,1,0:T(1,128)S(1)} %all_to_all.16.arrived_ref, f32[10,16,512]{2,1,0:T(8,128)S(1)} %get-tuple-element.59.part_ref, f32[10,24,640]{2,1,0:T(8,128)S(1)} %get-tuple-element.60.q0_ref, f32[10,24,640]{2,1,0:T(8,128)S(1)} %get-tuple-element.61.q1_ref, f32[10,24,640]{2,1,0:T(8,128)S(1)} %get-tuple-element.62.q2_ref), custom_call_target="tpu_custom_call" | custom-call | flops 1000000 | bytes 1000000 | tf_op jit(solution)/shard_map/pallas_call | solution.py:641
  (2 shorter events, 0.0 us)
Async XLA Ops:
  0.6 17.7 %copy-start = (f32[10,16,512]{2,1,0:T(8,128)S(1)}, f32[10,16,512]{2,1,0:T(8,128)}, u32[]{:S(2)}) copy-start(f32[10,16,512]{2,1,0:T(8,128)} %head_ref.5) | copy-start | bytes 983044
  0.6 17.7 %copy-start.1 = (s32[10,16,512]{2,1,0:T(8,128)S(1)}, s32[10,16,512]{2,1,0:T(8,128)}, u32[]{:S(2)}) copy-start(s32[10,16,512]{2,1,0:T(8,128)} %soil_ref.5) | copy-start | bytes 983044
  2.7 15.6 %copy-start.2 = (f32[4,16,512]{2,1,0:T(8,128)S(1)}, f32[4,16,512]{2,1,0:T(8,128)}, u32[]{:S(2)}) copy-start(f32[4,16,512]{2,1,0:T(8,128)} %forcing_ref.1) | copy-start | bytes 393220
  2.8 15.6 %copy-start.3 = (s32[16,512]{1,0:T(8,128)S(1)}, s32[16,512]{1,0:T(8,128)}, u32[]{:S(2)}) copy-start(s32[16,512]{1,0:T(8,128)} %slot_ref.1) | copy-start | bytes 98308
  2.8 15.5 %all-to-all-start = ((f32[32,8,128]{2,1,0:T(8,128)}), f32[32,8,128]{2,1,0:T(8,128)S(1)}, u32[]{:S(2)}, u32[]{:S(2)}) async-start(f32[32,8,128]{2,1,0:T(8,128)} %get-tuple-element.33), calls=%async_computation | async-start | bytes 262144 | tf_op jit(solution)/shard_map/all_to_all | solution.py:585
  10.1 8.3 %copy-start.4 = (f32[3,12]{1,0:T(4,128)S(1)}, f32[3,12]{1,0:T(4,128)}, u32[]{:S(2)}) copy-start(f32[3,12]{1,0:T(4,128)} %table_ref.5) | copy-start | bytes 436
  10.1 21.3 %collective-permute-start.4 = (f32[144,512]{1,0:T(8,128)}, f32[144,512]{1,0:T(8,128)S(1)}, u32[]{:S(2)}, u32[]{:S(2)}) collective-permute-start(f32[144,512]{1,0:T(8,128)} %get-tuple-element.39), channel_id=1, source_target_pairs={{0,4},{4,8},{8,12},{12,16},{16,20},{20,24},{24,28},{1,5},{5,9},{9,... | collective-permute-start | bytes 884744 | tf_op jit(solution)/shard_map/ppermute | solution.py:582
  13.8 17.6 %collective-permute-start.5 = (f32[144,512]{1,0:T(8,128)}, f32[144,512]{1,0:T(8,128)S(1)}, u32[]{:S(2)}, u32[]{:S(2)}) collective-permute-start(f32[144,512]{1,0:T(8,128)} %get-tuple-element.40), channel_id=1, source_target_pairs={{4,0},{8,4},{12,8},{16,12},{20,16},{24,20},{28,24},{5,1},{9,5},{13... | collective-permute-start | bytes 884744 | tf_op jit(solution)/shard_map/ppermute | solution.py:582
  22.1 3.5 %collective-permute-start = (f32[3,16,128]{2,1,0:T(8,128)S(1)}, f32[3,16,128]{2,1,0:T(8,128)S(1)}, u32[]{:S(2)}, u32[]{:S(2)}) collective-permute-start(f32[3,16,128]{2,1,0:T(8,128)S(1)} %get-tuple-element.35), channel_id=1, source_target_pairs={{0,1},{1,2},{2,3},{4,5},{5,6},{6,7},{8,9},{9,10},{10,11},{12,13},{... | collective-permute-start | bytes 73736 | tf_op jit(solution)/shard_map/ppermute | solution.py:582
  24.3 3.1 %collective-permute-start.1 = (f32[3,16,128]{2,1,0:T(8,128)S(1)}, f32[3,16,128]{2,1,0:T(8,128)S(1)}, u32[]{:S(2)}, u32[]{:S(2)}) collective-permute-start(f32[3,16,128]{2,1,0:T(8,128)S(1)} %get-tuple-element.36), channel_id=1, source_target_pairs={{1,0},{2,1},{3,2},{5,4},{6,5},{7,6},{9,8},{10,9},{11,10},{13,12},{... | collective-permute-start | bytes 73736 | tf_op jit(solution)/shard_map/ppermute | solution.py:582
  27.4 6.0 %collective-permute-start.2 = (f32[72,512]{1,0:T(8,128)S(1)}, f32[72,512]{1,0:T(8,128)S(1)}, u32[]{:S(2)}, u32[]{:S(2)}) collective-permute-start(f32[72,512]{1,0:T(8,128)S(1)} %get-tuple-element.37), channel_id=1, source_target_pairs={{0,4},{4,8},{8,12},{12,16},{16,20},{20,24},{24,28},{1,5},{5,9},{9,... | collective-permute-start | bytes 442376 | tf_op jit(solution)/shard_map/ppermute | solution.py:582
  30.1 7.2 %collective-permute-start.3 = (f32[72,512]{1,0:T(8,128)S(1)}, f32[72,512]{1,0:T(8,128)S(1)}, u32[]{:S(2)}, u32[]{:S(2)}) collective-permute-start(f32[72,512]{1,0:T(8,128)S(1)} %get-tuple-element.38), channel_id=1, source_target_pairs={{4,0},{8,4},{12,8},{16,12},{20,16},{24,20},{28,24},{5,1},{9,5},{13... | collective-permute-start | bytes 442376 | tf_op jit(solution)/shard_map/ppermute | solution.py:582

commit v9 on v8

--- a/solution.py
+++ b/solution.py
@@ -96,7 +96,7 @@
     return 1.0 / (1.0 + jnp.exp(-u))
 
 
-def source_kernel(
+def edge_source_kernel(
     table_ref, arrived_ref, head_ref, soil_ref, forcing_ref, slot_ref,
     source_ref, flux_ref, tab_ref, factor_ref,
 ):
@@ -133,14 +133,42 @@
         return 0
 
     lax.fori_loop(0, owners // 2, unpack, 0, unroll=16)
+    places = [(0, 0), (cols - LANES, LANES)]
+    land_columns(
+        table_ref, tab_ref, factor_ref, head_ref, soil_ref, forcing_ref, slot_ref, source_ref, flux_ref, places
+    )
+
+
+def inner_source_kernel(
+    table_ref, tab_ref, factor_ref, head_ref, soil_ref, forcing_ref, slot_ref, some_ref, part_ref,
+    source_ref, flux_ref,
+):
+    cols = head_ref.shape[2]
+    places = [(at, at) for at in range(LANES, cols - LANES, LANES)]
+    land_columns(
+        table_ref, tab_ref, factor_ref, head_ref, soil_ref, forcing_ref, slot_ref, source_ref, flux_ref, places
+    )
+    for whole_ref, piece_ref in ((source_ref, some_ref), (flux_ref, part_ref)):
+        for k in range(whole_ref.shape[0]):
+            whole_ref[k, :, 0:LANES] = piece_ref[k, :, 0:LANES]
+            whole_ref[k, :, cols - LANES : cols] = piece_ref[k, :, LANES : 2 * LANES]
+
+
+def land_columns(
+    table_ref, tab_ref, factor_ref, head_ref, soil_ref, forcing_ref, slot_ref, source_ref, flux_ref, places
+):
+    layers, rows, _ = head_ref.shape
+    halves_of = tab_ref.shape[0]
+    pairs = tab_ref.shape[1] - 1
     tables = table_rows(table_ref, rows)
     shape = (rows, LANES)
 
     def whole(block):
         return jnp.concatenate([block] * (rows // 8), axis=0)
 
-    for at_y in range(0, cols, LANES):
+    for at_y, put in places:
         here = (slice(0, rows), slice(at_y, at_y + LANES))
+        there = (slice(0, rows), slice(put, put + LANES))
         slot = slot_ref[here]
         land = slot >= 0
         value = jnp.maximum(slot, 0)
@@ -154,11 +182,11 @@
             return tuple(jnp.where(match, new, old) for new, old in zip(found, held))
 
         held = tuple([jnp.full(shape, 1, jnp.int32)] * (pairs + 1) + [jnp.full(shape, 1.0 / FIXED, f32)])
-        if owners <= 32:
-            for t in range(owners // 2):
+        if halves_of <= 16:
+            for t in range(halves_of):
                 held = pick(t, held)
         else:
-            held = lax.fori_loop(0, owners // 2, pick, held, unroll=8)
+            held = lax.fori_loop(0, halves_of, pick, held, unroll=8)
         *words, terms, factor = held
 
         def halves(word):
@@ -199,13 +227,13 @@
         infiltration = rainfall * ks_top / (rainfall + ks_top)
         infiltration = jnp.where(land, infiltration, 0.0)
         rate = jnp.where(land, rate, 0.0)
-        flux_ref[(0,) + here] = conductance * rate
-        flux_ref[(1,) + here] = infiltration
+        flux_ref[(0,) + there] = conductance * rate
+        flux_ref[(1,) + there] = infiltration
         for k in range(layers):
             value = -rate * uptake[k]
             if k == 0:
                 value = value + infiltration
-            source_ref[(k,) + here] = value
+            source_ref[(k,) + there] = value
 
 
 def strips(planes, shift_from):
@@ -230,12 +258,12 @@
     return jnp.concatenate([above, gap, below], axis=0)
 
 
-def strip_kernel(head_ref, soil_ref, src_ref, down_ref, up_ref):
+def strip_kernel(head_ref, soil_ref, some_ref, down_ref, up_ref):
     layers, _, cols = head_ref.shape
-    for out_ref, (part, shift) in zip((down_ref, up_ref), strip_parts(cols)):
+    for out_ref, (part, shift), at in zip((down_ref, up_ref), strip_parts(cols), (0, LANES)):
         out_ref[0] = strips([head_ref[k, :, part] for k in range(layers)], shift)
         out_ref[1] = strips([(soil_ref[k, :, part] + 1).astype(f32) for k in range(layers)], shift)
-        out_ref[2] = strips([src_ref[k, :, part] for k in range(layers)], shift)
+        out_ref[2] = strips([some_ref[k, :, at : at + LANES] for k in range(layers)], shift)
 
 
 def source_edge_kernel(src_ref, ylo_ref, yhi_ref, down_ref, up_ref):
@@ -304,67 +332,64 @@
     return cond, deriv, weighted * slope, weighted * sat
 
 
-def joined(main_ref, side_ref):
-    return lambda k: jnp.concatenate([main_ref[k], side_ref[k]], axis=1)
-
-
-def linearize(layers, head_of, cond_of, deriv_of, store_of, gain_of, mask, coefs, out_ref, tile):
+def joined(*refs):
+    return lambda k: jnp.concatenate([ref[k] for ref in refs], axis=1)
+
+
+def plain(ref):
+    return lambda k: ref[k]
+
+
+def face_of(here, there, extra=None):
+    mean = 0.5 * (here[1] + there[1])
+    drop = here[0] - there[0]
+    if extra is not None:
+        drop = drop + extra
+    return mean + here[2] * drop, mean - there[2] * drop, mean * drop
+
+
+def ring_faces(state, axis, inside=None):
+    a, b, face = face_of(state, [after(x, axis) for x in state])
+    if inside is not None:
+        a, b, face = (jnp.where(inside, x, 0.0) for x in (a, b, face))
+    return face - before(face, axis), a + before(b, axis), b, before(a, axis)
+
+
+def linearize(layers, state_of, store_of, y_faces, masked, coefs, finish):
     diag_ref, xp_ref, xm_ref, yp_ref, ym_ref, az_ref, bz_ref = coefs
-    rows, cols = tile
-
-    def masked(value):
-        own = value[:rows, cols:] * mask[:rows, cols:]
-        top = jnp.concatenate([value[:rows, :cols], own], axis=1)
-        return jnp.concatenate([top, value[rows:] * mask[rows:]], axis=0)
-
     above = None
     for k in range(layers):
-        head = head_of(k)
-        cond = cond_of(k)
-        deriv = deriv_of(k)
-        value = gain_of(k)
-        diag = store_of(k)
-        for plus_ref, minus_ref, axis in ((xp_ref, xm_ref, 0), (yp_ref, ym_ref, 1)):
-            mean = 0.5 * (cond + after(cond, axis))
-            drop = head - after(head, axis)
-            a = mean + deriv * drop
-            b = mean - after(deriv, axis) * drop
-            face = mean * drop
-            value = value + (face - before(face, axis))
-            diag = diag + (a + before(b, axis))
-            plus_ref[k] = masked(b)
-            minus_ref[k] = masked(before(a, axis))
+        state = state_of(k)
+        net_x, diag_x, xp, xm = ring_faces(state, 0)
+        net_y, diag_y, yp, ym = y_faces(k, state)
+        for ref, value in ((xp_ref, xp), (xm_ref, xm), (yp_ref, yp), (ym_ref, ym)):
+            ref[k] = masked(value)
         if k + 1 < layers:
-            mean = 0.5 * (cond + cond_of(k + 1))
-            drop = head - head_of(k + 1) + 1.0
-            a = mean + deriv * drop
-            b = mean - deriv_of(k + 1) * drop
+            a, b, face = face_of(state, state_of(k + 1), 1.0)
             az_ref[k] = a
             bz_ref[k] = b
-            face = mean * drop
         else:
-            a = 2.0 * deriv
-            face = cond
-        diag = diag + a
-        value = value + face
+            a, face = 2.0 * state[2], state[1]
+        diag = store_of(k) + diag_x + diag_y + a
+        value = net_x + net_y + face
         if above is not None:
             diag = diag + above[1]
             value = value - above[0]
         above = (face, b)
         diag_ref[k] = diag
-        out_ref[k] = masked(value)
+        finish(k, masked(value))
 
 
 def apply(v_ref, coefs, k):
-    diag_ref, xp_ref, xm_ref, yp_ref, ym_ref, az_ref, bz_ref = coefs
+    diag_of, xp_of, xm_of, yp_of, ym_of, az_of, bz_of = coefs
     v = v_ref[k]
-    value = diag_ref[k] * v
-    value = value - xp_ref[k] * after(v, 0) - xm_ref[k] * before(v, 0)
-    value = value - yp_ref[k] * after(v, 1) - ym_ref[k] * before(v, 1)
+    value = diag_of(k) * v
+    value = value - xp_of(k) * after(v, 0) - xm_of(k) * before(v, 0)
+    value = value - yp_of(k) * after(v, 1) - ym_of(k) * before(v, 1)
     if k > 0:
-        value = value - az_ref[k - 1] * v_ref[k - 1]
+        value = value - az_of(k - 1) * v_ref[k - 1]
     if k + 1 < v_ref.shape[0]:
-        value = value - bz_ref[k] * v_ref[k + 1]
+        value = value - bz_of(k) * v_ref[k + 1]
     return value
 
 
@@ -486,37 +511,104 @@
             ref[k] = value
 
 
+def flow_kernel(ext_ref, ks_ref, cond_ref, deriv_ref, store_ref, flow_ref, *coefs, rows):
+    layers, _, cols = ext_ref.shape
+    mask = (ks_ref[0] > 0.0).astype(f32)
+    inside = lane_iota(mask.shape) < cols - 1
+
+    def masked(value):
+        return jnp.concatenate([value[:rows], value[rows:] * mask[rows:]], axis=0)
+
+    def finish(k, value):
+        flow_ref[k] = value
+
+    linearize(
+        layers, lambda k: (ext_ref[k], cond_ref[k], deriv_ref[k]), plain(store_ref),
+        lambda k, state: ring_faces(state, 1, inside), masked, coefs, finish,
+    )
+
+
 def first_kernel(
     table_ref, src_ref, slo_ref, shi_ref, ylo_ref, yhi_ref,
-    ext_ref, ks_ref, cond_ref, deriv_ref, store_ref, water_ref,
-    ext_side, ks_side, steep_side, cap_side, base_ref, p0_ref, p1_ref, p2_ref, gram_ref,
-    cond_side, deriv_side, store_side, water_side, *coefs,
+    ext_ref, ks_ref, cond_ref, deriv_ref, water_ref, flow_ref, *rest,
 ):
+    mains, rest = rest[:7], rest[7:]
+    ext_side, ks_side, steep_side, cap_side, base_ref, p0_ref, p1_ref, p2_ref, gram_ref = rest[:9]
+    sides, (cond_side, deriv_side, store_side) = rest[9:16], rest[16:19]
+    diag_first, diag_last, yp_last, ym_first = rest[19:23]
     layers, rows, cols = src_ref.shape
     tables = table_rows(table_ref, rows + 2 * HALO)
     heads, soils, sources = tall_strips(layers, ylo_ref, yhi_ref, slo_ref, shi_ref)
+    start, end, middle = slice(0, LANES), slice(cols - LANES, cols), slice(LANES, cols - LANES)
+    lane = lane_iota((rows + 2 * HALO, LANES))
+    is_first, is_last = lane == 0, lane == LANES - 1
+
+    def source_of(k):
+        ends = ends_of(slo_ref, shi_ref, k, SOURCE_DEPTH, slice(0, cols))
+        return jnp.concatenate([src_ref[k], ends], axis=0)
+
     for k in range(layers):
         head = side(heads, k)
         index = side(soils, k).astype(jnp.int32)
         conduct, steep, capacity = (lookup(row, index) for row in tables)
-        values = (head, conduct, steep, capacity) + pointwise(head, conduct, steep, capacity)
-        outs = (ext_side, ks_side, steep_side, cap_side, cond_side, deriv_side, store_side, water_side)
-        for ref, value in zip(outs, values):
+        cond, deriv, store, water = pointwise(head, conduct, steep, capacity)
+        outs = (ext_side, ks_side, steep_side, cap_side, cond_side, deriv_side, store_side)
+        for ref, value in zip(outs, (head, conduct, steep, capacity, cond, deriv, store)):
             ref[k] = value
-    water_of = joined(water_ref, water_side)
-
-    def gain_of(k):
-        source = jnp.concatenate([src_ref[k], ends_of(slo_ref, shi_ref, k, SOURCE_DEPTH, slice(0, cols))], axis=0)
-        source = jnp.concatenate([source, side(sources, k)], axis=1)
-        water = water_of(k)
-        base_ref[k] = water + source
-        return water - base_ref[k]
+        base_ref[k, :, 0:cols] = water_ref[k] + source_of(k)
+        base_ref[k, :, cols:] = water + side(sources, k)
+        p0_ref[k, :, middle] = flow_ref[k, :, middle] + (water_ref[k, :, middle] - base_ref[k, :, middle])
+        p0_ref[k, :, cols:] = water - base_ref[k, :, cols:]
+
+    masks = [(ref > 0.0).astype(f32) for ref in (ks_ref[0, :, start], ks_ref[0, :, end], ks_side[0])]
+
+    def y_faces(k, state):
+        first = (ext_ref[k, :, start], cond_ref[k, :, start], deriv_ref[k, :, start])
+        last = (ext_ref[k, :, end], cond_ref[k, :, end], deriv_ref[k, :, end])
+        moved = [after(x, 1) for x in state]
+        ahead = [jnp.where(is_last, after(x, 1), y) for x, y in zip(first, moved)]
+        a, b, face = face_of(state, ahead)
+        a_in, b_in, face_in = (jnp.where(is_last, x, 0.0) for x in face_of(last, moved))
+        a_out, b_out, face_out = (before(x, 1) for x in (a, b, face))
+        a_pre, b_pre, face_pre = (before(x, 1) for x in (a_in, b_in, face_in))
+        gain = water_ref[k, :, end] - base_ref[k, :, end]
+        p0_ref[k, :, end] = flow_ref[k, :, end] + face_in * masks[1] + gain
+        diag_last[k] = mains[0][k, :, end] + a_in
+        yp_last[k] = mains[3][k, :, end] + b_in * masks[1]
+        gain = water_ref[k, :, start] - base_ref[k, :, start]
+        p0_ref[k, :, start] = flow_ref[k, :, start] - jnp.where(is_first, face_out, 0.0) * masks[0] + gain
+        diag_first[k] = mains[0][k, :, start] + jnp.where(is_first, b_out, 0.0)
+        ym_first[k] = mains[4][k, :, start] + jnp.where(is_first, a_out, 0.0) * masks[0]
+        a_pre, b_pre, face_pre = (
+            jnp.where(is_first, x, y)
+            for x, y in ((a_pre, a_out), (b_pre, b_out), (face_pre, face_out))
+        )
+        return face - face_pre, a + b_pre, b, a_pre
+
+    def finish(k, value):
+        p0_ref[k, :, cols:] = p0_ref[k, :, cols:] + value
 
     linearize(
-        layers, joined(ext_ref, ext_side), joined(cond_ref, cond_side), joined(deriv_ref, deriv_side),
-        joined(store_ref, store_side), gain_of,
-        (joined(ks_ref, ks_side)(0) > 0.0).astype(f32), coefs, p0_ref, (rows, cols),
-    )
+        layers, lambda k: (ext_side[k], cond_side[k], deriv_side[k]), plain(store_side),
+        y_faces, lambda value: value * masks[2], sides, finish,
+    )
+
+    def pieces(n, first_of, last_of):
+        main, beside = mains[n], sides[n]
+        return lambda k: jnp.concatenate(
+            [first_of(main, k), main[k, :, middle], last_of(main, k), beside[k]], axis=1
+        )
+
+    def of_start(ref, k):
+        return ref[k, :, start]
+
+    def of_end(ref, k):
+        return ref[k, :, end]
+
+    coefs = [joined(main, beside) for main, beside in zip(mains, sides)]
+    coefs[0] = pieces(0, lambda _, k: diag_first[k], lambda _, k: diag_last[k])
+    coefs[3] = pieces(3, of_start, lambda _, k: yp_last[k])
+    coefs[4] = pieces(4, lambda _, k: ym_first[k], of_end)
     powers((p0_ref, p1_ref, p2_ref), coefs, (rows, cols), gram_ref)
 
 
@@ -540,7 +632,7 @@
 
     old_of, ks_of = folded(joined(old_ref, old_side)), folded(joined(ks_ref, ks_side))
     steep_of, cap_of = folded(joined(steep_ref, steep_side)), folded(joined(cap_ref, cap_side))
-    base_of, *qs = (folded(lambda k, ref=ref: ref[k]) for ref in (base_ref, q0_ref, q1_ref, q2_ref))
+    base_of, *qs = (folded(plain(ref)) for ref in (base_ref, q0_ref, q1_ref, q2_ref))
     for k in range(layers):
         head = old_of(k)
         for value, q_of in zip(x, qs):
@@ -552,11 +644,21 @@
         deriv_ref[k] = deriv
         store_ref[k] = store
         gain_ref[k] = water - base_of(k)
+    mask = (ks_of(0) > 0.0).astype(f32)
+
+    def masked(value):
+        own = value[:rows, cols:] * mask[:rows, cols:]
+        top = jnp.concatenate([value[:rows, :cols], own], axis=1)
+        return jnp.concatenate([top, value[rows:] * mask[rows:]], axis=0)
+
+    def finish(k, value):
+        p0_ref[k] = value + gain_ref[k]
+
     linearize(
-        layers, *((lambda k, ref=ref: ref[k]) for ref in (ext_ref, cond_ref, deriv_ref, store_ref, gain_ref)),
-        (ks_of(0) > 0.0).astype(f32), coefs, p0_ref, (rows, cols),
-    )
-    powers((p0_ref, p1_ref, p2_ref), coefs, (rows, cols), gram_ref)
+        layers, lambda k: (ext_ref[k], cond_ref[k], deriv_ref[k]), plain(store_ref),
+        lambda k, state: ring_faces(state, 1), masked, coefs, finish,
+    )
+    powers((p0_ref, p1_ref, p2_ref), [plain(ref) for ref in coefs], (rows, cols), gram_ref)
 
 
 def last_kernel(arrived_ref, part_ref, q0_ref, q1_ref, q2_ref, head_ref):
@@ -602,18 +704,19 @@
     )(canopy, head_old, soil_type)
     arrived = spread(send, both)
     lo, hi = exchange(down, up, "gx")
+    columns = (head_old, soil_type, forcing, column_slot)
+    table = ((devices // 2, -(-layers // 2) + 1, 8, LANES), jnp.int32)
+    some, flux, tab, factor = call(
+        edge_source_kernel,
+        [((layers, rows, 2 * LANES), f32), ((2, rows, 2 * LANES), f32), table, ((devices // 2, 8, LANES), f32)],
+        6,
+        in_specs=[smem] + [vmem] * 5,
+    )(soil_table, arrived, *columns)
+    ydown, yup = call(strip_kernel, [((3, rows, LANES), f32)] * 2, 3)(head_old, soil_type, some)
+    ylo, yhi = exchange(ydown, yup, "gy")
     source, flux = call(
-        source_kernel,
-        [own, ((2, rows, cols), f32)],
-        6,
-        scratch=[
-            pltpu.VMEM((devices // 2, -(-layers // 2) + 1, 8, LANES), jnp.int32),
-            pltpu.VMEM((devices // 2, 8, LANES), f32),
-        ],
-        in_specs=[smem] + [vmem] * 5,
-    )(soil_table, arrived, head_old, soil_type, forcing, column_slot)
-    ydown, yup = call(strip_kernel, [((3, rows, LANES), f32)] * 2, 3)(head_old, soil_type, source)
-    ylo, yhi = exchange(ydown, yup, "gy")
+        inner_source_kernel, [own, ((2, rows, cols), f32)], 9, in_specs=[smem] + [vmem] * 8
+    )(soil_table, tab, factor, *columns, some, flux)
     sdown, sup = call(source_edge_kernel, [edge(SOURCE_DEPTH * layers + HALO + HALO // 2)] * 2, 3)(
         source, ylo, yhi
     )
@@ -622,14 +725,16 @@
     old, ks, steep, cap, cond, deriv, store, water = call(
         state_kernel, [main] * 8, 5, in_specs=[smem] + [vmem] * 4
     )(soil_table, head_old, soil_type, lo, hi)
-    held, held_side = [pltpu.VMEM(ext[0], f32)], [pltpu.VMEM(side_block[0], f32)]
+    flow, *coefs = call(functools.partial(flow_kernel, rows=rows), [main] * 8, 5)(
+        old, ks, cond, deriv, store
+    )
     old_s, ks_s, steep_s, cap_s, base, p0, p1, p2, gram = call(
         first_kernel,
         [side_block] * 4 + [ext] * 4 + [gram_block],
-        12,
-        scratch=held_side * 4 + held * 7,
-        in_specs=[smem] + [vmem] * 11,
-    )(soil_table, source, slo, shi, ylo, yhi, old, ks, cond, deriv, store, water)
+        19,
+        scratch=[pltpu.VMEM(side_block[0], f32)] * 14,
+        in_specs=[smem] + [vmem] * 18,
+    )(soil_table, source, slo, shi, ylo, yhi, old, ks, cond, deriv, water, flow, *coefs)
     sums = spread(gram, both)
     part, q0, q1, q2, gram = call(
         second_kernel,

time: 71.7 us -> 68.8 us (0.960)
  waiting for transfers between devices: 8.85 us -> 5.14 us
  blocking collectives: 22.5 us -> 23.3 us
    ppermute x3, waiting for transfers between devices: 5.63 us -> 1.91 us  [exchange(): lax.ppermute(to_lower, axis, down)]
    all_to_all x2, blocking collectives: 22.5 us -> 23.3 us  [spread(): return lax.all_to_all(x, axes, split_axis=0, concat_axis=0, tiled=True)]
    pallas_call x2 -> x4, Pallas kernels: 9.87 us -> 10.5 us  [the longest x1 4.71 us: shards(): call(first_kernel, [side_block] * 4 + [ext] * 4 + [gram_block], 19, scrat...]
  transfers between devices with their start and end apart: 7 -> 7, of which waited for: 3 -> 2; matrix products, arithmetic and copies ran while one was open for 0% -> 0% of each run, Pallas kernels for 8% -> 12%
where the time goes in v9:
time: 68.8 us; the launch traced here: 68.5 us
  blocking collectives  23.3 us (34%)
  Pallas kernels  19.8 us (29%)
  starting transfers between devices  19.4 us (28%)
  waiting for transfers between devices  5.14 us (7%)
  between operations  0.82 us (1%)
    all_to_all x2, blocking collectives, spread(): return lax.all_to_all(x, axes, split_axis=0, concat_axis=0, tiled=True)  23.3 us
    ppermute x3, starting transfers between devices, exchange(): lax.ppermute(to_upper, axis, up)  8.18 us
    all_to_all x1, starting transfers between devices, spread(): return lax.all_to_all(x, axes, split_axis=0, concat_axis=0, tiled=True)  7.3 us
    pallas_call x1, Pallas kernels, shards(): call(first_kernel, [side_block] * 4 + [ext] * 4 + [gram_block], 19, scrat...  4.71 us
    pallas_call x1, Pallas kernels, shards(): call(second_kernel, [own] + [((layers, rows + HALO, wide), f32)] * 3 + [g...  3.91 us
    ppermute x3, starting transfers between devices, exchange(): lax.ppermute(to_lower, axis, down)  3.88 us
    all_to_all x1, waiting for transfers between devices, spread(): return lax.all_to_all(x, axes, split_axis=0, concat_axis=0, tiled=True)  3.22 us
    pallas_call x1, Pallas kernels, shards(): call(inner_source_kernel, [own, ((2, rows, cols), f32)], 9, in_specs=[sme...  2.16 us
  transfers between devices with their start and end apart: 7, of which 2 were waited for; matrix products, arithmetic and copies ran while one was open for 0% of the time, Pallas kernels for 12%

profile of v9, /device:TPU:0, one launch (start us, length us, event | category | flops | bytes accessed | tf_op | source)
XLA Modules:
  0.0 68.5 jit_solution(14438831097803286906)
XLA Ops:
  0.6 0.0 copy-start
  0.6 0.0 copy-start.1
  0.6 2.1 %shard_map.77 = (f32[32,8,128]{2,1,0:T(8,128)}, f32[144,512]{1,0:T(8,128)}, f32[144,512]{1,0:T(8,128)}) custom-call(f32[13,2048]{1,0:T(8,128)} %canopy_hbm.1, f32[10,16,512]{2,1,0:T(8,128)} %head_ref.7, s32[10,16,512]{2,1,0:T(8,128)} %soil_ref.7), custom_call_target="tpu_custom_call" | custom-call | flops 1000000 | bytes 1000000 | tf_op jit(solution)/shard_map/pallas_call | solution.py:692
  2.8 0.0 copy-start.2
  2.8 0.0 copy-start.3
  2.8 7.3 %all-to-all-start = ((f32[32,8,128]{2,1,0:T(8,128)}), f32[32,8,128]{2,1,0:T(8,128)S(1)}, u32[]{:S(2)}, u32[]{:S(2)}) async-start(f32[32,8,128]{2,1,0:T(8,128)} %get-tuple-element.45), calls=%async_computation | async-start | bytes 262144 | tf_op jit(solution)/shard_map/all_to_all | solution.py:687
  10.1 0.0 copy-start.4
  10.1 3.7 %collective-permute-start.4 = (f32[144,512]{1,0:T(8,128)}, f32[144,512]{1,0:T(8,128)S(1)}, u32[]{:S(2)}, u32[]{:S(2)}) collective-permute-start(f32[144,512]{1,0:T(8,128)} %get-tuple-element.55), channel_id=1, source_target_pairs={{0,4},{4,8},{8,12},{12,16},{16,20},{20,24},{24,28},{1,5},{5,9},{9,... | collective-permute-start | bytes 884744 | tf_op jit(solution)/shard_map/ppermute | solution.py:684
  13.8 1.3 %collective-permute-start.5 = (f32[144,512]{1,0:T(8,128)}, f32[144,512]{1,0:T(8,128)S(1)}, u32[]{:S(2)}, u32[]{:S(2)}) collective-permute-start(f32[144,512]{1,0:T(8,128)} %get-tuple-element.56), channel_id=1, source_target_pairs={{4,0},{8,4},{12,8},{16,12},{20,16},{24,20},{28,24},{5,1},{9,5},{13... | collective-permute-start | bytes 884744 | tf_op jit(solution)/shard_map/ppermute | solution.py:684
  15.1 3.2 %all-to-all-done.arrived_ref = f32[32,8,128]{2,1,0:T(8,128)S(1)} async-done(((f32[32,8,128]{2,1,0:T(8,128)}), f32[32,8,128]{2,1,0:T(8,128)S(1)}, u32[]{:S(2)}, u32[]{:S(2)}) %all-to-all-start) | async-done | bytes 131104 | tf_op jit(solution)/shard_map/all_to_all | solution.py:687
  18.3 0.0 copy-done.3
  18.3 0.0 copy-done.4
  18.3 1.8 %shard_map.78 = (f32[10,16,256]{2,1,0:T(8,128)S(1)}, f32[2,16,256]{2,1,0:T(8,128)S(1)}, s32[16,6,8,128]{3,2,1,0:T(8,128)S(1)}, f32[16,8,128]{2,1,0:T(8,128)S(1)}) custom-call(f32[3,12]{1,0:T(4,128)S(1)} %copy-done.4, f32[32,8,128]{2,1,0:T(8,128)S(1)} %all-to-all-done.arrived_ref, f32[10,16,512]{2,1,0:T(8,128)S(1)} %copy-done, s32[10,16,512]{2,1,0:T(8,128)S(1)} %copy-done.1, ...), custom_call_target="tpu_custom_call" | custom-call | flops 1000000 | bytes 1000000 | tf_op jit(solution)/shard_map/pallas_call | solution.py:709
  20.2 0.2 shard_map.80
  20.4 2.2 %collective-permute-start = (f32[3,16,128]{2,1,0:T(8,128)S(1)}, f32[3,16,128]{2,1,0:T(8,128)S(1)}, u32[]{:S(2)}, u32[]{:S(2)}) collective-permute-start(f32[3,16,128]{2,1,0:T(8,128)S(1)} %get-tuple-element.51), channel_id=1, source_target_pairs={{0,1},{1,2},{2,3},{4,5},{5,6},{6,7},{8,9},{9,10},{10,11},{12,13},{... | collective-permute-start | bytes 73736 | tf_op jit(solution)/shard_map/ppermute | solution.py:684
  22.6 1.3 %collective-permute-start.1 = (f32[3,16,128]{2,1,0:T(8,128)S(1)}, f32[3,16,128]{2,1,0:T(8,128)S(1)}, u32[]{:S(2)}, u32[]{:S(2)}) collective-permute-start(f32[3,16,128]{2,1,0:T(8,128)S(1)} %get-tuple-element.52), channel_id=1, source_target_pairs={{1,0},{2,1},{3,2},{5,4},{6,5},{7,6},{9,8},{10,9},{11,10},{13,12},{... | collective-permute-start | bytes 73736 | tf_op jit(solution)/shard_map/ppermute | solution.py:684
  23.9 2.2 %shard_map.79 = (f32[10,16,512]{2,1,0:T(8,128)S(1)}, f32[2,16,512]{2,1,0:T(8,128)}) custom-call(f32[3,12]{1,0:T(4,128)S(1)} %copy-done.4, s32[16,6,8,128]{3,2,1,0:T(8,128)S(1)} %get-tuple-element.46.tab_ref, f32[16,8,128]{2,1,0:T(8,128)S(1)} %get-tuple-element.47.factor_ref, f32[10,16,512]{2,1,0:T(8,128)S(1)} %copy-done, s32[10,16,512]{2,1,0:T(8,128)S(1)} %copy-done.1, ...), custom_call_target="tpu_custom_call" | custom-call | flops 1000000 | bytes 1000000 | tf_op jit(solution)/shard_map/pallas_call | solution.py:717
  26.1 0.0 collective-permute-done.ylo_ref
  26.1 0.0 collective-permute-done.1.yhi_ref
  26.1 2.3 %collective-permute-start.2 = (f32[72,512]{1,0:T(8,128)S(1)}, f32[72,512]{1,0:T(8,128)S(1)}, u32[]{:S(2)}, u32[]{:S(2)}) collective-permute-start(f32[72,512]{1,0:T(8,128)S(1)} %get-tuple-element.53), channel_id=1, source_target_pairs={{0,4},{4,8},{8,12},{12,16},{16,20},{20,24},{24,28},{1,5},{5,9},{9,... | collective-permute-start | bytes 442376 | tf_op jit(solution)/shard_map/ppermute | solution.py:684
  28.4 1.3 %collective-permute-start.3 = (f32[72,512]{1,0:T(8,128)S(1)}, f32[72,512]{1,0:T(8,128)S(1)}, u32[]{:S(2)}, u32[]{:S(2)}) collective-permute-start(f32[72,512]{1,0:T(8,128)S(1)} %get-tuple-element.54), channel_id=1, source_target_pairs={{4,0},{8,4},{12,8},{16,12},{20,16},{24,20},{28,24},{5,1},{9,5},{13... | collective-permute-start | bytes 442376 | tf_op jit(solution)/shard_map/ppermute | solution.py:684
  29.7 0.0 collective-permute-done.4.lo_ref
  29.7 0.0 collective-permute-done.5.hi_ref
  29.7 2.0 %shard_map.82 = (f32[10,32,512]{2,1,0:T(8,128)S(1)}, f32[10,32,512]{2,1,0:T(8,128)S(1)}, f32[10,32,512]{2,1,0:T(8,128)S(1)}, f32[10,32,512]{2,1,0:T(8,128)S(1)},...) custom-call(f32[3,12]{1,0:T(4,128)S(1)} %copy-done.4, ...), custom_call_target="tpu_custom_call" | custom-call | flops 1000000 | bytes 1000000 | tf_op jit(solution)/shard_map/pallas_call | solution.py:725
  31.7 1.8 %shard_map.83 = (f32[10,32,512]{2,1,0:T(8,128)S(1)}, f32[10,32,512]{2,1,0:T(8,128)S(1)}, f32[10,32,512]{2,1,0:T(8,128)S(1)}, f32[10,32,512]{2,1,0:T(8,128)S(1)},...) custom-call(f32[10,32,512]{2,1,0:T(8,128)S(1)} %get-tuple-element.57, ...), custom_call_target="tpu_custom_call" | custom-call | flops 1000000 | bytes 1000000 | tf_op jit(solution)/shard_map/pallas_call | solution.py:728
  33.5 0.0 collective-permute-done.2.slo_ref
  33.5 1.9 %collective-permute-done.3.shi_ref = f32[72,512]{1,0:T(8,128)S(1)} collective-permute-done((f32[72,512]{1,0:T(8,128)S(1)}, f32[72,512]{1,0:T(8,128)S(1)}, u32[]{:S(2)}, u32[]{:S(2)}) %collective-permute-start.3) | collective-permute-done | bytes 147488 | tf_op jit(solution)/shard_map/ppermute | solution.py:684
  35.4 4.7 %shard_map.84 = (f32[10,32,128]{2,1,0:T(8,128)S(1)}, f32[10,32,128]{2,1,0:T(8,128)S(1)}, f32[10,32,128]{2,1,0:T(8,128)S(1)}, f32[10,32,128]{2,1,0:T(8,128)S(1)},...) custom-call(f32[3,12]{1,0:T(4,128)S(1)} %copy-done.4, ...), custom_call_target="tpu_custom_call" | custom-call | flops 1000000 | bytes 1000000 | tf_op jit(solution)/shard_map/pallas_call | solution.py:731
  40.2 14.5 %all_to_all.15.arrived_ref = f32[32,1,128]{2,1,0:T(1,128)S(1)} all-to-all(f32[32,1,128]{2,1,0:T(1,128)S(1)} %get-tuple-element.71), channel_id=1, replica_groups=mesh['gx'=8,'gy'=4] {'gx','gy'}, dimensions={0} | all-to-all | bytes 32768 | tf_op jit(solution)/shard_map/all_to_all | solution.py:687
  54.6 3.9 %shard_map.85 = (f32[10,16,512]{2,1,0:T(8,128)S(1)}, f32[10,24,640]{2,1,0:T(8,128)S(1)}, f32[10,24,640]{2,1,0:T(8,128)S(1)}, f32[10,24,640]{2,1,0:T(8,128)S(1)}, f32[32,1,128]{2,1,0:T(1,128)S(1)}) custom-call(f32[32,1,128]{2,1,0:T(1,128)S(1)} %all_to_all.15.arrived_ref, f32[10,32,512]{2,1,0:T(8,128)S(1)} %get-tuple-element.57.ext_ref.old_ref, ...), custom_call_target="tpu_custom_call" | custom-call | flops 1000000 | bytes 1000000 | tf_op jit(solution)/shard_map/pallas_call | solution.py:739
  58.6 8.8 %all_to_all.16.arrived_ref = f32[32,1,128]{2,1,0:T(1,128)S(1)} all-to-all(f32[32,1,128]{2,1,0:T(1,128)S(1)} %get-tuple-element.82), channel_id=1, replica_groups=mesh['gx'=8,'gy'=4] {'gx','gy'}, dimensions={0} | all-to-all | bytes 32768 | tf_op jit(solution)/shard_map/all_to_all | solution.py:687
  67.4 1.1 %shard_map.86 = f32[10,16,512]{2,1,0:T(8,128)} custom-call(f32[32,1,128]{2,1,0:T(1,128)S(1)} %all_to_all.16.arrived_ref, f32[10,16,512]{2,1,0:T(8,128)S(1)} %get-tuple-element.83.part_ref, f32[10,24,640]{2,1,0:T(8,128)S(1)} %get-tuple-element.84.q0_ref, f32[10,24,640]{2,1,0:T(8,128)S(1)} %get-tuple-element.85.q1_ref, f32[10,24,640]{2,1,0:T(8,128)S(1)} %get-tuple-element.86.q2_ref), custom_call_target="tpu_custom_call" | custom-call | flops 1000000 | bytes 1000000 | tf_op jit(solution)/shard_map/pallas_call | solution.py:746
  (4 shorter events, 0.0 us)
Async XLA Ops:
  0.6 17.7 %copy-start = (f32[10,16,512]{2,1,0:T(8,128)S(1)}, f32[10,16,512]{2,1,0:T(8,128)}, u32[]{:S(2)}) copy-start(f32[10,16,512]{2,1,0:T(8,128)} %head_ref.7) | copy-start | bytes 983044
  0.6 17.7 %copy-start.1 = (s32[10,16,512]{2,1,0:T(8,128)S(1)}, s32[10,16,512]{2,1,0:T(8,128)}, u32[]{:S(2)}) copy-start(s32[10,16,512]{2,1,0:T(8,128)} %soil_ref.7) | copy-start | bytes 983044
  2.8 15.6 %copy-start.2 = (f32[4,16,512]{2,1,0:T(8,128)S(1)}, f32[4,16,512]{2,1,0:T(8,128)}, u32[]{:S(2)}) copy-start(f32[4,16,512]{2,1,0:T(8,128)} %forcing_ref.3) | copy-start | bytes 393220
  2.8 15.6 %copy-start.3 = (s32[16,512]{1,0:T(8,128)S(1)}, s32[16,512]{1,0:T(8,128)}, u32[]{:S(2)}) copy-start(s32[16,512]{1,0:T(8,128)} %slot_ref.3) | copy-start | bytes 98308
  2.8 15.5 %all-to-all-start = ((f32[32,8,128]{2,1,0:T(8,128)}), f32[32,8,128]{2,1,0:T(8,128)S(1)}, u32[]{:S(2)}, u32[]{:S(2)}) async-start(f32[32,8,128]{2,1,0:T(8,128)} %get-tuple-element.45), calls=%async_computation | async-start | bytes 262144 | tf_op jit(solution)/shard_map/all_to_all | solution.py:687
  10.1 8.3 %copy-start.4 = (f32[3,12]{1,0:T(4,128)S(1)}, f32[3,12]{1,0:T(4,128)}, u32[]{:S(2)}) copy-start(f32[3,12]{1,0:T(4,128)} %table_ref.7) | copy-start | bytes 436
  10.1 19.6 %collective-permute-start.4 = (f32[144,512]{1,0:T(8,128)}, f32[144,512]{1,0:T(8,128)S(1)}, u32[]{:S(2)}, u32[]{:S(2)}) collective-permute-start(f32[144,512]{1,0:T(8,128)} %get-tuple-element.55), channel_id=1, source_target_pairs={{0,4},{4,8},{8,12},{12,16},{16,20},{20,24},{24,28},{1,5},{5,9},{9,... | collective-permute-start | bytes 884744 | tf_op jit(solution)/shard_map/ppermute | solution.py:684
  13.8 15.9 %collective-permute-start.5 = (f32[144,512]{1,0:T(8,128)}, f32[144,512]{1,0:T(8,128)S(1)}, u32[]{:S(2)}, u32[]{:S(2)}) collective-permute-start(f32[144,512]{1,0:T(8,128)} %get-tuple-element.56), channel_id=1, source_target_pairs={{4,0},{8,4},{12,8},{16,12},{20,16},{24,20},{28,24},{5,1},{9,5},{13... | collective-permute-start | bytes 884744 | tf_op jit(solution)/shard_map/ppermute | solution.py:684
  20.4 5.7 %collective-permute-start = (f32[3,16,128]{2,1,0:T(8,128)S(1)}, f32[3,16,128]{2,1,0:T(8,128)S(1)}, u32[]{:S(2)}, u32[]{:S(2)}) collective-permute-start(f32[3,16,128]{2,1,0:T(8,128)S(1)} %get-tuple-element.51), channel_id=1, source_target_pairs={{0,1},{1,2},{2,3},{4,5},{5,6},{6,7},{8,9},{9,10},{10,11},{12,13},{... | collective-permute-start | bytes 73736 | tf_op jit(solution)/shard_map/ppermute | solution.py:684
  22.6 3.5 %collective-permute-start.1 = (f32[3,16,128]{2,1,0:T(8,128)S(1)}, f32[3,16,128]{2,1,0:T(8,128)S(1)}, u32[]{:S(2)}, u32[]{:S(2)}) collective-permute-start(f32[3,16,128]{2,1,0:T(8,128)S(1)} %get-tuple-element.52), channel_id=1, source_target_pairs={{1,0},{2,1},{3,2},{5,4},{6,5},{7,6},{9,8},{10,9},{11,10},{13,12},{... | collective-permute-start | bytes 73736 | tf_op jit(solution)/shard_map/ppermute | solution.py:684
  26.1 7.4 %collective-permute-start.2 = (f32[72,512]{1,0:T(8,128)S(1)}, f32[72,512]{1,0:T(8,128)S(1)}, u32[]{:S(2)}, u32[]{:S(2)}) collective-permute-start(f32[72,512]{1,0:T(8,128)S(1)} %get-tuple-element.53), channel_id=1, source_target_pairs={{0,4},{4,8},{8,12},{12,16},{16,20},{20,24},{24,28},{1,5},{5,9},{9,... | collective-permute-start | bytes 442376 | tf_op jit(solution)/shard_map/ppermute | solution.py:684
  28.4 7.0 %collective-permute-start.3 = (f32[72,512]{1,0:T(8,128)S(1)}, f32[72,512]{1,0:T(8,128)S(1)}, u32[]{:S(2)}, u32[]{:S(2)}) collective-permute-start(f32[72,512]{1,0:T(8,128)S(1)} %get-tuple-element.54), channel_id=1, source_target_pairs={{4,0},{8,4},{12,8},{16,12},{20,16},{24,20},{28,24},{5,1},{9,5},{13... | collective-permute-start | bytes 442376 | tf_op jit(solution)/shard_map/ppermute | solution.py:684

commit v10 on v9

--- a/solution.py
+++ b/solution.py
@@ -258,23 +258,41 @@
     return jnp.concatenate([above, gap, below], axis=0)
 
 
-def strip_kernel(head_ref, soil_ref, some_ref, down_ref, up_ref):
+def strip_kernel(head_ref, soil_ref, some_ref, out_ref):
     layers, _, cols = head_ref.shape
-    for out_ref, (part, shift), at in zip((down_ref, up_ref), strip_parts(cols), (0, LANES)):
-        out_ref[0] = strips([head_ref[k, :, part] for k in range(layers)], shift)
-        out_ref[1] = strips([(soil_ref[k, :, part] + 1).astype(f32) for k in range(layers)], shift)
-        out_ref[2] = strips([some_ref[k, :, at : at + LANES] for k in range(layers)], shift)
-
-
-def source_edge_kernel(src_ref, ylo_ref, yhi_ref, down_ref, up_ref):
+    me = lax.axis_index("gy")
+    blocks = []
+    for (part, shift), at in zip(strip_parts(cols), (0, LANES)):
+        blocks.append(
+            (
+                strips([head_ref[k, :, part] for k in range(layers)], shift),
+                strips([(soil_ref[k, :, part] + 1).astype(f32) for k in range(layers)], shift),
+                strips([some_ref[k, :, at : at + LANES] for k in range(layers)], shift),
+            )
+        )
+    for field, (low, high) in enumerate(zip(*blocks)):
+        for d in range(out_ref.shape[0]):
+            out_ref[d, field] = jnp.where(d < me, low, high)
+
+
+def received(strip_ref, field):
+    me = lax.axis_index("gy")
+    count = strip_ref.shape[0]
+    below = strip_ref[jnp.maximum(me - 1, 0), field]
+    above = strip_ref[jnp.minimum(me + 1, count - 1), field]
+    return jnp.where(me > 0, below, 0.0), jnp.where(me + 1 < count, above, 0.0)
+
+
+def source_edge_kernel(src_ref, strip_ref, down_ref, up_ref):
     layers, rows, _ = src_ref.shape
     at = SOURCE_DEPTH * layers
+    pieces = [x for field in range(3) for x in received(strip_ref, field)]
     for out_ref, first in ((down_ref, 0), (up_ref, rows - HALO)):
         row = 0 if first == 0 else rows - SOURCE_DEPTH
         for k in range(layers):
             part = slice(SOURCE_DEPTH * k, SOURCE_DEPTH * (k + 1))
             out_ref[part] = src_ref[k][row : row + SOURCE_DEPTH]
-        blocks = [ref[f, first : first + HALO] for f in range(3) for ref in (ylo_ref, yhi_ref)]
+        blocks = [x[first : first + HALO] for x in pieces]
         half = HALO // 2
         tail = [block[h : h + half] for block in blocks[4:6] for h in (0, half)]
         for j in range(4):
@@ -294,14 +312,15 @@
     return jnp.concatenate(pieces, axis=0)
 
 
-def tall_strips(layers, ylo_ref, yhi_ref, slo_ref, shi_ref):
+def tall_strips(layers, strip_ref, slo_ref, shi_ref):
     at = SOURCE_DEPTH * layers
     out = []
     for field in range(3):
         pair = []
-        for which, ref in ((1, yhi_ref), (0, ylo_ref)):
+        below, above = received(strip_ref, field)
+        for which, piece in ((1, above), (0, below)):
             ends = [corner(shi_ref, at, field, which), corner(slo_ref, at, field, which)]
-            pair.append(jnp.concatenate([ref[field]] + ends, axis=0))
+            pair.append(jnp.concatenate([piece] + ends, axis=0))
         out.append(pair)
     return out
 
@@ -529,7 +548,7 @@
 
 
 def first_kernel(
-    table_ref, src_ref, slo_ref, shi_ref, ylo_ref, yhi_ref,
+    table_ref, src_ref, slo_ref, shi_ref, strip_ref,
     ext_ref, ks_ref, cond_ref, deriv_ref, water_ref, flow_ref, *rest,
 ):
     mains, rest = rest[:7], rest[7:]
@@ -538,7 +557,7 @@
     diag_first, diag_last, yp_last, ym_first = rest[19:23]
     layers, rows, cols = src_ref.shape
     tables = table_rows(table_ref, rows + 2 * HALO)
-    heads, soils, sources = tall_strips(layers, ylo_ref, yhi_ref, slo_ref, shi_ref)
+    heads, soils, sources = tall_strips(layers, strip_ref, slo_ref, shi_ref)
     start, end, middle = slice(0, LANES), slice(cols - LANES, cols), slice(LANES, cols - LANES)
     lane = lane_iota((rows + 2 * HALO, LANES))
     is_first, is_last = lane == 0, lane == LANES - 1
@@ -712,13 +731,15 @@
         6,
         in_specs=[smem] + [vmem] * 5,
     )(soil_table, arrived, *columns)
-    ydown, yup = call(strip_kernel, [((3, rows, LANES), f32)] * 2, 3)(head_old, soil_type, some)
-    ylo, yhi = exchange(ydown, yup, "gy")
+    (strip,) = call(strip_kernel, [((lax.axis_size("gy"), 3, rows, LANES), f32)], 3)(
+        head_old, soil_type, some
+    )
+    strip = spread(strip, "gy")
     source, flux = call(
         inner_source_kernel, [own, ((2, rows, cols), f32)], 9, in_specs=[smem] + [vmem] * 8
     )(soil_table, tab, factor, *columns, some, flux)
-    sdown, sup = call(source_edge_kernel, [edge(SOURCE_DEPTH * layers + HALO + HALO // 2)] * 2, 3)(
-        source, ylo, yhi
+    sdown, sup = call(source_edge_kernel, [edge(SOURCE_DEPTH * layers + HALO + HALO // 2)] * 2, 2)(
+        source, strip
     )
     slo, shi = exchange(sdown, sup, "gx")
     main, side_block = ((layers, tall, cols), f32), ((layers, tall, LANES), f32)
@@ -731,10 +752,10 @@
     old_s, ks_s, steep_s, cap_s, base, p0, p1, p2, gram = call(
         first_kernel,
         [side_block] * 4 + [ext] * 4 + [gram_block],
-        19,
+        18,
         scratch=[pltpu.VMEM(side_block[0], f32)] * 14,
-        in_specs=[smem] + [vmem] * 18,
-    )(soil_table, source, slo, shi, ylo, yhi, old, ks, cond, deriv, water, flow, *coefs)
+        in_specs=[smem] + [vmem] * 17,
+    )(soil_table, source, slo, shi, strip, old, ks, cond, deriv, water, flow, *coefs)
     sums = spread(gram, both)
     part, q0, q1, q2, gram = call(
         second_kernel,

time: 68.8 us -> 68.6 us (level)
  blocking collectives: 23.3 us -> 20 us
  waiting for transfers between devices: 5.14 us -> 7.41 us
    all_to_all x2, blocking collectives: 23.3 us -> 20 us  [spread(): return lax.all_to_all(x, axes, split_axis=0, concat_axis=0, tiled=True)]
    all_to_all x1 -> x2, starting transfers between devices: 7.3 us -> 10.6 us  [spread(): return lax.all_to_all(x, axes, split_axis=0, concat_axis=0, tiled=True)]
    all_to_all x1 -> x2, waiting for transfers between devices: 3.22 us -> 5.32 us  [spread(): return lax.all_to_all(x, axes, split_axis=0, concat_axis=0, tiled=True)]
    ppermute x3 -> x2, starting transfers between devices: 8.18 us -> 6.37 us  [exchange(): lax.ppermute(to_upper, axis, up)]
    ppermute x3 -> x2, starting transfers between devices: 3.88 us -> 2.58 us  [exchange(): lax.ppermute(to_lower, axis, down)]
    ppermute x3 -> x2, waiting for transfers between devices: 1.91 us -> 2.09 us  [exchange(): lax.ppermute(to_lower, axis, down)]
  transfers between devices with their start and end apart: 7 -> 6, of which waited for: 2 -> 3; matrix products, arithmetic and copies ran while one was open for 0% -> 0% of each run, Pallas kernels for 12% -> 13%
where the time goes in v10:
time: 68.6 us; the launch traced here: 68.2 us
  Pallas kernels  20.4 us (30%)
  blocking collectives  20 us (29%)
  starting transfers between devices  19.6 us (29%)
  waiting for transfers between devices  7.41 us (11%)
  between operations  0.8 us (1%)
    all_to_all x2, blocking collectives, spread(): return lax.all_to_all(x, axes, split_axis=0, concat_axis=0, tiled=True)  20 us
    all_to_all x2, starting transfers between devices, spread(): return lax.all_to_all(x, axes, split_axis=0, concat_axis=0, tiled=True)  10.6 us
    ppermute x2, starting transfers between devices, exchange(): lax.ppermute(to_upper, axis, up)  6.37 us
    all_to_all x2, waiting for transfers between devices, spread(): return lax.all_to_all(x, axes, split_axis=0, concat_axis=0, tiled=True)  5.32 us
    pallas_call x1, Pallas kernels, shards(): call(first_kernel, [side_block] * 4 + [ext] * 4 + [gram_block], 18, scrat...  4.65 us
    pallas_call x1, Pallas kernels, shards(): call(second_kernel, [own] + [((layers, rows + HALO, wide), f32)] * 3 + [g...  3.94 us
    ppermute x2, starting transfers between devices, exchange(): lax.ppermute(to_lower, axis, down)  2.58 us
    pallas_call x1, Pallas kernels, shards(): call(inner_source_kernel, [own, ((2, rows, cols), f32)], 9, in_specs=[sme...  2.16 us
  transfers between devices with their start and end apart: 6, of which 3 were waited for; matrix products, arithmetic and copies ran while one was open for 0% of the time, Pallas kernels for 13%

profile of v10, /device:TPU:0, one launch (start us, length us, event | category | flops | bytes accessed | tf_op | source)
XLA Modules:
  0.0 68.2 jit_solution(13125899782545955549)
XLA Ops:
  0.6 0.0 copy-start
  0.6 0.0 copy-start.1
  0.6 2.1 %shard_map.77 = (f32[32,8,128]{2,1,0:T(8,128)}, f32[144,512]{1,0:T(8,128)}, f32[144,512]{1,0:T(8,128)}) custom-call(f32[13,2048]{1,0:T(8,128)} %canopy_hbm.1, f32[10,16,512]{2,1,0:T(8,128)} %head_ref.7, s32[10,16,512]{2,1,0:T(8,128)} %soil_ref.7), custom_call_target="tpu_custom_call" | custom-call | flops 1000000 | bytes 1000000 | tf_op jit(solution)/shard_map/pallas_call | solution.py:711
  2.7 0.0 copy-start.2
  2.8 0.0 copy-start.3
  2.8 7.3 %all-to-all-start = ((f32[32,8,128]{2,1,0:T(8,128)}), f32[32,8,128]{2,1,0:T(8,128)S(1)}, u32[]{:S(2)}, u32[]{:S(2)}) async-start(f32[32,8,128]{2,1,0:T(8,128)} %get-tuple-element.43), calls=%async_computation | async-start | bytes 262144 | tf_op jit(solution)/shard_map/all_to_all | solution.py:706
  10.1 0.0 copy-start.4
  10.1 3.7 %collective-permute-start.2 = (f32[144,512]{1,0:T(8,128)}, f32[144,512]{1,0:T(8,128)S(1)}, u32[]{:S(2)}, u32[]{:S(2)}) collective-permute-start(f32[144,512]{1,0:T(8,128)} %get-tuple-element.51), channel_id=1, source_target_pairs={{0,4},{4,8},{8,12},{12,16},{16,20},{20,24},{24,28},{1,5},{5,9},{9,... | collective-permute-start | bytes 884744 | tf_op jit(solution)/shard_map/ppermute | solution.py:703
  13.8 1.3 %collective-permute-start.3 = (f32[144,512]{1,0:T(8,128)}, f32[144,512]{1,0:T(8,128)S(1)}, u32[]{:S(2)}, u32[]{:S(2)}) collective-permute-start(f32[144,512]{1,0:T(8,128)} %get-tuple-element.52), channel_id=1, source_target_pairs={{4,0},{8,4},{12,8},{16,12},{20,16},{24,20},{28,24},{5,1},{9,5},{13... | collective-permute-start | bytes 884744 | tf_op jit(solution)/shard_map/ppermute | solution.py:703
  15.1 3.2 %all-to-all-done.arrived_ref = f32[32,8,128]{2,1,0:T(8,128)S(1)} async-done(((f32[32,8,128]{2,1,0:T(8,128)}), f32[32,8,128]{2,1,0:T(8,128)S(1)}, u32[]{:S(2)}, u32[]{:S(2)}) %all-to-all-start) | async-done | bytes 131104 | tf_op jit(solution)/shard_map/all_to_all | solution.py:706
  18.3 0.0 copy-done
  18.3 0.0 copy-done.2
  18.3 0.0 copy-done.3
  18.3 0.0 copy-done.4
  18.3 1.8 %shard_map.78 = (f32[10,16,256]{2,1,0:T(8,128)S(1)}, f32[2,16,256]{2,1,0:T(8,128)S(1)}, s32[16,6,8,128]{3,2,1,0:T(8,128)S(1)}, f32[16,8,128]{2,1,0:T(8,128)S(1)}) custom-call(f32[3,12]{1,0:T(4,128)S(1)} %copy-done.4, f32[32,8,128]{2,1,0:T(8,128)S(1)} %all-to-all-done.arrived_ref, f32[10,16,512]{2,1,0:T(8,128)S(1)} %copy-done, s32[10,16,512]{2,1,0:T(8,128)S(1)} %copy-done.1, ...), custom_call_target="tpu_custom_call" | custom-call | flops 1000000 | bytes 1000000 | tf_op jit(solution)/shard_map/pallas_call | solution.py:728
  20.2 0.8 %shard_map.80 = f32[4,3,16,128]{3,2,1,0:T(8,128)} custom-call(f32[10,16,512]{2,1,0:T(8,128)S(1)} %copy-done, s32[10,16,512]{2,1,0:T(8,128)S(1)} %copy-done.1, f32[10,16,256]{2,1,0:T(8,128)S(1)} %get-tuple-element.46.some_ref), custom_call_target="tpu_custom_call" | custom-call | flops 1000000 | bytes 1000000 | tf_op jit(solution)/shard_map/pallas_call | solution.py:734
  21.0 3.3 %all-to-all-start.1 = ((f32[4,3,16,128]{3,2,1,0:T(8,128)}), f32[4,3,16,128]{3,2,1,0:T(8,128)S(1)}, u32[]{:S(2)}, u32[]{:S(2)}) async-start(f32[4,3,16,128]{3,2,1,0:T(8,128)} %shard_map.80), calls=%async_computation.1 | async-start | bytes 196608 | tf_op jit(solution)/shard_map/all_to_all | solution.py:706
  24.3 2.2 %shard_map.79 = (f32[10,16,512]{2,1,0:T(8,128)S(1)}, f32[2,16,512]{2,1,0:T(8,128)}) custom-call(f32[3,12]{1,0:T(4,128)S(1)} %copy-done.4, s32[16,6,8,128]{3,2,1,0:T(8,128)S(1)} %get-tuple-element.44.tab_ref, f32[16,8,128]{2,1,0:T(8,128)S(1)} %get-tuple-element.45.factor_ref, f32[10,16,512]{2,1,0:T(8,128)S(1)} %copy-done, s32[10,16,512]{2,1,0:T(8,128)S(1)} %copy-done.1, ...), custom_call_target="tpu_custom_call" | custom-call | flops 1000000 | bytes 1000000 | tf_op jit(solution)/shard_map/pallas_call | solution.py:738
  26.5 2.1 %all-to-all-done.1.strip_ref = f32[4,3,16,128]{3,2,1,0:T(8,128)S(1)} async-done(((f32[4,3,16,128]{3,2,1,0:T(8,128)}), f32[4,3,16,128]{3,2,1,0:T(8,128)S(1)}, u32[]{:S(2)}, u32[]{:S(2)}) %all-to-all-start.1) | async-done | bytes 98336 | tf_op jit(solution)/shard_map/all_to_all | solution.py:706
  28.6 2.7 %collective-permute-start = (f32[72,512]{1,0:T(8,128)S(1)}, f32[72,512]{1,0:T(8,128)S(1)}, u32[]{:S(2)}, u32[]{:S(2)}) collective-permute-start(f32[72,512]{1,0:T(8,128)S(1)} %get-tuple-element.49), channel_id=1, source_target_pairs={{0,4},{4,8},{8,12},{12,16},{16,20},{20,24},{24,28},{1,5},{5,9},{9,... | collective-permute-start | bytes 442376 | tf_op jit(solution)/shard_map/ppermute | solution.py:703
  31.3 1.3 %collective-permute-start.1 = (f32[72,512]{1,0:T(8,128)S(1)}, f32[72,512]{1,0:T(8,128)S(1)}, u32[]{:S(2)}, u32[]{:S(2)}) collective-permute-start(f32[72,512]{1,0:T(8,128)S(1)} %get-tuple-element.50), channel_id=1, source_target_pairs={{4,0},{8,4},{12,8},{16,12},{20,16},{24,20},{28,24},{5,1},{9,5},{13... | collective-permute-start | bytes 442376 | tf_op jit(solution)/shard_map/ppermute | solution.py:703
  32.6 0.0 collective-permute-done.2.lo_ref
  32.6 0.0 collective-permute-done.3.hi_ref
  32.6 2.0 %shard_map.82 = (f32[10,32,512]{2,1,0:T(8,128)S(1)}, f32[10,32,512]{2,1,0:T(8,128)S(1)}, f32[10,32,512]{2,1,0:T(8,128)S(1)}, f32[10,32,512]{2,1,0:T(8,128)S(1)},...) custom-call(f32[3,12]{1,0:T(4,128)S(1)} %copy-done.4, ...), custom_call_target="tpu_custom_call" | custom-call | flops 1000000 | bytes 1000000 | tf_op jit(solution)/shard_map/pallas_call | solution.py:746
  34.6 1.8 %shard_map.83 = (f32[10,32,512]{2,1,0:T(8,128)S(1)}, f32[10,32,512]{2,1,0:T(8,128)S(1)}, f32[10,32,512]{2,1,0:T(8,128)S(1)}, f32[10,32,512]{2,1,0:T(8,128)S(1)},...) custom-call(f32[10,32,512]{2,1,0:T(8,128)S(1)} %get-tuple-element.53, ...), custom_call_target="tpu_custom_call" | custom-call | flops 1000000 | bytes 1000000 | tf_op jit(solution)/shard_map/pallas_call | solution.py:749
  36.4 0.0 collective-permute-done.slo_ref
  36.4 2.1 %collective-permute-done.1.shi_ref = f32[72,512]{1,0:T(8,128)S(1)} collective-permute-done((f32[72,512]{1,0:T(8,128)S(1)}, f32[72,512]{1,0:T(8,128)S(1)}, u32[]{:S(2)}, u32[]{:S(2)}) %collective-permute-start.1) | collective-permute-done | bytes 147488 | tf_op jit(solution)/shard_map/ppermute | solution.py:703
  38.5 4.6 %shard_map.84 = (f32[10,32,128]{2,1,0:T(8,128)S(1)}, f32[10,32,128]{2,1,0:T(8,128)S(1)}, f32[10,32,128]{2,1,0:T(8,128)S(1)}, f32[10,32,128]{2,1,0:T(8,128)S(1)},...) custom-call(f32[3,12]{1,0:T(4,128)S(1)} %copy-done.4, ...), custom_call_target="tpu_custom_call" | custom-call | flops 1000000 | bytes 1000000 | tf_op jit(solution)/shard_map/pallas_call | solution.py:752
  43.2 11.2 %all_to_all.20.arrived_ref = f32[32,1,128]{2,1,0:T(1,128)S(1)} all-to-all(f32[32,1,128]{2,1,0:T(1,128)S(1)} %get-tuple-element.67), channel_id=1, replica_groups=mesh['gx'=8,'gy'=4] {'gx','gy'}, dimensions={0} | all-to-all | bytes 32768 | tf_op jit(solution)/shard_map/all_to_all | solution.py:706
  54.3 3.9 %shard_map.85 = (f32[10,16,512]{2,1,0:T(8,128)S(1)}, f32[10,24,640]{2,1,0:T(8,128)S(1)}, f32[10,24,640]{2,1,0:T(8,128)S(1)}, f32[10,24,640]{2,1,0:T(8,128)S(1)}, f32[32,1,128]{2,1,0:T(1,128)S(1)}) custom-call(f32[32,1,128]{2,1,0:T(1,128)S(1)} %all_to_all.20.arrived_ref, f32[10,32,512]{2,1,0:T(8,128)S(1)} %get-tuple-element.53.ext_ref.old_ref, ...), custom_call_target="tpu_custom_call" | custom-call | flops 1000000 | bytes 1000000 | tf_op jit(solution)/shard_map/pallas_call | solution.py:760
  58.3 8.8 %all_to_all.21.arrived_ref = f32[32,1,128]{2,1,0:T(1,128)S(1)} all-to-all(f32[32,1,128]{2,1,0:T(1,128)S(1)} %get-tuple-element.78), channel_id=1, replica_groups=mesh['gx'=8,'gy'=4] {'gx','gy'}, dimensions={0} | all-to-all | bytes 32768 | tf_op jit(solution)/shard_map/all_to_all | solution.py:706
  67.1 1.1 %shard_map.86 = f32[10,16,512]{2,1,0:T(8,128)} custom-call(f32[32,1,128]{2,1,0:T(1,128)S(1)} %all_to_all.21.arrived_ref, f32[10,16,512]{2,1,0:T(8,128)S(1)} %get-tuple-element.79.part_ref, f32[10,24,640]{2,1,0:T(8,128)S(1)} %get-tuple-element.80.q0_ref, f32[10,24,640]{2,1,0:T(8,128)S(1)} %get-tuple-element.81.q1_ref, f32[10,24,640]{2,1,0:T(8,128)S(1)} %get-tuple-element.82.q2_ref), custom_call_target="tpu_custom_call" | custom-call | flops 1000000 | bytes 1000000 | tf_op jit(solution)/shard_map/pallas_call | solution.py:767
  (2 shorter events, 0.0 us)
Async XLA Ops:
  0.6 17.7 %copy-start = (f32[10,16,512]{2,1,0:T(8,128)S(1)}, f32[10,16,512]{2,1,0:T(8,128)}, u32[]{:S(2)}) copy-start(f32[10,16,512]{2,1,0:T(8,128)} %head_ref.7) | copy-start | bytes 983044
  0.6 17.7 %copy-start.1 = (s32[10,16,512]{2,1,0:T(8,128)S(1)}, s32[10,16,512]{2,1,0:T(8,128)}, u32[]{:S(2)}) copy-start(s32[10,16,512]{2,1,0:T(8,128)} %soil_ref.7) | copy-start | bytes 983044
  2.7 15.6 %copy-start.2 = (f32[4,16,512]{2,1,0:T(8,128)S(1)}, f32[4,16,512]{2,1,0:T(8,128)}, u32[]{:S(2)}) copy-start(f32[4,16,512]{2,1,0:T(8,128)} %forcing_ref.3) | copy-start | bytes 393220
  2.8 15.6 %copy-start.3 = (s32[16,512]{1,0:T(8,128)S(1)}, s32[16,512]{1,0:T(8,128)}, u32[]{:S(2)}) copy-start(s32[16,512]{1,0:T(8,128)} %slot_ref.3) | copy-start | bytes 98308
  2.8 15.5 %all-to-all-start = ((f32[32,8,128]{2,1,0:T(8,128)}), f32[32,8,128]{2,1,0:T(8,128)S(1)}, u32[]{:S(2)}, u32[]{:S(2)}) async-start(f32[32,8,128]{2,1,0:T(8,128)} %get-tuple-element.43), calls=%async_computation | async-start | bytes 262144 | tf_op jit(solution)/shard_map/all_to_all | solution.py:706
  10.1 8.3 %copy-start.4 = (f32[3,12]{1,0:T(4,128)S(1)}, f32[3,12]{1,0:T(4,128)}, u32[]{:S(2)}) copy-start(f32[3,12]{1,0:T(4,128)} %table_ref.7) | copy-start | bytes 436
  10.1 22.5 %collective-permute-start.2 = (f32[144,512]{1,0:T(8,128)}, f32[144,512]{1,0:T(8,128)S(1)}, u32[]{:S(2)}, u32[]{:S(2)}) collective-permute-start(f32[144,512]{1,0:T(8,128)} %get-tuple-element.51), channel_id=1, source_target_pairs={{0,4},{4,8},{8,12},{12,16},{16,20},{20,24},{24,28},{1,5},{5,9},{9,... | collective-permute-start | bytes 884744 | tf_op jit(solution)/shard_map/ppermute | solution.py:703
  13.8 18.8 %collective-permute-start.3 = (f32[144,512]{1,0:T(8,128)}, f32[144,512]{1,0:T(8,128)S(1)}, u32[]{:S(2)}, u32[]{:S(2)}) collective-permute-start(f32[144,512]{1,0:T(8,128)} %get-tuple-element.52), channel_id=1, source_target_pairs={{4,0},{8,4},{12,8},{16,12},{20,16},{24,20},{28,24},{5,1},{9,5},{13... | collective-permute-start | bytes 884744 | tf_op jit(solution)/shard_map/ppermute | solution.py:703
  21.0 7.6 %all-to-all-start.1 = ((f32[4,3,16,128]{3,2,1,0:T(8,128)}), f32[4,3,16,128]{3,2,1,0:T(8,128)S(1)}, u32[]{:S(2)}, u32[]{:S(2)}) async-start(f32[4,3,16,128]{3,2,1,0:T(8,128)} %shard_map.80), calls=%async_computation.1 | async-start | bytes 196608 | tf_op jit(solution)/shard_map/all_to_all | solution.py:706
  28.6 7.8 %collective-permute-start = (f32[72,512]{1,0:T(8,128)S(1)}, f32[72,512]{1,0:T(8,128)S(1)}, u32[]{:S(2)}, u32[]{:S(2)}) collective-permute-start(f32[72,512]{1,0:T(8,128)S(1)} %get-tuple-element.49), channel_id=1, source_target_pairs={{0,4},{4,8},{8,12},{12,16},{16,20},{20,24},{24,28},{1,5},{5,9},{9,... | collective-permute-start | bytes 442376 | tf_op jit(solution)/shard_map/ppermute | solution.py:703
  31.3 7.2 %collective-permute-start.1 = (f32[72,512]{1,0:T(8,128)S(1)}, f32[72,512]{1,0:T(8,128)S(1)}, u32[]{:S(2)}, u32[]{:S(2)}) collective-permute-start(f32[72,512]{1,0:T(8,128)S(1)} %get-tuple-element.50), channel_id=1, source_target_pairs={{4,0},{8,4},{12,8},{16,12},{20,16},{24,20},{28,24},{5,1},{9,5},{13... | collective-permute-start | bytes 442376 | tf_op jit(solution)/shard_map/ppermute | solution.py:703

commit v11 on v10

--- a/solution.py
+++ b/solution.py
@@ -44,7 +44,7 @@
 
 
 def pack_kernel(
-    canopy_hbm, head_hbm, soil_hbm, send_ref, down_ref, up_ref, canopy_ref, head_ref, soil_ref, sems
+    canopy_hbm, head_hbm, soil_hbm, send_ref, near_ref, far_ref, canopy_ref, head_ref, soil_ref, sems
 ):
     copies = [
         pltpu.make_async_copy(canopy_hbm, canopy_ref, sems.at[0]),
@@ -65,12 +65,22 @@
     layers, rows, _ = head_ref.shape
     copies[1].wait()
     copies[2].wait()
-    for out_ref, part in ((down_ref, slice(0, STATE_DEPTH)), (up_ref, slice(rows - STATE_DEPTH, rows))):
-        for k in range(layers):
-            out_ref[STATE_DEPTH * k : STATE_DEPTH * (k + 1)] = head_ref[k][part]
-        for k in range(layers):
-            at = STATE_DEPTH * (layers + k)
-            out_ref[at : at + STATE_DEPTH] = (soil_ref[k] + 1).astype(f32)[part]
+    low_rows, high_rows = slice(0, STATE_DEPTH), slice(rows - STATE_DEPTH, rows)
+    upward = near_is_above()
+    for n in range(2 * layers):
+        plane = head_ref[n] if n < layers else (soil_ref[n - layers] + 1).astype(f32)
+        part = slice(STATE_DEPTH * n, STATE_DEPTH * (n + 1))
+        near_ref[part] = jnp.where(upward, plane[high_rows], plane[low_rows])
+        far_ref[part] = jnp.where(upward, plane[low_rows], plane[high_rows])
+
+
+def near_is_above():
+    return lax.rem(lax.axis_index("gx"), 2) == 0
+
+
+def below_above(near, far):
+    upward = near_is_above()
+    return jnp.where(upward, far, near), jnp.where(upward, near, far)
 
 
 def table_rows(table_ref, rows):
@@ -251,9 +261,9 @@
     return ((slice(0, LANES), 0), (slice(cols - LANES, cols), LANES - HALO))
 
 
-def ends_of(lo_ref, hi_ref, at, depth, part):
+def ends_of(near_ref, far_ref, at, depth, part):
     edge = slice(depth * at, depth * (at + 1))
-    above, below = hi_ref[edge, part], lo_ref[edge, part]
+    below, above = below_above(near_ref[edge, part], far_ref[edge, part])
     gap = jnp.zeros((2 * (HALO - depth), above.shape[1]), f32)
     return jnp.concatenate([above, gap, below], axis=0)
 
@@ -283,17 +293,18 @@
     return jnp.where(me > 0, below, 0.0), jnp.where(me + 1 < count, above, 0.0)
 
 
-def source_edge_kernel(src_ref, strip_ref, down_ref, up_ref):
+def source_edge_kernel(src_ref, strip_ref, near_ref, far_ref):
     layers, rows, _ = src_ref.shape
     at = SOURCE_DEPTH * layers
+    half = HALO // 2
+    upward = near_is_above()
     pieces = [x for field in range(3) for x in received(strip_ref, field)]
-    for out_ref, first in ((down_ref, 0), (up_ref, rows - HALO)):
-        row = 0 if first == 0 else rows - SOURCE_DEPTH
+    for out_ref, up in ((near_ref, upward), (far_ref, jnp.logical_not(upward))):
         for k in range(layers):
             part = slice(SOURCE_DEPTH * k, SOURCE_DEPTH * (k + 1))
-            out_ref[part] = src_ref[k][row : row + SOURCE_DEPTH]
-        blocks = [x[first : first + HALO] for x in pieces]
-        half = HALO // 2
+            plane = src_ref[k]
+            out_ref[part] = jnp.where(up, plane[rows - SOURCE_DEPTH :], plane[:SOURCE_DEPTH])
+        blocks = [jnp.where(up, x[rows - HALO :], x[:HALO]) for x in pieces]
         tail = [block[h : h + half] for block in blocks[4:6] for h in (0, half)]
         for j in range(4):
             out_ref[at : at + HALO, j * LANES : (j + 1) * LANES] = blocks[j]
@@ -312,15 +323,17 @@
     return jnp.concatenate(pieces, axis=0)
 
 
-def tall_strips(layers, strip_ref, slo_ref, shi_ref):
+def tall_strips(layers, strip_ref, snear_ref, sfar_ref):
     at = SOURCE_DEPTH * layers
     out = []
     for field in range(3):
         pair = []
         below, above = received(strip_ref, field)
         for which, piece in ((1, above), (0, below)):
-            ends = [corner(shi_ref, at, field, which), corner(slo_ref, at, field, which)]
-            pair.append(jnp.concatenate([piece] + ends, axis=0))
+            lower, upper = below_above(
+                corner(snear_ref, at, field, which), corner(sfar_ref, at, field, which)
+            )
+            pair.append(jnp.concatenate([piece, upper, lower], axis=0))
         out.append(pair)
     return out
 
@@ -512,16 +525,16 @@
 
 
 def state_kernel(
-    table_ref, head_ref, soil_ref, lo_ref, hi_ref,
+    table_ref, head_ref, soil_ref, near_ref, far_ref,
     ext_ref, ks_ref, steep_ref, cap_ref, cond_ref, deriv_ref, store_ref, water_ref,
 ):
     layers, rows, cols = head_ref.shape
     tables = table_rows(table_ref, rows + 2 * HALO)
     every = slice(0, cols)
     for k in range(layers):
-        ends = ends_of(lo_ref, hi_ref, k, STATE_DEPTH, every)
+        ends = ends_of(near_ref, far_ref, k, STATE_DEPTH, every)
         head = jnp.concatenate([head_ref[k], ends], axis=0)
-        ends = ends_of(lo_ref, hi_ref, layers + k, STATE_DEPTH, every)
+        ends = ends_of(near_ref, far_ref, layers + k, STATE_DEPTH, every)
         index = jnp.concatenate([soil_ref[k] + 1, ends.astype(jnp.int32)], axis=0)
         conduct, steep, capacity = (lookup(row, index) for row in tables)
         values = (head, conduct, steep, capacity) + pointwise(head, conduct, steep, capacity)
@@ -548,7 +561,7 @@
 
 
 def first_kernel(
-    table_ref, src_ref, slo_ref, shi_ref, strip_ref,
+    table_ref, src_ref, snear_ref, sfar_ref, strip_ref,
     ext_ref, ks_ref, cond_ref, deriv_ref, water_ref, flow_ref, *rest,
 ):
     mains, rest = rest[:7], rest[7:]
@@ -557,13 +570,13 @@
     diag_first, diag_last, yp_last, ym_first = rest[19:23]
     layers, rows, cols = src_ref.shape
     tables = table_rows(table_ref, rows + 2 * HALO)
-    heads, soils, sources = tall_strips(layers, strip_ref, slo_ref, shi_ref)
+    heads, soils, sources = tall_strips(layers, strip_ref, snear_ref, sfar_ref)
     start, end, middle = slice(0, LANES), slice(cols - LANES, cols), slice(LANES, cols - LANES)
     lane = lane_iota((rows + 2 * HALO, LANES))
     is_first, is_last = lane == 0, lane == LANES - 1
 
     def source_of(k):
-        ends = ends_of(slo_ref, shi_ref, k, SOURCE_DEPTH, slice(0, cols))
+        ends = ends_of(snear_ref, sfar_ref, k, SOURCE_DEPTH, slice(0, cols))
         return jnp.concatenate([src_ref[k], ends], axis=0)
 
     for k in range(layers):
@@ -696,11 +709,14 @@
     own, ext = ((layers, rows, cols), f32), ((layers, tall, wide), f32)
     gram_block = ((devices, 1, LANES), f32)
 
-    def exchange(to_lower, to_upper, axis):
-        size = lax.axis_size(axis)
-        up = [(i, i + 1) for i in range(size - 1)]
-        down = [(j, i) for i, j in up]
-        return lax.ppermute(to_upper, axis, up), lax.ppermute(to_lower, axis, down)
+    def exchange(to_near, to_far):
+        size = lax.axis_size("gx")
+        near = [(i, i + 1) for i in range(0, size - 1, 2)]
+        far = [(i, i + 1) for i in range(1, size - 1, 2)]
+        return tuple(
+            lax.ppermute(x, "gx", pairs + [(j, i) for i, j in pairs])
+            for x, pairs in ((to_near, near), (to_far, far))
+        )
 
     def spread(x, axes):
         return lax.all_to_all(x, axes, split_axis=0, concat_axis=0, tiled=True)
@@ -708,7 +724,7 @@
     def edge(count):
         return (-(-count // 8) * 8, cols), f32
 
-    send, down, up = call(
+    send, to_near, to_far = call(
         pack_kernel,
         [((devices, 8, LANES), f32)] + [edge(2 * STATE_DEPTH * layers)] * 2,
         3,
@@ -722,7 +738,7 @@
         grant=63400000,
     )(canopy, head_old, soil_type)
     arrived = spread(send, both)
-    lo, hi = exchange(down, up, "gx")
+    near, far = exchange(to_near, to_far)
     columns = (head_old, soil_type, forcing, column_slot)
     table = ((devices // 2, -(-layers // 2) + 1, 8, LANES), jnp.int32)
     some, flux, tab, factor = call(
@@ -738,14 +754,14 @@
     source, flux = call(
         inner_source_kernel, [own, ((2, rows, cols), f32)], 9, in_specs=[smem] + [vmem] * 8
     )(soil_table, tab, factor, *columns, some, flux)
-    sdown, sup = call(source_edge_kernel, [edge(SOURCE_DEPTH * layers + HALO + HALO // 2)] * 2, 2)(
+    to_near, to_far = call(source_edge_kernel, [edge(SOURCE_DEPTH * layers + HALO + HALO // 2)] * 2, 2)(
         source, strip
     )
-    slo, shi = exchange(sdown, sup, "gx")
+    snear, sfar = exchange(to_near, to_far)
     main, side_block = ((layers, tall, cols), f32), ((layers, tall, LANES), f32)
     old, ks, steep, cap, cond, deriv, store, water = call(
         state_kernel, [main] * 8, 5, in_specs=[smem] + [vmem] * 4
-    )(soil_table, head_old, soil_type, lo, hi)
+    )(soil_table, head_old, soil_type, near, far)
     flow, *coefs = call(functools.partial(flow_kernel, rows=rows), [main] * 8, 5)(
         old, ks, cond, deriv, store
     )
@@ -755,7 +771,7 @@
         18,
         scratch=[pltpu.VMEM(side_block[0], f32)] * 14,
         in_specs=[smem] + [vmem] * 17,
-    )(soil_table, source, slo, shi, strip, old, ks, cond, deriv, water, flow, *coefs)
+    )(soil_table, source, snear, sfar, strip, old, ks, cond, deriv, water, flow, *coefs)
     sums = spread(gram, both)
     part, q0, q1, q2, gram = call(
         second_kernel,

time: 68.6 us -> 65.3 us (0.952)
  starting transfers between devices: 19.6 us -> 14.5 us
  blocking collectives: 20 us -> 21.1 us
    ppermute x4, starting transfers between devices: 8.95 us -> 3.93 us  [exchange(): lax.ppermute(x, 'gx', pairs + [(j, i) for i, j in pairs])]
    all_to_all x2, waiting for transfers between devices: 5.32 us -> 7.9 us  [spread(): return lax.all_to_all(x, axes, split_axis=0, concat_axis=0, tiled=True)]
    ppermute x4, waiting for transfers between devices: 2.1 us -> 0.13 us  [exchange(): lax.ppermute(x, 'gx', pairs + [(j, i) for i, j in pairs])]
    all_to_all x2, blocking collectives: 20 us -> 21.1 us  [spread(): return lax.all_to_all(x, axes, split_axis=0, concat_axis=0, tiled=True)]
where the time goes in v11:
time: 65.3 us; the launch traced here: 64.9 us
  blocking collectives  21.1 us (32%)
  Pallas kernels  20.5 us (31%)
  starting transfers between devices  14.5 us (22%)
  waiting for transfers between devices  8.03 us (12%)
  between operations  0.78 us (1%)
    all_to_all x2, blocking collectives, spread(): return lax.all_to_all(x, axes, split_axis=0, concat_axis=0, tiled=True)  21.1 us
    all_to_all x2, starting transfers between devices, spread(): return lax.all_to_all(x, axes, split_axis=0, concat_axis=0, tiled=True)  10.6 us
    all_to_all x2, waiting for transfers between devices, spread(): return lax.all_to_all(x, axes, split_axis=0, concat_axis=0, tiled=True)  7.9 us
    pallas_call x1, Pallas kernels, shards(): call(first_kernel, [side_block] * 4 + [ext] * 4 + [gram_block], 18, scrat...  4.68 us
    pallas_call x1, Pallas kernels, shards(): call(second_kernel, [own] + [((layers, rows + HALO, wide), f32)] * 3 + [g...  3.94 us
    ppermute x4, starting transfers between devices, exchange(): lax.ppermute(x, 'gx', pairs + [(j, i) for i, j in pairs])  3.93 us
    pallas_call x1, Pallas kernels, shards(): call(inner_source_kernel, [own, ((2, rows, cols), f32)], 9, in_specs=[sme...  2.16 us
    pallas_call x1, Pallas kernels, shards(): call(pack_kernel, [((devices, 8, LANES), f32)] + [edge(2 * STATE_DEPTH *...  2.11 us
  transfers between devices with their start and end apart: 6, of which 3 were waited for; matrix products, arithmetic and copies ran while one was open for 0% of the time, Pallas kernels for 13%

profile of v11, /device:TPU:0, one launch (start us, length us, event | category | flops | bytes accessed | tf_op | source)
XLA Modules:
  0.0 64.9 jit_solution(10245426981360070732)
XLA Ops:
  0.6 0.0 copy-start
  0.6 0.0 copy-start.1
  0.6 2.1 %shard_map.77 = (f32[32,8,128]{2,1,0:T(8,128)}, f32[144,512]{1,0:T(8,128)}, f32[144,512]{1,0:T(8,128)}) custom-call(f32[13,2048]{1,0:T(8,128)} %canopy_hbm.1, f32[10,16,512]{2,1,0:T(8,128)} %head_ref.7, s32[10,16,512]{2,1,0:T(8,128)} %soil_ref.7), custom_call_target="tpu_custom_call" | custom-call | flops 1000000 | bytes 1000000 | tf_op jit(solution)/shard_map/pallas_call | solution.py:727
  2.8 0.0 copy-start.2
  2.8 0.0 copy-start.3
  2.8 7.3 %all-to-all-start = ((f32[32,8,128]{2,1,0:T(8,128)}), f32[32,8,128]{2,1,0:T(8,128)S(1)}, u32[]{:S(2)}, u32[]{:S(2)}) async-start(f32[32,8,128]{2,1,0:T(8,128)} %get-tuple-element.43), calls=%async_computation | async-start | bytes 262144 | tf_op jit(solution)/shard_map/all_to_all | solution.py:722
  10.1 0.0 copy-start.4
  10.1 1.8 %collective-permute-start.2 = (f32[144,512]{1,0:T(8,128)}, f32[144,512]{1,0:T(8,128)S(1)}, u32[]{:S(2)}, u32[]{:S(2)}) collective-permute-start(f32[144,512]{1,0:T(8,128)} %get-tuple-element.51), channel_id=1, source_target_pairs={{0,4},{8,12},{16,20},{24,28},{4,0},{12,8},{20,16},{28,24},{1,5},{9... | collective-permute-start | bytes 884744 | tf_op jit(solution)/shard_map/ppermute | solution.py:717
  11.9 0.7 %collective-permute-start.3 = (f32[144,512]{1,0:T(8,128)}, f32[144,512]{1,0:T(8,128)S(1)}, u32[]{:S(2)}, u32[]{:S(2)}) collective-permute-start(f32[144,512]{1,0:T(8,128)} %get-tuple-element.52), channel_id=1, source_target_pairs={{4,8},{12,16},{20,24},{8,4},{16,12},{24,20},{5,9},{13,17},{21,25},... | collective-permute-start | bytes 884744 | tf_op jit(solution)/shard_map/ppermute | solution.py:717
  12.6 5.8 %all-to-all-done.arrived_ref = f32[32,8,128]{2,1,0:T(8,128)S(1)} async-done(((f32[32,8,128]{2,1,0:T(8,128)}), f32[32,8,128]{2,1,0:T(8,128)S(1)}, u32[]{:S(2)}, u32[]{:S(2)}) %all-to-all-start) | async-done | bytes 131104 | tf_op jit(solution)/shard_map/all_to_all | solution.py:722
  18.4 0.0 copy-done.2
  18.4 0.0 copy-done.3
  18.5 0.0 copy-done.4
  18.5 1.8 %shard_map.78 = (f32[10,16,256]{2,1,0:T(8,128)S(1)}, f32[2,16,256]{2,1,0:T(8,128)S(1)}, s32[16,6,8,128]{3,2,1,0:T(8,128)S(1)}, f32[16,8,128]{2,1,0:T(8,128)S(1)}) custom-call(f32[3,12]{1,0:T(4,128)S(1)} %copy-done.4, f32[32,8,128]{2,1,0:T(8,128)S(1)} %all-to-all-done.arrived_ref, f32[10,16,512]{2,1,0:T(8,128)S(1)} %copy-done, s32[10,16,512]{2,1,0:T(8,128)S(1)} %copy-done.1, ...), custom_call_target="tpu_custom_call" | custom-call | flops 1000000 | bytes 1000000 | tf_op jit(solution)/shard_map/pallas_call | solution.py:744
  20.3 0.8 %shard_map.80 = f32[4,3,16,128]{3,2,1,0:T(8,128)} custom-call(f32[10,16,512]{2,1,0:T(8,128)S(1)} %copy-done, s32[10,16,512]{2,1,0:T(8,128)S(1)} %copy-done.1, f32[10,16,256]{2,1,0:T(8,128)S(1)} %get-tuple-element.46.some_ref), custom_call_target="tpu_custom_call" | custom-call | flops 1000000 | bytes 1000000 | tf_op jit(solution)/shard_map/pallas_call | solution.py:750
  21.1 3.3 %all-to-all-start.1 = ((f32[4,3,16,128]{3,2,1,0:T(8,128)}), f32[4,3,16,128]{3,2,1,0:T(8,128)S(1)}, u32[]{:S(2)}, u32[]{:S(2)}) async-start(f32[4,3,16,128]{3,2,1,0:T(8,128)} %shard_map.80), calls=%async_computation.1 | async-start | bytes 196608 | tf_op jit(solution)/shard_map/all_to_all | solution.py:722
  24.4 2.2 %shard_map.79 = (f32[10,16,512]{2,1,0:T(8,128)S(1)}, f32[2,16,512]{2,1,0:T(8,128)}) custom-call(f32[3,12]{1,0:T(4,128)S(1)} %copy-done.4, s32[16,6,8,128]{3,2,1,0:T(8,128)S(1)} %get-tuple-element.44.tab_ref, f32[16,8,128]{2,1,0:T(8,128)S(1)} %get-tuple-element.45.factor_ref, f32[10,16,512]{2,1,0:T(8,128)S(1)} %copy-done, s32[10,16,512]{2,1,0:T(8,128)S(1)} %copy-done.1, ...), custom_call_target="tpu_custom_call" | custom-call | flops 1000000 | bytes 1000000 | tf_op jit(solution)/shard_map/pallas_call | solution.py:754
  26.6 2.1 %all-to-all-done.1.strip_ref = f32[4,3,16,128]{3,2,1,0:T(8,128)S(1)} async-done(((f32[4,3,16,128]{3,2,1,0:T(8,128)}), f32[4,3,16,128]{3,2,1,0:T(8,128)S(1)}, u32[]{:S(2)}, u32[]{:S(2)}) %all-to-all-start.1) | async-done | bytes 98336 | tf_op jit(solution)/shard_map/all_to_all | solution.py:722
  28.7 0.1 shard_map.81
  28.8 0.8 %collective-permute-start = (f32[72,512]{1,0:T(8,128)S(1)}, f32[72,512]{1,0:T(8,128)S(1)}, u32[]{:S(2)}, u32[]{:S(2)}) collective-permute-start(f32[72,512]{1,0:T(8,128)S(1)} %get-tuple-element.49), channel_id=1, source_target_pairs={{0,4},{8,12},{16,20},{24,28},{4,0},{12,8},{20,16},{28,24},{1,5},{9... | collective-permute-start | bytes 442376 | tf_op jit(solution)/shard_map/ppermute | solution.py:717
  29.5 0.7 %collective-permute-start.1 = (f32[72,512]{1,0:T(8,128)S(1)}, f32[72,512]{1,0:T(8,128)S(1)}, u32[]{:S(2)}, u32[]{:S(2)}) collective-permute-start(f32[72,512]{1,0:T(8,128)S(1)} %get-tuple-element.50), channel_id=1, source_target_pairs={{4,8},{12,16},{20,24},{8,4},{16,12},{24,20},{5,9},{13,17},{21,25},... | collective-permute-start | bytes 442376 | tf_op jit(solution)/shard_map/ppermute | solution.py:717
  30.2 0.0 collective-permute-done.2.near_ref
  30.2 0.0 collective-permute-done.3.far_ref
  30.2 2.0 %shard_map.82 = (f32[10,32,512]{2,1,0:T(8,128)S(1)}, f32[10,32,512]{2,1,0:T(8,128)S(1)}, f32[10,32,512]{2,1,0:T(8,128)S(1)}, f32[10,32,512]{2,1,0:T(8,128)S(1)},...) custom-call(f32[3,12]{1,0:T(4,128)S(1)} %copy-done.4, ...), custom_call_target="tpu_custom_call" | custom-call | flops 1000000 | bytes 1000000 | tf_op jit(solution)/shard_map/pallas_call | solution.py:762
  32.2 1.8 %shard_map.83 = (f32[10,32,512]{2,1,0:T(8,128)S(1)}, f32[10,32,512]{2,1,0:T(8,128)S(1)}, f32[10,32,512]{2,1,0:T(8,128)S(1)}, f32[10,32,512]{2,1,0:T(8,128)S(1)},...) custom-call(f32[10,32,512]{2,1,0:T(8,128)S(1)} %get-tuple-element.53, ...), custom_call_target="tpu_custom_call" | custom-call | flops 1000000 | bytes 1000000 | tf_op jit(solution)/shard_map/pallas_call | solution.py:765
  34.0 0.1 collective-permute-done.snear_ref
  34.1 0.0 collective-permute-done.1.sfar_ref
  34.1 4.7 %shard_map.84 = (f32[10,32,128]{2,1,0:T(8,128)S(1)}, f32[10,32,128]{2,1,0:T(8,128)S(1)}, f32[10,32,128]{2,1,0:T(8,128)S(1)}, f32[10,32,128]{2,1,0:T(8,128)S(1)},...) custom-call(f32[3,12]{1,0:T(4,128)S(1)} %copy-done.4, ...), custom_call_target="tpu_custom_call" | custom-call | flops 1000000 | bytes 1000000 | tf_op jit(solution)/shard_map/pallas_call | solution.py:768
  38.8 12.3 %all_to_all.20.arrived_ref = f32[32,1,128]{2,1,0:T(1,128)S(1)} all-to-all(f32[32,1,128]{2,1,0:T(1,128)S(1)} %get-tuple-element.67), channel_id=1, replica_groups=mesh['gx'=8,'gy'=4] {'gx','gy'}, dimensions={0} | all-to-all | bytes 32768 | tf_op jit(solution)/shard_map/all_to_all | solution.py:722
  51.1 3.9 %shard_map.85 = (f32[10,16,512]{2,1,0:T(8,128)S(1)}, f32[10,24,640]{2,1,0:T(8,128)S(1)}, f32[10,24,640]{2,1,0:T(8,128)S(1)}, f32[10,24,640]{2,1,0:T(8,128)S(1)}, f32[32,1,128]{2,1,0:T(1,128)S(1)}) custom-call(f32[32,1,128]{2,1,0:T(1,128)S(1)} %all_to_all.20.arrived_ref, f32[10,32,512]{2,1,0:T(8,128)S(1)} %get-tuple-element.53.ext_ref.old_ref, ...), custom_call_target="tpu_custom_call" | custom-call | flops 1000000 | bytes 1000000 | tf_op jit(solution)/shard_map/pallas_call | solution.py:776
  55.0 8.8 %all_to_all.21.arrived_ref = f32[32,1,128]{2,1,0:T(1,128)S(1)} all-to-all(f32[32,1,128]{2,1,0:T(1,128)S(1)} %get-tuple-element.78), channel_id=1, replica_groups=mesh['gx'=8,'gy'=4] {'gx','gy'}, dimensions={0} | all-to-all | bytes 32768 | tf_op jit(solution)/shard_map/all_to_all | solution.py:722
  63.9 1.1 %shard_map.86 = f32[10,16,512]{2,1,0:T(8,128)} custom-call(f32[32,1,128]{2,1,0:T(1,128)S(1)} %all_to_all.21.arrived_ref, f32[10,16,512]{2,1,0:T(8,128)S(1)} %get-tuple-element.79.part_ref, f32[10,24,640]{2,1,0:T(8,128)S(1)} %get-tuple-element.80.q0_ref, f32[10,24,640]{2,1,0:T(8,128)S(1)} %get-tuple-element.81.q1_ref, f32[10,24,640]{2,1,0:T(8,128)S(1)} %get-tuple-element.82.q2_ref), custom_call_target="tpu_custom_call" | custom-call | flops 1000000 | bytes 1000000 | tf_op jit(solution)/shard_map/pallas_call | solution.py:783
  (2 shorter events, 0.0 us)
Async XLA Ops:
  0.6 17.8 %copy-start = (f32[10,16,512]{2,1,0:T(8,128)S(1)}, f32[10,16,512]{2,1,0:T(8,128)}, u32[]{:S(2)}) copy-start(f32[10,16,512]{2,1,0:T(8,128)} %head_ref.7) | copy-start | bytes 983044
  0.6 17.8 %copy-start.1 = (s32[10,16,512]{2,1,0:T(8,128)S(1)}, s32[10,16,512]{2,1,0:T(8,128)}, u32[]{:S(2)}) copy-start(s32[10,16,512]{2,1,0:T(8,128)} %soil_ref.7) | copy-start | bytes 983044
  2.8 15.7 %copy-start.2 = (f32[4,16,512]{2,1,0:T(8,128)S(1)}, f32[4,16,512]{2,1,0:T(8,128)}, u32[]{:S(2)}) copy-start(f32[4,16,512]{2,1,0:T(8,128)} %forcing_ref.3) | copy-start | bytes 393220
  2.8 15.7 %copy-start.3 = (s32[16,512]{1,0:T(8,128)S(1)}, s32[16,512]{1,0:T(8,128)}, u32[]{:S(2)}) copy-start(s32[16,512]{1,0:T(8,128)} %slot_ref.3) | copy-start | bytes 98308
  2.8 15.6 %all-to-all-start = ((f32[32,8,128]{2,1,0:T(8,128)}), f32[32,8,128]{2,1,0:T(8,128)S(1)}, u32[]{:S(2)}, u32[]{:S(2)}) async-start(f32[32,8,128]{2,1,0:T(8,128)} %get-tuple-element.43), calls=%async_computation | async-start | bytes 262144 | tf_op jit(solution)/shard_map/all_to_all | solution.py:722
  10.1 8.4 %copy-start.4 = (f32[3,12]{1,0:T(4,128)S(1)}, f32[3,12]{1,0:T(4,128)}, u32[]{:S(2)}) copy-start(f32[3,12]{1,0:T(4,128)} %table_ref.7) | copy-start | bytes 436
  10.1 20.1 %collective-permute-start.2 = (f32[144,512]{1,0:T(8,128)}, f32[144,512]{1,0:T(8,128)S(1)}, u32[]{:S(2)}, u32[]{:S(2)}) collective-permute-start(f32[144,512]{1,0:T(8,128)} %get-tuple-element.51), channel_id=1, source_target_pairs={{0,4},{8,12},{16,20},{24,28},{4,0},{12,8},{20,16},{28,24},{1,5},{9... | collective-permute-start | bytes 884744 | tf_op jit(solution)/shard_map/ppermute | solution.py:717
  11.9 18.3 %collective-permute-start.3 = (f32[144,512]{1,0:T(8,128)}, f32[144,512]{1,0:T(8,128)S(1)}, u32[]{:S(2)}, u32[]{:S(2)}) collective-permute-start(f32[144,512]{1,0:T(8,128)} %get-tuple-element.52), channel_id=1, source_target_pairs={{4,8},{12,16},{20,24},{8,4},{16,12},{24,20},{5,9},{13,17},{21,25},... | collective-permute-start | bytes 884744 | tf_op jit(solution)/shard_map/ppermute | solution.py:717
  21.1 7.6 %all-to-all-start.1 = ((f32[4,3,16,128]{3,2,1,0:T(8,128)}), f32[4,3,16,128]{3,2,1,0:T(8,128)S(1)}, u32[]{:S(2)}, u32[]{:S(2)}) async-start(f32[4,3,16,128]{3,2,1,0:T(8,128)} %shard_map.80), calls=%async_computation.1 | async-start | bytes 196608 | tf_op jit(solution)/shard_map/all_to_all | solution.py:722
  28.8 5.4 %collective-permute-start = (f32[72,512]{1,0:T(8,128)S(1)}, f32[72,512]{1,0:T(8,128)S(1)}, u32[]{:S(2)}, u32[]{:S(2)}) collective-permute-start(f32[72,512]{1,0:T(8,128)S(1)} %get-tuple-element.49), channel_id=1, source_target_pairs={{0,4},{8,12},{16,20},{24,28},{4,0},{12,8},{20,16},{28,24},{1,5},{9... | collective-permute-start | bytes 442376 | tf_op jit(solution)/shard_map/ppermute | solution.py:717
  29.5 4.6 %collective-permute-start.1 = (f32[72,512]{1,0:T(8,128)S(1)}, f32[72,512]{1,0:T(8,128)S(1)}, u32[]{:S(2)}, u32[]{:S(2)}) collective-permute-start(f32[72,512]{1,0:T(8,128)S(1)} %get-tuple-element.50), channel_id=1, source_target_pairs={{4,8},{12,16},{20,24},{8,4},{16,12},{24,20},{5,9},{13,17},{21,25},... | collective-permute-start | bytes 442376 | tf_op jit(solution)/shard_map/ppermute | solution.py:717

commit v12 on v11

--- a/solution.py
+++ b/solution.py
@@ -66,7 +66,7 @@
     copies[1].wait()
     copies[2].wait()
     low_rows, high_rows = slice(0, STATE_DEPTH), slice(rows - STATE_DEPTH, rows)
-    upward = near_is_above()
+    upward = near_is_above("gx")
     for n in range(2 * layers):
         plane = head_ref[n] if n < layers else (soil_ref[n - layers] + 1).astype(f32)
         part = slice(STATE_DEPTH * n, STATE_DEPTH * (n + 1))
@@ -74,12 +74,12 @@
         far_ref[part] = jnp.where(upward, plane[low_rows], plane[high_rows])
 
 
-def near_is_above():
-    return lax.rem(lax.axis_index("gx"), 2) == 0
-
-
-def below_above(near, far):
-    upward = near_is_above()
+def near_is_above(axis):
+    return lax.rem(lax.axis_index(axis), 2) == 0
+
+
+def below_above(near, far, axis):
+    upward = near_is_above(axis)
     return jnp.where(upward, far, near), jnp.where(upward, near, far)
 
 
@@ -263,14 +263,14 @@
 
 def ends_of(near_ref, far_ref, at, depth, part):
     edge = slice(depth * at, depth * (at + 1))
-    below, above = below_above(near_ref[edge, part], far_ref[edge, part])
+    below, above = below_above(near_ref[edge, part], far_ref[edge, part], "gx")
     gap = jnp.zeros((2 * (HALO - depth), above.shape[1]), f32)
     return jnp.concatenate([above, gap, below], axis=0)
 
 
-def strip_kernel(head_ref, soil_ref, some_ref, out_ref):
+def strip_kernel(head_ref, soil_ref, some_ref, near_ref, far_ref):
     layers, _, cols = head_ref.shape
-    me = lax.axis_index("gy")
+    upward = near_is_above("gy")
     blocks = []
     for (part, shift), at in zip(strip_parts(cols), (0, LANES)):
         blocks.append(
@@ -281,24 +281,16 @@
             )
         )
     for field, (low, high) in enumerate(zip(*blocks)):
-        for d in range(out_ref.shape[0]):
-            out_ref[d, field] = jnp.where(d < me, low, high)
-
-
-def received(strip_ref, field):
-    me = lax.axis_index("gy")
-    count = strip_ref.shape[0]
-    below = strip_ref[jnp.maximum(me - 1, 0), field]
-    above = strip_ref[jnp.minimum(me + 1, count - 1), field]
-    return jnp.where(me > 0, below, 0.0), jnp.where(me + 1 < count, above, 0.0)
-
-
-def source_edge_kernel(src_ref, strip_ref, near_ref, far_ref):
+        near_ref[field] = jnp.where(upward, high, low)
+        far_ref[field] = jnp.where(upward, low, high)
+
+
+def source_edge_kernel(src_ref, ynear_ref, yfar_ref, near_ref, far_ref):
     layers, rows, _ = src_ref.shape
     at = SOURCE_DEPTH * layers
     half = HALO // 2
-    upward = near_is_above()
-    pieces = [x for field in range(3) for x in received(strip_ref, field)]
+    upward = near_is_above("gx")
+    pieces = [x for field in range(3) for x in below_above(ynear_ref[field], yfar_ref[field], "gy")]
     for out_ref, up in ((near_ref, upward), (far_ref, jnp.logical_not(upward))):
         for k in range(layers):
             part = slice(SOURCE_DEPTH * k, SOURCE_DEPTH * (k + 1))
@@ -323,15 +315,15 @@
     return jnp.concatenate(pieces, axis=0)
 
 
-def tall_strips(layers, strip_ref, snear_ref, sfar_ref):
+def tall_strips(layers, ynear_ref, yfar_ref, snear_ref, sfar_ref):
     at = SOURCE_DEPTH * layers
     out = []
     for field in range(3):
         pair = []
-        below, above = received(strip_ref, field)
+        below, above = below_above(ynear_ref[field], yfar_ref[field], "gy")
         for which, piece in ((1, above), (0, below)):
             lower, upper = below_above(
-                corner(snear_ref, at, field, which), corner(sfar_ref, at, field, which)
+                corner(snear_ref, at, field, which), corner(sfar_ref, at, field, which), "gx"
             )
             pair.append(jnp.concatenate([piece, upper, lower], axis=0))
         out.append(pair)
@@ -561,7 +553,7 @@
 
 
 def first_kernel(
-    table_ref, src_ref, snear_ref, sfar_ref, strip_ref,
+    table_ref, src_ref, snear_ref, sfar_ref, ynear_ref, yfar_ref,
     ext_ref, ks_ref, cond_ref, deriv_ref, water_ref, flow_ref, *rest,
 ):
     mains, rest = rest[:7], rest[7:]
@@ -570,7 +562,7 @@
     diag_first, diag_last, yp_last, ym_first = rest[19:23]
     layers, rows, cols = src_ref.shape
     tables = table_rows(table_ref, rows + 2 * HALO)
-    heads, soils, sources = tall_strips(layers, strip_ref, snear_ref, sfar_ref)
+    heads, soils, sources = tall_strips(layers, ynear_ref, yfar_ref, snear_ref, sfar_ref)
     start, end, middle = slice(0, LANES), slice(cols - LANES, cols), slice(LANES, cols - LANES)
     lane = lane_iota((rows + 2 * HALO, LANES))
     is_first, is_last = lane == 0, lane == LANES - 1
@@ -709,12 +701,12 @@
     own, ext = ((layers, rows, cols), f32), ((layers, tall, wide), f32)
     gram_block = ((devices, 1, LANES), f32)
 
-    def exchange(to_near, to_far):
-        size = lax.axis_size("gx")
+    def exchange(to_near, to_far, axis):
+        size = lax.axis_size(axis)
         near = [(i, i + 1) for i in range(0, size - 1, 2)]
         far = [(i, i + 1) for i in range(1, size - 1, 2)]
         return tuple(
-            lax.ppermute(x, "gx", pairs + [(j, i) for i, j in pairs])
+            lax.ppermute(x, axis, pairs + [(j, i) for i, j in pairs])
             for x, pairs in ((to_near, near), (to_far, far))
         )
 
@@ -738,7 +730,7 @@
         grant=63400000,
     )(canopy, head_old, soil_type)
     arrived = spread(send, both)
-    near, far = exchange(to_near, to_far)
+    near, far = exchange(to_near, to_far, "gx")
     columns = (head_old, soil_type, forcing, column_slot)
     table = ((devices // 2, -(-layers // 2) + 1, 8, LANES), jnp.int32)
     some, flux, tab, factor = call(
@@ -747,17 +739,15 @@
         6,
         in_specs=[smem] + [vmem] * 5,
     )(soil_table, arrived, *columns)
-    (strip,) = call(strip_kernel, [((lax.axis_size("gy"), 3, rows, LANES), f32)], 3)(
-        head_old, soil_type, some
-    )
-    strip = spread(strip, "gy")
+    to_near, to_far = call(strip_kernel, [((3, rows, LANES), f32)] * 2, 3)(head_old, soil_type, some)
+    ynear, yfar = exchange(to_near, to_far, "gy")
     source, flux = call(
         inner_source_kernel, [own, ((2, rows, cols), f32)], 9, in_specs=[smem] + [vmem] * 8
     )(soil_table, tab, factor, *columns, some, flux)
-    to_near, to_far = call(source_edge_kernel, [edge(SOURCE_DEPTH * layers + HALO + HALO // 2)] * 2, 2)(
-        source, strip
-    )
-    snear, sfar = exchange(to_near, to_far)
+    to_near, to_far = call(source_edge_kernel, [edge(SOURCE_DEPTH * layers + HALO + HALO // 2)] * 2, 3)(
+        source, ynear, yfar
+    )
+    snear, sfar = exchange(to_near, to_far, "gx")
     main, side_block = ((layers, tall, cols), f32), ((layers, tall, LANES), f32)
     old, ks, steep, cap, cond, deriv, store, water = call(
         state_kernel, [main] * 8, 5, in_specs=[smem] + [vmem] * 4
@@ -768,10 +758,10 @@
     old_s, ks_s, steep_s, cap_s, base, p0, p1, p2, gram = call(
         first_kernel,
         [side_block] * 4 + [ext] * 4 + [gram_block],
-        18,
+        19,
         scratch=[pltpu.VMEM(side_block[0], f32)] * 14,
-        in_specs=[smem] + [vmem] * 17,
-    )(soil_table, source, snear, sfar, strip, old, ks, cond, deriv, water, flow, *coefs)
+        in_specs=[smem] + [vmem] * 18,
+    )(soil_table, source, snear, sfar, ynear, yfar, old, ks, cond, deriv, water, flow, *coefs)
     sums = spread(gram, both)
     part, q0, q1, q2, gram = call(
         second_kernel,

time: 65.3 us -> 63.6 us (0.974)
  blocking collectives: 21.1 us -> 23.7 us
  starting transfers between devices: 14.5 us -> 12 us
  waiting for transfers between devices: 8.03 us -> 7.12 us
  Pallas kernels: 20.5 us -> 19.8 us
    all_to_all x2 -> x1, starting transfers between devices: 10.6 us -> 7.3 us  [spread(): return lax.all_to_all(x, axes, split_axis=0, concat_axis=0, tiled=True)]
    all_to_all x2, blocking collectives: 21.1 us -> 23.7 us  [spread(): return lax.all_to_all(x, axes, split_axis=0, concat_axis=0, tiled=True)]
    all_to_all x2 -> x1, waiting for transfers between devices: 7.9 us -> 5.81 us  [spread(): return lax.all_to_all(x, axes, split_axis=0, concat_axis=0, tiled=True)]
    ppermute x4 -> x6, waiting for transfers between devices: 0.13 us -> 1.31 us  [exchange(): lax.ppermute(x, axis, pairs + [(j, i) for i, j in pairs])]
    ppermute x4 -> x6, starting transfers between devices: 3.93 us -> 4.67 us  [exchange(): lax.ppermute(x, axis, pairs + [(j, i) for i, j in pairs])]
  transfers between devices with their start and end apart: 6 -> 7, of which waited for: 3 -> 2; matrix products, arithmetic and copies ran while one was open for 0% -> 0% of each run, Pallas kernels for 13% -> 13%
where the time goes in v12:
time: 63.6 us; the launch traced here: 63.4 us
  blocking collectives  23.7 us (37%)
  Pallas kernels  19.8 us (31%)
  starting transfers between devices  12 us (19%)
  waiting for transfers between devices  7.12 us (11%)
  between operations  0.79 us (1%)
    all_to_all x2, blocking collectives, spread(): return lax.all_to_all(x, axes, split_axis=0, concat_axis=0, tiled=True)  23.7 us
    all_to_all x1, starting transfers between devices, spread(): return lax.all_to_all(x, axes, split_axis=0, concat_axis=0, tiled=True)  7.3 us
    all_to_all x1, waiting for transfers between devices, spread(): return lax.all_to_all(x, axes, split_axis=0, concat_axis=0, tiled=True)  5.81 us
    pallas_call x1, Pallas kernels, shards(): call(first_kernel, [side_block] * 4 + [ext] * 4 + [gram_block], 19, scrat...  4.68 us
    ppermute x6, starting transfers between devices, exchange(): lax.ppermute(x, axis, pairs + [(j, i) for i, j in pairs])  4.67 us
    pallas_call x1, Pallas kernels, shards(): call(second_kernel, [own] + [((layers, rows + HALO, wide), f32)] * 3 + [g...  3.91 us
    pallas_call x1, Pallas kernels, shards(): call(inner_source_kernel, [own, ((2, rows, cols), f32)], 9, in_specs=[sme...  2.16 us
    pallas_call x1, Pallas kernels, shards(): call(pack_kernel, [((devices, 8, LANES), f32)] + [edge(2 * STATE_DEPTH *...  2.12 us
  transfers between devices with their start and end apart: 7, of which 2 were waited for; matrix products, arithmetic and copies ran while one was open for 0% of the time, Pallas kernels for 13%

profile of v12, /device:TPU:0, one launch (start us, length us, event | category | flops | bytes accessed | tf_op | source)
XLA Modules:
  0.0 63.4 jit_solution(2403224325802856023)
XLA Ops:
  0.6 0.0 copy-start
  0.6 0.0 copy-start.1
  0.6 2.1 %shard_map.77 = (f32[32,8,128]{2,1,0:T(8,128)}, f32[144,512]{1,0:T(8,128)}, f32[144,512]{1,0:T(8,128)}) custom-call(f32[13,2048]{1,0:T(8,128)} %canopy_hbm.1, f32[10,16,512]{2,1,0:T(8,128)} %head_ref.7, s32[10,16,512]{2,1,0:T(8,128)} %soil_ref.7), custom_call_target="tpu_custom_call" | custom-call | flops 1000000 | bytes 1000000 | tf_op jit(solution)/shard_map/pallas_call | solution.py:719
  2.8 0.0 copy-start.2
  2.8 0.0 copy-start.3
  2.8 7.3 %all-to-all-start = ((f32[32,8,128]{2,1,0:T(8,128)}), f32[32,8,128]{2,1,0:T(8,128)S(1)}, u32[]{:S(2)}, u32[]{:S(2)}) async-start(f32[32,8,128]{2,1,0:T(8,128)} %get-tuple-element.45), calls=%async_computation | async-start | bytes 262144 | tf_op jit(solution)/shard_map/all_to_all | solution.py:714
  10.1 0.0 copy-start.4
  10.1 1.8 %collective-permute-start.4 = (f32[144,512]{1,0:T(8,128)}, f32[144,512]{1,0:T(8,128)S(1)}, u32[]{:S(2)}, u32[]{:S(2)}) collective-permute-start(f32[144,512]{1,0:T(8,128)} %get-tuple-element.55), channel_id=1, source_target_pairs={{0,4},{8,12},{16,20},{24,28},{4,0},{12,8},{20,16},{28,24},{1,5},{9... | collective-permute-start | bytes 884744 | tf_op jit(solution)/shard_map/ppermute | solution.py:709
  12.0 0.7 %collective-permute-start.5 = (f32[144,512]{1,0:T(8,128)}, f32[144,512]{1,0:T(8,128)S(1)}, u32[]{:S(2)}, u32[]{:S(2)}) collective-permute-start(f32[144,512]{1,0:T(8,128)} %get-tuple-element.56), channel_id=1, source_target_pairs={{4,8},{12,16},{20,24},{8,4},{16,12},{24,20},{5,9},{13,17},{21,25},... | collective-permute-start | bytes 884744 | tf_op jit(solution)/shard_map/ppermute | solution.py:709
  12.6 5.8 %all-to-all-done.arrived_ref = f32[32,8,128]{2,1,0:T(8,128)S(1)} async-done(((f32[32,8,128]{2,1,0:T(8,128)}), f32[32,8,128]{2,1,0:T(8,128)S(1)}, u32[]{:S(2)}, u32[]{:S(2)}) %all-to-all-start) | async-done | bytes 131104 | tf_op jit(solution)/shard_map/all_to_all | solution.py:714
  18.4 0.0 copy-done.1
  18.5 1.8 %shard_map.78 = (f32[10,16,256]{2,1,0:T(8,128)S(1)}, f32[2,16,256]{2,1,0:T(8,128)S(1)}, s32[16,6,8,128]{3,2,1,0:T(8,128)S(1)}, f32[16,8,128]{2,1,0:T(8,128)S(1)}) custom-call(f32[3,12]{1,0:T(4,128)S(1)} %copy-done.4, f32[32,8,128]{2,1,0:T(8,128)S(1)} %all-to-all-done.arrived_ref, f32[10,16,512]{2,1,0:T(8,128)S(1)} %copy-done, s32[10,16,512]{2,1,0:T(8,128)S(1)} %copy-done.1, ...), custom_call_target="tpu_custom_call" | custom-call | flops 1000000 | bytes 1000000 | tf_op jit(solution)/shard_map/pallas_call | solution.py:736
  20.3 0.2 shard_map.80
  20.5 0.2 collective-permute-start
  20.7 0.7 %collective-permute-start.1 = (f32[3,16,128]{2,1,0:T(8,128)S(1)}, f32[3,16,128]{2,1,0:T(8,128)S(1)}, u32[]{:S(2)}, u32[]{:S(2)}) collective-permute-start(f32[3,16,128]{2,1,0:T(8,128)S(1)} %get-tuple-element.52), channel_id=1, source_target_pairs={{1,2},{2,1},{5,6},{6,5},{9,10},{10,9},{13,14},{14,13},{17,18},{18,... | collective-permute-start | bytes 73736 | tf_op jit(solution)/shard_map/ppermute | solution.py:709
  21.3 2.2 %shard_map.79 = (f32[10,16,512]{2,1,0:T(8,128)S(1)}, f32[2,16,512]{2,1,0:T(8,128)}) custom-call(f32[3,12]{1,0:T(4,128)S(1)} %copy-done.4, s32[16,6,8,128]{3,2,1,0:T(8,128)S(1)} %get-tuple-element.46.tab_ref, f32[16,8,128]{2,1,0:T(8,128)S(1)} %get-tuple-element.47.factor_ref, f32[10,16,512]{2,1,0:T(8,128)S(1)} %copy-done, s32[10,16,512]{2,1,0:T(8,128)S(1)} %copy-done.1, ...), custom_call_target="tpu_custom_call" | custom-call | flops 1000000 | bytes 1000000 | tf_op jit(solution)/shard_map/pallas_call | solution.py:744
  23.5 0.0 collective-permute-done.ynear_ref
  23.5 0.0 collective-permute-done.1.yfar_ref
  23.5 0.1 shard_map.81
  23.6 0.7 %collective-permute-start.2 = (f32[72,512]{1,0:T(8,128)S(1)}, f32[72,512]{1,0:T(8,128)S(1)}, u32[]{:S(2)}, u32[]{:S(2)}) collective-permute-start(f32[72,512]{1,0:T(8,128)S(1)} %get-tuple-element.53), channel_id=1, source_target_pairs={{0,4},{8,12},{16,20},{24,28},{4,0},{12,8},{20,16},{28,24},{1,5},{9... | collective-permute-start | bytes 442376 | tf_op jit(solution)/shard_map/ppermute | solution.py:709
  24.3 0.7 %collective-permute-start.3 = (f32[72,512]{1,0:T(8,128)S(1)}, f32[72,512]{1,0:T(8,128)S(1)}, u32[]{:S(2)}, u32[]{:S(2)}) collective-permute-start(f32[72,512]{1,0:T(8,128)S(1)} %get-tuple-element.54), channel_id=1, source_target_pairs={{4,8},{12,16},{20,24},{8,4},{16,12},{24,20},{5,9},{13,17},{21,25},... | collective-permute-start | bytes 442376 | tf_op jit(solution)/shard_map/ppermute | solution.py:709
  24.9 1.3 %collective-permute-done.4.near_ref = f32[144,512]{1,0:T(8,128)S(1)} collective-permute-done((f32[144,512]{1,0:T(8,128)}, f32[144,512]{1,0:T(8,128)S(1)}, u32[]{:S(2)}, u32[]{:S(2)}) %collective-permute-start.4) | collective-permute-done | bytes 294944 | tf_op jit(solution)/shard_map/ppermute | solution.py:709
  26.2 0.0 collective-permute-done.5.far_ref
  26.2 2.0 %shard_map.82 = (f32[10,32,512]{2,1,0:T(8,128)S(1)}, f32[10,32,512]{2,1,0:T(8,128)S(1)}, f32[10,32,512]{2,1,0:T(8,128)S(1)}, f32[10,32,512]{2,1,0:T(8,128)S(1)},...) custom-call(f32[3,12]{1,0:T(4,128)S(1)} %copy-done.4, ...), custom_call_target="tpu_custom_call" | custom-call | flops 1000000 | bytes 1000000 | tf_op jit(solution)/shard_map/pallas_call | solution.py:752
  28.2 1.8 %shard_map.83 = (f32[10,32,512]{2,1,0:T(8,128)S(1)}, f32[10,32,512]{2,1,0:T(8,128)S(1)}, f32[10,32,512]{2,1,0:T(8,128)S(1)}, f32[10,32,512]{2,1,0:T(8,128)S(1)},...) custom-call(f32[10,32,512]{2,1,0:T(8,128)S(1)} %get-tuple-element.57, ...), custom_call_target="tpu_custom_call" | custom-call | flops 1000000 | bytes 1000000 | tf_op jit(solution)/shard_map/pallas_call | solution.py:755
  30.0 0.0 collective-permute-done.2.snear_ref
  30.0 0.0 collective-permute-done.3.sfar_ref
  30.0 4.7 %shard_map.84 = (f32[10,32,128]{2,1,0:T(8,128)S(1)}, f32[10,32,128]{2,1,0:T(8,128)S(1)}, f32[10,32,128]{2,1,0:T(8,128)S(1)}, f32[10,32,128]{2,1,0:T(8,128)S(1)},...) custom-call(f32[3,12]{1,0:T(4,128)S(1)} %copy-done.4, ...), custom_call_target="tpu_custom_call" | custom-call | flops 1000000 | bytes 1000000 | tf_op jit(solution)/shard_map/pallas_call | solution.py:758
  34.7 14.8 %all_to_all.15.arrived_ref = f32[32,1,128]{2,1,0:T(1,128)S(1)} all-to-all(f32[32,1,128]{2,1,0:T(1,128)S(1)} %get-tuple-element.71), channel_id=1, replica_groups=mesh['gx'=8,'gy'=4] {'gx','gy'}, dimensions={0} | all-to-all | bytes 32768 | tf_op jit(solution)/shard_map/all_to_all | solution.py:714
  49.6 3.9 %shard_map.85 = (f32[10,16,512]{2,1,0:T(8,128)S(1)}, f32[10,24,640]{2,1,0:T(8,128)S(1)}, f32[10,24,640]{2,1,0:T(8,128)S(1)}, f32[10,24,640]{2,1,0:T(8,128)S(1)}, f32[32,1,128]{2,1,0:T(1,128)S(1)}) custom-call(f32[32,1,128]{2,1,0:T(1,128)S(1)} %all_to_all.15.arrived_ref, f32[10,32,512]{2,1,0:T(8,128)S(1)} %get-tuple-element.57.ext_ref.old_ref, ...), custom_call_target="tpu_custom_call" | custom-call | flops 1000000 | bytes 1000000 | tf_op jit(solution)/shard_map/pallas_call | solution.py:766
  53.5 8.8 %all_to_all.16.arrived_ref = f32[32,1,128]{2,1,0:T(1,128)S(1)} all-to-all(f32[32,1,128]{2,1,0:T(1,128)S(1)} %get-tuple-element.82), channel_id=1, replica_groups=mesh['gx'=8,'gy'=4] {'gx','gy'}, dimensions={0} | all-to-all | bytes 32768 | tf_op jit(solution)/shard_map/all_to_all | solution.py:714
  62.3 1.1 %shard_map.86 = f32[10,16,512]{2,1,0:T(8,128)} custom-call(f32[32,1,128]{2,1,0:T(1,128)S(1)} %all_to_all.16.arrived_ref, f32[10,16,512]{2,1,0:T(8,128)S(1)} %get-tuple-element.83.part_ref, f32[10,24,640]{2,1,0:T(8,128)S(1)} %get-tuple-element.84.q0_ref, f32[10,24,640]{2,1,0:T(8,128)S(1)} %get-tuple-element.85.q1_ref, f32[10,24,640]{2,1,0:T(8,128)S(1)} %get-tuple-element.86.q2_ref), custom_call_target="tpu_custom_call" | custom-call | flops 1000000 | bytes 1000000 | tf_op jit(solution)/shard_map/pallas_call | solution.py:773
  (4 shorter events, 0.0 us)
Async XLA Ops:
  0.6 17.8 %copy-start = (f32[10,16,512]{2,1,0:T(8,128)S(1)}, f32[10,16,512]{2,1,0:T(8,128)}, u32[]{:S(2)}) copy-start(f32[10,16,512]{2,1,0:T(8,128)} %head_ref.7) | copy-start | bytes 983044
  0.6 17.8 %copy-start.1 = (s32[10,16,512]{2,1,0:T(8,128)S(1)}, s32[10,16,512]{2,1,0:T(8,128)}, u32[]{:S(2)}) copy-start(s32[10,16,512]{2,1,0:T(8,128)} %soil_ref.7) | copy-start | bytes 983044
  2.8 15.7 %copy-start.2 = (f32[4,16,512]{2,1,0:T(8,128)S(1)}, f32[4,16,512]{2,1,0:T(8,128)}, u32[]{:S(2)}) copy-start(f32[4,16,512]{2,1,0:T(8,128)} %forcing_ref.3) | copy-start | bytes 393220
  2.8 15.7 %copy-start.3 = (s32[16,512]{1,0:T(8,128)S(1)}, s32[16,512]{1,0:T(8,128)}, u32[]{:S(2)}) copy-start(s32[16,512]{1,0:T(8,128)} %slot_ref.3) | copy-start | bytes 98308
  2.8 15.6 %all-to-all-start = ((f32[32,8,128]{2,1,0:T(8,128)}), f32[32,8,128]{2,1,0:T(8,128)S(1)}, u32[]{:S(2)}, u32[]{:S(2)}) async-start(f32[32,8,128]{2,1,0:T(8,128)} %get-tuple-element.45), calls=%async_computation | async-start | bytes 262144 | tf_op jit(solution)/shard_map/all_to_all | solution.py:714
  10.1 8.4 %copy-start.4 = (f32[3,12]{1,0:T(4,128)S(1)}, f32[3,12]{1,0:T(4,128)}, u32[]{:S(2)}) copy-start(f32[3,12]{1,0:T(4,128)} %table_ref.7) | copy-start | bytes 436
  10.1 16.1 %collective-permute-start.4 = (f32[144,512]{1,0:T(8,128)}, f32[144,512]{1,0:T(8,128)S(1)}, u32[]{:S(2)}, u32[]{:S(2)}) collective-permute-start(f32[144,512]{1,0:T(8,128)} %get-tuple-element.55), channel_id=1, source_target_pairs={{0,4},{8,12},{16,20},{24,28},{4,0},{12,8},{20,16},{28,24},{1,5},{9... | collective-permute-start | bytes 884744 | tf_op jit(solution)/shard_map/ppermute | solution.py:709
  12.0 14.3 %collective-permute-start.5 = (f32[144,512]{1,0:T(8,128)}, f32[144,512]{1,0:T(8,128)S(1)}, u32[]{:S(2)}, u32[]{:S(2)}) collective-permute-start(f32[144,512]{1,0:T(8,128)} %get-tuple-element.56), channel_id=1, source_target_pairs={{4,8},{12,16},{20,24},{8,4},{16,12},{24,20},{5,9},{13,17},{21,25},... | collective-permute-start | bytes 884744 | tf_op jit(solution)/shard_map/ppermute | solution.py:709
  20.5 3.0 %collective-permute-start = (f32[3,16,128]{2,1,0:T(8,128)S(1)}, f32[3,16,128]{2,1,0:T(8,128)S(1)}, u32[]{:S(2)}, u32[]{:S(2)}) collective-permute-start(f32[3,16,128]{2,1,0:T(8,128)S(1)} %get-tuple-element.51), channel_id=1, source_target_pairs={{0,1},{2,3},{1,0},{3,2},{4,5},{6,7},{5,4},{7,6},{8,9},{10,11},{9,8... | collective-permute-start | bytes 73736 | tf_op jit(solution)/shard_map/ppermute | solution.py:709
  20.7 2.8 %collective-permute-start.1 = (f32[3,16,128]{2,1,0:T(8,128)S(1)}, f32[3,16,128]{2,1,0:T(8,128)S(1)}, u32[]{:S(2)}, u32[]{:S(2)}) collective-permute-start(f32[3,16,128]{2,1,0:T(8,128)S(1)} %get-tuple-element.52), channel_id=1, source_target_pairs={{1,2},{2,1},{5,6},{6,5},{9,10},{10,9},{13,14},{14,13},{17,18},{18,... | collective-permute-start | bytes 73736 | tf_op jit(solution)/shard_map/ppermute | solution.py:709
  23.6 6.4 %collective-permute-start.2 = (f32[72,512]{1,0:T(8,128)S(1)}, f32[72,512]{1,0:T(8,128)S(1)}, u32[]{:S(2)}, u32[]{:S(2)}) collective-permute-start(f32[72,512]{1,0:T(8,128)S(1)} %get-tuple-element.53), channel_id=1, source_target_pairs={{0,4},{8,12},{16,20},{24,28},{4,0},{12,8},{20,16},{28,24},{1,5},{9... | collective-permute-start | bytes 442376 | tf_op jit(solution)/shard_map/ppermute | solution.py:709
  24.3 5.8 %collective-permute-start.3 = (f32[72,512]{1,0:T(8,128)S(1)}, f32[72,512]{1,0:T(8,128)S(1)}, u32[]{:S(2)}, u32[]{:S(2)}) collective-permute-start(f32[72,512]{1,0:T(8,128)S(1)} %get-tuple-element.54), channel_id=1, source_target_pairs={{4,8},{12,16},{20,24},{8,4},{16,12},{24,20},{5,9},{13,17},{21,25},... | collective-permute-start | bytes 442376 | tf_op jit(solution)/shard_map/ppermute | solution.py:709

commit v13 on v12

--- a/solution.py
+++ b/solution.py
@@ -44,7 +44,7 @@
 
 
 def pack_kernel(
-    canopy_hbm, head_hbm, soil_hbm, send_ref, near_ref, far_ref, canopy_ref, head_ref, soil_ref, sems
+    canopy_hbm, head_hbm, soil_hbm, send_ref, near_ref, canopy_ref, head_ref, soil_ref, sems
 ):
     copies = [
         pltpu.make_async_copy(canopy_hbm, canopy_ref, sems.at[0]),
@@ -65,13 +65,19 @@
     layers, rows, _ = head_ref.shape
     copies[1].wait()
     copies[2].wait()
-    low_rows, high_rows = slice(0, STATE_DEPTH), slice(rows - STATE_DEPTH, rows)
-    upward = near_is_above("gx")
+    state_edge(head_ref, soil_ref, near_ref, near_is_above("gx"))
+
+
+def state_edge(head_ref, soil_ref, out_ref, upward):
+    layers, rows, _ = head_ref.shape
     for n in range(2 * layers):
         plane = head_ref[n] if n < layers else (soil_ref[n - layers] + 1).astype(f32)
-        part = slice(STATE_DEPTH * n, STATE_DEPTH * (n + 1))
-        near_ref[part] = jnp.where(upward, plane[high_rows], plane[low_rows])
-        far_ref[part] = jnp.where(upward, plane[low_rows], plane[high_rows])
+        value = jnp.where(upward, plane[rows - STATE_DEPTH :], plane[:STATE_DEPTH])
+        out_ref[STATE_DEPTH * n : STATE_DEPTH * (n + 1)] = value
+
+
+def far_edge_kernel(head_ref, soil_ref, _, far_ref):
+    state_edge(head_ref, soil_ref, far_ref, jnp.logical_not(near_is_above("gx")))
 
 
 def near_is_above(axis):
@@ -268,21 +274,22 @@
     return jnp.concatenate([above, gap, below], axis=0)
 
 
-def strip_kernel(head_ref, soil_ref, some_ref, near_ref, far_ref):
+def strip_kernel(head_ref, soil_ref, src_ref, out_ref, *, near, end):
     layers, _, cols = head_ref.shape
     upward = near_is_above("gy")
+    if not near:
+        upward = jnp.logical_not(upward)
     blocks = []
-    for (part, shift), at in zip(strip_parts(cols), (0, LANES)):
+    for (part, shift), at in zip(strip_parts(cols), (0, end)):
         blocks.append(
             (
                 strips([head_ref[k, :, part] for k in range(layers)], shift),
                 strips([(soil_ref[k, :, part] + 1).astype(f32) for k in range(layers)], shift),
-                strips([some_ref[k, :, at : at + LANES] for k in range(layers)], shift),
+                strips([src_ref[k, :, at : at + LANES] for k in range(layers)], shift),
             )
         )
     for field, (low, high) in enumerate(zip(*blocks)):
-        near_ref[field] = jnp.where(upward, high, low)
-        far_ref[field] = jnp.where(upward, low, high)
+        out_ref[field] = jnp.where(upward, high, low)
 
 
 def source_edge_kernel(src_ref, ynear_ref, yfar_ref, near_ref, far_ref):
@@ -701,14 +708,9 @@
     own, ext = ((layers, rows, cols), f32), ((layers, tall, wide), f32)
     gram_block = ((devices, 1, LANES), f32)
 
-    def exchange(to_near, to_far, axis):
-        size = lax.axis_size(axis)
-        near = [(i, i + 1) for i in range(0, size - 1, 2)]
-        far = [(i, i + 1) for i in range(1, size - 1, 2)]
-        return tuple(
-            lax.ppermute(x, axis, pairs + [(j, i) for i, j in pairs])
-            for x, pairs in ((to_near, near), (to_far, far))
-        )
+    def to_partner(x, axis, first):
+        pairs = [(i, i + 1) for i in range(first, lax.axis_size(axis) - 1, 2)]
+        return lax.ppermute(x, axis, pairs + [(j, i) for i, j in pairs])
 
     def spread(x, axes):
         return lax.all_to_all(x, axes, split_axis=0, concat_axis=0, tiled=True)
@@ -716,9 +718,9 @@
     def edge(count):
         return (-(-count // 8) * 8, cols), f32
 
-    send, to_near, to_far = call(
+    send, to_near = call(
         pack_kernel,
-        [((devices, 8, LANES), f32)] + [edge(2 * STATE_DEPTH * layers)] * 2,
+        [((devices, 8, LANES), f32), edge(2 * STATE_DEPTH * layers)],
         3,
         scratch=[
             pltpu.VMEM(canopy.shape, f32),
@@ -730,7 +732,7 @@
         grant=63400000,
     )(canopy, head_old, soil_type)
     arrived = spread(send, both)
-    near, far = exchange(to_near, to_far, "gx")
+    near = to_partner(to_near, "gx", 0)
     columns = (head_old, soil_type, forcing, column_slot)
     table = ((devices // 2, -(-layers // 2) + 1, 8, LANES), jnp.int32)
     some, flux, tab, factor = call(
@@ -739,15 +741,29 @@
         6,
         in_specs=[smem] + [vmem] * 5,
     )(soil_table, arrived, *columns)
-    to_near, to_far = call(strip_kernel, [((3, rows, LANES), f32)] * 2, 3)(head_old, soil_type, some)
-    ynear, yfar = exchange(to_near, to_far, "gy")
+    (to_far,) = call(
+        far_edge_kernel,
+        [edge(2 * STATE_DEPTH * layers)],
+        3,
+        in_specs=[vmem] * 2 + [pl.BlockSpec(memory_space=pl.ANY)],
+    )(head_old, soil_type, some)
+    far = to_partner(to_far, "gx", 1)
+    strip = [((3, rows, LANES), f32)]
+    (to_near,) = call(functools.partial(strip_kernel, near=True, end=LANES), strip, 3)(
+        head_old, soil_type, some
+    )
+    ynear = to_partner(to_near, "gy", 0)
     source, flux = call(
         inner_source_kernel, [own, ((2, rows, cols), f32)], 9, in_specs=[smem] + [vmem] * 8
     )(soil_table, tab, factor, *columns, some, flux)
+    (to_far,) = call(functools.partial(strip_kernel, near=False, end=cols - LANES), strip, 3)(
+        head_old, soil_type, source
+    )
+    yfar = to_partner(to_far, "gy", 1)
     to_near, to_far = call(source_edge_kernel, [edge(SOURCE_DEPTH * layers + HALO + HALO // 2)] * 2, 3)(
         source, ynear, yfar
     )
-    snear, sfar = exchange(to_near, to_far, "gx")
+    snear, sfar = to_partner(to_near, "gx", 0), to_partner(to_far, "gx", 1)
     main, side_block = ((layers, tall, cols), f32), ((layers, tall, LANES), f32)
     old, ks, steep, cap, cond, deriv, store, water = call(
         state_kernel, [main] * 8, 5, in_specs=[smem] + [vmem] * 4

time: 63.6 us -> 67.9 us (1.068)
  starting transfers between devices: 12 us -> 14.7 us
  blocking collectives: 23.7 us -> 25.2 us
    ppermute x6, starting transfers between devices: 4.67 us -> 7.41 us  [to_partner(): return lax.ppermute(x, axis, pairs + [(j, i) for i, j in pairs])]
    all_to_all x2, blocking collectives: 23.7 us -> 25.2 us  [spread(): return lax.all_to_all(x, axes, split_axis=0, concat_axis=0, tiled=True)]
    ppermute x6, waiting for transfers between devices: 1.31 us -> 0.43 us  [to_partner(): return lax.ppermute(x, axis, pairs + [(j, i) for i, j in pairs])]
    all_to_all x1, waiting for transfers between devices: 5.81 us -> 6.5 us  [spread(): return lax.all_to_all(x, axes, split_axis=0, concat_axis=0, tiled=True)]
    pallas_call x2 -> x4, Pallas kernels: 2.3 us -> 2.46 us  [the longest x1 2.01 us: shards(): call(pack_kernel, [((devices, 8, LANES), f32), edge(2 * STATE_DEPTH * lay...]
  transfers between devices with their start and end apart: 7 -> 7, of which waited for: 2 -> 2; matrix products, arithmetic and copies ran while one was open for 0% -> 0% of each run, Pallas kernels for 13% -> 12%
where the time goes in v13:
time: 67.9 us; the launch traced here: 67.6 us
  blocking collectives  25.2 us (37%)
  Pallas kernels  19.9 us (29%)
  starting transfers between devices  14.7 us (22%)
  waiting for transfers between devices  6.93 us (10%)
  between operations  0.82 us (1%)
    all_to_all x2, blocking collectives, spread(): return lax.all_to_all(x, axes, split_axis=0, concat_axis=0, tiled=True)  25.2 us
    ppermute x6, starting transfers between devices, to_partner(): return lax.ppermute(x, axis, pairs + [(j, i) for i, j in pairs])  7.41 us
    all_to_all x1, starting transfers between devices, spread(): return lax.all_to_all(x, axes, split_axis=0, concat_axis=0, tiled=True)  7.3 us
    all_to_all x1, waiting for transfers between devices, spread(): return lax.all_to_all(x, axes, split_axis=0, concat_axis=0, tiled=True)  6.5 us
    pallas_call x1, Pallas kernels, shards(): call(first_kernel, [side_block] * 4 + [ext] * 4 + [gram_block], 19, scrat...  4.68 us
    pallas_call x1, Pallas kernels, shards(): call(second_kernel, [own] + [((layers, rows + HALO, wide), f32)] * 3 + [g...  3.88 us
    pallas_call x1, Pallas kernels, shards(): call(inner_source_kernel, [own, ((2, rows, cols), f32)], 9, in_specs=[sme...  2.17 us
    pallas_call x1, Pallas kernels, shards(): call(pack_kernel, [((devices, 8, LANES), f32), edge(2 * STATE_DEPTH * lay...  2.01 us
  transfers between devices with their start and end apart: 7, of which 2 were waited for; matrix products, arithmetic and copies ran while one was open for 0% of the time, Pallas kernels for 12%

profile of v13, /device:TPU:0, one launch (start us, length us, event | category | flops | bytes accessed | tf_op | source)
XLA Modules:
  0.0 67.6 jit_solution(7426901452954444659)
XLA Ops:
  0.6 2.0 %shard_map.77 = (f32[32,8,128]{2,1,0:T(8,128)}, f32[144,512]{1,0:T(8,128)}) custom-call(f32[13,2048]{1,0:T(8,128)} %canopy_hbm.1, f32[10,16,512]{2,1,0:T(8,128)} %head_ref.11, s32[10,16,512]{2,1,0:T(8,128)} %soil_ref.11), custom_call_target="tpu_custom_call" | custom-call | flops 1000000 | bytes 1000000 | tf_op jit(solution)/shard_map/pallas_call | solution.py:721
  2.7 0.0 copy-start.2
  2.7 0.0 copy-start.3
  2.7 0.0 copy-start.4
  2.7 7.3 %all-to-all-start = ((f32[32,8,128]{2,1,0:T(8,128)}), f32[32,8,128]{2,1,0:T(8,128)S(1)}, u32[]{:S(2)}, u32[]{:S(2)}) async-start(f32[32,8,128]{2,1,0:T(8,128)} %get-tuple-element.42), calls=%async_computation | async-start | bytes 262144 | tf_op jit(solution)/shard_map/all_to_all | solution.py:716
  10.0 1.8 %collective-permute-start.4 = (f32[144,512]{1,0:T(8,128)}, f32[144,512]{1,0:T(8,128)S(1)}, u32[]{:S(2)}, u32[]{:S(2)}) collective-permute-start(f32[144,512]{1,0:T(8,128)} %get-tuple-element.50), channel_id=1, source_target_pairs={{0,4},{8,12},{16,20},{24,28},{4,0},{12,8},{20,16},{28,24},{1,5},{9... | collective-permute-start | bytes 884744 | tf_op jit(solution)/shard_map/ppermute | solution.py:713
  11.8 6.5 %all-to-all-done.arrived_ref = f32[32,8,128]{2,1,0:T(8,128)S(1)} async-done(((f32[32,8,128]{2,1,0:T(8,128)}), f32[32,8,128]{2,1,0:T(8,128)S(1)}, u32[]{:S(2)}, u32[]{:S(2)}) %all-to-all-start) | async-done | bytes 131104 | tf_op jit(solution)/shard_map/all_to_all | solution.py:716
  18.3 0.0 copy-done
  18.4 1.8 %shard_map.78 = (f32[10,16,256]{2,1,0:T(8,128)S(1)}, f32[2,16,256]{2,1,0:T(8,128)S(1)}, s32[16,6,8,128]{3,2,1,0:T(8,128)S(1)}, f32[16,8,128]{2,1,0:T(8,128)S(1)}) custom-call(f32[3,12]{1,0:T(4,128)S(1)} %copy-done.4, f32[32,8,128]{2,1,0:T(8,128)S(1)} %all-to-all-done.arrived_ref, f32[10,16,512]{2,1,0:T(8,128)S(1)} %copy-done, s32[10,16,512]{2,1,0:T(8,128)S(1)} %copy-done.1, ...), custom_call_target="tpu_custom_call" | custom-call | flops 1000000 | bytes 1000000 | tf_op jit(solution)/shard_map/pallas_call | solution.py:738
  20.2 0.1 shard_map.83
  20.3 0.7 %collective-permute-start.5 = (f32[144,512]{1,0:T(8,128)S(1)}, f32[144,512]{1,0:T(8,128)S(1)}, u32[]{:S(2)}, u32[]{:S(2)}) collective-permute-start(f32[144,512]{1,0:T(8,128)S(1)} %shard_map.83), channel_id=1, source_target_pairs={{4,8},{12,16},{20,24},{8,4},{16,12},{24,20},{5,9},{13,17},{21,25},... | collective-permute-start | bytes 884744 | tf_op jit(solution)/shard_map/ppermute | solution.py:713
  21.0 0.2 shard_map.80
  21.2 2.2 %shard_map.79 = (f32[10,16,512]{2,1,0:T(8,128)S(1)}, f32[2,16,512]{2,1,0:T(8,128)}) custom-call(f32[3,12]{1,0:T(4,128)S(1)} %copy-done.4, s32[16,6,8,128]{3,2,1,0:T(8,128)S(1)} %get-tuple-element.43.tab_ref, f32[16,8,128]{2,1,0:T(8,128)S(1)} %get-tuple-element.44.factor_ref, f32[10,16,512]{2,1,0:T(8,128)S(1)} %copy-done, s32[10,16,512]{2,1,0:T(8,128)S(1)} %copy-done.1, ...), custom_call_target="tpu_custom_call" | custom-call | flops 1000000 | bytes 1000000 | tf_op jit(solution)/shard_map/pallas_call | solution.py:756
  23.3 0.2 shard_map.81
  23.5 0.2 collective-permute-start
  23.7 0.7 collective-permute-start.1
  24.4 0.4 collective-permute-done.ynear_ref
  24.8 0.0 collective-permute-done.1.yfar_ref
  24.8 0.1 shard_map.82
  24.9 3.4 %collective-permute-start.2 = (f32[72,512]{1,0:T(8,128)S(1)}, f32[72,512]{1,0:T(8,128)S(1)}, u32[]{:S(2)}, u32[]{:S(2)}) collective-permute-start(f32[72,512]{1,0:T(8,128)S(1)} %get-tuple-element.48), channel_id=1, source_target_pairs={{0,4},{8,12},{16,20},{24,28},{4,0},{12,8},{20,16},{28,24},{1,5},{9... | collective-permute-start | bytes 442376 | tf_op jit(solution)/shard_map/ppermute | solution.py:713
  28.3 0.7 collective-permute-start.3
  28.9 0.0 collective-permute-done.4.near_ref
  29.0 0.0 collective-permute-done.5.far_ref
  29.0 2.0 %shard_map.84 = (f32[10,32,512]{2,1,0:T(8,128)S(1)}, f32[10,32,512]{2,1,0:T(8,128)S(1)}, f32[10,32,512]{2,1,0:T(8,128)S(1)}, f32[10,32,512]{2,1,0:T(8,128)S(1)},...) custom-call(f32[3,12]{1,0:T(4,128)S(1)} %copy-done.4, ...), custom_call_target="tpu_custom_call" | custom-call | flops 1000000 | bytes 1000000 | tf_op jit(solution)/shard_map/pallas_call | solution.py:768
  31.0 1.8 %shard_map.85 = (f32[10,32,512]{2,1,0:T(8,128)S(1)}, f32[10,32,512]{2,1,0:T(8,128)S(1)}, f32[10,32,512]{2,1,0:T(8,128)S(1)}, f32[10,32,512]{2,1,0:T(8,128)S(1)},...) custom-call(f32[10,32,512]{2,1,0:T(8,128)S(1)} %get-tuple-element.51, ...), custom_call_target="tpu_custom_call" | custom-call | flops 1000000 | bytes 1000000 | tf_op jit(solution)/shard_map/pallas_call | solution.py:771
  32.8 0.0 collective-permute-done.2.snear_ref
  32.8 0.0 collective-permute-done.3.sfar_ref
  32.8 4.7 %shard_map.86 = (f32[10,32,128]{2,1,0:T(8,128)S(1)}, f32[10,32,128]{2,1,0:T(8,128)S(1)}, f32[10,32,128]{2,1,0:T(8,128)S(1)}, f32[10,32,128]{2,1,0:T(8,128)S(1)},...) custom-call(f32[3,12]{1,0:T(4,128)S(1)} %copy-done.4, ...), custom_call_target="tpu_custom_call" | custom-call | flops 1000000 | bytes 1000000 | tf_op jit(solution)/shard_map/pallas_call | solution.py:774
  37.5 16.4 %all_to_all.15.arrived_ref = f32[32,1,128]{2,1,0:T(1,128)S(1)} all-to-all(f32[32,1,128]{2,1,0:T(1,128)S(1)} %get-tuple-element.65), channel_id=1, replica_groups=mesh['gx'=8,'gy'=4] {'gx','gy'}, dimensions={0} | all-to-all | bytes 32768 | tf_op jit(solution)/shard_map/all_to_all | solution.py:716
  53.9 3.9 %shard_map.87 = (f32[10,16,512]{2,1,0:T(8,128)S(1)}, f32[10,24,640]{2,1,0:T(8,128)S(1)}, f32[10,24,640]{2,1,0:T(8,128)S(1)}, f32[10,24,640]{2,1,0:T(8,128)S(1)}, f32[32,1,128]{2,1,0:T(1,128)S(1)}) custom-call(f32[32,1,128]{2,1,0:T(1,128)S(1)} %all_to_all.15.arrived_ref, f32[10,32,512]{2,1,0:T(8,128)S(1)} %get-tuple-element.51.ext_ref.old_ref, ...), custom_call_target="tpu_custom_call" | custom-call | flops 1000000 | bytes 1000000 | tf_op jit(solution)/shard_map/pallas_call | solution.py:782
  57.8 8.8 %all_to_all.16.arrived_ref = f32[32,1,128]{2,1,0:T(1,128)S(1)} all-to-all(f32[32,1,128]{2,1,0:T(1,128)S(1)} %get-tuple-element.76), channel_id=1, replica_groups=mesh['gx'=8,'gy'=4] {'gx','gy'}, dimensions={0} | all-to-all | bytes 32768 | tf_op jit(solution)/shard_map/all_to_all | solution.py:716
  66.6 1.0 %shard_map.88 = f32[10,16,512]{2,1,0:T(8,128)} custom-call(f32[32,1,128]{2,1,0:T(1,128)S(1)} %all_to_all.16.arrived_ref, f32[10,16,512]{2,1,0:T(8,128)S(1)} %get-tuple-element.77.part_ref, f32[10,24,640]{2,1,0:T(8,128)S(1)} %get-tuple-element.78.q0_ref, f32[10,24,640]{2,1,0:T(8,128)S(1)} %get-tuple-element.79.q1_ref, f32[10,24,640]{2,1,0:T(8,128)S(1)} %get-tuple-element.80.q2_ref), custom_call_target="tpu_custom_call" | custom-call | flops 1000000 | bytes 1000000 | tf_op jit(solution)/shard_map/pallas_call | solution.py:789
  (6 shorter events, 0.0 us)
Async XLA Ops:
  0.6 17.7 %copy-start = (f32[10,16,512]{2,1,0:T(8,128)S(1)}, f32[10,16,512]{2,1,0:T(8,128)}, u32[]{:S(2)}) copy-start(f32[10,16,512]{2,1,0:T(8,128)} %head_ref.11) | copy-start | bytes 983044
  0.6 17.7 %copy-start.1 = (s32[10,16,512]{2,1,0:T(8,128)S(1)}, s32[10,16,512]{2,1,0:T(8,128)}, u32[]{:S(2)}) copy-start(s32[10,16,512]{2,1,0:T(8,128)} %soil_ref.11) | copy-start | bytes 983044
  2.7 15.7 %copy-start.2 = (f32[4,16,512]{2,1,0:T(8,128)S(1)}, f32[4,16,512]{2,1,0:T(8,128)}, u32[]{:S(2)}) copy-start(f32[4,16,512]{2,1,0:T(8,128)} %forcing_ref.3) | copy-start | bytes 393220
  2.7 15.7 %copy-start.3 = (s32[16,512]{1,0:T(8,128)S(1)}, s32[16,512]{1,0:T(8,128)}, u32[]{:S(2)}) copy-start(s32[16,512]{1,0:T(8,128)} %slot_ref.3) | copy-start | bytes 98308
  2.7 15.7 %copy-start.4 = (f32[3,12]{1,0:T(4,128)S(1)}, f32[3,12]{1,0:T(4,128)}, u32[]{:S(2)}) copy-start(f32[3,12]{1,0:T(4,128)} %table_ref.7) | copy-start | bytes 436
  2.7 15.6 %all-to-all-start = ((f32[32,8,128]{2,1,0:T(8,128)}), f32[32,8,128]{2,1,0:T(8,128)S(1)}, u32[]{:S(2)}, u32[]{:S(2)}) async-start(f32[32,8,128]{2,1,0:T(8,128)} %get-tuple-element.42), calls=%async_computation | async-start | bytes 262144 | tf_op jit(solution)/shard_map/all_to_all | solution.py:716
  10.0 18.9 %collective-permute-start.4 = (f32[144,512]{1,0:T(8,128)}, f32[144,512]{1,0:T(8,128)S(1)}, u32[]{:S(2)}, u32[]{:S(2)}) collective-permute-start(f32[144,512]{1,0:T(8,128)} %get-tuple-element.50), channel_id=1, source_target_pairs={{0,4},{8,12},{16,20},{24,28},{4,0},{12,8},{20,16},{28,24},{1,5},{9... | collective-permute-start | bytes 884744 | tf_op jit(solution)/shard_map/ppermute | solution.py:713
  20.3 8.7 %collective-permute-start.5 = (f32[144,512]{1,0:T(8,128)S(1)}, f32[144,512]{1,0:T(8,128)S(1)}, u32[]{:S(2)}, u32[]{:S(2)}) collective-permute-start(f32[144,512]{1,0:T(8,128)S(1)} %shard_map.83), channel_id=1, source_target_pairs={{4,8},{12,16},{20,24},{8,4},{16,12},{24,20},{5,9},{13,17},{21,25},... | collective-permute-start | bytes 884744 | tf_op jit(solution)/shard_map/ppermute | solution.py:713
  23.5 1.3 %collective-permute-start = (f32[3,16,128]{2,1,0:T(8,128)S(1)}, f32[3,16,128]{2,1,0:T(8,128)S(1)}, u32[]{:S(2)}, u32[]{:S(2)}) collective-permute-start(f32[3,16,128]{2,1,0:T(8,128)S(1)} %shard_map.80), channel_id=1, source_target_pairs={{0,1},{2,3},{1,0},{3,2},{4,5},{6,7},{5,4},{7,6},{8,9},{10,11},{9,8... | collective-permute-start | bytes 73736 | tf_op jit(solution)/shard_map/ppermute | solution.py:713
  23.7 1.1 %collective-permute-start.1 = (f32[3,16,128]{2,1,0:T(8,128)S(1)}, f32[3,16,128]{2,1,0:T(8,128)S(1)}, u32[]{:S(2)}, u32[]{:S(2)}) collective-permute-start(f32[3,16,128]{2,1,0:T(8,128)S(1)} %shard_map.81), channel_id=1, source_target_pairs={{1,2},{2,1},{5,6},{6,5},{9,10},{10,9},{13,14},{14,13},{17,18},{18,... | collective-permute-start | bytes 73736 | tf_op jit(solution)/shard_map/ppermute | solution.py:713
  24.9 7.9 %collective-permute-start.2 = (f32[72,512]{1,0:T(8,128)S(1)}, f32[72,512]{1,0:T(8,128)S(1)}, u32[]{:S(2)}, u32[]{:S(2)}) collective-permute-start(f32[72,512]{1,0:T(8,128)S(1)} %get-tuple-element.48), channel_id=1, source_target_pairs={{0,4},{8,12},{16,20},{24,28},{4,0},{12,8},{20,16},{28,24},{1,5},{9... | collective-permute-start | bytes 442376 | tf_op jit(solution)/shard_map/ppermute | solution.py:713
  28.3 4.5 %collective-permute-start.3 = (f32[72,512]{1,0:T(8,128)S(1)}, f32[72,512]{1,0:T(8,128)S(1)}, u32[]{:S(2)}, u32[]{:S(2)}) collective-permute-start(f32[72,512]{1,0:T(8,128)S(1)} %get-tuple-element.49), channel_id=1, source_target_pairs={{4,8},{12,16},{20,24},{8,4},{16,12},{24,20},{5,9},{13,17},{21,25},... | collective-permute-start | bytes 442376 | tf_op jit(solution)/shard_map/ppermute | solution.py:713

commit v14 on v12

--- a/solution.py
+++ b/solution.py
@@ -150,7 +150,7 @@
 
 
 def inner_source_kernel(
-    table_ref, tab_ref, factor_ref, head_ref, soil_ref, forcing_ref, slot_ref, some_ref, part_ref,
+    table_ref, tab_ref, factor_ref, head_ref, soil_ref, forcing_ref, slot_ref, some_ref,
     source_ref, flux_ref,
 ):
     cols = head_ref.shape[2]
@@ -158,10 +158,14 @@
     land_columns(
         table_ref, tab_ref, factor_ref, head_ref, soil_ref, forcing_ref, slot_ref, source_ref, flux_ref, places
     )
-    for whole_ref, piece_ref in ((source_ref, some_ref), (flux_ref, part_ref)):
-        for k in range(whole_ref.shape[0]):
-            whole_ref[k, :, 0:LANES] = piece_ref[k, :, 0:LANES]
-            whole_ref[k, :, cols - LANES : cols] = piece_ref[k, :, LANES : 2 * LANES]
+    put_edges(source_ref, some_ref)
+
+
+def put_edges(whole_ref, piece_ref):
+    cols = whole_ref.shape[2]
+    for k in range(whole_ref.shape[0]):
+        whole_ref[k, :, 0:LANES] = piece_ref[k, :, 0:LANES]
+        whole_ref[k, :, cols - LANES : cols] = piece_ref[k, :, LANES : 2 * LANES]
 
 
 def land_columns(
@@ -685,8 +689,14 @@
     powers((p0_ref, p1_ref, p2_ref), [plain(ref) for ref in coefs], (rows, cols), gram_ref)
 
 
-def last_kernel(arrived_ref, part_ref, q0_ref, q1_ref, q2_ref, head_ref):
+def last_kernel(
+    arrived_ref, part_ref, q0_ref, q1_ref, q2_ref, inner_ref, piece_ref, head_ref, flux_ref
+):
     layers, rows, cols = part_ref.shape
+    middle = slice(LANES, cols - LANES)
+    for n in range(flux_ref.shape[0]):
+        flux_ref[n, :, middle] = inner_ref[n, :, middle]
+    put_edges(flux_ref, piece_ref)
     x = solve(arrived_ref)
     for k in range(layers):
         own = (k, slice(0, rows), slice(0, cols))
@@ -733,7 +743,7 @@
     near, far = exchange(to_near, to_far, "gx")
     columns = (head_old, soil_type, forcing, column_slot)
     table = ((devices // 2, -(-layers // 2) + 1, 8, LANES), jnp.int32)
-    some, flux, tab, factor = call(
+    some, piece, tab, factor = call(
         edge_source_kernel,
         [((layers, rows, 2 * LANES), f32), ((2, rows, 2 * LANES), f32), table, ((devices // 2, 8, LANES), f32)],
         6,
@@ -741,9 +751,10 @@
     )(soil_table, arrived, *columns)
     to_near, to_far = call(strip_kernel, [((3, rows, LANES), f32)] * 2, 3)(head_old, soil_type, some)
     ynear, yfar = exchange(to_near, to_far, "gy")
-    source, flux = call(
-        inner_source_kernel, [own, ((2, rows, cols), f32)], 9, in_specs=[smem] + [vmem] * 8
-    )(soil_table, tab, factor, *columns, some, flux)
+    both_fluxes = ((2, rows, cols), f32)
+    source, inner = call(inner_source_kernel, [own, both_fluxes], 8, in_specs=[smem] + [vmem] * 7)(
+        soil_table, tab, factor, *columns, some
+    )
     to_near, to_far = call(source_edge_kernel, [edge(SOURCE_DEPTH * layers + HALO + HALO // 2)] * 2, 3)(
         source, ynear, yfar
     )
@@ -770,7 +781,7 @@
         scratch=[pltpu.VMEM((layers, rows + HALO, wide), f32)] * 12,
     )(sums, old, ks, steep, cap, old_s, ks_s, steep_s, cap_s, base, p0, p1, p2)
     sums = spread(gram, both)
-    (head,) = call(last_kernel, [own], 5)(sums, part, q0, q1, q2)
+    head, flux = call(last_kernel, [own, both_fluxes], 7)(sums, part, q0, q1, q2, inner, piece)
     return head, flux
 
 

time: 63.6 us -> 63.7 us (level)
  transfers between devices with their start and end apart: 7 -> 7, of which waited for: 2 -> 2; matrix products, arithmetic and copies ran while one was open for 0% -> 0% of each run, Pallas kernels for 13% -> 12%
where the time goes in v14:
time: 63.7 us; the launch traced here: 63.4 us
  blocking collectives  23.7 us (37%)
  Pallas kernels  19.2 us (30%)
  starting transfers between devices  12 us (19%)
  waiting for transfers between devices  7.72 us (12%)
  between operations  0.81 us (1%)
    all_to_all x2, blocking collectives, spread(): return lax.all_to_all(x, axes, split_axis=0, concat_axis=0, tiled=True)  23.7 us
    all_to_all x1, starting transfers between devices, spread(): return lax.all_to_all(x, axes, split_axis=0, concat_axis=0, tiled=True)  7.3 us
    all_to_all x1, waiting for transfers between devices, spread(): return lax.all_to_all(x, axes, split_axis=0, concat_axis=0, tiled=True)  5.81 us
    pallas_call x1, Pallas kernels, shards(): call(first_kernel, [side_block] * 4 + [ext] * 4 + [gram_block], 19, scrat...  4.68 us
    ppermute x6, starting transfers between devices, exchange(): lax.ppermute(x, axis, pairs + [(j, i) for i, j in pairs])  4.67 us
    pallas_call x1, Pallas kernels, shards(): call(second_kernel, [own] + [((layers, rows + HALO, wide), f32)] * 3 + [g...  3.91 us
    pallas_call x1, Pallas kernels, shards(): call(pack_kernel, [((devices, 8, LANES), f32)] + [edge(2 * STATE_DEPTH *...  2.12 us
    pallas_call x1, Pallas kernels, shards(): call(state_kernel, [main] * 8, 5, in_specs=[smem] + [vmem] * 4)  1.98 us
  transfers between devices with their start and end apart: 7, of which 2 were waited for; matrix products, arithmetic and copies ran while one was open for 0% of the time, Pallas kernels for 12%

profile of v14, /device:TPU:0, one launch (start us, length us, event | category | flops | bytes accessed | tf_op | source)
XLA Modules:
  0.0 63.4 jit_solution(1956901583736317823)
XLA Ops:
  0.6 0.0 copy-start
  0.6 0.0 copy-start.1
  0.6 2.1 %shard_map.77 = (f32[32,8,128]{2,1,0:T(8,128)}, f32[144,512]{1,0:T(8,128)}, f32[144,512]{1,0:T(8,128)}) custom-call(f32[13,2048]{1,0:T(8,128)} %canopy_hbm.1, f32[10,16,512]{2,1,0:T(8,128)} %head_ref.7, s32[10,16,512]{2,1,0:T(8,128)} %soil_ref.7), custom_call_target="tpu_custom_call" | custom-call | flops 1000000 | bytes 1000000 | tf_op jit(solution)/shard_map/pallas_call | solution.py:729
  2.8 0.0 copy-start.2
  2.8 0.0 copy-start.3
  2.8 7.3 %all-to-all-start = ((f32[32,8,128]{2,1,0:T(8,128)}), f32[32,8,128]{2,1,0:T(8,128)S(1)}, u32[]{:S(2)}, u32[]{:S(2)}) async-start(f32[32,8,128]{2,1,0:T(8,128)} %get-tuple-element.45), calls=%async_computation | async-start | bytes 262144 | tf_op jit(solution)/shard_map/all_to_all | solution.py:724
  10.1 0.0 copy-start.4
  10.1 1.8 %collective-permute-start.4 = (f32[144,512]{1,0:T(8,128)}, f32[144,512]{1,0:T(8,128)S(1)}, u32[]{:S(2)}, u32[]{:S(2)}) collective-permute-start(f32[144,512]{1,0:T(8,128)} %get-tuple-element.54), channel_id=1, source_target_pairs={{0,4},{8,12},{16,20},{24,28},{4,0},{12,8},{20,16},{28,24},{1,5},{9... | collective-permute-start | bytes 884744 | tf_op jit(solution)/shard_map/ppermute | solution.py:719
  12.0 0.7 %collective-permute-start.5 = (f32[144,512]{1,0:T(8,128)}, f32[144,512]{1,0:T(8,128)S(1)}, u32[]{:S(2)}, u32[]{:S(2)}) collective-permute-start(f32[144,512]{1,0:T(8,128)} %get-tuple-element.55), channel_id=1, source_target_pairs={{4,8},{12,16},{20,24},{8,4},{16,12},{24,20},{5,9},{13,17},{21,25},... | collective-permute-start | bytes 884744 | tf_op jit(solution)/shard_map/ppermute | solution.py:719
  12.6 5.8 %all-to-all-done.arrived_ref = f32[32,8,128]{2,1,0:T(8,128)S(1)} async-done(((f32[32,8,128]{2,1,0:T(8,128)}), f32[32,8,128]{2,1,0:T(8,128)S(1)}, u32[]{:S(2)}, u32[]{:S(2)}) %all-to-all-start) | async-done | bytes 131104 | tf_op jit(solution)/shard_map/all_to_all | solution.py:724
  18.4 0.0 copy-done.2
  18.5 1.8 %shard_map.78 = (f32[10,16,256]{2,1,0:T(8,128)S(1)}, f32[2,16,256]{2,1,0:T(8,128)S(1)}, s32[16,6,8,128]{3,2,1,0:T(8,128)S(1)}, f32[16,8,128]{2,1,0:T(8,128)S(1)}) custom-call(f32[3,12]{1,0:T(4,128)S(1)} %copy-done.4, f32[32,8,128]{2,1,0:T(8,128)S(1)} %all-to-all-done.arrived_ref, f32[10,16,512]{2,1,0:T(8,128)S(1)} %copy-done, s32[10,16,512]{2,1,0:T(8,128)S(1)} %copy-done.1, ...), custom_call_target="tpu_custom_call" | custom-call | flops 1000000 | bytes 1000000 | tf_op jit(solution)/shard_map/pallas_call | solution.py:746
  20.3 0.2 shard_map.80
  20.5 0.2 collective-permute-start
  20.7 0.7 %collective-permute-start.1 = (f32[3,16,128]{2,1,0:T(8,128)S(1)}, f32[3,16,128]{2,1,0:T(8,128)S(1)}, u32[]{:S(2)}, u32[]{:S(2)}) collective-permute-start(f32[3,16,128]{2,1,0:T(8,128)S(1)} %get-tuple-element.51), channel_id=1, source_target_pairs={{1,2},{2,1},{5,6},{6,5},{9,10},{10,9},{13,14},{14,13},{17,18},{18,... | collective-permute-start | bytes 73736 | tf_op jit(solution)/shard_map/ppermute | solution.py:719
  21.3 1.5 %shard_map.79 = (f32[10,16,512]{2,1,0:T(8,128)S(1)}, f32[2,16,512]{2,1,0:T(8,128)S(1)}) custom-call(f32[3,12]{1,0:T(4,128)S(1)} %copy-done.4, s32[16,6,8,128]{3,2,1,0:T(8,128)S(1)} %get-tuple-element.46.tab_ref, f32[16,8,128]{2,1,0:T(8,128)S(1)} %get-tuple-element.47.factor_ref, f32[10,16,512]{2,1,0:T(8,128)S(1)} %copy-done, s32[10,16,512]{2,1,0:T(8,128)S(1)} %copy-done.1, ...), custom_call_target="tpu_custom_call" | custom-call | flops 1000000 | bytes 1000000 | tf_op jit(solution)/shard_map/pallas_call | solution.py:755
  22.9 0.0 collective-permute-done.ynear_ref
  22.9 0.0 collective-permute-done.1.yfar_ref
  22.9 0.1 shard_map.81
  23.0 0.7 %collective-permute-start.2 = (f32[72,512]{1,0:T(8,128)S(1)}, f32[72,512]{1,0:T(8,128)S(1)}, u32[]{:S(2)}, u32[]{:S(2)}) collective-permute-start(f32[72,512]{1,0:T(8,128)S(1)} %get-tuple-element.52), channel_id=1, source_target_pairs={{0,4},{8,12},{16,20},{24,28},{4,0},{12,8},{20,16},{28,24},{1,5},{9... | collective-permute-start | bytes 442376 | tf_op jit(solution)/shard_map/ppermute | solution.py:719
  23.7 0.7 %collective-permute-start.3 = (f32[72,512]{1,0:T(8,128)S(1)}, f32[72,512]{1,0:T(8,128)S(1)}, u32[]{:S(2)}, u32[]{:S(2)}) collective-permute-start(f32[72,512]{1,0:T(8,128)S(1)} %get-tuple-element.53), channel_id=1, source_target_pairs={{4,8},{12,16},{20,24},{8,4},{16,12},{24,20},{5,9},{13,17},{21,25},... | collective-permute-start | bytes 442376 | tf_op jit(solution)/shard_map/ppermute | solution.py:719
  24.3 1.9 %collective-permute-done.4.near_ref = f32[144,512]{1,0:T(8,128)S(1)} collective-permute-done((f32[144,512]{1,0:T(8,128)}, f32[144,512]{1,0:T(8,128)S(1)}, u32[]{:S(2)}, u32[]{:S(2)}) %collective-permute-start.4) | collective-permute-done | bytes 294944 | tf_op jit(solution)/shard_map/ppermute | solution.py:719
  26.2 0.0 collective-permute-done.5.far_ref
  26.2 2.0 %shard_map.82 = (f32[10,32,512]{2,1,0:T(8,128)S(1)}, f32[10,32,512]{2,1,0:T(8,128)S(1)}, f32[10,32,512]{2,1,0:T(8,128)S(1)}, f32[10,32,512]{2,1,0:T(8,128)S(1)},...) custom-call(f32[3,12]{1,0:T(4,128)S(1)} %copy-done.4, ...), custom_call_target="tpu_custom_call" | custom-call | flops 1000000 | bytes 1000000 | tf_op jit(solution)/shard_map/pallas_call | solution.py:763
  28.2 1.8 %shard_map.83 = (f32[10,32,512]{2,1,0:T(8,128)S(1)}, f32[10,32,512]{2,1,0:T(8,128)S(1)}, f32[10,32,512]{2,1,0:T(8,128)S(1)}, f32[10,32,512]{2,1,0:T(8,128)S(1)},...) custom-call(f32[10,32,512]{2,1,0:T(8,128)S(1)} %get-tuple-element.56, ...), custom_call_target="tpu_custom_call" | custom-call | flops 1000000 | bytes 1000000 | tf_op jit(solution)/shard_map/pallas_call | solution.py:766
  30.0 0.0 collective-permute-done.2.snear_ref
  30.0 0.0 collective-permute-done.3.sfar_ref
  30.0 4.7 %shard_map.84 = (f32[10,32,128]{2,1,0:T(8,128)S(1)}, f32[10,32,128]{2,1,0:T(8,128)S(1)}, f32[10,32,128]{2,1,0:T(8,128)S(1)}, f32[10,32,128]{2,1,0:T(8,128)S(1)},...) custom-call(f32[3,12]{1,0:T(4,128)S(1)} %copy-done.4, ...), custom_call_target="tpu_custom_call" | custom-call | flops 1000000 | bytes 1000000 | tf_op jit(solution)/shard_map/pallas_call | solution.py:769
  34.7 14.8 %all_to_all.15.arrived_ref = f32[32,1,128]{2,1,0:T(1,128)S(1)} all-to-all(f32[32,1,128]{2,1,0:T(1,128)S(1)} %get-tuple-element.70), channel_id=1, replica_groups=mesh['gx'=8,'gy'=4] {'gx','gy'}, dimensions={0} | all-to-all | bytes 32768 | tf_op jit(solution)/shard_map/all_to_all | solution.py:724
  49.6 3.9 %shard_map.85 = (f32[10,16,512]{2,1,0:T(8,128)S(1)}, f32[10,24,640]{2,1,0:T(8,128)S(1)}, f32[10,24,640]{2,1,0:T(8,128)S(1)}, f32[10,24,640]{2,1,0:T(8,128)S(1)}, f32[32,1,128]{2,1,0:T(1,128)S(1)}) custom-call(f32[32,1,128]{2,1,0:T(1,128)S(1)} %all_to_all.15.arrived_ref, f32[10,32,512]{2,1,0:T(8,128)S(1)} %get-tuple-element.56.ext_ref.old_ref, ...), custom_call_target="tpu_custom_call" | custom-call | flops 1000000 | bytes 1000000 | tf_op jit(solution)/shard_map/pallas_call | solution.py:777
  53.5 8.8 %all_to_all.16.arrived_ref = f32[32,1,128]{2,1,0:T(1,128)S(1)} all-to-all(f32[32,1,128]{2,1,0:T(1,128)S(1)} %get-tuple-element.81), channel_id=1, replica_groups=mesh['gx'=8,'gy'=4] {'gx','gy'}, dimensions={0} | all-to-all | bytes 32768 | tf_op jit(solution)/shard_map/all_to_all | solution.py:724
  62.3 1.1 %shard_map.86 = (f32[10,16,512]{2,1,0:T(8,128)}, f32[2,16,512]{2,1,0:T(8,128)}) custom-call(f32[32,1,128]{2,1,0:T(1,128)S(1)} %all_to_all.16.arrived_ref, f32[10,16,512]{2,1,0:T(8,128)S(1)} %get-tuple-element.82.part_ref, f32[10,24,640]{2,1,0:T(8,128)S(1)} %get-tuple-element.83.q0_ref, f32[10,24,640]{2,1,0:T(8,128)S(1)} %get-tuple-element.84.q1_ref, ...), custom_call_target="tpu_custom_call" | custom-call | flops 1000000 | bytes 1000000 | tf_op jit(solution)/shard_map/pallas_call | solution.py:784
  (4 shorter events, 0.0 us)
Async XLA Ops:
  0.6 17.8 %copy-start = (f32[10,16,512]{2,1,0:T(8,128)S(1)}, f32[10,16,512]{2,1,0:T(8,128)}, u32[]{:S(2)}) copy-start(f32[10,16,512]{2,1,0:T(8,128)} %head_ref.7) | copy-start | bytes 983044
  0.6 17.8 %copy-start.1 = (s32[10,16,512]{2,1,0:T(8,128)S(1)}, s32[10,16,512]{2,1,0:T(8,128)}, u32[]{:S(2)}) copy-start(s32[10,16,512]{2,1,0:T(8,128)} %soil_ref.7) | copy-start | bytes 983044
  2.8 15.7 %copy-start.2 = (f32[4,16,512]{2,1,0:T(8,128)S(1)}, f32[4,16,512]{2,1,0:T(8,128)}, u32[]{:S(2)}) copy-start(f32[4,16,512]{2,1,0:T(8,128)} %forcing_ref.3) | copy-start | bytes 393220
  2.8 15.7 %copy-start.3 = (s32[16,512]{1,0:T(8,128)S(1)}, s32[16,512]{1,0:T(8,128)}, u32[]{:S(2)}) copy-start(s32[16,512]{1,0:T(8,128)} %slot_ref.3) | copy-start | bytes 98308
  2.8 15.6 %all-to-all-start = ((f32[32,8,128]{2,1,0:T(8,128)}), f32[32,8,128]{2,1,0:T(8,128)S(1)}, u32[]{:S(2)}, u32[]{:S(2)}) async-start(f32[32,8,128]{2,1,0:T(8,128)} %get-tuple-element.45), calls=%async_computation | async-start | bytes 262144 | tf_op jit(solution)/shard_map/all_to_all | solution.py:724
  10.1 8.4 %copy-start.4 = (f32[3,12]{1,0:T(4,128)S(1)}, f32[3,12]{1,0:T(4,128)}, u32[]{:S(2)}) copy-start(f32[3,12]{1,0:T(4,128)} %table_ref.7) | copy-start | bytes 436
  10.1 16.1 %collective-permute-start.4 = (f32[144,512]{1,0:T(8,128)}, f32[144,512]{1,0:T(8,128)S(1)}, u32[]{:S(2)}, u32[]{:S(2)}) collective-permute-start(f32[144,512]{1,0:T(8,128)} %get-tuple-element.54), channel_id=1, source_target_pairs={{0,4},{8,12},{16,20},{24,28},{4,0},{12,8},{20,16},{28,24},{1,5},{9... | collective-permute-start | bytes 884744 | tf_op jit(solution)/shard_map/ppermute | solution.py:719
  12.0 14.3 %collective-permute-start.5 = (f32[144,512]{1,0:T(8,128)}, f32[144,512]{1,0:T(8,128)S(1)}, u32[]{:S(2)}, u32[]{:S(2)}) collective-permute-start(f32[144,512]{1,0:T(8,128)} %get-tuple-element.55), channel_id=1, source_target_pairs={{4,8},{12,16},{20,24},{8,4},{16,12},{24,20},{5,9},{13,17},{21,25},... | collective-permute-start | bytes 884744 | tf_op jit(solution)/shard_map/ppermute | solution.py:719
  20.5 2.4 %collective-permute-start = (f32[3,16,128]{2,1,0:T(8,128)S(1)}, f32[3,16,128]{2,1,0:T(8,128)S(1)}, u32[]{:S(2)}, u32[]{:S(2)}) collective-permute-start(f32[3,16,128]{2,1,0:T(8,128)S(1)} %get-tuple-element.50), channel_id=1, source_target_pairs={{0,1},{2,3},{1,0},{3,2},{4,5},{6,7},{5,4},{7,6},{8,9},{10,11},{9,8... | collective-permute-start | bytes 73736 | tf_op jit(solution)/shard_map/ppermute | solution.py:719
  20.7 2.2 %collective-permute-start.1 = (f32[3,16,128]{2,1,0:T(8,128)S(1)}, f32[3,16,128]{2,1,0:T(8,128)S(1)}, u32[]{:S(2)}, u32[]{:S(2)}) collective-permute-start(f32[3,16,128]{2,1,0:T(8,128)S(1)} %get-tuple-element.51), channel_id=1, source_target_pairs={{1,2},{2,1},{5,6},{6,5},{9,10},{10,9},{13,14},{14,13},{17,18},{18,... | collective-permute-start | bytes 73736 | tf_op jit(solution)/shard_map/ppermute | solution.py:719
  23.0 7.0 %collective-permute-start.2 = (f32[72,512]{1,0:T(8,128)S(1)}, f32[72,512]{1,0:T(8,128)S(1)}, u32[]{:S(2)}, u32[]{:S(2)}) collective-permute-start(f32[72,512]{1,0:T(8,128)S(1)} %get-tuple-element.52), channel_id=1, source_target_pairs={{0,4},{8,12},{16,20},{24,28},{4,0},{12,8},{20,16},{28,24},{1,5},{9... | collective-permute-start | bytes 442376 | tf_op jit(solution)/shard_map/ppermute | solution.py:719
  23.7 6.4 %collective-permute-start.3 = (f32[72,512]{1,0:T(8,128)S(1)}, f32[72,512]{1,0:T(8,128)S(1)}, u32[]{:S(2)}, u32[]{:S(2)}) collective-permute-start(f32[72,512]{1,0:T(8,128)S(1)} %get-tuple-element.53), channel_id=1, source_target_pairs={{4,8},{12,16},{20,24},{8,4},{16,12},{24,20},{5,9},{13,17},{21,25},... | collective-permute-start | bytes 442376 | tf_op jit(solution)/shard_map/ppermute | solution.py:719

commit v15 on v14

--- a/solution.py
+++ b/solution.py
@@ -72,6 +72,10 @@
         part = slice(STATE_DEPTH * n, STATE_DEPTH * (n + 1))
         near_ref[part] = jnp.where(upward, plane[high_rows], plane[low_rows])
         far_ref[part] = jnp.where(upward, plane[low_rows], plane[high_rows])
+
+
+def pass_kernel(*_):
+    pass
 
 
 def near_is_above(axis):
@@ -711,14 +715,12 @@
     own, ext = ((layers, rows, cols), f32), ((layers, tall, wide), f32)
     gram_block = ((devices, 1, LANES), f32)
 
+    def to_partner(x, axis, first):
+        pairs = [(i, i + 1) for i in range(first, lax.axis_size(axis) - 1, 2)]
+        return lax.ppermute(x, axis, pairs + [(j, i) for i, j in pairs])
+
     def exchange(to_near, to_far, axis):
-        size = lax.axis_size(axis)
-        near = [(i, i + 1) for i in range(0, size - 1, 2)]
-        far = [(i, i + 1) for i in range(1, size - 1, 2)]
-        return tuple(
-            lax.ppermute(x, axis, pairs + [(j, i) for i, j in pairs])
-            for x, pairs in ((to_near, near), (to_far, far))
-        )
+        return to_partner(to_near, axis, 0), to_partner(to_far, axis, 1)
 
     def spread(x, axes):
         return lax.all_to_all(x, axes, split_axis=0, concat_axis=0, tiled=True)
@@ -739,8 +741,19 @@
         in_specs=[pl.BlockSpec(memory_space=pl.ANY)] * 3,
         grant=63400000,
     )(canopy, head_old, soil_type)
+    near = to_partner(to_near, "gx", 0)
+    anywhere = pl.BlockSpec(memory_space=pl.ANY)
+    send, to_far = pl.pallas_call(
+        pass_kernel,
+        out_shape=[jax.ShapeDtypeStruct(x.shape, x.dtype) for x in (send, to_far)],
+        in_specs=[anywhere] * 2,
+        out_specs=[anywhere] * 2,
+        input_output_aliases={0: 0, 1: 1},
+        compiler_params=pltpu.CompilerParams(vmem_limit_bytes=63400000),
+        cost_estimate=pl.CostEstimate(flops=1000000000, bytes_accessed=1000000, transcendentals=0),
+    )(send, to_far)
     arrived = spread(send, both)
-    near, far = exchange(to_near, to_far, "gx")
+    far = to_partner(to_far, "gx", 1)
     columns = (head_old, soil_type, forcing, column_slot)
     table = ((devices // 2, -(-layers // 2) + 1, 8, LANES), jnp.int32)
     some, piece, tab, factor = call(

time: 63.7 us -> 66.2 us (1.039)
  starting transfers between devices: 12 us -> 14.6 us
  blocking collectives: 23.7 us -> 21.9 us
  waiting for transfers between devices: 7.72 us -> 9.41 us
    ppermute x6, waiting for transfers between devices: 1.91 us -> 6.31 us  [to_partner(): return lax.ppermute(x, axis, pairs + [(j, i) for i, j in pairs])]
    all_to_all x1, waiting for transfers between devices: 5.81 us -> 3.1 us  [spread(): return lax.all_to_all(x, axes, split_axis=0, concat_axis=0, tiled=True)]
    ppermute x6, starting transfers between devices: 4.67 us -> 7.34 us  [to_partner(): return lax.ppermute(x, axis, pairs + [(j, i) for i, j in pairs])]
    all_to_all x2, blocking collectives: 23.7 us -> 21.9 us  [spread(): return lax.all_to_all(x, axes, split_axis=0, concat_axis=0, tiled=True)]
  transfers between devices with their start and end apart: 7 -> 7, of which waited for: 2 -> 3; matrix products, arithmetic and copies ran while one was open for 0% -> 0% of each run, Pallas kernels for 12% -> 11%
where the time goes in v15:
time: 66.2 us; the launch traced here: 65.9 us
  blocking collectives  21.9 us (33%)
  Pallas kernels  19.1 us (29%)
  starting transfers between devices  14.6 us (22%)
  waiting for transfers between devices  9.41 us (14%)
  between operations  0.83 us (1%)
    all_to_all x2, blocking collectives, spread(): return lax.all_to_all(x, axes, split_axis=0, concat_axis=0, tiled=True)  21.9 us
    ppermute x6, starting transfers between devices, to_partner(): return lax.ppermute(x, axis, pairs + [(j, i) for i, j in pairs])  7.34 us
    all_to_all x1, starting transfers between devices, spread(): return lax.all_to_all(x, axes, split_axis=0, concat_axis=0, tiled=True)  7.3 us
    ppermute x6, waiting for transfers between devices, to_partner(): return lax.ppermute(x, axis, pairs + [(j, i) for i, j in pairs])  6.31 us
    pallas_call x1, Pallas kernels, shards(): call(first_kernel, [side_block] * 4 + [ext] * 4 + [gram_block], 19, scrat...  4.66 us
    pallas_call x1, Pallas kernels, shards(): call(second_kernel, [own] + [((layers, rows + HALO, wide), f32)] * 3 + [g...  3.91 us
    all_to_all x1, waiting for transfers between devices, spread(): return lax.all_to_all(x, axes, split_axis=0, concat_axis=0, tiled=True)  3.1 us
    pallas_call x1, Pallas kernels, shards(): call(pack_kernel, [((devices, 8, LANES), f32)] + [edge(2 * STATE_DEPTH *...  2.06 us
  transfers between devices with their start and end apart: 7, of which 3 were waited for; matrix products, arithmetic and copies ran while one was open for 0% of the time, Pallas kernels for 11%

profile of v15, /device:TPU:0, one launch (start us, length us, event | category | flops | bytes accessed | tf_op | source)
XLA Modules:
  0.0 65.9 jit_solution(12340245256849104530)
XLA Ops:
  0.6 2.1 %shard_map.77 = (f32[32,8,128]{2,1,0:T(8,128)}, f32[144,512]{1,0:T(8,128)}, f32[144,512]{1,0:T(8,128)}) custom-call(f32[13,2048]{1,0:T(8,128)} %canopy_hbm.1, f32[10,16,512]{2,1,0:T(8,128)} %head_ref.7, s32[10,16,512]{2,1,0:T(8,128)} %soil_ref.7), custom_call_target="tpu_custom_call" | custom-call | flops 1000000 | bytes 1000000 | tf_op jit(solution)/shard_map/pallas_call | solution.py:731
  2.7 0.0 copy-start.5
  2.7 0.0 copy-start
  2.7 0.0 copy-start.1
  2.7 0.0 copy-start.2
  2.8 0.0 copy-start.3
  2.8 7.3 %all-to-all-start = ((f32[32,8,128]{2,1,0:T(8,128)}), f32[32,8,128]{2,1,0:T(8,128)S(1)}, u32[]{:S(2)}, u32[]{:S(2)}) async-start(f32[32,8,128]{2,1,0:T(8,128)} %get-tuple-element.49), calls=%async_computation | async-start | bytes 262144 | tf_op jit(solution)/shard_map/all_to_all | solution.py:726
  10.1 0.0 copy-start.4
  10.1 0.7 %collective-permute-start.5 = (f32[144,512]{1,0:T(8,128)}, f32[144,512]{1,0:T(8,128)S(1)}, u32[]{:S(2)}, u32[]{:S(2)}) collective-permute-start(f32[144,512]{1,0:T(8,128)} %get-tuple-element.59), channel_id=1, source_target_pairs={{4,8},{12,16},{20,24},{8,4},{16,12},{24,20},{5,9},{13,17},{21,25},... | collective-permute-start | bytes 884744 | tf_op jit(solution)/shard_map/ppermute | solution.py:720
  10.8 4.5 %collective-permute-start.4 = (f32[144,512]{1,0:T(8,128)S(1)}, f32[144,512]{1,0:T(8,128)S(1)}, u32[]{:S(2)}, u32[]{:S(2)}) collective-permute-start(f32[144,512]{1,0:T(8,128)S(1)} %copy-done.5), channel_id=1, source_target_pairs={{0,4},{8,12},{16,20},{24,28},{4,0},{12,8},{20,16},{28,24},{1,5},{9... | collective-permute-start | bytes 884744 | tf_op jit(solution)/shard_map/ppermute | solution.py:720
  15.3 3.1 %all-to-all-done.arrived_ref = f32[32,8,128]{2,1,0:T(8,128)S(1)} async-done(((f32[32,8,128]{2,1,0:T(8,128)}), f32[32,8,128]{2,1,0:T(8,128)S(1)}, u32[]{:S(2)}, u32[]{:S(2)}) %all-to-all-start) | async-done | bytes 131104 | tf_op jit(solution)/shard_map/all_to_all | solution.py:726
  18.4 1.8 %shard_map.79 = (f32[10,16,256]{2,1,0:T(8,128)S(1)}, f32[2,16,256]{2,1,0:T(8,128)S(1)}, s32[16,6,8,128]{3,2,1,0:T(8,128)S(1)}, f32[16,8,128]{2,1,0:T(8,128)S(1)}) custom-call(f32[3,12]{1,0:T(4,128)S(1)} %copy-done.4, f32[32,8,128]{2,1,0:T(8,128)S(1)} %all-to-all-done.arrived_ref, f32[10,16,512]{2,1,0:T(8,128)S(1)} %copy-done, s32[10,16,512]{2,1,0:T(8,128)S(1)} %copy-done.1, ...), custom_call_target="tpu_custom_call" | custom-call | flops 1000000 | bytes 1000000 | tf_op jit(solution)/shard_map/pallas_call | solution.py:759
  20.3 0.2 shard_map.81
  20.5 0.2 collective-permute-start
  20.7 0.7 collective-permute-start.1
  21.3 1.5 %shard_map.80 = (f32[10,16,512]{2,1,0:T(8,128)S(1)}, f32[2,16,512]{2,1,0:T(8,128)S(1)}) custom-call(f32[3,12]{1,0:T(4,128)S(1)} %copy-done.4, s32[16,6,8,128]{3,2,1,0:T(8,128)S(1)} %get-tuple-element.50.tab_ref, f32[16,8,128]{2,1,0:T(8,128)S(1)} %get-tuple-element.51.factor_ref, f32[10,16,512]{2,1,0:T(8,128)S(1)} %copy-done, s32[10,16,512]{2,1,0:T(8,128)S(1)} %copy-done.1, ...), custom_call_target="tpu_custom_call" | custom-call | flops 1000000 | bytes 1000000 | tf_op jit(solution)/shard_map/pallas_call | solution.py:768
  22.9 0.0 collective-permute-done.ynear_ref
  22.9 0.0 collective-permute-done.1.yfar_ref
  22.9 0.1 shard_map.82
  23.0 0.6 collective-permute-start.2
  23.6 0.7 collective-permute-start.3
  24.3 0.0 collective-permute-done.5.far_ref
  24.3 3.9 %collective-permute-done.4.near_ref = f32[144,512]{1,0:T(8,128)S(1)} collective-permute-done((f32[144,512]{1,0:T(8,128)S(1)}, f32[144,512]{1,0:T(8,128)S(1)}, u32[]{:S(2)}, u32[]{:S(2)}) %collective-permute-start.4) | collective-permute-done | bytes 294944 | tf_op jit(solution)/shard_map/ppermute | solution.py:720
  28.1 2.0 %shard_map.83 = (f32[10,32,512]{2,1,0:T(8,128)S(1)}, f32[10,32,512]{2,1,0:T(8,128)S(1)}, f32[10,32,512]{2,1,0:T(8,128)S(1)}, f32[10,32,512]{2,1,0:T(8,128)S(1)},...) custom-call(f32[3,12]{1,0:T(4,128)S(1)} %copy-done.4, ...), custom_call_target="tpu_custom_call" | custom-call | flops 1000000 | bytes 1000000 | tf_op jit(solution)/shard_map/pallas_call | solution.py:776
  30.1 1.8 %shard_map.84 = (f32[10,32,512]{2,1,0:T(8,128)S(1)}, f32[10,32,512]{2,1,0:T(8,128)S(1)}, f32[10,32,512]{2,1,0:T(8,128)S(1)}, f32[10,32,512]{2,1,0:T(8,128)S(1)},...) custom-call(f32[10,32,512]{2,1,0:T(8,128)S(1)} %get-tuple-element.60, ...), custom_call_target="tpu_custom_call" | custom-call | flops 1000000 | bytes 1000000 | tf_op jit(solution)/shard_map/pallas_call | solution.py:779
  31.9 2.4 %collective-permute-done.2.snear_ref = f32[72,512]{1,0:T(8,128)S(1)} collective-permute-done((f32[72,512]{1,0:T(8,128)S(1)}, f32[72,512]{1,0:T(8,128)S(1)}, u32[]{:S(2)}, u32[]{:S(2)}) %collective-permute-start.2) | collective-permute-done | bytes 147488 | tf_op jit(solution)/shard_map/ppermute | solution.py:720
  34.4 0.0 collective-permute-done.3.sfar_ref
  34.4 4.7 %shard_map.85 = (f32[10,32,128]{2,1,0:T(8,128)S(1)}, f32[10,32,128]{2,1,0:T(8,128)S(1)}, f32[10,32,128]{2,1,0:T(8,128)S(1)}, f32[10,32,128]{2,1,0:T(8,128)S(1)},...) custom-call(f32[3,12]{1,0:T(4,128)S(1)} %copy-done.4, ...), custom_call_target="tpu_custom_call" | custom-call | flops 1000000 | bytes 1000000 | tf_op jit(solution)/shard_map/pallas_call | solution.py:782
  39.0 13.1 %all_to_all.15.arrived_ref = f32[32,1,128]{2,1,0:T(1,128)S(1)} all-to-all(f32[32,1,128]{2,1,0:T(1,128)S(1)} %get-tuple-element.74), channel_id=1, replica_groups=mesh['gx'=8,'gy'=4] {'gx','gy'}, dimensions={0} | all-to-all | bytes 32768 | tf_op jit(solution)/shard_map/all_to_all | solution.py:726
  52.1 3.9 %shard_map.86 = (f32[10,16,512]{2,1,0:T(8,128)S(1)}, f32[10,24,640]{2,1,0:T(8,128)S(1)}, f32[10,24,640]{2,1,0:T(8,128)S(1)}, f32[10,24,640]{2,1,0:T(8,128)S(1)}, f32[32,1,128]{2,1,0:T(1,128)S(1)}) custom-call(f32[32,1,128]{2,1,0:T(1,128)S(1)} %all_to_all.15.arrived_ref, f32[10,32,512]{2,1,0:T(8,128)S(1)} %get-tuple-element.60.ext_ref.old_ref, ...), custom_call_target="tpu_custom_call" | custom-call | flops 1000000 | bytes 1000000 | tf_op jit(solution)/shard_map/pallas_call | solution.py:790
  56.0 8.8 %all_to_all.16.arrived_ref = f32[32,1,128]{2,1,0:T(1,128)S(1)} all-to-all(f32[32,1,128]{2,1,0:T(1,128)S(1)} %get-tuple-element.85), channel_id=1, replica_groups=mesh['gx'=8,'gy'=4] {'gx','gy'}, dimensions={0} | all-to-all | bytes 32768 | tf_op jit(solution)/shard_map/all_to_all | solution.py:726
  64.9 1.1 %shard_map.87 = (f32[10,16,512]{2,1,0:T(8,128)}, f32[2,16,512]{2,1,0:T(8,128)}) custom-call(f32[32,1,128]{2,1,0:T(1,128)S(1)} %all_to_all.16.arrived_ref, f32[10,16,512]{2,1,0:T(8,128)S(1)} %get-tuple-element.86.part_ref, f32[10,24,640]{2,1,0:T(8,128)S(1)} %get-tuple-element.87.q0_ref, f32[10,24,640]{2,1,0:T(8,128)S(1)} %get-tuple-element.88.q1_ref, ...), custom_call_target="tpu_custom_call" | custom-call | flops 1000000 | bytes 1000000 | tf_op jit(solution)/shard_map/pallas_call | solution.py:797
  (7 shorter events, 0.0 us)
Async XLA Ops:
  2.7 8.1 %copy-start.5 = (f32[144,512]{1,0:T(8,128)S(1)}, f32[144,512]{1,0:T(8,128)}, u32[]{:S(2)}) copy-start(f32[144,512]{1,0:T(8,128)} %get-tuple-element.58) | copy-start | bytes 884740
  2.7 15.7 %copy-start = (f32[10,16,512]{2,1,0:T(8,128)S(1)}, f32[10,16,512]{2,1,0:T(8,128)}, u32[]{:S(2)}) copy-start(f32[10,16,512]{2,1,0:T(8,128)} %head_ref.7) | copy-start | bytes 983044
  2.7 15.7 %copy-start.1 = (s32[10,16,512]{2,1,0:T(8,128)S(1)}, s32[10,16,512]{2,1,0:T(8,128)}, u32[]{:S(2)}) copy-start(s32[10,16,512]{2,1,0:T(8,128)} %soil_ref.7) | copy-start | bytes 983044
  2.7 15.7 %copy-start.2 = (f32[4,16,512]{2,1,0:T(8,128)S(1)}, f32[4,16,512]{2,1,0:T(8,128)}, u32[]{:S(2)}) copy-start(f32[4,16,512]{2,1,0:T(8,128)} %forcing_ref.3) | copy-start | bytes 393220
  2.8 15.7 %copy-start.3 = (s32[16,512]{1,0:T(8,128)S(1)}, s32[16,512]{1,0:T(8,128)}, u32[]{:S(2)}) copy-start(s32[16,512]{1,0:T(8,128)} %slot_ref.3) | copy-start | bytes 98308
  2.8 15.6 %all-to-all-start = ((f32[32,8,128]{2,1,0:T(8,128)}), f32[32,8,128]{2,1,0:T(8,128)S(1)}, u32[]{:S(2)}, u32[]{:S(2)}) async-start(f32[32,8,128]{2,1,0:T(8,128)} %get-tuple-element.49), calls=%async_computation | async-start | bytes 262144 | tf_op jit(solution)/shard_map/all_to_all | solution.py:726
  10.1 8.4 %copy-start.4 = (f32[3,12]{1,0:T(4,128)S(1)}, f32[3,12]{1,0:T(4,128)}, u32[]{:S(2)}) copy-start(f32[3,12]{1,0:T(4,128)} %table_ref.7) | copy-start | bytes 436
  10.1 14.2 %collective-permute-start.5 = (f32[144,512]{1,0:T(8,128)}, f32[144,512]{1,0:T(8,128)S(1)}, u32[]{:S(2)}, u32[]{:S(2)}) collective-permute-start(f32[144,512]{1,0:T(8,128)} %get-tuple-element.59), channel_id=1, source_target_pairs={{4,8},{12,16},{20,24},{8,4},{16,12},{24,20},{5,9},{13,17},{21,25},... | collective-permute-start | bytes 884744 | tf_op jit(solution)/shard_map/ppermute | solution.py:720
  10.8 17.4 %collective-permute-start.4 = (f32[144,512]{1,0:T(8,128)S(1)}, f32[144,512]{1,0:T(8,128)S(1)}, u32[]{:S(2)}, u32[]{:S(2)}) collective-permute-start(f32[144,512]{1,0:T(8,128)S(1)} %copy-done.5), channel_id=1, source_target_pairs={{0,4},{8,12},{16,20},{24,28},{4,0},{12,8},{20,16},{28,24},{1,5},{9... | collective-permute-start | bytes 884744 | tf_op jit(solution)/shard_map/ppermute | solution.py:720
  20.5 2.4 %collective-permute-start = (f32[3,16,128]{2,1,0:T(8,128)S(1)}, f32[3,16,128]{2,1,0:T(8,128)S(1)}, u32[]{:S(2)}, u32[]{:S(2)}) collective-permute-start(f32[3,16,128]{2,1,0:T(8,128)S(1)} %get-tuple-element.54), channel_id=1, source_target_pairs={{0,1},{2,3},{1,0},{3,2},{4,5},{6,7},{5,4},{7,6},{8,9},{10,11},{9,8... | collective-permute-start | bytes 73736 | tf_op jit(solution)/shard_map/ppermute | solution.py:720
  20.7 2.2 %collective-permute-start.1 = (f32[3,16,128]{2,1,0:T(8,128)S(1)}, f32[3,16,128]{2,1,0:T(8,128)S(1)}, u32[]{:S(2)}, u32[]{:S(2)}) collective-permute-start(f32[3,16,128]{2,1,0:T(8,128)S(1)} %get-tuple-element.55), channel_id=1, source_target_pairs={{1,2},{2,1},{5,6},{6,5},{9,10},{10,9},{13,14},{14,13},{17,18},{18,... | collective-permute-start | bytes 73736 | tf_op jit(solution)/shard_map/ppermute | solution.py:720
  23.0 11.4 %collective-permute-start.2 = (f32[72,512]{1,0:T(8,128)S(1)}, f32[72,512]{1,0:T(8,128)S(1)}, u32[]{:S(2)}, u32[]{:S(2)}) collective-permute-start(f32[72,512]{1,0:T(8,128)S(1)} %get-tuple-element.56), channel_id=1, source_target_pairs={{0,4},{8,12},{16,20},{24,28},{4,0},{12,8},{20,16},{28,24},{1,5},{9... | collective-permute-start | bytes 442376 | tf_op jit(solution)/shard_map/ppermute | solution.py:720
  23.6 10.8 %collective-permute-start.3 = (f32[72,512]{1,0:T(8,128)S(1)}, f32[72,512]{1,0:T(8,128)S(1)}, u32[]{:S(2)}, u32[]{:S(2)}) collective-permute-start(f32[72,512]{1,0:T(8,128)S(1)} %get-tuple-element.57), channel_id=1, source_target_pairs={{4,8},{12,16},{20,24},{8,4},{16,12},{24,20},{5,9},{13,17},{21,25},... | collective-permute-start | bytes 442376 | tf_op jit(solution)/shard_map/ppermute | solution.py:720
